TPU v7x, 128 devices: a whole 4x4x4 slice. The times are simulated.
128 devices in a mesh: row: 8 (over y, core), col: 16 (over x, z).
Axes of the slice: x: 4, y: 4, z: 4, core: 2. Of those that a mesh axis runs over, the one named last changes fastest.
Arguments:
- x_paper: bfloat16 [32768, 768], P(('row', 'col')), may hold values from -6 to 6
- x_author: bfloat16 [32768, 768], P(('row', 'col')), may hold values from -6 to 6
- cite_nbr: int32 [32768, 16], P(('row', 'col')), may hold values from -1 to 4095, as said below
- write_src: int32 [128, 128, 4], P(('row', 'col')), may hold values from -1 to 255, as said below
- write_dst: int32 [128, 128, 4], P(('row', 'col')), may hold values from -1 to 255, as said below
- w_self_paper: bfloat16 [768, 1024], replicated, may hold values from -0.21875 to 0.21875
- w_cite: bfloat16 [768, 1024], replicated, may hold values from -0.21875 to 0.21875
- w_write: bfloat16 [768, 1024], replicated, may hold values from -0.21875 to 0.21875
- w_self_author: bfloat16 [768, 1024], replicated, may hold values from -0.21875 to 0.21875
- w_written: bfloat16 [768, 1024], replicated, may hold values from -0.21875 to 0.21875
- grad_paper: bfloat16 [32768, 1024], P(('row', 'col')), may hold values from -24 to 24
- grad_author: bfloat16 [32768, 1024], P(('row', 'col')), may hold values from -24 to 24
Outputs:
- out_paper: bfloat16 [32768, 1024], P(('row', 'col'))
- out_author: bfloat16 [32768, 1024], P(('row', 'col'))
- dx_paper: bfloat16 [32768, 768], P(('row', 'col'))
- dx_author: bfloat16 [32768, 768], P(('row', 'col'))
- dweights: float32 [5, 768, 1024], P(None, 'row', 'col')
Inputs may be any that keep to these rules, and one draw needn't show every extreme that they name: `cite_nbr`: entries of a row that are -1 stand for no citation and come after all others; a value e >= 0 names the paper at position e of the paper's own block row. Some paper has all 16 entries. write_src[s, d, j] is -1 (empty slot) exactly where write_dst[d, s, j] is -1; otherwise it is an author position on device s. Some device d has every slot from every device s filled. write_dst[d, s, j] is -1 exactly where write_src[s, d, j] is -1; otherwise it is a paper position on device d. A paper may have several edges, also from one author.
All inputs are finite; a program needn't handle non-finite values.
Results may differ from a plain program's by a relative error of at most 0.0054.
Values may be sent and summed in bfloat16 or wider, within the bound.
No kernel may reach another device: no remote copies, remote signals or barrier semaphores. Data moves between devices by JAX's collectives and lax.ppermute only.
A program may use at most 192 MiB of HBM per device.

v0:
```python
import jax
import jax.numpy as jnp
from jax import lax
from jax.sharding import PartitionSpec as P


def match_table(entries, columns):
    accum = jnp.zeros((entries.shape[0], columns.shape[0]), jnp.float32)
    for slot in range(entries.shape[1]):
        accum = accum + (entries[:, slot : slot + 1] == columns[None, :]).astype(jnp.float32)
    return accum.astype(jnp.bfloat16)


def select_rows(values, positions):
    live = (positions >= 0)[..., None]
    picked = values[jnp.maximum(positions, 0)]
    return jnp.where(live, picked, jnp.zeros_like(picked))


def project_back(delta, weight):
    return lax.dot_general(
        delta, weight, (((1,), (1,)), ((), ())), preferred_element_type=jnp.float32
    )


def contract_rows(left_side, right_side):
    return lax.dot_general(
        left_side, right_side, (((0,), (0,)), ((), ())), preferred_element_type=jnp.float32
    )


def silu_slope(value):
    sigma = jax.nn.sigmoid(value)
    return sigma * (1.0 + value * (1.0 - sigma))


def edge_rows(from_authors, from_papers):
    stacked = jnp.stack([from_authors, from_papers])
    width = stacked.shape[-1]
    arrived = lax.all_to_all(stacked, ("row", "col"), split_axis=1, concat_axis=1, tiled=True)
    return (arrived[0].reshape(-1, width), arrived[1].reshape(-1, width))


def per_device(
    x_paper,
    x_author,
    cite_nbr,
    write_src,
    write_dst,
    w_self_paper,
    w_cite,
    w_write,
    w_self_author,
    w_written,
    grad_paper,
    grad_author,
):
    papers = x_paper.shape[0]
    authors = x_author.shape[0]
    cnt_cite = jnp.maximum(jnp.sum((cite_nbr >= 0).astype(jnp.float32), axis=1, keepdims=True), 1.0)
    rows_in = lax.all_gather(x_paper, "col", axis=0, tiled=True)
    columns = lax.iota(jnp.int32, rows_in.shape[0])
    cite_total = jnp.dot(
        match_table(cite_nbr, columns), rows_in, preferred_element_type=jnp.float32
    )
    cited = (cite_total / cnt_cite).astype(jnp.bfloat16)
    send_list = write_src[0]
    take_list = write_dst[0]
    table_paper = (take_list.reshape(-1)[None, :] == lax.iota(jnp.int32, papers)[:, None]).astype(
        jnp.bfloat16
    )
    table_author = (send_list.reshape(-1)[None, :] == lax.iota(jnp.int32, authors)[:, None]).astype(
        jnp.bfloat16
    )
    cnt_write = jnp.maximum(jnp.sum(table_paper, axis=1, keepdims=True, dtype=jnp.float32), 1.0)
    cnt_written = jnp.maximum(jnp.sum(table_author, axis=1, keepdims=True, dtype=jnp.float32), 1.0)
    into_papers, into_authors = edge_rows(
        select_rows(x_author, send_list), select_rows(x_paper, take_list)
    )
    written = (
        jnp.dot(table_paper, into_papers, preferred_element_type=jnp.float32) / cnt_write
    ).astype(jnp.bfloat16)
    authored = (
        jnp.dot(table_author, into_authors, preferred_element_type=jnp.float32) / cnt_written
    ).astype(jnp.bfloat16)
    pre_paper = (
        jnp.dot(x_paper, w_self_paper, preferred_element_type=jnp.float32)
        + jnp.dot(cited, w_cite, preferred_element_type=jnp.float32)
        + jnp.dot(written, w_write, preferred_element_type=jnp.float32)
    )
    pre_author = jnp.dot(x_author, w_self_author, preferred_element_type=jnp.float32) + jnp.dot(
        authored, w_written, preferred_element_type=jnp.float32
    )
    out_paper = jax.nn.silu(pre_paper).astype(jnp.bfloat16)
    out_author = jax.nn.silu(pre_author).astype(jnp.bfloat16)
    dpre_paper = (grad_paper.astype(jnp.float32) * silu_slope(pre_paper)).astype(jnp.bfloat16)
    dpre_author = (grad_author.astype(jnp.float32) * silu_slope(pre_author)).astype(jnp.bfloat16)
    dz_cite = (project_back(dpre_paper, w_cite) / cnt_cite).astype(jnp.bfloat16)
    dz_write = (project_back(dpre_paper, w_write) / cnt_write).astype(jnp.bfloat16)
    dz_written = (project_back(dpre_author, w_written) / cnt_written).astype(jnp.bfloat16)
    columns = lax.iota(jnp.int32, lax.axis_size("col") * papers)
    cite_grad = lax.psum_scatter(
        contract_rows(match_table(cite_nbr, columns), dz_cite),
        "col",
        scatter_dimension=0,
        tiled=True,
    )
    back_papers, back_authors = edge_rows(
        select_rows(dz_written, send_list), select_rows(dz_write, take_list)
    )
    dx_paper = (
        project_back(dpre_paper, w_self_paper)
        + cite_grad
        + jnp.dot(table_paper, back_papers, preferred_element_type=jnp.float32)
    ).astype(jnp.bfloat16)
    dx_author = (
        project_back(dpre_author, w_self_author)
        + jnp.dot(table_author, back_authors, preferred_element_type=jnp.float32)
    ).astype(jnp.bfloat16)
    local_grads = jnp.stack(
        [
            contract_rows(x_paper, dpre_paper),
            contract_rows(cited, dpre_paper),
            contract_rows(written, dpre_paper),
            contract_rows(x_author, dpre_author),
            contract_rows(authored, dpre_author),
        ]
    )
    halfway = lax.psum_scatter(local_grads, "row", scatter_dimension=1, tiled=True)
    summed = lax.psum_scatter(halfway, "col", scatter_dimension=2, tiled=True)
    devices_all = lax.axis_size("row") * lax.axis_size("col")
    paper_scale = float(papers * devices_all) ** (-0.5)
    author_scale = float(authors * devices_all) ** (-0.5)
    factors = jnp.array(
        [paper_scale, paper_scale, paper_scale, author_scale, author_scale], jnp.float32
    )
    dweights = summed * factors[:, None, None]
    return (out_paper, out_author, dx_paper, dx_author, dweights)


def solution(mesh):
    placed = (
        P(("row", "col"), None),
        P(("row", "col"), None),
        P(("row", "col"), None),
        P(("row", "col"), None, None),
        P(("row", "col"), None, None),
        P(),
        P(),
        P(),
        P(),
        P(),
        P(("row", "col"), None),
        P(("row", "col"), None),
    )
    return jax.shard_map(
        per_device,
        mesh=mesh,
        in_specs=placed,
        out_specs=(
            P(("row", "col"), None),
            P(("row", "col"), None),
            P(("row", "col"), None),
            P(("row", "col"), None),
            P(None, "row", "col"),
        ),
        check_vma=False,
    )
```

profile of v0, /device:TPU:0, one launch (start us, length us, event | category | flops | bytes accessed | tf_op | source)
XLA Modules:
  0.0 443.5 jit_solution(9588760327123963689)
XLA Ops:
  7.2 0.7 all-gather.2.cloned.1.call-update
  7.9 0.7 compare_bitcast_fusion
  8.6 0.1 copy.49
  8.8 0.7 compare_bitcast_fusion.1
  9.4 0.1 copy.46
  9.6 0.7 broadcast_maximum_fusion
  10.5 0.7 broadcast_maximum_fusion.1
  11.4 2.0 gather_fusion.1
  13.5 1.1 gather.23
  14.6 2.0 gather_fusion
  16.6 1.1 gather.21
  17.7 1.6 bitcast_select_fusion.2
  19.3 1.6 bitcast_select_fusion.3
  20.9 2.3 pad_maximum_fusion
  23.1 11.6 %all-to-all-start = ((bf16[2,128,4,768]{3,2,0,1:T(4,128)(2,1)}), bf16[2,128,4,768]{3,2,0,1:T(4,128)(2,1)}, u32[]{:S(2)}, u32[]{:S(2)}) async-start(bf16[2,128,4,768]{3,2,0,1:T(4,128)(2,1)} %pad_maximum_fusion), calls=%async_computation | async-start | bytes 3145728 | tf_op jit(solution)/shard_map/all_to_all | solution.py:40
  35.3 0.1 convert_reduce_fusion
  35.4 0.1 convert_reduce_fusion.1
  35.6 3.0 fusion.19
  38.6 2.9 fusion.20
  41.5 17.3 %all-to-all-done = bf16[2,128,4,768]{3,2,0,1:T(4,128)(2,1)} async-done(((bf16[2,128,4,768]{3,2,0,1:T(4,128)(2,1)}), bf16[2,128,4,768]{3,2,0,1:T(4,128)(2,1)}, u32[]{:S(2)}, u32[]{:S(2)}) %all-to-all-start) | async-done | bytes 1572896 | tf_op jit(solution)/shard_map/all_to_all | solution.py:40
  58.8 3.0 fusion.17
  61.8 2.5 reshape_squeeze.13
  64.3 1.1 reshape_squeeze.12
  65.4 1.7 fusion.1
  67.1 2.4 fusion
  69.5 1.7 multiply_convert_fusion
  71.3 16.6 %all-gather.2.cloned.1.call-done = bf16[4096,768]{1,0:T(8,128)(2,1)} async-done(((bf16[256,768]{1,0:T(8,128)(2,1)}), bf16[4096,768]{1,0:T(8,128)(2,1)}) %all-gather.2.cloned.1.call-update) | async-done | bytes 6291472 | tf_op jit(solution)/shard_map/all_gather | solution.py:61
  87.9 12.6 %fusion.7 = bf16[256,768]{1,0:T(8,128)(2,1)S(1)} fusion(bf16[4096,768]{1,0:T(8,128)(2,1)} %all-gather.2.cloned.1.call-done, f32[256]{0:T(256)S(1)} %broadcast_maximum_fusion.4, s32[256]{0:T(256)S(1)} %bitcast.123, s32[256]{0:T(256)S(1)} %bitcast.95, s32[256]{0:T(256)S(1)} %bitcast.97, s32[256]{0:T(256)S(1)} %bitcast.99, s32[256]{0:T(256)S(1)} %bitcast.101, ...), kind=kOutput, calls=%fused_computation.47 | convolution fusion | flops 1661337600 | bytes 6702080 | tf_op jit(solution)/shard_map/dot_general | solution.py:63
  100.4 0.6 convolution_add_fusion.2
  101.1 2.0 multiply_convert_fusion.1
  103.0 2.3 bitcast_dynamic-update-slice_fusion.1
  105.4 2.4 bitcast_dynamic-update-slice_fusion.4
  107.7 2.2 bitcast_dynamic-update-slice_fusion.3
  110.0 2.4 bitcast_dynamic-update-slice_fusion
  112.4 2.2 bitcast_dynamic-update-slice_fusion.2
  114.6 21.0 %copy.61 = f32[5,768,1024]{2,0,1:T(8,128)} copy(f32[5,768,1024]{1,2,0:T(8,128)} %bitcast_dynamic-update-slice_fusion.2) | data formatting | bytes 31457280
  135.6 21.5 %copy.63 = f32[96,8,5,1024]{3,1,2,0:T(8,128)} copy(f32[96,8,5,1024]{3,2,1,0:T(8,128)} %bitcast.90) | data formatting | bytes 31457280
  157.1 0.4 reduce-scatter.6.cloned.1.call-start
  157.6 14.6 %fusion.8 = f32[4096,768]{1,0:T(8,128)} fusion(bf16[256,1024]{1,0:T(8,128)(2,1)S(1)} %get-tuple-element.11, bf16[768,1024]{1,0:T(8,128)(2,1)S(1)} %copy-done, f32[256]{0:T(256)S(1)} %broadcast_maximum_fusion.4, s32[256]{0:T(256)S(1)} %bitcast.124, s32[256]{0:T(256)S(1)} %bitcast.96, s32[256]{0:T(256)S(1)} %bitcast.98, s32[256]{0:T(256)S(1)} %bitcast.100, ...), kind=kOutput, calls=%fused_computation.48 | convolution fusion | flops 2063990784 | bytes 14697472 | tf_op jit(solution)/shard_map/dot_general | solution.py:27
  172.2 0.2 reduce-scatter.8.cloned.1.call-start
  172.5 71.8 %reduce-scatter.10.cloned.1.call-done = f32[96,5120]{1,0:T(8,128)} async-done(((f32[768,5120]{1,0:T(8,128)}), f32[96,5120]{1,0:T(8,128)}) %reduce-scatter.10.cloned.1.call-update) | async-done | bytes 1966096
  244.2 3.8 reshape.136
  248.0 3.6 copy.62
  251.7 2.0 fusion.5
  253.7 2.7 gather_fusion.2
  256.4 1.7 gather.25
  258.1 1.4 bitcast_select_fusion.1
  259.6 2.0 fusion.6
  261.6 2.7 gather_fusion.3
  264.3 1.7 gather.27
  266.0 0.5 bitcast_select_fusion
  266.5 3.3 pad_maximum_fusion.1
  269.8 8.7 %all-to-all-start.1 = ((bf16[2,128,4,768]{3,2,0,1:T(4,128)(2,1)}), bf16[2,128,4,768]{3,2,0,1:T(4,128)(2,1)}, u32[]{:S(2)}, u32[]{:S(2)}) async-start(bf16[2,128,4,768]{3,2,0,1:T(4,128)(2,1)} %pad_maximum_fusion.1), calls=%async_computation.2 | async-start | bytes 3145728 | tf_op jit(solution)/shard_map/all_to_all | solution.py:40
  278.4 2.9 fusion.21
  281.4 31.7 %all-to-all-done.1 = bf16[2,128,4,768]{3,2,0,1:T(4,128)(2,1)} async-done(((bf16[2,128,4,768]{3,2,0,1:T(4,128)(2,1)}), bf16[2,128,4,768]{3,2,0,1:T(4,128)(2,1)}, u32[]{:S(2)}, u32[]{:S(2)}) %all-to-all-start.1) | async-done | bytes 1572896 | tf_op jit(solution)/shard_map/all_to_all | solution.py:40
  313.1 2.8 fusion.16
  315.9 1.1 reshape_squeeze.15
  317.0 1.6 reshape_squeeze.14
  318.6 2.7 fusion.3
  321.3 36.5 %reduce-scatter.6.cloned.1.call-done = f32[256,768]{1,0:T(8,128)} async-done(((f32[4096,768]{1,0:T(8,128)}), f32[256,768]{1,0:T(8,128)}) %reduce-scatter.6.cloned.1.call-update) | async-done | bytes 786448 | tf_op jit(solution)/shard_map/reduce_scatter | solution.py:102
  357.8 2.2 convolution_add_fusion.5
  360.0 1.1 fusion.2
  361.1 74.1 %reduce-scatter.8.cloned.1.call-done = f32[5,96,64]{1,2,0:T(8,128)} async-done(((f32[5,96,1024]{1,2,0:T(8,128)}), f32[5,96,64]{1,2,0:T(8,128)}) %reduce-scatter.8.cloned.1.call-update) | async-done | bytes 122896 | tf_op jit(solution)/shard_map/reduce_scatter | solution.py:130
  435.2 1.6 broadcast_multiply_fusion
  (49 shorter events, 1.1 us)
Async XLA Ops:
  7.2 93.3 %copy-start = (bf16[768,1024]{1,0:T(8,128)(2,1)S(1)}, bf16[768,1024]{1,0:T(8,128)(2,1)}, u32[]{:S(2)}) copy-start(bf16[768,1024]{1,0:T(8,128)(2,1)} %param.19) | copy-start | bytes 4718596
  7.2 4.2 copy-start.1
  7.2 80.7 %all-gather.2.cloned.1.call-start = ((), (), s32[]{:S(2)}) async-start(), calls=%async_computation.5 | async-start | bytes 6684672 | tf_op jit(solution)/shard_map/all_gather | solution.py:61
  11.4 3.2 copy-start.2
  19.2 15.6 %copy-start.9 = (s32[1,128,4]{1,2,0:T(4,128)S(1)}, s32[1,128,4]{1,2,0:T(4,128)}, u32[]{:S(2)}) copy-start(s32[1,128,4]{1,2,0:T(4,128)} %param.16) | copy-start | bytes 6148
  19.3 15.7 %copy-start.10 = (s32[1,128,4]{1,2,0:T(4,128)S(1)}, s32[1,128,4]{1,2,0:T(4,128)}, u32[]{:S(2)}) copy-start(s32[1,128,4]{1,2,0:T(4,128)} %param.17) | copy-start | bytes 6148
  19.3 16.3 %copy-start.8 = (s32[256,16]{0,1:T(8,128)S(1)}, s32[256,16]{0,1:T(8,128)}, u32[]{:S(2)}) copy-start(s32[256,16]{0,1:T(8,128)} %param.15) | copy-start | bytes 49156
  23.1 35.7 %all-to-all-start = ((bf16[2,128,4,768]{3,2,0,1:T(4,128)(2,1)}), bf16[2,128,4,768]{3,2,0,1:T(4,128)(2,1)}, u32[]{:S(2)}, u32[]{:S(2)}) async-start(bf16[2,128,4,768]{3,2,0,1:T(4,128)(2,1)} %pad_maximum_fusion), calls=%async_computation | async-start | bytes 3145728 | tf_op jit(solution)/shard_map/all_to_all | solution.py:40
  34.8 209.5 %reduce-scatter.10.cloned.1.call-start = ((), (), s32[]{:S(2)}) async-start(), calls=%async_computation.8 | async-start | bytes 17694720
  65.4 4.1 copy-start.4
  65.4 4.1 copy-start.11
  65.4 4.1 copy-start.13
  67.1 4.2 copy-start.5
  87.9 12.6 %copy-start.3 = (f32[256,1024]{1,0:T(8,128)S(1)}, f32[256,1024]{1,0:T(8,128)}, u32[]{:S(2)}) copy-start(f32[256,1024]{1,0:T(8,128)} %fusion.19) | copy-start | bytes 3145732
  87.9 13.2 %copy-start.7 = (bf16[256,768]{1,0:T(8,128)(2,1)S(1)}, bf16[256,768]{1,0:T(8,128)(2,1)}, u32[]{:S(2)}) copy-start(bf16[256,768]{1,0:T(8,128)(2,1)} %fusion) | copy-start | bytes 1179652
  87.9 13.2 %copy-start.12 = (bf16[768,1024]{1,0:T(8,128)(2,1)S(1)}, bf16[768,1024]{1,0:T(8,128)(2,1)}, u32[]{:S(2)}) copy-start(bf16[768,1024]{1,0:T(8,128)(2,1)} %param.20) | copy-start | bytes 4718596
  87.9 13.2 %copy-start.14 = (bf16[256,1024]{1,0:T(8,128)(2,1)S(1)}, bf16[256,1024]{1,0:T(8,128)(2,1)}, u32[]{:S(2)}) copy-start(bf16[256,1024]{1,0:T(8,128)(2,1)} %param.23) | copy-start | bytes 1572868
  107.7 4.6 %copy-start.6 = (bf16[256,768]{1,0:T(8,128)(2,1)S(1)}, bf16[256,768]{1,0:T(8,128)(2,1)}, u32[]{:S(2)}) copy-start(bf16[256,768]{1,0:T(8,128)(2,1)} %copy-done.5) | copy-start | bytes 1179652
  157.1 200.6 %reduce-scatter.6.cloned.1.call-start = ((), (), s32[]{:S(2)}) async-start(), calls=%async_computation.6 | async-start | bytes 13369344 | tf_op jit(solution)/shard_map/reduce_scatter | solution.py:102
  172.2 263.0 %reduce-scatter.8.cloned.1.call-start = ((), (), s32[]{:S(2)}) async-start(), calls=%async_computation.7 | async-start | bytes 2785280 | tf_op jit(solution)/shard_map/reduce_scatter | solution.py:130
  269.8 43.3 %all-to-all-start.1 = ((bf16[2,128,4,768]{3,2,0,1:T(4,128)(2,1)}), bf16[2,128,4,768]{3,2,0,1:T(4,128)(2,1)}, u32[]{:S(2)}, u32[]{:S(2)}) async-start(bf16[2,128,4,768]{3,2,0,1:T(4,128)(2,1)} %pad_maximum_fusion.1), calls=%async_computation.2 | async-start | bytes 3145728 | tf_op jit(solution)/shard_map/all_to_all | solution.py:40
Sparse Core Ops, SparseCore 0:
  10.2 77.5 all-gather.1
  157.3 86.9 reduce-scatter.9
  247.7 110.0 reduce-scatter.5
  360.9 74.2 reduce-scatter.7
where the time goes:
time: 451 us; the launch traced here: 444 us
  waiting for transfers between devices  249 us (55%)
  local copies, waits for them, and re-layouts  78.3 us (17%)
  matrix products  66.1 us (15%)
  starting transfers between devices  21 us (5%)
  other arithmetic  15.2 us (3%)
  between operations  14.3 us (3%)
    reduce_scatter x1, waiting for transfers between devices, per_device(): summed = lax.psum_scatter(halfway, 'col', scatter_dimension=2, tiled=True)  74.1 us
    unnamed x5, waiting for transfers between devices  72.5 us
    unnamed x36, local copies, waits for them, and re-layouts  50.2 us
    all_to_all x2, waiting for transfers between devices, edge_rows(): lax.all_to_all(stacked, ('row', 'col'), split_axis=1, concat_axis=1, tile...  49 us
    reduce_scatter x1, waiting for transfers between devices, per_device(): lax.psum_scatter(contract_rows(match_table(cite_nbr, columns), dz_cite),...  36.5 us
    dot_general x6, matrix products, contract_rows(): lax.dot_general(left_side, right_side, (((0,), (0,)), ((), ())), preferre...  26.2 us
    all_to_all x2, starting transfers between devices, edge_rows(): lax.all_to_all(stacked, ('row', 'col'), split_axis=1, concat_axis=1, tile...  20.3 us
    all_gather x1, waiting for transfers between devices, per_device(): rows_in = lax.all_gather(x_paper, 'col', axis=0, tiled=True)  16.6 us
  transfers between devices with their start and end apart: 6, of which 6 were waited for; matrix products, arithmetic and copies ran while one was open for 20% of the time, Pallas kernels for 0%

commit v1 on v0

v1 whole, which is shorter than its diff:
```python
import jax
import jax.numpy as jnp
from jax import lax
from jax.sharding import PartitionSpec as P

BF = jnp.bfloat16
F32 = jnp.float32
MASKS = (4, 1, 12, 3)
ORDERS = tuple(tuple(MASKS[(q + k) % 4] for k in range(4)) for q in range(4))


def dot(a, b, dims=((1,), (0,))):
    return lax.dot_general(a, b, (dims, ((), ())), preferred_element_type=F32)


def gather_col(block):
    rows = block.shape[0] // 4
    parts = [block[q * rows : (q + 1) * rows] for q in range(4)]
    last = [None] * 4
    for k in range(4):
        for q in range(4):
            mask = ORDERS[q][k]
            got = lax.ppermute(parts[q], "col", [(i, i ^ mask) for i in range(16)])
            if k < 3:
                parts[q] = jnp.concatenate([parts[q], got], axis=0)
            else:
                last[q] = got
    return parts, last


def source_masks():
    table = []
    for q in range(4):
        masks = []
        for m in range(16):
            value = 0
            for k in range(4):
                if (m >> k) & 1:
                    value ^= ORDERS[q][k]
            masks.append(value)
        table.append(masks)
    return table


def column_of(entries, col):
    diff = (entries >> 8) ^ col
    bits = {}
    for axis, (near, far) in enumerate(((4, 12), (1, 3))):
        d = (diff >> 2) if axis == 0 else (diff & 3)
        bits[far] = d >> 1
        bits[near] = (d & 1) ^ (d >> 1)
    quarter = (entries >> 6) & 3
    place = jnp.zeros_like(entries)
    for q in range(4):
        m = jnp.zeros_like(entries)
        for k in range(4):
            m = m + (bits[ORDERS[q][k]] << k)
        place = jnp.where(quarter == q, m, place)
    return jnp.where(entries >= 0, quarter * 1024 + place * 64 + (entries & 63), -1)


def edge_lists(write_src, write_dst):
    none = jnp.full_like(write_src, -1)
    pick = jnp.concatenate([write_src, jnp.where(write_dst >= 0, write_dst + 256, -1)], axis=1)
    into_paper = jnp.concatenate([write_dst, none], axis=1)
    into_author = jnp.concatenate([none, write_src], axis=1)
    return pick.reshape(-1), into_paper.reshape(-1), into_author.reshape(-1)


def exchange(rows):
    sent = rows.reshape(128, 8, rows.shape[-1])
    got = lax.all_to_all(sent, ("row", "col"), split_axis=0, concat_axis=0, tiled=True)
    return got.reshape(1024, rows.shape[-1])


def other_core(value):
    return lax.ppermute(value, "row", [(i, i ^ 1) for i in range(8)])


def over_y(parts):
    got = lax.all_to_all(
        parts, "row", split_axis=0, concat_axis=0, tiled=True,
        axis_index_groups=[[0, 2, 4, 6], [1, 3, 5, 7]],
    )
    return jnp.sum(got.astype(F32), axis=0)


def silu_and_slope(value):
    sigma = jax.nn.sigmoid(value)
    return (value * sigma).astype(BF), sigma * (1.0 + value * (1.0 - sigma))


def per_device(
    x_paper, x_author, cite_nbr, write_src, write_dst,
    w_self_paper, w_cite, w_write, w_self_author, w_written, grad_paper, grad_author,
):
    col = lax.axis_index("col")
    core = lax.axis_index("row") & 1

    pick, into_paper, into_author = edge_lists(write_src[0], write_dst[0])
    picker = (pick[:, None] == lax.iota(jnp.int32, 512)[None, :]).astype(BF)
    ids = lax.iota(jnp.int32, 256)[:, None]
    adder = jnp.concatenate(
        [(into_paper[None, :] == ids), (into_author[None, :] == ids)], axis=0
    ).astype(BF)
    both = jnp.concatenate([x_author, x_paper], axis=0)
    arrived = exchange(dot(picker, both).astype(BF))

    first, last = gather_col(x_paper)
    cnt_cite = jnp.maximum(jnp.sum((cite_nbr >= 0).astype(F32), axis=1, keepdims=True), 1.0)
    places = column_of(cite_nbr, col)
    columns = lax.iota(jnp.int32, 4096)
    table = jnp.zeros((256, 4096), F32)
    for slot in range(16):
        table = table + (places[:, slot : slot + 1] == columns[None, :]).astype(F32)
    table = lax.optimization_barrier(table.astype(BF))

    all_nbr = lax.all_gather(cite_nbr, "col", axis=0, tiled=True).reshape(16, 4, 64, 16)
    sources = jnp.array(source_masks(), jnp.int32) ^ col
    ordered = jnp.concatenate([all_nbr[:, q][sources[q]] for q in range(4)], axis=0)
    ordered = ordered.reshape(4096, 16).T
    own = ids + col * 256
    back_table = jnp.zeros((256, 4096), F32)
    for slot in range(16):
        back_table = back_table + (ordered[slot : slot + 1, :] == own).astype(F32)
    back_table = lax.optimization_barrier(back_table.astype(BF))

    lane = lax.iota(jnp.int32, 384)
    target = (lane // 96) * 192 + lane % 96
    rows768 = lax.iota(jnp.int32, 768)[:, None]
    mine = (rows768 == (target + core * 96)[None, :]).astype(BF)
    theirs = (rows768 == (target + (1 - core) * 96)[None, :]).astype(BF)

    cnt = jnp.maximum(jnp.sum(adder.astype(F32), axis=1, keepdims=True), 1.0)
    edge_mean = (dot(adder, arrived) / cnt).astype(BF)
    written, authored = edge_mean[:256], edge_mean[256:]

    pre_author = dot(x_author, w_self_author) + dot(authored, w_written)
    out_author, slope = silu_and_slope(pre_author)
    dpre_author = (grad_author.astype(F32) * slope).astype(BF)
    dz_written = (dot(dpre_author, w_written, ((1,), (1,))) / cnt[256:]).astype(BF)
    dx_author_own = dot(dpre_author, w_self_author, ((1,), (1,)))

    def weight_parts(lefts, dpre):
        left = jnp.concatenate(lefts, axis=0)
        kept = dot(left, mine).astype(BF)
        given = other_core(dot(left, theirs).astype(BF))
        dpre_other = other_core(dpre)
        right = jnp.concatenate([dpre, dpre_other], axis=0)
        outs = []
        for i in range(len(lefts)):
            pair = jnp.concatenate([kept[256 * i : 256 * i + 256], given[256 * i : 256 * i + 256]], axis=0)
            outs.append(dot(pair, right, ((0,), (0,))).astype(BF).reshape(4, 96, 1024))
        return over_y(jnp.stack(outs, axis=1))

    sums_author = weight_parts([x_author, authored], dpre_author)

    cite_total = jnp.zeros((256, 768), F32)
    for q in range(4):
        cite_total = cite_total + dot(table[:, q * 1024 : q * 1024 + 512], first[q])
        cite_total = cite_total + dot(table[:, q * 1024 + 512 : q * 1024 + 1024], last[q])
    cited = (cite_total / cnt_cite).astype(BF)
    pre_paper = dot(x_paper, w_self_paper) + dot(written, w_write) + dot(cited, w_cite)
    out_paper, slope = silu_and_slope(pre_paper)
    dpre_paper = (grad_paper.astype(F32) * slope).astype(BF)
    dz_cite = (dot(dpre_paper, w_cite, ((1,), (1,))) / cnt_cite).astype(BF)
    first, last = gather_col(dz_cite)
    dz_write = (dot(dpre_paper, w_write, ((1,), (1,))) / cnt[:256]).astype(BF)
    back = exchange(dot(picker, jnp.concatenate([dz_written, dz_write], axis=0)).astype(BF))
    dx_paper_own = dot(dpre_paper, w_self_paper, ((1,), (1,)))
    sums_paper = weight_parts([x_paper, cited, written], dpre_paper)

    sums = jnp.concatenate([sums_paper, sums_author], axis=0).reshape(480, 1024)
    cols = sums.T.astype(BF).reshape(16, 64, 480)
    got = lax.all_to_all(cols, "col", split_axis=0, concat_axis=0, tiled=True)
    total = jnp.sum(got.astype(F32), axis=0) * (32768.0 ** -0.5)
    dweights = total.reshape(64, 5, 96).transpose(1, 2, 0)

    edge_sum = dot(adder, back)
    dx_author = (dx_author_own + edge_sum[256:]).astype(BF)
    acc = dx_paper_own + edge_sum[:256]
    for q in range(4):
        acc = acc + dot(back_table[:, q * 1024 : q * 1024 + 512], first[q])
        acc = acc + dot(back_table[:, q * 1024 + 512 : q * 1024 + 1024], last[q])
    dx_paper = acc.astype(BF)
    return (out_paper, out_author, dx_paper, dx_author, dweights)


def solution(mesh):
    part = P(("row", "col"), None)
    part3 = P(("row", "col"), None, None)
    return jax.shard_map(
        per_device,
        mesh=mesh,
        in_specs=(part, part, part, part3, part3, P(), P(), P(), P(), P(), part, part),
        out_specs=(part, part, part, part, P(None, "row", "col")),
        check_vma=False,
    )
```

time: 451 us -> 309 us (0.69)
  waiting for transfers between devices: 249 us -> 45.6 us
  local copies, waits for them, and re-layouts: 78.3 us -> 18.6 us
  starting transfers between devices: 21 us -> 79.1 us
  blocking collectives: 0 us -> 38.3 us
  other arithmetic: 15.2 us -> 49.7 us
  between operations: 14.3 us -> 2.01 us
  matrix products: 66.1 us -> 70.7 us
    reduce_scatter x2 -> x0, waiting for transfers between devices: 111 us -> none  [the longest x1 74.1 us: per_device(): summed = lax.psum_scatter(halfway, 'col', scatter_dimension=2, tiled=True)]
    unnamed x5 -> x0, waiting for transfers between devices: 72.5 us -> none
    ppermute x0 -> x36, starting transfers between devices: none -> 48.7 us  [the longest x32 48.1 us: gather_col(): got = lax.ppermute(parts[q], 'col', [(i, i ^ mask) for i in range(16)])]
    unnamed x36 -> x133, local copies, waits for them, and re-layouts: 50.2 us -> 6.05 us
    all_gather x0 -> x1, blocking collectives: none -> 38.3 us  [per_device(): lax.all_gather(cite_nbr, 'col', axis=0, tiled=True).reshape(16, 4, 64, 16)]
    all_to_all x2 -> x5, waiting for transfers between devices: 49 us -> 11.8 us  [the longest x2 6.91 us: over_y(): lax.all_to_all(parts, 'row', split_axis=0, concat_axis=0, tiled=True, axi...]
    ppermute x0 -> x36, waiting for transfers between devices: none -> 33.7 us  [the longest x32 33.7 us: gather_col(): got = lax.ppermute(parts[q], 'col', [(i, i ^ mask) for i in range(16)])]
    concatenate x0 -> x27, other arithmetic: none -> 23 us  [the longest x24 21 us: gather_col(): parts[q] = jnp.concatenate([parts[q], got], axis=0)]
  transfers between devices with their start and end apart: 6 -> 41, of which waited for: 6 -> 12; matrix products, arithmetic and copies ran while one was open for 20% -> 39% of each run, Pallas kernels for 0% -> 0%
where the time goes in v1:
time: 309 us; the launch traced here: 304 us
  starting transfers between devices  79.1 us (26%)
  matrix products  70.7 us (23%)
  other arithmetic  49.7 us (16%)
  waiting for transfers between devices  45.6 us (15%)
  blocking collectives  38.3 us (12%)
  local copies, waits for them, and re-layouts  18.6 us (6%)
    dot_general x39, matrix products, dot(): return lax.dot_general(a, b, (dims, ((), ())), preferred_element_type=F32)  70.7 us
    ppermute x32, starting transfers between devices, gather_col(): got = lax.ppermute(parts[q], 'col', [(i, i ^ mask) for i in range(16)])  48.1 us
    all_gather x1, blocking collectives, per_device(): lax.all_gather(cite_nbr, 'col', axis=0, tiled=True).reshape(16, 4, 64, 16)  38.3 us
    ppermute x32, waiting for transfers between devices, gather_col(): got = lax.ppermute(parts[q], 'col', [(i, i ^ mask) for i in range(16)])  33.7 us
    concatenate x24, other arithmetic, gather_col(): parts[q] = jnp.concatenate([parts[q], got], axis=0)  21 us
    all_to_all x2, starting transfers between devices, exchange(): lax.all_to_all(sent, ('row', 'col'), split_axis=0, concat_axis=0, tiled=T...  16.4 us
    convert_element_type x1, other arithmetic, per_device(): table = lax.optimization_barrier(table.astype(BF))  10.1 us
    all_to_all x2, starting transfers between devices, over_y(): lax.all_to_all(parts, 'row', split_axis=0, concat_axis=0, tiled=True, axi...  9.3 us
  transfers between devices with their start and end apart: 41, of which 12 were waited for; matrix products, arithmetic and copies ran while one was open for 39% of the time, Pallas kernels for 0%

profile of v1, /device:TPU:0, one launch (start us, length us, event | category | flops | bytes accessed | tf_op | source)
XLA Modules:
  0.0 304.0 jit_solution(9321887454117376485)
XLA Ops:
  1.8 4.2 %collective-permute-start.12 = (bf16[64,768]{1,0:T(8,128)(2,1)S(1)}, bf16[64,768]{1,0:T(8,128)(2,1)}, u32[]{:S(2)}, u32[]{:S(2)}) collective-permute-start(bf16[64,768]{1,0:T(8,128)(2,1)S(1)} %get-tuple-element.52), channel_id=1, source_target_pairs={{0,3},{1,2},{2,1},{3,0},{4,7},{5,6},{6,5},{7,4},{8,11},{9,10},{10,... | collective-permute-start | bytes 294920 | tf_op jit(solution)/shard_map/ppermute | solution.py:23
  6.0 2.8 collective-permute-start.8
  11.2 3.3 %fusion.9 = bf16[128,8,768]{2,1,0:T(8,128)(2,1)} fusion(s32[1024]{0:T(1024)S(1)} %eq.543, bf16[256,768]{1,0:T(8,128)(2,1)} %param.14, bf16[256,768]{1,0:T(8,128)(2,1)} %param.13), kind=kOutput, calls=%fused_computation.38 | convolution fusion | flops 808189952 | bytes 2363392 | tf_op jit(solution)/shard_map/dot_general | solution.py:13
  14.5 8.3 %all-to-all-start = ((bf16[128,8,768]{2,1,0:T(8,128)(2,1)}), bf16[128,8,768]{2,1,0:T(8,128)(2,1)}, u32[]{:S(2)}, u32[]{:S(2)}) async-start(bf16[128,8,768]{2,1,0:T(8,128)(2,1)} %fusion.9), calls=%async_computation | async-start | bytes 3145728 | tf_op jit(solution)/shard_map/all_to_all | solution.py:72
  23.0 38.3 %all_gather.3 = s32[4096,16]{0,1:T(8,128)} all-gather(s32[256,16]{0,1:T(8,128)S(1)} %copy-done.38), channel_id=1, replica_groups=mesh['row'=8,'col'=16] {'col'}, dimensions={0}, use_global_device_ids=true | all-gather | bytes 278528 | tf_op jit(solution)/shard_map/all_gather | solution.py:118
  64.4 3.3 %fusion.128 = f32[256,1024]{1,0:T(8,128)} fusion(bf16[256,768]{1,0:T(8,128)(2,1)} %param.13, bf16[768,1024]{1,0:T(8,128)(2,1)} %param.18), kind=kOutput, calls=%fused_computation.244 | convolution fusion | flops 402653184 | bytes 3014656 | tf_op jit(solution)/shard_map/dot_general | solution.py:13
  67.6 1.6 fusion.129
  75.0 10.1 %add_convert_fusion.1 = bf16[256,4096]{1,0:T(8,128)(2,1)S(1)} fusion(s32[256]{0:T(256)S(1)} %bitcast.151, s32[256]{0:T(256)S(1)} %bitcast.152, s32[256]{0:T(256)S(1)} %bitcast.153, s32[256]{0:T(256)S(1)} %bitcast.154, s32[256]{0:T(256)S(1)} %bitcast.155, s32[256]{0:T(256)S(1)} %bitcast.156, s32[256]{0:T(256)S(1)} %bitcast.157, s32[256]{0:T(256)S(1)} %bitcast.158, ...), kind=kLoop, calls=%fused_computation.5 | loop fusion | flops 50331648 | bytes 2113536 | tf_op jit(solution)/shard_map/convert_element_type | solution.py:116
  85.1 7.6 %add_convert_fusion = bf16[256,4096]{1,0:T(8,128)(2,1)} fusion(s32[4096]{0:T(1024)S(1)} %bitcast.132, s32[4096]{0:T(1024)S(1)} %bitcast.133, s32[4096]{0:T(1024)S(1)} %bitcast.134, s32[4096]{0:T(1024)S(1)} %bitcast.135, s32[4096]{0:T(1024)S(1)} %bitcast.136, s32[4096]{0:T(1024)S(1)} %bitcast.137, s32[4096]{0:T(1024)S(1)} %bitcast.138, s32[4096]{0:T(1024)S(1)} %bitcast.139, ...), kind=kLoop, calls=%fused_computation.4 | loop fusion | flops 50331648 | bytes 2360320 | tf_op jit(solution)/shard_map/convert_element_type | solution.py:126
  94.6 2.1 collective-permute-start.9
  101.2 1.8 collective-permute-start.14
  103.9 1.5 collective-permute-start.10
  108.5 2.3 collective-permute-start.2
  117.2 4.7 %collective-permute-done.2 = bf16[256,768]{1,0:T(8,128)(2,1)S(1)} collective-permute-done((bf16[256,768]{1,0:T(8,128)(2,1)S(1)}, bf16[256,768]{1,0:T(8,128)(2,1)S(1)}, u32[]{:S(2)}, u32[]{:S(2)}) %collective-permute-start.2) | collective-permute-done | bytes 393248 | tf_op jit(solution)/shard_map/ppermute | solution.py:23
  122.8 2.3 collective-permute-start.3
  129.0 2.8 collective-permute-done.15
  133.0 3.1 %collective-permute-done.3 = bf16[512,768]{1,0:T(8,128)(2,1)S(1)} collective-permute-done((bf16[512,768]{1,0:T(8,128)(2,1)S(1)}, bf16[512,768]{1,0:T(8,128)(2,1)S(1)}, u32[]{:S(2)}, u32[]{:S(2)}) %collective-permute-start.3) | collective-permute-done | bytes 786464 | tf_op jit(solution)/shard_map/ppermute | solution.py:23
  136.5 2.2 fusion.24
  138.8 2.4 divide_convert_fusion
  142.3 1.6 convolution_convert_fusion.5
  148.6 1.9 multiply_convert_fusion.1
  150.6 1.8 fusion.27
  153.3 1.9 multiply_convert_fusion
  156.5 1.7 fusion.26
  158.2 1.7 fusion.25
  161.0 2.2 fusion.8
  163.2 8.1 %all-to-all-start.1 = ((bf16[128,8,768]{2,1,0:T(8,128)(2,1)}), bf16[128,8,768]{2,1,0:T(8,128)(2,1)S(1)}, u32[]{:S(2)}, u32[]{:S(2)}) async-start(bf16[128,8,768]{2,1,0:T(8,128)(2,1)} %fusion.8), calls=%async_computation.1 | async-start | bytes 3145728 | tf_op jit(solution)/shard_map/all_to_all | solution.py:72
  172.4 2.7 collective-permute-start.24
  175.2 15.7 %collective-permute-done.20 = bf16[64,768]{1,0:T(8,128)(2,1)S(1)} collective-permute-done((bf16[64,768]{1,0:T(8,128)(2,1)S(1)}, bf16[64,768]{1,0:T(8,128)(2,1)S(1)}, u32[]{:S(2)}, u32[]{:S(2)}) %collective-permute-start.20) | collective-permute-done | bytes 98336 | tf_op jit(solution)/shard_map/ppermute | solution.py:23
  192.7 1.6 collective-permute-start.17
  194.4 2.3 collective-permute-done.28
  196.7 3.5 %collective-permute-start.21 = (bf16[128,768]{1,0:T(8,128)(2,1)S(1)}, bf16[128,768]{1,0:T(8,128)(2,1)S(1)}, u32[]{:S(2)}, u32[]{:S(2)}) collective-permute-start(bf16[128,768]{1,0:T(8,128)(2,1)S(1)} %pad_maximum_fusion.39), channel_id=1, source_target_pairs={{0,12},{1,13},{2,14},{3,15},{4,8},{5,9},{6,10},{7,11},{8,4},{9,5},... | collective-permute-start | bytes 589832 | tf_op jit(solution)/shard_map/ppermute | solution.py:23
  200.2 2.6 collective-permute-start.25
  205.6 1.6 collective-permute-done.25
  208.0 1.5 collective-permute-done.29
  209.5 3.2 %collective-permute-start.18 = (bf16[256,768]{1,0:T(8,128)(2,1)}, bf16[256,768]{1,0:T(8,128)(2,1)S(1)}, u32[]{:S(2)}, u32[]{:S(2)}) collective-permute-start(bf16[256,768]{1,0:T(8,128)(2,1)} %pad_maximum_fusion.27), channel_id=1, source_target_pairs={{0,12},{1,13},{2,14},{3,15},{4,8},{5,9},{6,10},{7,11},{8,4},{9,5},... | collective-permute-start | bytes 1179656 | tf_op jit(solution)/shard_map/ppermute | solution.py:23
  213.5 2.5 collective-permute-start.22
  217.2 1.8 convolution_convert_fusion.1
  219.1 1.8 convolution_convert_fusion
  223.0 2.7 convolution_convert_fusion.4
  227.0 4.3 %all-to-all-start.3 = ((bf16[4,2,96,1024]{3,2,1,0:T(8,128)(2,1)}), bf16[4,2,96,1024]{3,2,1,0:T(8,128)(2,1)}, u32[]{:S(2)}, u32[]{:S(2)}) async-start(bf16[4,2,96,1024]{3,2,1,0:T(8,128)(2,1)} %pad_maximum_fusion.1), calls=%async_computation.3 | async-start | bytes 3145728 | tf_op jit(solution)/shard_map/all_to_all | solution.py:81
  231.4 2.0 convolution_convert_fusion.3
  233.4 1.9 convolution_convert_fusion.2
  235.3 1.6 pad_maximum_fusion
  239.0 1.9 pad_maximum_fusion.14
  241.0 2.0 collective-permute-start.23
  242.9 2.0 pad_maximum_fusion.15
  246.3 1.9 pad_maximum_fusion.16
  248.5 2.3 fusion.67
  250.9 5.0 %all-to-all-start.2 = ((bf16[4,3,96,1024]{3,2,1,0:T(8,128)(2,1)}), bf16[4,3,96,1024]{3,2,1,0:T(8,128)(2,1)S(1)}, u32[]{:S(2)}, u32[]{:S(2)}) async-start(bf16[4,3,96,1024]{3,2,1,0:T(8,128)(2,1)} %pad_maximum_fusion), calls=%async_computation.2 | async-start | bytes 4718592 | tf_op jit(solution)/shard_map/all_to_all | solution.py:81
  255.8 2.5 fusion.63
  258.3 2.3 fusion.59
  260.6 1.5 fusion.69
  262.1 2.4 fusion.65
  264.5 2.5 fusion.61
  267.1 2.4 fusion.57
  269.4 2.2 fusion.4
  271.7 2.6 reduce.1
  274.2 6.9 %all-to-all-done.2 = bf16[4,3,96,1024]{3,2,1,0:T(8,128)(2,1)S(1)} async-done(((bf16[4,3,96,1024]{3,2,1,0:T(8,128)(2,1)}), bf16[4,3,96,1024]{3,2,1,0:T(8,128)(2,1)S(1)}, u32[]{:S(2)}, u32[]{:S(2)}) %all-to-all-start.2) | async-done | bytes 2359328 | tf_op jit(solution)/shard_map/all_to_all | solution.py:81
  285.2 4.7 %all-to-all-start.4 = ((bf16[16,64,480]{2,1,0:T(8,128)(2,1)}), bf16[16,64,480]{2,1,0:T(8,128)(2,1)S(1)}, u32[]{:S(2)}, u32[]{:S(2)}) async-start(bf16[16,64,480]{2,1,0:T(8,128)(2,1)} %bitcast.122), calls=%async_computation.4 | async-start | bytes 2097152 | tf_op jit(solution)/shard_map/all_to_all | solution.py:175
  290.0 2.8 fusion.29
  292.9 1.8 convolution_add_fusion.5
  294.8 3.2 %fusion.28 = bf16[256,768]{1,0:T(8,128)(2,1)} fusion(f32[256,768]{1,0:T(8,128)S(1)} %copy-done.9, f32[256,768]{1,0:T(8,128)} %fusion.59, f32[256,768]{1,0:T(8,128)S(1)} %copy-done.8, f32[256,768]{1,0:T(8,128)} %fusion.63, f32[256,768]{1,0:T(8,128)S(1)} %copy-done.7, f32[256,768]{1,0:T(8,128)} %fusion.67, f32[256,768]{1,0:T(8,128)S(1)} %fusion.69, ...), kind=kOutput, calls=%fused_computation.74 | convolution fusion | flops 206241792 | bytes 7733248 | tf_op jit(solution)/shard_map/dot_general | solution.py:13
  297.9 4.9 %all-to-all-done.4 = bf16[16,64,480]{2,1,0:T(8,128)(2,1)S(1)} async-done(((bf16[16,64,480]{2,1,0:T(8,128)(2,1)}), bf16[16,64,480]{2,1,0:T(8,128)(2,1)S(1)}, u32[]{:S(2)}, u32[]{:S(2)}) %all-to-all-start.4) | async-done | bytes 983072 | tf_op jit(solution)/shard_map/all_to_all | solution.py:175
  (268 shorter events, 65.0 us)
Async XLA Ops:
  0.6 147.5 %copy-start = (bf16[768,1024]{1,0:T(8,128)(2,1)S(1)}, bf16[768,1024]{1,0:T(8,128)(2,1)}, u32[]{:S(2)}) copy-start(bf16[768,1024]{1,0:T(8,128)(2,1)} %param.19) | copy-start | bytes 4718596
  1.8 90.8 %collective-permute-start.12 = (bf16[64,768]{1,0:T(8,128)(2,1)S(1)}, bf16[64,768]{1,0:T(8,128)(2,1)}, u32[]{:S(2)}, u32[]{:S(2)}) collective-permute-start(bf16[64,768]{1,0:T(8,128)(2,1)S(1)} %get-tuple-element.52), channel_id=1, source_target_pairs={{0,3},{1,2},{2,1},{3,0},{4,7},{5,6},{6,5},{7,4},{8,11},{9,10},{10,... | collective-permute-start | bytes 294920 | tf_op jit(solution)/shard_map/ppermute | solution.py:23
  6.0 87.7 %collective-permute-start.8 = (bf16[64,768]{1,0:T(8,128)(2,1)S(1)}, bf16[64,768]{1,0:T(8,128)(2,1)}, u32[]{:S(2)}, u32[]{:S(2)}) collective-permute-start(bf16[64,768]{1,0:T(8,128)(2,1)S(1)} %get-tuple-element.50), channel_id=1, source_target_pairs={{0,12},{1,13},{2,14},{3,15},{4,8},{5,9},{6,10},{7,11},{8,4},{9,5},... | collective-permute-start | bytes 294920 | tf_op jit(solution)/shard_map/ppermute | solution.py:23
  8.8 87.9 %collective-permute-start.4 = (bf16[64,768]{1,0:T(8,128)(2,1)S(1)}, bf16[64,768]{1,0:T(8,128)(2,1)}, u32[]{:S(2)}, u32[]{:S(2)}) collective-permute-start(bf16[64,768]{1,0:T(8,128)(2,1)S(1)} %get-tuple-element.51), channel_id=1, source_target_pairs={{0,1},{1,0},{2,3},{3,2},{4,5},{5,4},{6,7},{7,6},{8,9},{9,8},{10,11... | collective-permute-start | bytes 294920 | tf_op jit(solution)/shard_map/ppermute | solution.py:23
  8.8 90.1 %collective-permute-start = (bf16[64,768]{1,0:T(8,128)(2,1)S(1)}, bf16[64,768]{1,0:T(8,128)(2,1)}, u32[]{:S(2)}, u32[]{:S(2)}) collective-permute-start(bf16[64,768]{1,0:T(8,128)(2,1)S(1)} %get-tuple-element.49), channel_id=1, source_target_pairs={{0,4},{1,5},{2,6},{3,7},{4,0},{5,1},{6,2},{7,3},{8,12},{9,13},{10,... | collective-permute-start | bytes 294920 | tf_op jit(solution)/shard_map/ppermute | solution.py:23
  14.5 8.3 %copy-start.40 = (s32[1,128,4]{1,2,0:T(4,128)S(1)}, s32[1,128,4]{1,2,0:T(4,128)}, u32[]{:S(2)}) copy-start(s32[1,128,4]{1,2,0:T(4,128)} %param.16) | copy-start | bytes 6148
  14.5 8.4 %copy-start.38 = (s32[256,16]{0,1:T(8,128)S(1)}, s32[256,16]{0,1:T(8,128)}, u32[]{:S(2)}) copy-start(s32[256,16]{0,1:T(8,128)} %param.15) | copy-start | bytes 49156
  14.5 48.2 %copy-start.39 = (s32[1,128,4]{1,2,0:T(4,128)S(1)}, s32[1,128,4]{1,2,0:T(4,128)}, u32[]{:S(2)}) copy-start(s32[1,128,4]{1,2,0:T(4,128)} %param.17) | copy-start | bytes 6148
  14.5 124.2 %all-to-all-start = ((bf16[128,8,768]{2,1,0:T(8,128)(2,1)}), bf16[128,8,768]{2,1,0:T(8,128)(2,1)}, u32[]{:S(2)}, u32[]{:S(2)}) async-start(bf16[128,8,768]{2,1,0:T(8,128)(2,1)} %fusion.9), calls=%async_computation | async-start | bytes 3145728 | tf_op jit(solution)/shard_map/all_to_all | solution.py:72
  64.3 3.3 %copy-start.2 = (bf16[768,1024]{1,0:T(8,128)(2,1)S(1)}, bf16[768,1024]{1,0:T(8,128)(2,1)}, u32[]{:S(2)}) copy-start(bf16[768,1024]{1,0:T(8,128)(2,1)} %param.21) | copy-start | bytes 4718596
  64.3 3.3 %copy-start.31 = (bf16[256,768]{1,0:T(8,128)(2,1)S(1)}, bf16[256,768]{1,0:T(8,128)(2,1)}, u32[]{:S(2)}) copy-start(bf16[256,768]{1,0:T(8,128)(2,1)} %param.14) | copy-start | bytes 1179652
  93.6 6.7 %collective-permute-start.13 = (bf16[128,768]{1,0:T(8,128)(2,1)S(1)}, bf16[128,768]{1,0:T(8,128)(2,1)S(1)}, u32[]{:S(2)}, u32[]{:S(2)}) collective-permute-start(bf16[128,768]{1,0:T(8,128)(2,1)S(1)} %pad_maximum_fusion.37), channel_id=1, source_target_pairs={{0,4},{1,5},{2,6},{3,7},{4,0},{5,1},{6,2},{7,3},{8,12},{9,13},{10,... | collective-permute-start | bytes 589832 | tf_op jit(solution)/shard_map/ppermute | solution.py:23
  94.6 8.3 %collective-permute-start.9 = (bf16[128,768]{1,0:T(8,128)(2,1)S(1)}, bf16[128,768]{1,0:T(8,128)(2,1)S(1)}, u32[]{:S(2)}, u32[]{:S(2)}) collective-permute-start(bf16[128,768]{1,0:T(8,128)(2,1)S(1)} %pad_maximum_fusion.36), channel_id=1, source_target_pairs={{0,3},{1,2},{2,1},{3,0},{4,7},{5,6},{6,5},{7,4},{8,11},{9,10},{10,... | collective-permute-start | bytes 589832 | tf_op jit(solution)/shard_map/ppermute | solution.py:23
  97.6 7.7 %collective-permute-start.5 = (bf16[128,768]{1,0:T(8,128)(2,1)S(1)}, bf16[128,768]{1,0:T(8,128)(2,1)S(1)}, u32[]{:S(2)}, u32[]{:S(2)}) collective-permute-start(bf16[128,768]{1,0:T(8,128)(2,1)S(1)} %pad_maximum_fusion.35), channel_id=1, source_target_pairs={{0,12},{1,13},{2,14},{3,15},{4,8},{5,9},{6,10},{7,11},{8,4},{9,5},... | collective-permute-start | bytes 589832 | tf_op jit(solution)/shard_map/ppermute | solution.py:23
  99.8 7.8 %collective-permute-start.1 = (bf16[128,768]{1,0:T(8,128)(2,1)S(1)}, bf16[128,768]{1,0:T(8,128)(2,1)S(1)}, u32[]{:S(2)}, u32[]{:S(2)}) collective-permute-start(bf16[128,768]{1,0:T(8,128)(2,1)S(1)} %pad_maximum_fusion.34), channel_id=1, source_target_pairs={{0,1},{1,0},{2,3},{3,2},{4,5},{5,4},{6,7},{7,6},{8,9},{9,8},{10,11... | collective-permute-start | bytes 589832 | tf_op jit(solution)/shard_map/ppermute | solution.py:23
  101.2 9.6 %collective-permute-start.14 = (bf16[256,768]{1,0:T(8,128)(2,1)S(1)}, bf16[256,768]{1,0:T(8,128)(2,1)S(1)}, u32[]{:S(2)}, u32[]{:S(2)}) collective-permute-start(bf16[256,768]{1,0:T(8,128)(2,1)S(1)} %pad_maximum_fusion.26), channel_id=1, source_target_pairs={{0,1},{1,0},{2,3},{3,2},{4,5},{5,4},{6,7},{7,6},{8,9},{9,8},{10,11... | collective-permute-start | bytes 1179656 | tf_op jit(solution)/shard_map/ppermute | solution.py:23
  103.9 9.3 %collective-permute-start.10 = (bf16[256,768]{1,0:T(8,128)(2,1)S(1)}, bf16[256,768]{1,0:T(8,128)(2,1)S(1)}, u32[]{:S(2)}, u32[]{:S(2)}) collective-permute-start(bf16[256,768]{1,0:T(8,128)(2,1)S(1)} %pad_maximum_fusion.25), channel_id=1, source_target_pairs={{0,4},{1,5},{2,6},{3,7},{4,0},{5,1},{6,2},{7,3},{8,12},{9,13},{10,... | collective-permute-start | bytes 1179656 | tf_op jit(solution)/shard_map/ppermute | solution.py:23
  106.3 9.4 %collective-permute-start.6 = (bf16[256,768]{1,0:T(8,128)(2,1)S(1)}, bf16[256,768]{1,0:T(8,128)(2,1)S(1)}, u32[]{:S(2)}, u32[]{:S(2)}) collective-permute-start(bf16[256,768]{1,0:T(8,128)(2,1)S(1)} %pad_maximum_fusion.24), channel_id=1, source_target_pairs={{0,3},{1,2},{2,1},{3,0},{4,7},{5,6},{6,5},{7,4},{8,11},{9,10},{10,... | collective-permute-start | bytes 1179656 | tf_op jit(solution)/shard_map/ppermute | solution.py:23
  108.5 13.3 %collective-permute-start.2 = (bf16[256,768]{1,0:T(8,128)(2,1)S(1)}, bf16[256,768]{1,0:T(8,128)(2,1)S(1)}, u32[]{:S(2)}, u32[]{:S(2)}) collective-permute-start(bf16[256,768]{1,0:T(8,128)(2,1)S(1)} %pad_maximum_fusion.23), channel_id=1, source_target_pairs={{0,12},{1,13},{2,14},{3,15},{4,8},{5,9},{6,10},{7,11},{8,4},{9,5},... | collective-permute-start | bytes 1179656 | tf_op jit(solution)/shard_map/ppermute | solution.py:23
  111.8 20.0 %collective-permute-start.15 = (bf16[512,768]{1,0:T(8,128)(2,1)S(1)}, bf16[512,768]{1,0:T(8,128)(2,1)S(1)}, u32[]{:S(2)}, u32[]{:S(2)}) collective-permute-start(bf16[512,768]{1,0:T(8,128)(2,1)S(1)} %pad_maximum_fusion.12), channel_id=1, source_target_pairs={{0,12},{1,13},{2,14},{3,15},{4,8},{5,9},{6,10},{7,11},{8,4},{9,5},... | collective-permute-start | bytes 2359304 | tf_op jit(solution)/shard_map/ppermute | solution.py:23
  114.1 18.1 %collective-permute-start.11 = (bf16[512,768]{1,0:T(8,128)(2,1)S(1)}, bf16[512,768]{1,0:T(8,128)(2,1)S(1)}, u32[]{:S(2)}, u32[]{:S(2)}) collective-permute-start(bf16[512,768]{1,0:T(8,128)(2,1)S(1)} %pad_maximum_fusion.11), channel_id=1, source_target_pairs={{0,1},{1,0},{2,3},{3,2},{4,5},{5,4},{6,7},{7,6},{8,9},{9,8},{10,11... | collective-permute-start | bytes 2359304 | tf_op jit(solution)/shard_map/ppermute | solution.py:23
  116.6 16.0 %collective-permute-start.7 = (bf16[512,768]{1,0:T(8,128)(2,1)S(1)}, bf16[512,768]{1,0:T(8,128)(2,1)S(1)}, u32[]{:S(2)}, u32[]{:S(2)}) collective-permute-start(bf16[512,768]{1,0:T(8,128)(2,1)S(1)} %pad_maximum_fusion.10), channel_id=1, source_target_pairs={{0,4},{1,5},{2,6},{3,7},{4,0},{5,1},{6,2},{7,3},{8,12},{9,13},{10,... | collective-permute-start | bytes 2359304 | tf_op jit(solution)/shard_map/ppermute | solution.py:23
  122.8 13.3 %collective-permute-start.3 = (bf16[512,768]{1,0:T(8,128)(2,1)S(1)}, bf16[512,768]{1,0:T(8,128)(2,1)S(1)}, u32[]{:S(2)}, u32[]{:S(2)}) collective-permute-start(bf16[512,768]{1,0:T(8,128)(2,1)S(1)} %pad_maximum_fusion.9), channel_id=1, source_target_pairs={{0,3},{1,2},{2,1},{3,0},{4,7},{5,6},{6,5},{7,4},{8,11},{9,10},{10,... | collective-permute-start | bytes 2359304 | tf_op jit(solution)/shard_map/ppermute | solution.py:23
  132.6 3.9 %copy-start.57 = (f32[256]{0:T(256)S(1)}, f32[256]{0:T(256)}, u32[]{:S(2)}) copy-start(f32[256]{0:T(256)} %broadcast_maximum_fusion.1) | copy-start | bytes 3076
  150.5 2.8 copy-start.60
  150.5 2.8 copy-start.63
  150.5 72.5 %collective-permute-start.33 = (bf16[256,1024]{1,0:T(8,128)(2,1)}, bf16[256,1024]{1,0:T(8,128)(2,1)}, u32[]{:S(2)}, u32[]{:S(2)}) collective-permute-start(bf16[256,1024]{1,0:T(8,128)(2,1)} %get-tuple-element.27), channel_id=1, source_target_pairs={{0,16},{16,0},{32,48},{48,32},{64,80},{80,64},{96,112},{112,96},{1... | collective-permute-start | bytes 1572872 | tf_op jit(solution)/shard_map/ppermute | solution.py:77
  153.3 3.2 %copy-start.59 = (f32[256]{0:T(256)S(1)}, f32[256]{0:T(256)}, u32[]{:S(2)}) copy-start(f32[256]{0:T(256)} %get-tuple-element.86) | copy-start | bytes 3076
  155.2 61.9 %collective-permute-start.35 = (bf16[256,1024]{1,0:T(8,128)(2,1)}, bf16[256,1024]{1,0:T(8,128)(2,1)}, u32[]{:S(2)}, u32[]{:S(2)}) collective-permute-start(bf16[256,1024]{1,0:T(8,128)(2,1)} %get-tuple-element.25), channel_id=1, source_target_pairs={{0,16},{16,0},{32,48},{48,32},{64,80},{80,64},{96,112},{112,96},{1... | collective-permute-start | bytes 1572872 | tf_op jit(solution)/shard_map/ppermute | solution.py:77
  155.6 58.0 %collective-permute-start.34 = (bf16[512,384]{1,0:T(8,128)(2,1)}, bf16[512,384]{1,0:T(8,128)(2,1)}, u32[]{:S(2)}, u32[]{:S(2)}) collective-permute-start(bf16[512,384]{1,0:T(8,128)(2,1)} %convolution_convert_fusion.7), channel_id=1, source_target_pairs={{0,16},{16,0},{32,48},{48,32},{64,80},{80,64},{96,112},{112,96},{1... | collective-permute-start | bytes 1179656 | tf_op jit(solution)/shard_map/ppermute | solution.py:77
  160.0 12.5 %collective-permute-start.16 = (bf16[64,768]{1,0:T(8,128)(2,1)S(1)}, bf16[64,768]{1,0:T(8,128)(2,1)S(1)}, u32[]{:S(2)}, u32[]{:S(2)}) collective-permute-start(bf16[64,768]{1,0:T(8,128)(2,1)S(1)} %get-tuple-element.45), channel_id=1, source_target_pairs={{0,4},{1,5},{2,6},{3,7},{4,0},{5,1},{6,2},{7,3},{8,12},{9,13},{10,... | collective-permute-start | bytes 294920 | tf_op jit(solution)/shard_map/ppermute | solution.py:23
  163.2 62.6 %all-to-all-start.1 = ((bf16[128,8,768]{2,1,0:T(8,128)(2,1)}), bf16[128,8,768]{2,1,0:T(8,128)(2,1)S(1)}, u32[]{:S(2)}, u32[]{:S(2)}) async-start(bf16[128,8,768]{2,1,0:T(8,128)(2,1)} %fusion.8), calls=%async_computation.1 | async-start | bytes 3145728 | tf_op jit(solution)/shard_map/all_to_all | solution.py:72
  171.3 19.6 %collective-permute-start.20 = (bf16[64,768]{1,0:T(8,128)(2,1)S(1)}, bf16[64,768]{1,0:T(8,128)(2,1)S(1)}, u32[]{:S(2)}, u32[]{:S(2)}) collective-permute-start(bf16[64,768]{1,0:T(8,128)(2,1)S(1)} %get-tuple-element.48), channel_id=1, source_target_pairs={{0,1},{1,0},{2,3},{3,2},{4,5},{5,4},{6,7},{7,6},{8,9},{9,8},{10,11... | collective-permute-start | bytes 294920 | tf_op jit(solution)/shard_map/ppermute | solution.py:23
  172.4 64.5 %copy-start.12 = (bf16[64,768]{1,0:T(8,128)(2,1)}, bf16[64,768]{1,0:T(8,128)(2,1)S(1)}, u32[]{:S(2)}) copy-start(bf16[64,768]{1,0:T(8,128)(2,1)S(1)} %collective-permute-done.16) | copy-start | bytes 294916
  172.4 34.8 %copy-start.61 = (bf16[768,384]{1,0:T(8,128)(2,1)S(1)}, bf16[768,384]{1,0:T(8,128)(2,1)}, u32[]{:S(2)}) copy-start(bf16[768,384]{1,0:T(8,128)(2,1)} %convolution_convert_fusion.5) | copy-start | bytes 1769476
  172.4 20.3 %collective-permute-start.24 = (bf16[64,768]{1,0:T(8,128)(2,1)S(1)}, bf16[64,768]{1,0:T(8,128)(2,1)S(1)}, u32[]{:S(2)}, u32[]{:S(2)}) collective-permute-start(bf16[64,768]{1,0:T(8,128)(2,1)S(1)} %get-tuple-element.47), channel_id=1, source_target_pairs={{0,12},{1,13},{2,14},{3,15},{4,8},{5,9},{6,10},{7,11},{8,4},{9,5},... | collective-permute-start | bytes 294920 | tf_op jit(solution)/shard_map/ppermute | solution.py:23
  190.9 5.9 %collective-permute-start.28 = (bf16[64,768]{1,0:T(8,128)(2,1)S(1)}, bf16[64,768]{1,0:T(8,128)(2,1)S(1)}, u32[]{:S(2)}, u32[]{:S(2)}) collective-permute-start(bf16[64,768]{1,0:T(8,128)(2,1)S(1)} %get-tuple-element.46), channel_id=1, source_target_pairs={{0,3},{1,2},{2,1},{3,0},{4,7},{5,6},{6,5},{7,4},{8,11},{9,10},{10,... | collective-permute-start | bytes 294920 | tf_op jit(solution)/shard_map/ppermute | solution.py:23
  192.7 7.5 %collective-permute-start.17 = (bf16[128,768]{1,0:T(8,128)(2,1)S(1)}, bf16[128,768]{1,0:T(8,128)(2,1)S(1)}, u32[]{:S(2)}, u32[]{:S(2)}) collective-permute-start(bf16[128,768]{1,0:T(8,128)(2,1)S(1)} %pad_maximum_fusion.38), channel_id=1, source_target_pairs={{0,1},{1,0},{2,3},{3,2},{4,5},{5,4},{6,7},{7,6},{8,9},{9,8},{10,11... | collective-permute-start | bytes 589832 | tf_op jit(solution)/shard_map/ppermute | solution.py:23
  196.7 7.1 %collective-permute-start.21 = (bf16[128,768]{1,0:T(8,128)(2,1)S(1)}, bf16[128,768]{1,0:T(8,128)(2,1)S(1)}, u32[]{:S(2)}, u32[]{:S(2)}) collective-permute-start(bf16[128,768]{1,0:T(8,128)(2,1)S(1)} %pad_maximum_fusion.39), channel_id=1, source_target_pairs={{0,12},{1,13},{2,14},{3,15},{4,8},{5,9},{6,10},{7,11},{8,4},{9,5},... | collective-permute-start | bytes 589832 | tf_op jit(solution)/shard_map/ppermute | solution.py:23
  200.2 36.7 %copy-start.10 = (bf16[128,768]{1,0:T(8,128)(2,1)}, bf16[128,768]{1,0:T(8,128)(2,1)S(1)}, u32[]{:S(2)}) copy-start(bf16[128,768]{1,0:T(8,128)(2,1)S(1)} %collective-permute-done.17) | copy-start | bytes 589828
  200.2 7.0 %collective-permute-start.25 = (bf16[128,768]{1,0:T(8,128)(2,1)S(1)}, bf16[128,768]{1,0:T(8,128)(2,1)S(1)}, u32[]{:S(2)}, u32[]{:S(2)}) collective-permute-start(bf16[128,768]{1,0:T(8,128)(2,1)S(1)} %pad_maximum_fusion.40), channel_id=1, source_target_pairs={{0,3},{1,2},{2,1},{3,0},{4,7},{5,6},{6,5},{7,4},{8,11},{9,10},{10,... | collective-permute-start | bytes 589832 | tf_op jit(solution)/shard_map/ppermute | solution.py:23
  203.6 13.6 %copy-start.37 = (bf16[256,384]{1,0:T(8,128)(2,1)S(1)}, bf16[256,384]{1,0:T(8,128)(2,1)}, u32[]{:S(2)}) copy-start(bf16[256,384]{1,0:T(8,128)(2,1)} %get-tuple-element.41) | copy-start | bytes 589828
  203.9 4.1 %copy-start.29 = (bf16[128,768]{1,0:T(8,128)(2,1)}, bf16[128,768]{1,0:T(8,128)(2,1)S(1)}, u32[]{:S(2)}) copy-start(bf16[128,768]{1,0:T(8,128)(2,1)S(1)} %collective-permute-done.21) | copy-start | bytes 589828
  203.9 5.7 %collective-permute-start.29 = (bf16[128,768]{1,0:T(8,128)(2,1)S(1)}, bf16[128,768]{1,0:T(8,128)(2,1)S(1)}, u32[]{:S(2)}, u32[]{:S(2)}) collective-permute-start(bf16[128,768]{1,0:T(8,128)(2,1)S(1)} %pad_maximum_fusion.41), channel_id=1, source_target_pairs={{0,4},{1,5},{2,6},{3,7},{4,0},{5,1},{6,2},{7,3},{8,12},{9,13},{10,... | collective-permute-start | bytes 589832 | tf_op jit(solution)/shard_map/ppermute | solution.py:23
  207.2 15.0 %collective-permute-start.32 = (bf16[768,384]{1,0:T(8,128)(2,1)S(1)}, bf16[768,384]{1,0:T(8,128)(2,1)S(1)}, u32[]{:S(2)}, u32[]{:S(2)}) collective-permute-start(bf16[768,384]{1,0:T(8,128)(2,1)S(1)} %copy-done.61), channel_id=1, source_target_pairs={{0,16},{16,0},{32,48},{48,32},{64,80},{80,64},{96,112},{112,96},{1... | collective-permute-start | bytes 1769480 | tf_op jit(solution)/shard_map/ppermute | solution.py:77
  209.5 27.4 %collective-permute-start.18 = (bf16[256,768]{1,0:T(8,128)(2,1)}, bf16[256,768]{1,0:T(8,128)(2,1)S(1)}, u32[]{:S(2)}, u32[]{:S(2)}) collective-permute-start(bf16[256,768]{1,0:T(8,128)(2,1)} %pad_maximum_fusion.27), channel_id=1, source_target_pairs={{0,12},{1,13},{2,14},{3,15},{4,8},{5,9},{6,10},{7,11},{8,4},{9,5},... | collective-permute-start | bytes 1179656 | tf_op jit(solution)/shard_map/ppermute | solution.py:23
  213.5 25.5 %collective-permute-start.22 = (bf16[256,768]{1,0:T(8,128)(2,1)}, bf16[256,768]{1,0:T(8,128)(2,1)}, u32[]{:S(2)}, u32[]{:S(2)}) collective-permute-start(bf16[256,768]{1,0:T(8,128)(2,1)} %pad_maximum_fusion.28), channel_id=1, source_target_pairs={{0,3},{1,2},{2,1},{3,0},{4,7},{5,6},{6,5},{7,4},{8,11},{9,10},{10,... | collective-permute-start | bytes 1179656 | tf_op jit(solution)/shard_map/ppermute | solution.py:23
  217.1 25.8 %collective-permute-start.26 = (bf16[256,768]{1,0:T(8,128)(2,1)}, bf16[256,768]{1,0:T(8,128)(2,1)}, u32[]{:S(2)}, u32[]{:S(2)}) collective-permute-start(bf16[256,768]{1,0:T(8,128)(2,1)} %pad_maximum_fusion.29), channel_id=1, source_target_pairs={{0,4},{1,5},{2,6},{3,7},{4,0},{5,1},{6,2},{7,3},{8,12},{9,13},{10,... | collective-permute-start | bytes 1179656 | tf_op jit(solution)/shard_map/ppermute | solution.py:23
  222.2 24.1 %collective-permute-start.30 = (bf16[256,768]{1,0:T(8,128)(2,1)}, bf16[256,768]{1,0:T(8,128)(2,1)}, u32[]{:S(2)}, u32[]{:S(2)}) collective-permute-start(bf16[256,768]{1,0:T(8,128)(2,1)} %pad_maximum_fusion.30), channel_id=1, source_target_pairs={{0,1},{1,0},{2,3},{3,2},{4,5},{5,4},{6,7},{7,6},{8,9},{9,8},{10,11... | collective-permute-start | bytes 1179656 | tf_op jit(solution)/shard_map/ppermute | solution.py:23
  227.0 23.9 %all-to-all-start.3 = ((bf16[4,2,96,1024]{3,2,1,0:T(8,128)(2,1)}), bf16[4,2,96,1024]{3,2,1,0:T(8,128)(2,1)}, u32[]{:S(2)}, u32[]{:S(2)}) async-start(bf16[4,2,96,1024]{3,2,1,0:T(8,128)(2,1)} %pad_maximum_fusion.1), calls=%async_computation.3 | async-start | bytes 3145728 | tf_op jit(solution)/shard_map/all_to_all | solution.py:81
  237.0 4.0 %copy-start.19 = (bf16[256,768]{1,0:T(8,128)(2,1)}, bf16[256,768]{1,0:T(8,128)(2,1)S(1)}, u32[]{:S(2)}) copy-start(bf16[256,768]{1,0:T(8,128)(2,1)S(1)} %collective-permute-done.18) | copy-start | bytes 1179652
  237.9 22.7 %collective-permute-start.19 = (bf16[512,768]{1,0:T(8,128)(2,1)}, bf16[512,768]{1,0:T(8,128)(2,1)}, u32[]{:S(2)}, u32[]{:S(2)}) collective-permute-start(bf16[512,768]{1,0:T(8,128)(2,1)} %pad_maximum_fusion.13), channel_id=1, source_target_pairs={{0,3},{1,2},{2,1},{3,0},{4,7},{5,6},{6,5},{7,4},{8,11},{9,10},{10,... | collective-permute-start | bytes 2359304 | tf_op jit(solution)/shard_map/ppermute | solution.py:23
  241.0 21.1 %collective-permute-start.23 = (bf16[512,768]{1,0:T(8,128)(2,1)}, bf16[512,768]{1,0:T(8,128)(2,1)}, u32[]{:S(2)}, u32[]{:S(2)}) collective-permute-start(bf16[512,768]{1,0:T(8,128)(2,1)} %pad_maximum_fusion.14), channel_id=1, source_target_pairs={{0,4},{1,5},{2,6},{3,7},{4,0},{5,1},{6,2},{7,3},{8,12},{9,13},{10,... | collective-permute-start | bytes 2359304 | tf_op jit(solution)/shard_map/ppermute | solution.py:23
  244.9 19.6 %collective-permute-start.27 = (bf16[512,768]{1,0:T(8,128)(2,1)}, bf16[512,768]{1,0:T(8,128)(2,1)}, u32[]{:S(2)}, u32[]{:S(2)}) collective-permute-start(bf16[512,768]{1,0:T(8,128)(2,1)} %pad_maximum_fusion.15), channel_id=1, source_target_pairs={{0,1},{1,0},{2,3},{3,2},{4,5},{5,4},{6,7},{7,6},{8,9},{9,8},{10,11... | collective-permute-start | bytes 2359304 | tf_op jit(solution)/shard_map/ppermute | solution.py:23
  248.3 18.8 %collective-permute-start.31 = (bf16[512,768]{1,0:T(8,128)(2,1)}, bf16[512,768]{1,0:T(8,128)(2,1)}, u32[]{:S(2)}, u32[]{:S(2)}) collective-permute-start(bf16[512,768]{1,0:T(8,128)(2,1)} %pad_maximum_fusion.16), channel_id=1, source_target_pairs={{0,12},{1,13},{2,14},{3,15},{4,8},{5,9},{6,10},{7,11},{8,4},{9,5},... | collective-permute-start | bytes 2359304 | tf_op jit(solution)/shard_map/ppermute | solution.py:23
  250.9 30.3 %all-to-all-start.2 = ((bf16[4,3,96,1024]{3,2,1,0:T(8,128)(2,1)}), bf16[4,3,96,1024]{3,2,1,0:T(8,128)(2,1)S(1)}, u32[]{:S(2)}, u32[]{:S(2)}) async-start(bf16[4,3,96,1024]{3,2,1,0:T(8,128)(2,1)} %pad_maximum_fusion), calls=%async_computation.2 | async-start | bytes 4718592 | tf_op jit(solution)/shard_map/all_to_all | solution.py:81
  264.5 4.9 %copy-start.15 = (bf16[128,8,768]{2,1,0:T(8,128)(2,1)S(1)}, bf16[128,8,768]{2,1,0:T(8,128)(2,1)}, u32[]{:S(2)}) copy-start(bf16[128,8,768]{2,1,0:T(8,128)(2,1)} %copy-done.14) | copy-start | bytes 4718596
  264.5 4.9 %copy-start.24 = (pred[256,1024]{1,0:T(32,128)(4,1)S(1)}, pred[256,1024]{1,0:T(32,128)(4,1)}, u32[]{:S(2)}) copy-start(pred[256,1024]{1,0:T(32,128)(4,1)} %copy-done.22) | copy-start | bytes 786436
  264.5 4.9 %copy-start.27 = (pred[256,1024]{1,0:T(32,128)(4,1)S(1)}, pred[256,1024]{1,0:T(32,128)(4,1)}, u32[]{:S(2)}) copy-start(pred[256,1024]{1,0:T(32,128)(4,1)} %copy-done.25) | copy-start | bytes 786436
  283.8 6.1 %copy-start.3 = (bf16[768,1024]{1,0:T(8,128)(2,1)S(1)}, bf16[768,1024]{1,0:T(8,128)(2,1)}, u32[]{:S(2)}) copy-start(bf16[768,1024]{1,0:T(8,128)(2,1)} %param.21) | copy-start | bytes 4718596
  285.2 17.7 %all-to-all-start.4 = ((bf16[16,64,480]{2,1,0:T(8,128)(2,1)}), bf16[16,64,480]{2,1,0:T(8,128)(2,1)S(1)}, u32[]{:S(2)}, u32[]{:S(2)}) async-start(bf16[16,64,480]{2,1,0:T(8,128)(2,1)} %bitcast.122), calls=%async_computation.4 | async-start | bytes 2097152 | tf_op jit(solution)/shard_map/all_to_all | solution.py:175
  290.0 2.8 copy-start.4
  290.0 2.8 copy-start.16
  294.8 9.1 %copy-start.1 = (bf16[768,1024]{1,0:T(8,128)(2,1)S(1)}, bf16[768,1024]{1,0:T(8,128)(2,1)}, u32[]{:S(2)}) copy-start(bf16[768,1024]{1,0:T(8,128)(2,1)} %param.19) | copy-start | bytes 4718596
  (42 other events, 60.9 us)

commit v2 on v1

v2 whole, which is shorter than its diff:
```python
import functools

import jax
import jax.numpy as jnp
from jax import lax
from jax.experimental import pallas as pl
from jax.experimental.pallas import tpu as pltpu
from jax.sharding import PartitionSpec as P

BF = jnp.bfloat16
F32 = jnp.float32
I32 = jnp.int32
MIB = 1024 * 1024
MASKS = (4, 1, 12, 3)
ORDERS = tuple(tuple(MASKS[(q + k) % 4] for k in range(4)) for q in range(4))
IN_VMEM = pl.BlockSpec(memory_space=pltpu.VMEM)
ANYWHERE = pl.BlockSpec(memory_space=pl.ANY)
IN_SMEM = pl.BlockSpec(memory_space=pltpu.SMEM)


def dot(a, b, dims=((1,), (0,))):
    return lax.dot_general(a, b, (dims, ((), ())), preferred_element_type=F32)


def shape(dims, kind):
    return jax.ShapeDtypeStruct(dims, kind)


def params(mib):
    return pltpu.CompilerParams(vmem_limit_bytes=mib * MIB)


def join_kernel(*refs):
    n = (len(refs) - 1) // 3
    sems = refs[-1]
    copies = []
    for i in range(n):
        a, b, out = refs[2 * i], refs[2 * i + 1], refs[2 * n + i]
        rows = a.shape[0]
        copies.append(pltpu.make_async_copy(a, out.at[pl.ds(0, rows)], sems.at[2 * i]))
        copies.append(pltpu.make_async_copy(b, out.at[pl.ds(rows, rows)], sems.at[2 * i + 1]))
    for copy in copies:
        copy.start()
    for copy in copies:
        copy.wait()


def join(pairs):
    n = len(pairs)
    flat = [v for pair in pairs for v in pair]
    outs = [shape((2 * a.shape[0],) + a.shape[1:], a.dtype) for a, _ in pairs]
    return pl.pallas_call(
        join_kernel,
        out_shape=outs,
        in_specs=[ANYWHERE] * (2 * n),
        out_specs=[ANYWHERE] * n,
        scratch_shapes=[pltpu.SemaphoreType.DMA((2 * n,))],
        name="join",
    )(*flat)


def travel(parts, k):
    pairs = []
    for q, part in enumerate(parts):
        mask = ORDERS[q % 4][k]
        pairs.append((part, lax.ppermute(part, "col", [(i, i ^ mask) for i in range(16)])))
    return pairs


def source_mask(q, m):
    value = 0
    for k in range(4):
        if (m >> k) & 1:
            value ^= ORDERS[q][k]
    return value


def column_of(entries, col):
    diff = (entries >> 8) ^ col
    bits = {}
    for axis, (near, far) in enumerate(((4, 12), (1, 3))):
        d = (diff >> 2) if axis == 0 else (diff & 3)
        bits[far] = d >> 1
        bits[near] = (d & 1) ^ (d >> 1)
    quarter = (entries >> 6) & 3
    place = jnp.zeros_like(entries)
    for q in range(4):
        m = jnp.zeros_like(entries)
        for k in range(4):
            m = m + (bits[ORDERS[q][k]] << k)
        place = jnp.where(quarter == q, m, place)
    return jnp.where(entries >= 0, quarter * 1024 + place * 64 + (entries & 63), -1)


def table_kernel(col_ref, nbr_ref, token_ref, out_ref):
    places = column_of(nbr_ref[...], col_ref[0])

    @pl.loop(0, 16)
    def _(t):
        lanes = lax.broadcasted_iota(I32, (256, 256), 1) + t * 256
        acc = jnp.zeros((256, 256), F32)
        for slot in range(16):
            acc = acc + jnp.where(places[:, slot : slot + 1] == lanes, 1.0, 0.0)
        out_ref[:, pl.ds(pl.multiple_of(t * 256, 256), 256)] = acc.astype(BF)


def cite_table(col, nbr, token):
    return pl.pallas_call(
        table_kernel,
        out_shape=shape((256, 4096), BF),
        in_specs=[IN_SMEM, IN_VMEM, ANYWHERE],
        out_specs=IN_VMEM,
        compiler_params=params(16),
        cost_estimate=pl.CostEstimate(flops=10**9, bytes_accessed=3 * 10**6, transcendentals=0),
        name="cite_table",
    )(col, nbr, token)


def back_table_kernel(col_ref, a_ref, b_ref, out_ref):
    col = col_ref[0]
    own = lax.broadcasted_iota(I32, (256, 256), 0) + col * 256
    for m in range(16):
        half = a_ref if m < 8 else b_ref
        acc = jnp.zeros((256, 256), F32)
        for slot in range(16):
            acc = acc + jnp.where(half[m % 8, slot : slot + 1, :] == own, 1.0, 0.0)
        block = col ^ source_mask(0, m)
        out_ref[:, pl.ds(pl.multiple_of(block * 256, 256), 256)] = acc.astype(BF)


def cited_by_table(col, a, b):
    return pl.pallas_call(
        back_table_kernel,
        out_shape=shape((256, 4096), BF),
        in_specs=[IN_SMEM, IN_VMEM, IN_VMEM],
        out_specs=IN_VMEM,
        compiler_params=params(16),
        cost_estimate=pl.CostEstimate(flops=10**9, bytes_accessed=3 * 10**6, transcendentals=0),
        name="cited_by_table",
    )(col, a, b)


def edge_lists(write_src, write_dst):
    none = jnp.full_like(write_src, -1)
    pick = jnp.concatenate([write_src, jnp.where(write_dst >= 0, write_dst + 256, -1)], axis=1)
    into_paper = jnp.concatenate([write_dst, none], axis=1)
    into_author = jnp.concatenate([none, write_src], axis=1)
    return pick.reshape(-1), into_paper.reshape(1, -1), into_author.reshape(1, -1)


def exchange(rows):
    sent = rows.reshape(128, 8, rows.shape[-1])
    got = lax.all_to_all(sent, ("row", "col"), split_axis=0, concat_axis=0, tiled=True)
    return got.reshape(1024, rows.shape[-1])


def other_core(value):
    return lax.ppermute(value, "row", [(i, i ^ 1) for i in range(8)])


def over_y(parts):
    return lax.all_to_all(
        parts, "row", split_axis=0, concat_axis=0, tiled=True,
        axis_index_groups=[[0, 2, 4, 6], [1, 3, 5, 7]],
    )


def silu_and_slope(value):
    sigma = 1.0 / (1.0 + jnp.exp(-value))
    return (value * sigma).astype(BF), sigma * (1.0 + value * (1.0 - sigma))


def author_kernel(
    arrived_ref, into_paper_ref, into_author_ref, x_author_ref, x_paper_ref, grad_ref,
    w_sa_hbm, w_wn_hbm, w_sp_hbm, w_wr_hbm,
    out_ref, pack_ref, dz_ref, dx_ref, pre_ref, adder_ref, cnt_ref,
    w_sa, w_wn, w_sp, w_wr, sems,
):
    copies = []
    for i, (a, b) in enumerate(((w_sa_hbm, w_sa), (w_wn_hbm, w_wn), (w_sp_hbm, w_sp), (w_wr_hbm, w_wr))):
        copies.append(pltpu.make_async_copy(a, b, sems.at[i]))
        copies[-1].start()
    ids = lax.broadcasted_iota(I32, (256, 1024), 0)
    means = []
    for i, ref in enumerate((into_paper_ref, into_author_ref)):
        hit = jnp.where(ref[...] == ids, 1.0, 0.0)
        cnt = jnp.maximum(jnp.sum(hit, axis=1, keepdims=True), 1.0)
        cnt_ref[pl.ds(256 * i, 256), :] = jnp.broadcast_to(cnt, (256, 128))
        hit = hit.astype(BF)
        adder_ref[pl.ds(256 * i, 256), :] = hit
        means.append((dot(hit, arrived_ref[...]) / cnt).astype(BF))
    written, authored = means
    x_author, x_paper = x_author_ref[...], x_paper_ref[...]
    copies[0].wait()
    copies[1].wait()
    pre = dot(x_author, w_sa[...]) + dot(authored, w_wn[...])
    out, slope = silu_and_slope(pre)
    out_ref[...] = out
    dpre = (grad_ref[...].astype(F32) * slope).astype(BF)
    pack_ref[:, pl.ds(0, 768)] = x_author
    pack_ref[:, pl.ds(768, 768)] = authored
    pack_ref[:, pl.ds(1536, 768)] = x_paper
    pack_ref[:, pl.ds(2304, 768)] = written
    pack_ref[:, pl.ds(3072, 1024)] = dpre
    dz_ref[...] = (dot(dpre, w_wn[...], ((1,), (1,))) / cnt_ref[pl.ds(256, 256), pl.ds(0, 1)]).astype(BF)
    dx_ref[...] = dot(dpre, w_sa[...], ((1,), (1,)))
    copies[2].wait()
    copies[3].wait()
    pre_ref[...] = dot(x_paper, w_sp[...]) + dot(written, w_wr[...])


def author_step(arrived, into_paper, into_author, x_author, x_paper, grad, w_sa, w_wn, w_sp, w_wr):
    weight = pltpu.VMEM((768, 1024), BF)
    return pl.pallas_call(
        author_kernel,
        out_shape=[
            shape((256, 1024), BF), shape((256, 4096), BF), shape((256, 768), BF), shape((256, 768), F32),
            shape((256, 1024), F32), shape((512, 1024), BF), shape((512, 128), F32),
        ],
        in_specs=[IN_VMEM] * 6 + [ANYWHERE] * 4,
        out_specs=[IN_VMEM] * 7,
        scratch_shapes=[weight] * 4 + [pltpu.SemaphoreType.DMA((4,))],
        compiler_params=params(40),
        cost_estimate=pl.CostEstimate(flops=4 * 10**9, bytes_accessed=15 * 10**6, transcendentals=0),
        name="author_step",
    )(arrived, into_paper, into_author, x_author, x_paper, grad, w_sa, w_wn, w_sp, w_wr)


def half_kernel(offset, *refs):
    table_ref, blocks, out_ref = refs[0], refs[1:5], refs[5]
    acc = jnp.zeros((256, 768), F32)
    for q in range(4):
        acc = acc + dot(table_ref[:, pl.ds(q * 1024 + offset, 512)], blocks[q][...])
    out_ref[...] = acc


def first_half(table, blocks):
    return pl.pallas_call(
        functools.partial(half_kernel, 0),
        out_shape=shape((256, 768), F32),
        in_specs=[IN_VMEM] * 5,
        out_specs=IN_VMEM,
        compiler_params=params(24),
        cost_estimate=pl.CostEstimate(flops=2 * 10**9, bytes_accessed=5 * 10**6, transcendentals=0),
        name="first_half",
    )(table, *blocks)


def paper_kernel(
    table_ref, b0, b1, b2, b3, first_ref, nbr_ref, pre_ref, grad_ref, w_hbm,
    out_ref, pack_ref, dz_ref, w_ref, sem,
):
    copy = pltpu.make_async_copy(w_hbm, w_ref, sem)
    copy.start()
    total = first_ref[...]
    for q, block in enumerate((b0, b1, b2, b3)):
        total = total + dot(table_ref[:, pl.ds(q * 1024 + 512, 512)], block[...])
    cnt = jnp.sum(jnp.where(nbr_ref[...] >= 0, 1.0, 0.0), axis=1, keepdims=True)
    cnt = jnp.maximum(cnt, 1.0)
    cited = (total / cnt).astype(BF)
    pack_ref[:, pl.ds(0, 768)] = cited
    copy.wait()
    out, slope = silu_and_slope(pre_ref[...] + dot(cited, w_ref[...]))
    out_ref[...] = out
    dpre = (grad_ref[...].astype(F32) * slope).astype(BF)
    pack_ref[:, pl.ds(768, 1024)] = dpre
    dz_ref[...] = (dot(dpre, w_ref[...], ((1,), (1,))) / cnt).astype(BF)


def paper_step(table, blocks, first, nbr, pre, grad, w_cite):
    return pl.pallas_call(
        paper_kernel,
        out_shape=[shape((256, 1024), BF), shape((256, 1792), BF), shape((256, 768), BF)],
        in_specs=[IN_VMEM] * 9 + [ANYWHERE],
        out_specs=[IN_VMEM] * 3,
        scratch_shapes=[pltpu.VMEM((768, 1024), BF), pltpu.SemaphoreType.DMA],
        compiler_params=params(32),
        cost_estimate=pl.CostEstimate(flops=3 * 10**9, bytes_accessed=10 * 10**6, transcendentals=0),
        name="paper_step",
    )(table, *blocks, first, nbr, pre, grad, w_cite)


def edge_back_kernel(pack_ref, cnt_ref, w_wr_hbm, w_sp_hbm, dz_ref, dx_ref, w_wr, w_sp, sems):
    copies = [pltpu.make_async_copy(w_wr_hbm, w_wr, sems.at[0]), pltpu.make_async_copy(w_sp_hbm, w_sp, sems.at[1])]
    for copy in copies:
        copy.start()
    dpre = pack_ref[:, pl.ds(768, 1024)]
    copies[0].wait()
    dz_ref[...] = (dot(dpre, w_wr[...], ((1,), (1,))) / cnt_ref[pl.ds(0, 256), pl.ds(0, 1)]).astype(BF)
    copies[1].wait()
    dx_ref[...] = dot(dpre, w_sp[...], ((1,), (1,)))


def edge_back(pack, cnt, w_write, w_self):
    return pl.pallas_call(
        edge_back_kernel,
        out_shape=[shape((256, 768), BF), shape((256, 768), F32)],
        in_specs=[IN_VMEM, IN_VMEM, ANYWHERE, ANYWHERE],
        out_specs=[IN_VMEM] * 2,
        scratch_shapes=[pltpu.VMEM((768, 1024), BF)] * 2 + [pltpu.SemaphoreType.DMA((2,))],
        compiler_params=params(16),
        cost_estimate=pl.CostEstimate(flops=10**9, bytes_accessed=5 * 10**6, transcendentals=0),
        name="edge_back",
    )(pack, cnt, w_write, w_self)


def weight_kernel(lefts, right, core_ref, *refs):
    ins, out_ref, turned = refs[: -2], refs[-2], refs[-1]
    core = core_ref[0]
    own, other, lane = right
    dpre = jnp.concatenate([ins[own][:, pl.ds(lane, 1024)], ins[other][:, pl.ds(lane, 1024)]], axis=0)
    for i, (own, other, lane) in enumerate(lefts):
        for k, ref in enumerate((ins[own], ins[other])):
            turned[i, :, pl.ds(256 * k, 256)] = ref[:, pl.ds(lane, 768)].T
        rows = []
        for y in range(4):
            start = pl.multiple_of((2 * y + core) * 96, 32)
            rows.append(turned[i, pl.ds(start, 96), :])
        product = dot(jnp.concatenate(rows, axis=0), dpre).astype(BF)
        for y in range(4):
            out_ref[y, i] = product[96 * y : 96 * y + 96]


def weight_parts(core, arrays, lefts, right):
    n = len(lefts)
    return pl.pallas_call(
        functools.partial(weight_kernel, lefts, right),
        out_shape=shape((4, n, 96, 1024), BF),
        in_specs=[IN_SMEM] + [IN_VMEM] * len(arrays),
        out_specs=IN_VMEM,
        scratch_shapes=[pltpu.VMEM((n, 768, 512), BF)],
        compiler_params=params(32),
        cost_estimate=pl.CostEstimate(flops=2 * 10**9, bytes_accessed=8 * 10**6, transcendentals=0),
        name="weight_parts",
    )(core, *arrays)


def y_sum_kernel(paper_ref, author_ref, out_ref, stack):
    for m in range(5):
        ref, i = (paper_ref, m) if m < 3 else (author_ref, m - 3)
        total = ref[0, i].astype(F32)
        for y in range(1, 4):
            total = total + ref[y, i].astype(F32)
        stack[pl.ds(96 * m, 96), :] = total
    stack[pl.ds(480, 32), :] = jnp.zeros((32, 1024), F32)
    for j in range(16):
        if j % 2 == 0:
            turned = stack[:, pl.ds(64 * j, 128)].T.astype(BF)
        out_ref[j] = turned[64 * (j % 2) : 64 * (j % 2) + 64]


def y_sum(paper, author):
    return pl.pallas_call(
        y_sum_kernel,
        out_shape=shape((16, 64, 512), BF),
        in_specs=[IN_VMEM] * 2,
        out_specs=IN_VMEM,
        scratch_shapes=[pltpu.VMEM((512, 1024), F32)],
        compiler_params=params(20),
        name="y_sum",
    )(paper, author)


def last_sum_kernel(got_ref, out_ref):
    total = got_ref[0].astype(F32)
    for j in range(1, 16):
        total = total + got_ref[j].astype(F32)
    total = total * (32768.0 ** -0.5)
    for m in range(5):
        out_ref[m] = total[:, 96 * m : 96 * m + 96]


def last_sum(got):
    return pl.pallas_call(
        last_sum_kernel,
        out_shape=shape((5, 64, 96), F32),
        in_specs=[IN_VMEM],
        out_specs=IN_VMEM,
        compiler_params=params(8),
        name="last_sum",
    )(got)


def per_device(
    x_paper, x_author, cite_nbr, write_src, write_dst,
    w_self_paper, w_cite, w_write, w_self_author, w_written, grad_paper, grad_author,
):
    col = lax.axis_index("col").astype(I32).reshape(1)
    core = (lax.axis_index("row") & 1).astype(I32).reshape(1)

    pick, into_paper, into_author = edge_lists(write_src[0], write_dst[0])
    picker = (pick[:, None] == lax.iota(I32, 512)[None, :]).astype(BF)
    rows = dot(picker, jnp.concatenate([x_author, x_paper], axis=0)).astype(BF)
    arrived = exchange(rows)

    parts = [x_paper[64 * q : 64 * q + 64] for q in range(4)] + [cite_nbr.T.reshape(1, 16, 256)]
    parts = join(travel(parts, 0))
    table = cite_table(col, cite_nbr, parts[0])
    parts = join(travel(parts, 1))
    parts = join(travel(parts, 2))
    pairs = travel(parts, 3)
    cite_first = first_half(table, [pair[0] for pair in pairs[:4]])

    out_author, pack_a, dz_written, dx_author_own, pre_paper, adder, cnt = author_step(
        arrived, into_paper, into_author, x_author, x_paper, grad_author,
        w_self_author, w_written, w_self_paper, w_write,
    )
    pack_a_other = other_core(pack_a)
    parts_author = weight_parts(core, [pack_a, pack_a_other], [(0, 1, 0), (0, 1, 768)], (0, 1, 3072))
    got_author = over_y(parts_author)

    out_paper, pack_p, dz_cite = paper_step(
        table, [pair[1] for pair in pairs[:4]], cite_first, cite_nbr, pre_paper, grad_paper, w_cite
    )
    gathered = lax.all_gather(dz_cite, "col", axis=0, tiled=True)
    pack_p_other = other_core(pack_p)
    dz_write, dx_paper_own = edge_back(pack_p, cnt, w_write, w_self_paper)
    rows = dot(picker, jnp.concatenate([dz_written, dz_write], axis=0)).astype(BF)
    parts_paper = weight_parts(
        core, [pack_a, pack_a_other, pack_p, pack_p_other],
        [(0, 1, 1536), (2, 3, 0), (0, 1, 2304)], (2, 3, 768),
    )
    got_paper = over_y(parts_paper)
    back = exchange(rows)
    back_table = cited_by_table(col, pairs[4][0], pairs[4][1])

    got = lax.all_to_all(y_sum(got_paper, got_author), "col", split_axis=0, concat_axis=0, tiled=True)
    dweights = last_sum(got).transpose(0, 2, 1)

    edge_sum = dot(adder, back)
    dx_author = (dx_author_own + edge_sum[256:]).astype(BF)
    dx_paper = (dot(back_table, gathered) + (dx_paper_own + edge_sum[:256])).astype(BF)
    return (out_paper, out_author, dx_paper, dx_author, dweights)


def solution(mesh):
    part = P(("row", "col"), None)
    part3 = P(("row", "col"), None, None)
    return jax.shard_map(
        per_device,
        mesh=mesh,
        in_specs=(part, part, part, part3, part3, P(), P(), P(), P(), P(), part, part),
        out_specs=(part, part, part, part, P(None, "row", "col")),
        check_vma=False,
    )
```

time: 309 us -> 431 us (1.39)
  Pallas kernels: 0 us -> 219 us
  matrix products: 70.7 us -> 14.7 us
  waiting for transfers between devices: 45.6 us -> 100 us
  other arithmetic: 49.7 us -> 2.2 us
  blocking collectives: 38.3 us -> 0 us
  starting transfers between devices: 79.1 us -> 56.8 us
  between operations: 2.01 us -> 14.8 us
    pallas_call x0 -> x13, Pallas kernels: none -> 219 us  [the longest x3 177 us: join(): pl.pallas_call(join_kernel, out_shape=outs, in_specs=[ANYWHERE] * (2 * n)...]
    dot_general x39 -> x4, matrix products: 70.7 us -> 14.7 us  [dot(): return lax.dot_general(a, b, (dims, ((), ())), preferred_element_type=F32)]
    all_gather x1 -> x0, blocking collectives: 38.3 us -> none  [per_device(): lax.all_gather(cite_nbr, 'col', axis=0, tiled=True).reshape(16, 4, 64, 16)]
    all_to_all x2, waiting for transfers between devices: 6.91 us -> 33 us  [over_y(): lax.all_to_all(parts, 'row', split_axis=0, concat_axis=0, tiled=True, axi...]
    concatenate x26 -> x0, other arithmetic: 22.3 us -> none  [the longest x24 21 us: gather_col(): parts[q] = jnp.concatenate([parts[q], got], axis=0)]
    ppermute x32 -> x20, starting transfers between devices: 48.1 us -> 26.6 us  [travel(): lax.ppermute(part, 'col', [(i, i ^ mask) for i in range(16)])]
    all_to_all x2, waiting for transfers between devices: 0.01 us -> 20.9 us  [exchange(): lax.all_to_all(sent, ('row', 'col'), split_axis=0, concat_axis=0, tiled=T...]
    convert_element_type x2 -> x1, other arithmetic: 17.6 us -> 0.82 us  [per_device(): dx_author = (dx_author_own + edge_sum[256:]).astype(BF)]
  transfers between devices with their start and end apart: 41 -> 28, of which waited for: 12 -> 13; matrix products, arithmetic and copies ran while one was open for 39% -> 2% of each run, Pallas kernels for 0% -> 49%
where the time goes in v2:
time: 431 us; the launch traced here: 430 us
  Pallas kernels  219 us (51%)
  waiting for transfers between devices  100 us (23%)
  starting transfers between devices  56.8 us (13%)
  local copies, waits for them, and re-layouts  22.3 us (5%)
  between operations  14.8 us (3%)
  matrix products  14.7 us (3%)
    pallas_call x3, Pallas kernels, join(): pl.pallas_call(join_kernel, out_shape=outs, in_specs=[ANYWHERE] * (2 * n)...  177 us
    ppermute x20, waiting for transfers between devices, travel(): lax.ppermute(part, 'col', [(i, i ^ mask) for i in range(16)])  39.8 us
    all_to_all x2, waiting for transfers between devices, over_y(): lax.all_to_all(parts, 'row', split_axis=0, concat_axis=0, tiled=True, axi...  33 us
    ppermute x20, starting transfers between devices, travel(): lax.ppermute(part, 'col', [(i, i ^ mask) for i in range(16)])  26.6 us
    unnamed x129, local copies, waits for them, and re-layouts  21.8 us
    all_to_all x2, waiting for transfers between devices, exchange(): lax.all_to_all(sent, ('row', 'col'), split_axis=0, concat_axis=0, tiled=T...  20.9 us
    all_to_all x2, starting transfers between devices, exchange(): lax.all_to_all(sent, ('row', 'col'), split_axis=0, concat_axis=0, tiled=T...  18.7 us
    dot_general x4, matrix products, dot(): return lax.dot_general(a, b, (dims, ((), ())), preferred_element_type=F32)  14.7 us
  transfers between devices with their start and end apart: 28, of which 13 were waited for; matrix products, arithmetic and copies ran while one was open for 2% of the time, Pallas kernels for 49%

profile of v2, /device:TPU:0, one launch (start us, length us, event | category | flops | bytes accessed | tf_op | source)
XLA Modules:
  0.0 430.2 jit_solution(15497160634273664241)
XLA Ops:
  7.9 0.7 pad_add_fusion
  8.7 3.4 fusion.7
  12.1 11.6 %all-to-all-start = ((bf16[128,8,768]{2,1,0:T(8,128)(2,1)}), bf16[128,8,768]{2,1,0:T(8,128)(2,1)}, u32[]{:S(2)}, u32[]{:S(2)}) async-start(bf16[128,8,768]{2,1,0:T(8,128)(2,1)} %fusion.7), calls=%async_computation | async-start | bytes 3145728 | tf_op jit(solution)/shard_map/all_to_all | solution.py:153
  23.9 1.0 collective-permute-start
  24.8 1.6 collective-permute-start.1
  26.4 2.1 collective-permute-start.2
  28.5 2.3 collective-permute-start.3
  31.5 12.4 %collective-permute-done.4.refs_9_ = s32[1,16,256]{2,1,0:T(8,128)S(1)} collective-permute-done((s32[1,16,256]{2,1,0:T(8,128)S(1)}, s32[1,16,256]{2,1,0:T(8,128)S(1)}, u32[]{:S(2)}, u32[]{:S(2)}) %collective-permute-start.4) | collective-permute-done | bytes 16416 | tf_op jit(solution)/shard_map/ppermute | solution.py:66
  43.9 0.8 collective-permute-done.2.refs_5_
  46.0 26.0 %join.3 = (bf16[128,768]{1,0:T(8,128)(2,1)}, bf16[128,768]{1,0:T(8,128)(2,1)}, bf16[128,768]{1,0:T(8,128)(2,1)}, bf16[128,768]{1,0:T(8,128)(2,1)}, s32[2,16,256]{2,1,0:T(8,128)}) custom-call(bf16[64,768]{1,0:T(8,128)(2,1)} %copy-done.47, bf16[64,768]{1,0:T(8,128)(2,1)} %copy-done.52, bf16[64,768]{1,0:T(8,128)(2,1)} %copy-done.46, ...), custom_call_target="tpu_custom_call" | custom-call | tf_op jit(solution)/shard_map/join/pallas_call | solution.py:52
  72.0 1.7 collective-permute-start.5
  73.7 1.9 collective-permute-start.6
  75.6 2.0 collective-permute-start.7
  78.0 0.8 collective-permute-start.9
  78.8 3.3 collective-permute-done.9.refs_9_
  82.1 1.4 collective-permute-done.7.refs_5_
  84.9 50.8 %join.4 = (bf16[256,768]{1,0:T(8,128)(2,1)}, bf16[256,768]{1,0:T(8,128)(2,1)}, bf16[256,768]{1,0:T(8,128)(2,1)}, bf16[256,768]{1,0:T(8,128)(2,1)}, s32[4,16,256]{2,1,0:T(8,128)}) custom-call(bf16[128,768]{1,0:T(8,128)(2,1)} %get-tuple-element.32.token_ref.refs_0_, bf16[128,768]{1,0:T(8,128)(2,1)} %copy-done.48, bf16[128,768]{1,0:T(8,128)(2,1)} %get-tuple-element.33.refs_2_, ...), custom_call_target="tpu_custom_call" | custom-call | tf_op jit(solution)/shard_map/join/pallas_call | solution.py:52
  135.7 1.2 collective-permute-start.10
  136.9 2.2 collective-permute-start.11
  139.1 1.8 collective-permute-start.14
  140.9 7.4 %collective-permute-done.14.refs_9_ = s32[4,16,256]{2,1,0:T(8,128)S(1)} collective-permute-done((s32[4,16,256]{2,1,0:T(8,128)}, s32[4,16,256]{2,1,0:T(8,128)S(1)}, u32[]{:S(2)}, u32[]{:S(2)}) %collective-permute-start.14) | collective-permute-done | bytes 65568 | tf_op jit(solution)/shard_map/ppermute | solution.py:66
  149.4 0.7 copy-done.43
  150.2 100.5 %join.5 = (bf16[512,768]{1,0:T(8,128)(2,1)}, bf16[512,768]{1,0:T(8,128)(2,1)}, bf16[512,768]{1,0:T(8,128)(2,1)}, bf16[512,768]{1,0:T(8,128)(2,1)}, s32[8,16,256]{2,1,0:T(8,128)}) custom-call(bf16[256,768]{1,0:T(8,128)(2,1)} %get-tuple-element.37.refs_0_, bf16[256,768]{1,0:T(8,128)(2,1)} %copy-done.40, bf16[256,768]{1,0:T(8,128)(2,1)} %get-tuple-element.38.refs_2_, ...), custom_call_target="tpu_custom_call" | custom-call | tf_op jit(solution)/shard_map/join/pallas_call | solution.py:52
  250.6 1.5 collective-permute-start.15
  252.2 2.4 collective-permute-start.18
  255.4 10.5 %cite_table.1.refs_0_.table_ref = bf16[256,4096]{1,0:T(8,128)(2,1)S(1)} custom-call(s32[1]{0:T(128)} %bitcast.col_ref, s32[256,16]{1,0:T(8,128)S(1)} %copy.21.nbr_ref, bf16[128,768]{1,0:T(8,128)(2,1)S(1)} %copy-done.15), custom_call_target="tpu_custom_call" | custom-call | flops 1000000000 | bytes 3000000 | tf_op jit(solution)/shard_map/cite_table/pallas_call | solution.py:108
  266.1 1.0 first_half.1.first_ref
  267.1 1.3 copy-done.31
  268.4 0.9 copy-done.34
  269.3 1.4 copy-done.18
  270.7 1.4 copy-done.19
  272.1 1.0 copy-done.27
  273.1 1.0 copy-done.29
  274.1 6.9 %author_step.1 = (bf16[256,1024]{1,0:T(8,128)(2,1)}, bf16[256,4096]{1,0:T(8,128)(2,1)}, bf16[256,768]{1,0:T(8,128)(2,1)S(1)}, f32[256,768]{1,0:T(8,128)S(1)}, f3...) custom-call(bf16[1024,768]{1,0:T(8,128)(2,1)} %bitcast.7.arrived_ref, ...), custom_call_target="tpu_custom_call" | custom-call | flops 4000000000 | bytes 15000000 | tf_op jit(solution)/shard_map/author_step/pallas_call | solution.py:214
  281.2 6.3 %paper_step.1 = (bf16[256,1024]{1,0:T(8,128)(2,1)}, bf16[256,1792]{1,0:T(8,128)(2,1)S(1)}, bf16[256,768]{1,0:T(8,128)(2,1)}) custom-call(bf16[256,4096]{1,0:T(8,128)(2,1)S(1)} %copy-done.32, bf16[512,768]{1,0:T(8,128)(2,1)} %collective-permute-done.15.b0, bf16[512,768]{1,0:T(8,128)(2,1)} %collective-permute-done.16.b1, ...), custom_call_target="tpu_custom_call" | custom-call | flops 3000000000 | bytes 10000000 | tf_op jit(solution)/shard_map/paper_step/pallas_call | solution.py:271
  287.7 4.3 collective-permute-done.20.refs_1_
  292.0 2.8 weight_parts.3
  294.8 1.1 copy-done.9
  296.0 3.6 all-to-all-start.3
  299.8 2.4 collective-permute-done.21.refs_3_
  302.2 1.6 copy-done.4
  303.8 3.4 weight_parts.2
  307.2 1.5 copy-done
  308.7 12.2 %all-to-all-done.3.author_ref = bf16[4,2,96,1024]{3,2,1,0:T(8,128)(2,1)S(1)} async-done(((bf16[4,2,96,1024]{3,2,1,0:T(8,128)(2,1)}), bf16[4,2,96,1024]{3,2,1,0:T(8,128)(2,1)S(1)}, u32[]{:S(2)}, u32[]{:S(2)}) %all-to-all-start.3) | async-done | bytes 1572896 | tf_op jit(solution)/shard_map/all_to_all | solution.py:162
  320.8 1.1 copy-done.1
  322.0 3.9 all-to-all-start.2
  325.9 1.5 copy-done.6
  327.3 1.4 copy-done.8
  328.8 1.7 edge_back.1
  330.5 0.9 copy-done.25
  331.4 2.2 fusion.6
  333.6 20.8 %all-to-all-done.2.paper_ref = bf16[4,3,96,1024]{3,2,1,0:T(8,128)(2,1)S(1)} async-done(((bf16[4,3,96,1024]{3,2,1,0:T(8,128)(2,1)}), bf16[4,3,96,1024]{3,2,1,0:T(8,128)(2,1)S(1)}, u32[]{:S(2)}, u32[]{:S(2)}) %all-to-all-start.2) | async-done | bytes 2359328 | tf_op jit(solution)/shard_map/all_to_all | solution.py:162
  354.5 7.1 %all-to-all-start.1 = ((bf16[128,8,768]{2,1,0:T(8,128)(2,1)}), bf16[128,8,768]{2,1,0:T(8,128)(2,1)}, u32[]{:S(2)}, u32[]{:S(2)}) async-start(bf16[128,8,768]{2,1,0:T(8,128)(2,1)} %fusion.6), calls=%async_computation.1 | async-start | bytes 3145728 | tf_op jit(solution)/shard_map/all_to_all | solution.py:153
  361.6 1.4 copy-done.2
  363.0 1.8 y_sum.1
  364.8 20.9 %all-to-all-done.1 = bf16[128,8,768]{2,1,0:T(8,128)(2,1)} async-done(((bf16[128,8,768]{2,1,0:T(8,128)(2,1)}), bf16[128,8,768]{2,1,0:T(8,128)(2,1)}, u32[]{:S(2)}, u32[]{:S(2)}) %all-to-all-start.1) | async-done | bytes 1572896 | tf_op jit(solution)/shard_map/all_to_all | solution.py:153
  385.6 3.7 all-to-all-start.4
  389.3 3.1 collective-permute-start.19
  392.4 13.6 %collective-permute-done.19.b_ref = s32[8,16,256]{2,1,0:T(8,128)S(1)} collective-permute-done((s32[8,16,256]{2,1,0:T(8,128)S(1)}, s32[8,16,256]{2,1,0:T(8,128)S(1)}, u32[]{:S(2)}, u32[]{:S(2)}) %collective-permute-start.19) | collective-permute-done | bytes 131104 | tf_op jit(solution)/shard_map/ppermute | solution.py:66
  406.0 6.4 %cited_by_table.1 = bf16[256,4096]{1,0:T(8,128)(2,1)S(1)} custom-call(s32[1]{0:T(128)} %bitcast.col_ref, s32[8,16,256]{2,1,0:T(8,128)S(1)} %copy-done.30, s32[8,16,256]{2,1,0:T(8,128)S(1)} %collective-permute-done.19.b_ref), custom_call_target="tpu_custom_call" | custom-call | flops 1000000000 | bytes 3000000 | tf_op jit(solution)/shard_map/cited_by_table/pallas_call | solution.py:132
  412.5 3.2 fusion.4
  415.7 0.8 fusion.11
  416.5 0.9 last_sum.1
  417.4 6.0 %fusion.8 = bf16[256,768]{1,0:T(8,128)(2,1)} fusion(bf16[256,4096]{1,0:T(8,128)(2,1)} %copy-done.33, bf16[4096,768]{1,0:T(8,128)(2,1)} %all-gather.2.cloned.1.call-done, f32[256,768]{1,0:T(8,128)S(1)} %copy-done.26, f32[512,768]{1,0:T(8,128)S(1)} %fusion.4), kind=kOutput, calls=%fused_computation.10 | convolution fusion | flops 1611202560 | bytes 10354688 | tf_op jit(solution)/shard_map/dot_general | solution.py:22
  (149 shorter events, 6.9 us)
Async XLA Ops:
  12.1 11.7 %copy-start.12 = (bf16[256,768]{1,0:T(8,128)(2,1)S(1)}, bf16[256,768]{1,0:T(8,128)(2,1)}, u32[]{:S(2)}) copy-start(bf16[256,768]{1,0:T(8,128)(2,1)} %x_paper_ref.1) | copy-start | bytes 1179652
  12.1 18.8 %copy-start.57 = (s32[256,16]{0,1:T(8,128)S(1)}, s32[256,16]{0,1:T(8,128)}, u32[]{:S(2)}) copy-start(s32[256,16]{0,1:T(8,128)} %param.14) | copy-start | bytes 49156
  12.1 257.1 %all-to-all-start = ((bf16[128,8,768]{2,1,0:T(8,128)(2,1)}), bf16[128,8,768]{2,1,0:T(8,128)(2,1)}, u32[]{:S(2)}, u32[]{:S(2)}) async-start(bf16[128,8,768]{2,1,0:T(8,128)(2,1)} %fusion.7), calls=%async_computation | async-start | bytes 3145728 | tf_op jit(solution)/shard_map/all_to_all | solution.py:153
  23.7 393.7 %all-gather.2.cloned.1.call-start = ((), (), s32[]{:S(2)}) async-start(), calls=%async_computation.5 | async-start | bytes 6684672 | tf_op jit(solution)/shard_map/all_gather | solution.py:415
  23.8 21.5 %copy-start.44 = (bf16[64,768]{1,0:T(8,128)(2,1)}, bf16[64,768]{1,0:T(8,128)(2,1)S(1)}, u32[]{:S(2)}) copy-start(bf16[64,768]{1,0:T(8,128)(2,1)S(1)} %get-tuple-element.59.refs_6_) | copy-start | bytes 294916
  23.8 21.5 %copy-start.45 = (bf16[64,768]{1,0:T(8,128)(2,1)}, bf16[64,768]{1,0:T(8,128)(2,1)S(1)}, u32[]{:S(2)}) copy-start(bf16[64,768]{1,0:T(8,128)(2,1)S(1)} %get-tuple-element.60.refs_4_) | copy-start | bytes 294916
  23.8 21.5 %copy-start.46 = (bf16[64,768]{1,0:T(8,128)(2,1)}, bf16[64,768]{1,0:T(8,128)(2,1)S(1)}, u32[]{:S(2)}) copy-start(bf16[64,768]{1,0:T(8,128)(2,1)S(1)} %get-tuple-element.61.refs_2_) | copy-start | bytes 294916
  23.9 21.4 %copy-start.47 = (bf16[64,768]{1,0:T(8,128)(2,1)}, bf16[64,768]{1,0:T(8,128)(2,1)S(1)}, u32[]{:S(2)}) copy-start(bf16[64,768]{1,0:T(8,128)(2,1)S(1)} %get-tuple-element.62.refs_0_) | copy-start | bytes 294916
  23.9 20.0 %collective-permute-start = (bf16[64,768]{1,0:T(8,128)(2,1)S(1)}, bf16[64,768]{1,0:T(8,128)(2,1)S(1)}, u32[]{:S(2)}, u32[]{:S(2)}) collective-permute-start(bf16[64,768]{1,0:T(8,128)(2,1)S(1)} %get-tuple-element.62.refs_0_), channel_id=1, source_target_pairs={{0,4},{1,5},{2,6},{3,7},{4,0},{5,1},{6,2},{7,3},{8,12},{9,13},{10,... | collective-permute-start | bytes 294920 | tf_op jit(solution)/shard_map/ppermute | solution.py:66
  24.8 19.0 %collective-permute-start.1 = (bf16[64,768]{1,0:T(8,128)(2,1)S(1)}, bf16[64,768]{1,0:T(8,128)(2,1)S(1)}, u32[]{:S(2)}, u32[]{:S(2)}) collective-permute-start(bf16[64,768]{1,0:T(8,128)(2,1)S(1)} %get-tuple-element.61.refs_2_), channel_id=1, source_target_pairs={{0,1},{1,0},{2,3},{3,2},{4,5},{5,4},{6,7},{7,6},{8,9},{9,8},{10,11... | collective-permute-start | bytes 294920 | tf_op jit(solution)/shard_map/ppermute | solution.py:66
  26.4 18.3 %collective-permute-start.2 = (bf16[64,768]{1,0:T(8,128)(2,1)S(1)}, bf16[64,768]{1,0:T(8,128)(2,1)S(1)}, u32[]{:S(2)}, u32[]{:S(2)}) collective-permute-start(bf16[64,768]{1,0:T(8,128)(2,1)S(1)} %get-tuple-element.60.refs_4_), channel_id=1, source_target_pairs={{0,12},{1,13},{2,14},{3,15},{4,8},{5,9},{6,10},{7,11},{8,4},{9,5},... | collective-permute-start | bytes 294920 | tf_op jit(solution)/shard_map/ppermute | solution.py:66
  28.5 16.8 %collective-permute-start.3 = (bf16[64,768]{1,0:T(8,128)(2,1)S(1)}, bf16[64,768]{1,0:T(8,128)(2,1)S(1)}, u32[]{:S(2)}, u32[]{:S(2)}) collective-permute-start(bf16[64,768]{1,0:T(8,128)(2,1)S(1)} %get-tuple-element.59.refs_6_), channel_id=1, source_target_pairs={{0,3},{1,2},{2,1},{3,0},{4,7},{5,6},{6,5},{7,4},{8,11},{9,10},{10,... | collective-permute-start | bytes 294920 | tf_op jit(solution)/shard_map/ppermute | solution.py:66
  30.9 13.0 %collective-permute-start.4 = (s32[1,16,256]{2,1,0:T(8,128)S(1)}, s32[1,16,256]{2,1,0:T(8,128)S(1)}, u32[]{:S(2)}, u32[]{:S(2)}) collective-permute-start(s32[1,16,256]{2,1,0:T(8,128)S(1)} %bitcast.22), channel_id=1, source_target_pairs={{0,4},{1,5},{2,6},{3,7},{4,0},{5,1},{6,2},{7,3},{8,12},{9,13},{10,... | collective-permute-start | bytes 49160 | tf_op jit(solution)/shard_map/ppermute | solution.py:66
  72.0 10.1 %collective-permute-start.5 = (bf16[128,768]{1,0:T(8,128)(2,1)}, bf16[128,768]{1,0:T(8,128)(2,1)S(1)}, u32[]{:S(2)}, u32[]{:S(2)}) collective-permute-start(bf16[128,768]{1,0:T(8,128)(2,1)} %get-tuple-element.32.token_ref.refs_0_), channel_id=1, source_target_pairs={{0,1},{1,0},{2,3},{3,2},{4,5},{5,4},{6,7},{7,6},{8,9},{9,8},{10,11... | collective-permute-start | bytes 589832 | tf_op jit(solution)/shard_map/ppermute | solution.py:66
  73.7 8.4 %collective-permute-start.6 = (bf16[128,768]{1,0:T(8,128)(2,1)}, bf16[128,768]{1,0:T(8,128)(2,1)S(1)}, u32[]{:S(2)}, u32[]{:S(2)}) collective-permute-start(bf16[128,768]{1,0:T(8,128)(2,1)} %get-tuple-element.33.refs_2_), channel_id=1, source_target_pairs={{0,12},{1,13},{2,14},{3,15},{4,8},{5,9},{6,10},{7,11},{8,4},{9,5},... | collective-permute-start | bytes 589832 | tf_op jit(solution)/shard_map/ppermute | solution.py:66
  75.6 7.8 %collective-permute-start.7 = (bf16[128,768]{1,0:T(8,128)(2,1)}, bf16[128,768]{1,0:T(8,128)(2,1)S(1)}, u32[]{:S(2)}, u32[]{:S(2)}) collective-permute-start(bf16[128,768]{1,0:T(8,128)(2,1)} %get-tuple-element.34.refs_4_), channel_id=1, source_target_pairs={{0,3},{1,2},{2,1},{3,0},{4,7},{5,6},{6,5},{7,4},{8,11},{9,10},{10,... | collective-permute-start | bytes 589832 | tf_op jit(solution)/shard_map/ppermute | solution.py:66
  77.7 6.0 %collective-permute-start.8 = (bf16[128,768]{1,0:T(8,128)(2,1)}, bf16[128,768]{1,0:T(8,128)(2,1)S(1)}, u32[]{:S(2)}, u32[]{:S(2)}) collective-permute-start(bf16[128,768]{1,0:T(8,128)(2,1)} %get-tuple-element.35.refs_6_), channel_id=1, source_target_pairs={{0,4},{1,5},{2,6},{3,7},{4,0},{5,1},{6,2},{7,3},{8,12},{9,13},{10,... | collective-permute-start | bytes 589832 | tf_op jit(solution)/shard_map/ppermute | solution.py:66
  78.0 4.1 collective-permute-start.9
  82.1 1.6 copy-start.59
  82.1 1.6 copy-start.48
  82.1 1.6 copy-start.49
  135.7 12.6 %collective-permute-start.10 = (bf16[256,768]{1,0:T(8,128)(2,1)}, bf16[256,768]{1,0:T(8,128)(2,1)S(1)}, u32[]{:S(2)}, u32[]{:S(2)}) collective-permute-start(bf16[256,768]{1,0:T(8,128)(2,1)} %get-tuple-element.37.refs_0_), channel_id=1, source_target_pairs={{0,12},{1,13},{2,14},{3,15},{4,8},{5,9},{6,10},{7,11},{8,4},{9,5},... | collective-permute-start | bytes 1179656 | tf_op jit(solution)/shard_map/ppermute | solution.py:66
  136.9 11.4 %collective-permute-start.11 = (bf16[256,768]{1,0:T(8,128)(2,1)}, bf16[256,768]{1,0:T(8,128)(2,1)S(1)}, u32[]{:S(2)}, u32[]{:S(2)}) collective-permute-start(bf16[256,768]{1,0:T(8,128)(2,1)} %get-tuple-element.38.refs_2_), channel_id=1, source_target_pairs={{0,3},{1,2},{2,1},{3,0},{4,7},{5,6},{6,5},{7,4},{8,11},{9,10},{10,... | collective-permute-start | bytes 1179656 | tf_op jit(solution)/shard_map/ppermute | solution.py:66
  139.0 9.3 %collective-permute-start.12 = (bf16[256,768]{1,0:T(8,128)(2,1)}, bf16[256,768]{1,0:T(8,128)(2,1)S(1)}, u32[]{:S(2)}, u32[]{:S(2)}) collective-permute-start(bf16[256,768]{1,0:T(8,128)(2,1)} %get-tuple-element.39.refs_4_), channel_id=1, source_target_pairs={{0,4},{1,5},{2,6},{3,7},{4,0},{5,1},{6,2},{7,3},{8,12},{9,13},{10,... | collective-permute-start | bytes 1179656 | tf_op jit(solution)/shard_map/ppermute | solution.py:66
  139.0 9.3 %collective-permute-start.13 = (bf16[256,768]{1,0:T(8,128)(2,1)}, bf16[256,768]{1,0:T(8,128)(2,1)S(1)}, u32[]{:S(2)}, u32[]{:S(2)}) collective-permute-start(bf16[256,768]{1,0:T(8,128)(2,1)} %get-tuple-element.40.refs_6_), channel_id=1, source_target_pairs={{0,1},{1,0},{2,3},{3,2},{4,5},{5,4},{6,7},{7,6},{8,9},{9,8},{10,11... | collective-permute-start | bytes 1179656 | tf_op jit(solution)/shard_map/ppermute | solution.py:66
  139.0 115.6 %copy-start.58 = (s32[256,16]{0,1:T(8,128)S(1)}, s32[256,16]{0,1:T(8,128)}, u32[]{:S(2)}) copy-start(s32[256,16]{0,1:T(8,128)} %param.14) | copy-start | bytes 49156
  139.0 115.7 %copy-start.62 = (s32[1,128,4]{1,2,0:T(4,128)S(1)}, s32[1,128,4]{1,2,0:T(4,128)}, u32[]{:S(2)}) copy-start(s32[1,128,4]{1,2,0:T(4,128)} %param.15) | copy-start | bytes 6148
  139.1 116.0 %copy-start.61 = (s32[1,128,4]{1,2,0:T(4,128)S(1)}, s32[1,128,4]{1,2,0:T(4,128)}, u32[]{:S(2)}) copy-start(s32[1,128,4]{1,2,0:T(4,128)} %param.16) | copy-start | bytes 6148
  139.1 116.4 %copy-start.15 = (bf16[128,768]{1,0:T(8,128)(2,1)S(1)}, bf16[128,768]{1,0:T(8,128)(2,1)}, u32[]{:S(2)}) copy-start(bf16[128,768]{1,0:T(8,128)(2,1)} %get-tuple-element.32.token_ref.refs_0_) | copy-start | bytes 589828
  139.1 9.2 %collective-permute-start.14 = (s32[4,16,256]{2,1,0:T(8,128)}, s32[4,16,256]{2,1,0:T(8,128)S(1)}, u32[]{:S(2)}, u32[]{:S(2)}) collective-permute-start(s32[4,16,256]{2,1,0:T(8,128)} %get-tuple-element.41.refs_8_), channel_id=1, source_target_pairs={{0,12},{1,13},{2,14},{3,15},{4,8},{5,9},{6,10},{7,11},{8,4},{9,5},... | collective-permute-start | bytes 196616 | tf_op jit(solution)/shard_map/ppermute | solution.py:66
  250.6 30.5 %collective-permute-start.15 = (bf16[512,768]{1,0:T(8,128)(2,1)}, bf16[512,768]{1,0:T(8,128)(2,1)}, u32[]{:S(2)}, u32[]{:S(2)}) collective-permute-start(bf16[512,768]{1,0:T(8,128)(2,1)} %get-tuple-element.42.refs_1_), channel_id=1, source_target_pairs={{0,3},{1,2},{2,1},{3,0},{4,7},{5,6},{6,5},{7,4},{8,11},{9,10},{10,... | collective-permute-start | bytes 2359304 | tf_op jit(solution)/shard_map/ppermute | solution.py:66
  252.1 29.0 %collective-permute-start.16 = (bf16[512,768]{1,0:T(8,128)(2,1)}, bf16[512,768]{1,0:T(8,128)(2,1)}, u32[]{:S(2)}, u32[]{:S(2)}) collective-permute-start(bf16[512,768]{1,0:T(8,128)(2,1)} %get-tuple-element.43.refs_2_), channel_id=1, source_target_pairs={{0,4},{1,5},{2,6},{3,7},{4,0},{5,1},{6,2},{7,3},{8,12},{9,13},{10,... | collective-permute-start | bytes 2359304 | tf_op jit(solution)/shard_map/ppermute | solution.py:66
  252.2 28.9 %collective-permute-start.17 = (bf16[512,768]{1,0:T(8,128)(2,1)}, bf16[512,768]{1,0:T(8,128)(2,1)}, u32[]{:S(2)}, u32[]{:S(2)}) collective-permute-start(bf16[512,768]{1,0:T(8,128)(2,1)} %get-tuple-element.44.refs_3_), channel_id=1, source_target_pairs={{0,1},{1,0},{2,3},{3,2},{4,5},{5,4},{6,7},{7,6},{8,9},{9,8},{10,11... | collective-permute-start | bytes 2359304 | tf_op jit(solution)/shard_map/ppermute | solution.py:66
  252.2 28.9 %collective-permute-start.18 = (bf16[512,768]{1,0:T(8,128)(2,1)}, bf16[512,768]{1,0:T(8,128)(2,1)}, u32[]{:S(2)}, u32[]{:S(2)}) collective-permute-start(bf16[512,768]{1,0:T(8,128)(2,1)} %get-tuple-element.45.refs_4_), channel_id=1, source_target_pairs={{0,12},{1,13},{2,14},{3,15},{4,8},{5,9},{6,10},{7,11},{8,4},{9,5},... | collective-permute-start | bytes 2359304 | tf_op jit(solution)/shard_map/ppermute | solution.py:66
  255.4 10.6 %copy-start.21 = (bf16[512,768]{1,0:T(8,128)(2,1)S(1)}, bf16[512,768]{1,0:T(8,128)(2,1)}, u32[]{:S(2)}) copy-start(bf16[512,768]{1,0:T(8,128)(2,1)} %get-tuple-element.45.refs_4_) | copy-start | bytes 2359300
  255.4 10.6 %copy-start.22 = (bf16[512,768]{1,0:T(8,128)(2,1)S(1)}, bf16[512,768]{1,0:T(8,128)(2,1)}, u32[]{:S(2)}) copy-start(bf16[512,768]{1,0:T(8,128)(2,1)} %get-tuple-element.44.refs_3_) | copy-start | bytes 2359300
  255.4 10.6 %copy-start.23 = (bf16[512,768]{1,0:T(8,128)(2,1)S(1)}, bf16[512,768]{1,0:T(8,128)(2,1)}, u32[]{:S(2)}) copy-start(bf16[512,768]{1,0:T(8,128)(2,1)} %get-tuple-element.43.refs_2_) | copy-start | bytes 2359300
  255.4 10.6 %copy-start.24 = (bf16[512,768]{1,0:T(8,128)(2,1)S(1)}, bf16[512,768]{1,0:T(8,128)(2,1)}, u32[]{:S(2)}) copy-start(bf16[512,768]{1,0:T(8,128)(2,1)} %get-tuple-element.42.refs_1_) | copy-start | bytes 2359300
  266.0 3.2 copy-start.5
  266.0 3.2 copy-start.7
  274.1 7.0 %copy-start.17 = (s32[256,16]{1,0:T(8,128)S(1)}, s32[256,16]{1,0:T(8,128)}, u32[]{:S(2)}) copy-start(s32[256,16]{1,0:T(8,128)} %copy-done.16) | copy-start | bytes 49156
  274.1 7.1 %copy-start.20 = (bf16[768,1024]{1,0:T(8,128)(2,1)S(1)}, bf16[768,1024]{1,0:T(8,128)(2,1)}, u32[]{:S(2)}) copy-start(bf16[768,1024]{1,0:T(8,128)(2,1)} %w_hbm.1) | copy-start | bytes 4718596
  274.1 7.1 %copy-start.28 = (bf16[256,1024]{1,0:T(8,128)(2,1)S(1)}, bf16[256,1024]{1,0:T(8,128)(2,1)}, u32[]{:S(2)}) copy-start(bf16[256,1024]{1,0:T(8,128)(2,1)} %grad_ref.3) | copy-start | bytes 1572868
  274.1 7.1 %copy-start.32 = (bf16[256,4096]{1,0:T(8,128)(2,1)S(1)}, bf16[256,4096]{1,0:T(8,128)(2,1)}, u32[]{:S(2)}) copy-start(bf16[256,4096]{1,0:T(8,128)(2,1)} %copy-done.31) | copy-start | bytes 6291460
  274.1 7.1 %copy-start.35 = (f32[256,768]{1,0:T(8,128)S(1)}, f32[256,768]{1,0:T(8,128)}, u32[]{:S(2)}) copy-start(f32[256,768]{1,0:T(8,128)} %copy-done.34) | copy-start | bytes 2359300
  281.1 6.5 %copy-start.10 = (f32[256,768]{1,0:T(8,128)}, f32[256,768]{1,0:T(8,128)S(1)}, u32[]{:S(2)}) copy-start(f32[256,768]{1,0:T(8,128)S(1)} %get-tuple-element.57) | copy-start | bytes 2359300
  281.1 6.5 %copy-start.13 = (f32[512,128]{1,0:T(8,128)}, f32[512,128]{1,0:T(8,128)S(1)}, u32[]{:S(2)}) copy-start(f32[512,128]{1,0:T(8,128)S(1)} %get-tuple-element.52.cnt_ref) | copy-start | bytes 786436
  281.1 6.5 %copy-start.36 = (bf16[512,1024]{1,0:T(8,128)(2,1)}, bf16[512,1024]{1,0:T(8,128)(2,1)S(1)}, u32[]{:S(2)}) copy-start(bf16[512,1024]{1,0:T(8,128)(2,1)S(1)} %get-tuple-element.54) | copy-start | bytes 3145732
  281.1 6.5 %copy-start.38 = (bf16[256,768]{1,0:T(8,128)(2,1)}, bf16[256,768]{1,0:T(8,128)(2,1)S(1)}, u32[]{:S(2)}) copy-start(bf16[256,768]{1,0:T(8,128)(2,1)S(1)} %get-tuple-element.55) | copy-start | bytes 1179652
  281.2 6.4 %copy-start.3 = (bf16[256,4096]{1,0:T(8,128)(2,1)S(1)}, bf16[256,4096]{1,0:T(8,128)(2,1)}, u32[]{:S(2)}) copy-start(bf16[256,4096]{1,0:T(8,128)(2,1)} %get-tuple-element.58.refs_0_) | copy-start | bytes 6291460
  287.6 4.4 %collective-permute-start.20 = (bf16[256,4096]{1,0:T(8,128)(2,1)S(1)}, bf16[256,4096]{1,0:T(8,128)(2,1)}, u32[]{:S(2)}, u32[]{:S(2)}) collective-permute-start(bf16[256,4096]{1,0:T(8,128)(2,1)S(1)} %copy-done.3), channel_id=1, source_target_pairs={{0,16},{16,0},{32,48},{48,32},{64,80},{80,64},{96,112},{112,96},{1... | collective-permute-start | bytes 6291464 | tf_op jit(solution)/shard_map/ppermute | solution.py:158
  296.0 24.9 %all-to-all-start.3 = ((bf16[4,2,96,1024]{3,2,1,0:T(8,128)(2,1)}), bf16[4,2,96,1024]{3,2,1,0:T(8,128)(2,1)S(1)}, u32[]{:S(2)}, u32[]{:S(2)}) async-start(bf16[4,2,96,1024]{3,2,1,0:T(8,128)(2,1)} %copy-done.9), calls=%async_computation.3 | async-start | bytes 3145728 | tf_op jit(solution)/shard_map/all_to_all | solution.py:162
  299.6 2.6 collective-permute-start.21
  308.7 17.2 %copy-start.14 = (f32[512,128]{1,0:T(8,128)S(1)}, f32[512,128]{1,0:T(8,128)}, u32[]{:S(2)}) copy-start(f32[512,128]{1,0:T(8,128)} %copy-done.13) | copy-start | bytes 786436
  322.0 32.5 %all-to-all-start.2 = ((bf16[4,3,96,1024]{3,2,1,0:T(8,128)(2,1)}), bf16[4,3,96,1024]{3,2,1,0:T(8,128)(2,1)S(1)}, u32[]{:S(2)}, u32[]{:S(2)}) async-start(bf16[4,3,96,1024]{3,2,1,0:T(8,128)(2,1)} %copy-done), calls=%async_computation.2 | async-start | bytes 4718592 | tf_op jit(solution)/shard_map/all_to_all | solution.py:162
  328.8 2.6 copy-start.39
  354.5 31.2 %all-to-all-start.1 = ((bf16[128,8,768]{2,1,0:T(8,128)(2,1)}), bf16[128,8,768]{2,1,0:T(8,128)(2,1)}, u32[]{:S(2)}, u32[]{:S(2)}) async-start(bf16[128,8,768]{2,1,0:T(8,128)(2,1)} %fusion.6), calls=%async_computation.1 | async-start | bytes 3145728 | tf_op jit(solution)/shard_map/all_to_all | solution.py:153
  364.8 24.6 %copy-start.30 = (s32[8,16,256]{2,1,0:T(8,128)S(1)}, s32[8,16,256]{2,1,0:T(8,128)}, u32[]{:S(2)}) copy-start(s32[8,16,256]{2,1,0:T(8,128)} %get-tuple-element.49.a_ref) | copy-start | bytes 393220
  385.6 30.9 %all-to-all-start.4 = ((bf16[16,64,512]{2,1,0:T(8,128)(2,1)}), bf16[16,64,512]{2,1,0:T(8,128)(2,1)S(1)}, u32[]{:S(2)}, u32[]{:S(2)}) async-start(bf16[16,64,512]{2,1,0:T(8,128)(2,1)} %y_sum.1), calls=%async_computation.4 | async-start | bytes 2097152 | tf_op jit(solution)/shard_map/all_to_all | solution.py:427
  389.3 23.1 %copy-start.37 = (bf16[512,1024]{1,0:T(8,128)(2,1)S(1)}, bf16[512,1024]{1,0:T(8,128)(2,1)}, u32[]{:S(2)}) copy-start(bf16[512,1024]{1,0:T(8,128)(2,1)} %copy-done.36) | copy-start | bytes 3145732
  389.3 16.7 %collective-permute-start.19 = (s32[8,16,256]{2,1,0:T(8,128)S(1)}, s32[8,16,256]{2,1,0:T(8,128)S(1)}, u32[]{:S(2)}, u32[]{:S(2)}) collective-permute-start(s32[8,16,256]{2,1,0:T(8,128)S(1)} %copy-done.30), channel_id=1, source_target_pairs={{0,3},{1,2},{2,1},{3,0},{4,7},{5,6},{6,5},{7,4},{8,11},{9,10},{10,... | collective-permute-start | bytes 393224 | tf_op jit(solution)/shard_map/ppermute | solution.py:66
  412.5 3.2 copy-start.33
  412.5 3.2 copy-start.11
  415.7 1.7 copy-start.26
  (27 other events, 29.6 us)
Sparse Core Ops, SparseCore 0:
  287.7 60.9 all-gather.1

commit v3 on v2

v3 whole, which is shorter than its diff:
```python
import functools

import jax
import jax.numpy as jnp
from jax import lax
from jax.experimental import pallas as pl
from jax.experimental.pallas import tpu as pltpu
from jax.sharding import PartitionSpec as P

BF = jnp.bfloat16
F32 = jnp.float32
I32 = jnp.int32
MIB = 1024 * 1024
I16 = jnp.int16
CYCLE = (4, 1, 12, 3)
IN_VMEM = pl.BlockSpec(memory_space=pltpu.VMEM)
ANYWHERE = pl.BlockSpec(memory_space=pl.ANY)
IN_SMEM = pl.BlockSpec(memory_space=pltpu.SMEM)


def dot(a, b, dims=((1,), (0,))):
    return lax.dot_general(a, b, (dims, ((), ())), preferred_element_type=F32)


def shape(dims, kind):
    return jax.ShapeDtypeStruct(dims, kind)


def params(mib):
    return pltpu.CompilerParams(vmem_limit_bytes=mib * MIB)


def join_kernel(n, *refs):
    outs = refs[len(refs) - n :]
    for i in range(n):
        a, b, out = refs[2 * i], refs[2 * i + 1], outs[i]
        rows = a.shape[0]
        out[pl.ds(0, rows)] = a[...]
        out[pl.ds(rows, rows)] = b[...]


def join(pairs, tokens=()):
    n = len(pairs)
    flat = [v for pair in pairs for v in pair]
    outs = [shape((2 * a.shape[0],) + a.shape[1:], a.dtype) for a, _ in pairs]
    return pl.pallas_call(
        functools.partial(join_kernel, n),
        out_shape=outs,
        in_specs=[IN_VMEM] * (2 * n) + [ANYWHERE] * len(tokens),
        out_specs=[IN_VMEM] * n,
        compiler_params=params(16),
        name="join",
    )(*flat, *tokens)


def travel(parts, k):
    pairs = []
    for h, part in enumerate(parts):
        masks = [CYCLE[(k + 2 * (h & 1) + c) % 4] for c in range(2)]
        perm = [(r * 16 + c, r * 16 + (c ^ masks[r & 1])) for r in range(8) for c in range(16)]
        pairs.append((part, lax.ppermute(part, ("row", "col"), perm)))
    return pairs


def column_of(entries, col, core):
    diff = (entries >> 8) ^ col
    bits = {}
    for axis, (near, far) in enumerate(((4, 12), (1, 3))):
        d = ((diff >> 2) & 3) if axis == 0 else (diff & 3)
        bits[far] = d >> 1
        bits[near] = (d & 1) ^ (d >> 1)
    half = (entries >> 7) & 1
    turn = (2 * half + core) & 3
    place = jnp.zeros_like(entries)
    for s in range(4):
        m = jnp.zeros_like(entries)
        for k in range(4):
            m = m + (bits[CYCLE[(k + s) % 4]] << k)
        place = jnp.where(turn == s, m, place)
    return half * 2048 + place * 128 + (entries & 127)


def table_kernel(place_ref, nbr_ref, token_ref, out_ref, wide):
    nbr = nbr_ref[...]
    places = column_of(jnp.maximum(nbr, 0), place_ref[0], place_ref[1])
    live = nbr >= 0
    high = jnp.where(live, places & 4032, -64).astype(F32).astype(BF)
    low = jnp.where(live, places & 63, 0).astype(F32).astype(BF)
    slot = lax.broadcasted_iota(I32, (32, 2048), 0) & 15
    spread = jnp.where(slot == (lax.broadcasted_iota(I32, (32, 2048), 1) >> 7), 1.0, 0.0).astype(BF)
    wide[...] = dot(jnp.concatenate([high, low], axis=1), spread).astype(I32).astype(I16)
    base = lax.broadcasted_iota(I32, (256, 128), 1)
    one, zero = jnp.ones((), BF), jnp.zeros((), BF)

    @pl.loop(0, 32)
    def _(t):
        lanes = (base + t * 128).astype(I16)
        acc = jnp.zeros((256, 128), BF)
        for slot in range(16):
            acc = acc + jnp.where(wide[:, pl.ds(slot * 128, 128)] == lanes, one, zero)
        out_ref[:, pl.ds(pl.multiple_of(t * 128, 128), 128)] = acc


def cite_table(place, nbr, token):
    return pl.pallas_call(
        table_kernel,
        out_shape=shape((256, 4096), BF),
        in_specs=[IN_SMEM, IN_VMEM, ANYWHERE],
        out_specs=IN_VMEM,
        scratch_shapes=[pltpu.VMEM((256, 2048), I16)],
        compiler_params=params(16),
        cost_estimate=pl.CostEstimate(flops=10**9, bytes_accessed=3 * 10**6, transcendentals=0),
        name="cite_table",
    )(place, nbr, token)


def back_table_kernel(place_ref, a_ref, b_ref, token_ref, out_ref):
    own = (lax.broadcasted_iota(I32, (256, 128), 0) + place_ref[0] * 256).astype(I16)
    one, zero = jnp.ones((), BF), jnp.zeros((), BF)
    for m in range(16):
        lists = (a_ref if m < 8 else b_ref)[m % 8].astype(I16)
        for h in range(2):
            acc = jnp.zeros((256, 128), BF)
            for slot in range(16):
                acc = acc + jnp.where(lists[slot : slot + 1, 128 * h : 128 * h + 128] == own, one, zero)
            place = m if h == 0 else (m >> 2) | ((m & 3) << 2)
            out_ref[:, pl.ds(h * 2048 + place * 128, 128)] = acc


def cited_by_table(place, a, b, token):
    return pl.pallas_call(
        back_table_kernel,
        out_shape=shape((256, 4096), BF),
        in_specs=[IN_SMEM, IN_VMEM, IN_VMEM, ANYWHERE],
        out_specs=IN_VMEM,
        compiler_params=params(16),
        cost_estimate=pl.CostEstimate(flops=10**9, bytes_accessed=3 * 10**6, transcendentals=0),
        name="cited_by_table",
    )(place, a, b, token)


def edge_lists(write_src, write_dst):
    none = jnp.full_like(write_src, -1)
    pick = jnp.concatenate([write_src, jnp.where(write_dst >= 0, write_dst + 256, -1)], axis=1)
    into_paper = jnp.concatenate([write_dst, none], axis=1)
    into_author = jnp.concatenate([none, write_src], axis=1)
    return pick.reshape(-1), into_paper.reshape(1, -1), into_author.reshape(1, -1)


def exchange(rows):
    sent = rows.reshape(128, 8, rows.shape[-1])
    got = lax.all_to_all(sent, ("row", "col"), split_axis=0, concat_axis=0, tiled=True)
    return got.reshape(1024, rows.shape[-1])


def other_core(value):
    return lax.ppermute(value, "row", [(i, i ^ 1) for i in range(8)])


def over_y(parts):
    got = [parts[0]]
    for d in range(1, 4):
        perm = [(2 * y + c, 2 * ((y + d) % 4) + c) for y in range(4) for c in range(2)]
        got.append(lax.ppermute(parts[d], "row", perm))
    return got


def silu_and_slope(value):
    sigma = 1.0 / (1.0 + jnp.exp(-value))
    return (value * sigma).astype(BF), sigma * (1.0 + value * (1.0 - sigma))


def author_kernel(
    arrived_ref, into_paper_ref, into_author_ref, x_author_ref, x_paper_ref, grad_ref,
    w_sa_hbm, w_wn_hbm, w_sp_hbm, w_wr_hbm,
    out_ref, pack_ref, dz_ref, dx_ref, pre_ref, adder_ref, cnt_ref,
    w_sa, w_wn, w_sp, w_wr, sems,
):
    copies = []
    for i, (a, b) in enumerate(((w_sa_hbm, w_sa), (w_wn_hbm, w_wn), (w_sp_hbm, w_sp), (w_wr_hbm, w_wr))):
        copies.append(pltpu.make_async_copy(a, b, sems.at[i]))
        copies[-1].start()
    ids = lax.broadcasted_iota(I32, (256, 1024), 0)
    means = []
    for i, ref in enumerate((into_paper_ref, into_author_ref)):
        hit = jnp.where(ref[...] == ids, 1.0, 0.0)
        cnt = jnp.maximum(jnp.sum(hit, axis=1, keepdims=True), 1.0)
        cnt_ref[pl.ds(256 * i, 256), :] = jnp.broadcast_to(cnt, (256, 128))
        hit = hit.astype(BF)
        adder_ref[pl.ds(256 * i, 256), :] = hit
        means.append((dot(hit, arrived_ref[...]) / cnt).astype(BF))
    written, authored = means
    x_author, x_paper = x_author_ref[...], x_paper_ref[...]
    copies[0].wait()
    copies[1].wait()
    pre = dot(x_author, w_sa[...]) + dot(authored, w_wn[...])
    out, slope = silu_and_slope(pre)
    out_ref[...] = out
    dpre = (grad_ref[...].astype(F32) * slope).astype(BF)
    pack_ref[:, pl.ds(0, 768)] = x_author
    pack_ref[:, pl.ds(768, 768)] = authored
    pack_ref[:, pl.ds(1536, 768)] = x_paper
    pack_ref[:, pl.ds(2304, 768)] = written
    pack_ref[:, pl.ds(3072, 1024)] = dpre
    dz_ref[...] = (dot(dpre, w_wn[...], ((1,), (1,))) / cnt_ref[pl.ds(256, 256), pl.ds(0, 1)]).astype(BF)
    dx_ref[...] = dot(dpre, w_sa[...], ((1,), (1,)))
    copies[2].wait()
    copies[3].wait()
    pre_ref[...] = dot(x_paper, w_sp[...]) + dot(written, w_wr[...])


def author_step(arrived, into_paper, into_author, x_author, x_paper, grad, w_sa, w_wn, w_sp, w_wr):
    weight = pltpu.VMEM((768, 1024), BF)
    return pl.pallas_call(
        author_kernel,
        out_shape=[
            shape((256, 1024), BF), shape((256, 4096), BF), shape((256, 768), BF), shape((256, 768), F32),
            shape((256, 1024), F32), shape((512, 1024), BF), shape((512, 128), F32),
        ],
        in_specs=[IN_VMEM] * 6 + [ANYWHERE] * 4,
        out_specs=[IN_VMEM] * 7,
        scratch_shapes=[weight] * 4 + [pltpu.SemaphoreType.DMA((4,))],
        compiler_params=params(40),
        cost_estimate=pl.CostEstimate(flops=4 * 10**9, bytes_accessed=15 * 10**6, transcendentals=0),
        name="author_step",
    )(arrived, into_paper, into_author, x_author, x_paper, grad, w_sa, w_wn, w_sp, w_wr)


def first_kernel(table_ref, b0, b1, out_ref):
    acc = dot(table_ref[:, pl.ds(0, 1024)], b0[...]) + dot(table_ref[:, pl.ds(2048, 1024)], b1[...])
    out_ref[...] = acc


def first_half(table, blocks):
    return pl.pallas_call(
        first_kernel,
        out_shape=shape((256, 768), F32),
        in_specs=[IN_VMEM] * 3,
        out_specs=IN_VMEM,
        compiler_params=params(24),
        cost_estimate=pl.CostEstimate(flops=2 * 10**9, bytes_accessed=5 * 10**6, transcendentals=0),
        name="first_half",
    )(table, *blocks)


def last_kernel(table_ref, b0, b1, first_ref, own_ref, out_ref):
    acc = dot(table_ref[:, pl.ds(1024, 1024)], b0[...]) + dot(table_ref[:, pl.ds(3072, 1024)], b1[...])
    out_ref[...] = (acc + (first_ref[...] + own_ref[...])).astype(BF)


def last_half(table, blocks, first, own):
    return pl.pallas_call(
        last_kernel,
        out_shape=shape((256, 768), BF),
        in_specs=[IN_VMEM] * 5,
        out_specs=IN_VMEM,
        compiler_params=params(24),
        cost_estimate=pl.CostEstimate(flops=2 * 10**9, bytes_accessed=5 * 10**6, transcendentals=0),
        name="last_half",
    )(table, *blocks, first, own)


def edge_add_kernel(adder_ref, back_ref, author_ref, paper_ref, out_ref, sum_ref):
    back = back_ref[...]
    sum_ref[...] = paper_ref[...] + dot(adder_ref[pl.ds(0, 256), :], back)
    out_ref[...] = (author_ref[...] + dot(adder_ref[pl.ds(256, 256), :], back)).astype(BF)


def edge_add(adder, back, author, paper):
    return pl.pallas_call(
        edge_add_kernel,
        out_shape=[shape((256, 768), BF), shape((256, 768), F32)],
        in_specs=[IN_VMEM] * 4,
        out_specs=[IN_VMEM] * 2,
        compiler_params=params(16),
        cost_estimate=pl.CostEstimate(flops=10**9, bytes_accessed=5 * 10**6, transcendentals=0),
        name="edge_add",
    )(adder, back, author, paper)


def paper_kernel(
    table_ref, b0, b1, first_ref, nbr_ref, pre_ref, grad_ref, w_hbm, token_ref,
    out_ref, pack_ref, dz_ref, w_ref, sem,
):
    copy = pltpu.make_async_copy(w_hbm, w_ref, sem)
    copy.start()
    total = first_ref[...]
    for h, block in enumerate((b0, b1)):
        total = total + dot(table_ref[:, pl.ds(h * 2048 + 1024, 1024)], block[...])
    cnt = jnp.sum(jnp.where(nbr_ref[...] >= 0, 1.0, 0.0), axis=1, keepdims=True)
    cnt = jnp.maximum(cnt, 1.0)
    cited = (total / cnt).astype(BF)
    pack_ref[:, pl.ds(0, 768)] = cited
    copy.wait()
    out, slope = silu_and_slope(pre_ref[...] + dot(cited, w_ref[...]))
    out_ref[...] = out
    dpre = (grad_ref[...].astype(F32) * slope).astype(BF)
    pack_ref[:, pl.ds(768, 1024)] = dpre
    dz_ref[...] = (dot(dpre, w_ref[...], ((1,), (1,))) / cnt).astype(BF)


def paper_step(table, blocks, first, nbr, pre, grad, w_cite, token):
    return pl.pallas_call(
        paper_kernel,
        out_shape=[shape((256, 1024), BF), shape((256, 1792), BF), shape((256, 768), BF)],
        in_specs=[IN_VMEM] * 7 + [ANYWHERE] * 2,
        out_specs=[IN_VMEM] * 3,
        scratch_shapes=[pltpu.VMEM((768, 1024), BF), pltpu.SemaphoreType.DMA],
        compiler_params=params(32),
        cost_estimate=pl.CostEstimate(flops=3 * 10**9, bytes_accessed=10 * 10**6, transcendentals=0),
        name="paper_step",
    )(table, *blocks, first, nbr, pre, grad, w_cite, token)


def edge_back_kernel(pack_ref, cnt_ref, w_wr_hbm, w_sp_hbm, dz_ref, dx_ref, w_wr, w_sp, sems):
    copies = [pltpu.make_async_copy(w_wr_hbm, w_wr, sems.at[0]), pltpu.make_async_copy(w_sp_hbm, w_sp, sems.at[1])]
    for copy in copies:
        copy.start()
    dpre = pack_ref[:, pl.ds(768, 1024)]
    copies[0].wait()
    dz_ref[...] = (dot(dpre, w_wr[...], ((1,), (1,))) / cnt_ref[pl.ds(0, 256), pl.ds(0, 1)]).astype(BF)
    copies[1].wait()
    dx_ref[...] = dot(dpre, w_sp[...], ((1,), (1,)))


def edge_back(pack, cnt, w_write, w_self):
    return pl.pallas_call(
        edge_back_kernel,
        out_shape=[shape((256, 768), BF), shape((256, 768), F32)],
        in_specs=[IN_VMEM, IN_VMEM, ANYWHERE, ANYWHERE],
        out_specs=[IN_VMEM] * 2,
        scratch_shapes=[pltpu.VMEM((768, 1024), BF)] * 2 + [pltpu.SemaphoreType.DMA((2,))],
        compiler_params=params(16),
        cost_estimate=pl.CostEstimate(flops=10**9, bytes_accessed=5 * 10**6, transcendentals=0),
        name="edge_back",
    )(pack, cnt, w_write, w_self)


def weight_kernel(lefts, right, place_ref, *refs):
    ins, outs, turned = refs[:-5], refs[-5:-1], refs[-1]
    core, y = place_ref[1], place_ref[2]
    own, other, lane = right
    dpre = jnp.concatenate([ins[own][:, pl.ds(lane, 1024)], ins[other][:, pl.ds(lane, 1024)]], axis=0)
    for i, (own, other, lane) in enumerate(lefts):
        for k, ref in enumerate((ins[own], ins[other])):
            turned[i, :, pl.ds(256 * k, 256)] = ref[:, pl.ds(lane, 768)].T
        rows = []
        for d in range(4):
            start = pl.multiple_of((2 * ((y + d) & 3) + core) * 96, 32)
            rows.append(turned[i, pl.ds(start, 96), :])
        product = dot(jnp.concatenate(rows, axis=0), dpre).astype(BF)
        for d in range(4):
            outs[d][i] = product[96 * d : 96 * d + 96]


def weight_parts(place, arrays, lefts, right):
    n = len(lefts)
    return pl.pallas_call(
        functools.partial(weight_kernel, lefts, right),
        out_shape=[shape((n, 96, 1024), BF)] * 4,
        in_specs=[IN_SMEM] + [IN_VMEM] * len(arrays),
        out_specs=[IN_VMEM] * 4,
        scratch_shapes=[pltpu.VMEM((n, 768, 512), BF)],
        compiler_params=params(32),
        cost_estimate=pl.CostEstimate(flops=2 * 10**9, bytes_accessed=8 * 10**6, transcendentals=0),
        name="weight_parts",
    )(place, *arrays)


def y_sum_kernel(*refs):
    papers, authors, out_ref, stack = refs[:4], refs[4:8], refs[8], refs[9]
    for m in range(5):
        group, i = (papers, m) if m < 3 else (authors, m - 3)
        total = group[0][i].astype(F32)
        for y in range(1, 4):
            total = total + group[y][i].astype(F32)
        stack[pl.ds(96 * m, 96), :] = total
    stack[pl.ds(480, 32), :] = jnp.zeros((32, 1024), F32)
    for j in range(0, 16, 2):
        turned = stack[:, pl.ds(64 * j, 128)].T.astype(BF)
        out_ref[j] = turned[:64]
        out_ref[j + 1] = turned[64:]


def y_sum(paper, author):
    return pl.pallas_call(
        y_sum_kernel,
        out_shape=shape((16, 64, 512), BF),
        in_specs=[IN_VMEM] * 8,
        out_specs=IN_VMEM,
        scratch_shapes=[pltpu.VMEM((512, 1024), F32)],
        compiler_params=params(20),
        name="y_sum",
    )(*paper, *author)


def last_sum_kernel(got_ref, out_ref):
    total = got_ref[0].astype(F32)
    for j in range(1, 16):
        total = total + got_ref[j].astype(F32)
    total = total * (32768.0 ** -0.5)
    for m in range(5):
        out_ref[m] = total[:, 96 * m : 96 * m + 96]


def last_sum(got):
    return pl.pallas_call(
        last_sum_kernel,
        out_shape=shape((5, 64, 96), F32),
        in_specs=[IN_VMEM],
        out_specs=IN_VMEM,
        compiler_params=params(8),
        name="last_sum",
    )(got)


def per_device(
    x_paper, x_author, cite_nbr, write_src, write_dst,
    w_self_paper, w_cite, w_write, w_self_author, w_written, grad_paper, grad_author,
):
    row = lax.axis_index("row")
    place = jnp.stack([lax.axis_index("col"), row & 1, row >> 1]).astype(I32)

    parts = [x_paper[:128], x_paper[128:], cite_nbr.T.reshape(1, 16, 256)]
    parts = join(travel(parts, 0))

    pick, into_paper, into_author = edge_lists(write_src[0], write_dst[0])
    picker = (pick[:, None] == lax.iota(I32, 512)[None, :]).astype(BF)
    rows = dot(picker, jnp.concatenate([x_author, x_paper], axis=0)).astype(BF)
    arrived = exchange(rows)

    table = cite_table(place, cite_nbr, parts[0])
    parts = join(travel(parts, 1), (table,))
    parts = join(travel(parts, 2))
    pairs = travel(parts, 3)
    cite_first = first_half(table, [pair[0] for pair in pairs[:2]])

    out_author, pack_a, dz_written, dx_author_own, pre_paper, adder, cnt = author_step(
        arrived, into_paper, into_author, x_author, x_paper, grad_author,
        w_self_author, w_written, w_self_paper, w_write,
    )
    pack_a_other = other_core(pack_a)
    parts_author = weight_parts(place, [pack_a, pack_a_other], [(0, 1, 0), (0, 1, 768)], (0, 1, 3072))
    got_author = over_y(parts_author)

    out_paper, pack_p, dz_cite = paper_step(
        table, [pair[1] for pair in pairs[:2]], cite_first, cite_nbr, pre_paper, grad_paper, w_cite, parts_author[0]
    )
    pack_p_other = other_core(pack_p)
    back_pairs = travel([dz_cite[:128], dz_cite[128:]], 0)
    dz_write, dx_paper_own = edge_back(pack_p, cnt, w_write, w_self_paper)
    parts_paper = weight_parts(
        place, [pack_a, pack_a_other, pack_p, pack_p_other],
        [(0, 1, 1536), (2, 3, 0), (0, 1, 2304)], (2, 3, 768),
    )
    parts = join(back_pairs, (parts_paper[0],))
    got_paper = over_y(parts_paper)
    rows = dot(picker, jnp.concatenate([dz_written, dz_write], axis=0)).astype(BF)
    parts = join(travel(parts, 1), (rows,))
    back = exchange(rows)
    back_table = cited_by_table(place, pairs[2][0], pairs[2][1], parts[0])
    parts = join(travel(parts, 2), (back_table,))
    back_pairs = travel(parts, 3)
    back_first = first_half(back_table, [pair[0] for pair in back_pairs])

    got = lax.all_to_all(y_sum(got_paper, got_author), "col", split_axis=0, concat_axis=0, tiled=True)
    dweights = last_sum(got).transpose(0, 2, 1)

    dx_author, dx_paper_own = edge_add(adder, back, dx_author_own, dx_paper_own)
    dx_paper = last_half(back_table, [pair[1] for pair in back_pairs], back_first, dx_paper_own)
    return (out_paper, out_author, dx_paper, dx_author, dweights)


def solution(mesh):
    part = P(("row", "col"), None)
    part3 = P(("row", "col"), None, None)
    return jax.shard_map(
        per_device,
        mesh=mesh,
        in_specs=(part, part, part, part3, part3, P(), P(), P(), P(), P(), part, part),
        out_specs=(part, part, part, part, P(None, "row", "col")),
        check_vma=False,
    )
```

time: 431 us -> 223 us (0.52)
  Pallas kernels: 219 us -> 48.5 us
  waiting for transfers between devices: 100 us -> 83.8 us
  between operations: 14.8 us -> 1.15 us
  matrix products: 14.7 us -> 5.61 us
  starting transfers between devices: 56.8 us -> 64.9 us
  local copies, waits for them, and re-layouts: 22.3 us -> 17.1 us
    pallas_call x4 -> x10, Pallas kernels: 178 us -> 18 us  [the longest x6 8.81 us: join(): pl.pallas_call(functools.partial(join_kernel, n), out_shape=outs, in_spec...]
    ppermute x20 -> x26, waiting for transfers between devices: 39.8 us -> 73.8 us  [the longest x20 51.1 us: travel(): pairs.append((part, lax.ppermute(part, ('row', 'col'), perm)))]
    all_to_all x2 -> x0, waiting for transfers between devices: 33 us -> none  [over_y(): lax.all_to_all(parts, 'row', split_axis=0, concat_axis=0, tiled=True, axi...]
    all_to_all x2, waiting for transfers between devices: 20.9 us -> 0.01 us  [exchange(): lax.all_to_all(sent, ('row', 'col'), split_axis=0, concat_axis=0, tiled=T...]
    ppermute x20 -> x26, starting transfers between devices: 26.6 us -> 37.2 us  [the longest x20 27.2 us: travel(): pairs.append((part, lax.ppermute(part, ('row', 'col'), perm)))]
    all_to_all x1, waiting for transfers between devices: 0.01 us -> 10 us  [per_device(): lax.all_to_all(y_sum(got_paper, got_author), 'col', split_axis=0, concat_...]
    dot_general x4 -> x2, matrix products: 14.7 us -> 5.61 us  [dot(): return lax.dot_general(a, b, (dims, ((), ())), preferred_element_type=F32)]
    all_to_all x2 -> x0, starting transfers between devices: 7.47 us -> none  [over_y(): lax.all_to_all(parts, 'row', split_axis=0, concat_axis=0, tiled=True, axi...]
  transfers between devices with their start and end apart: 28 -> 31, of which waited for: 13 -> 10; matrix products, arithmetic and copies ran while one was open for 2% -> 1% of each run, Pallas kernels for 49% -> 18%
where the time goes in v3:
time: 223 us
  waiting for transfers between devices  83.8 us (38%)
  starting transfers between devices  64.9 us (29%)
  Pallas kernels  48.5 us (22%)
  local copies, waits for them, and re-layouts  17.1 us (8%)
  matrix products  5.61 us (3%)
    ppermute x20, waiting for transfers between devices, travel(): pairs.append((part, lax.ppermute(part, ('row', 'col'), perm)))  51.1 us
    ppermute x20, starting transfers between devices, travel(): pairs.append((part, lax.ppermute(part, ('row', 'col'), perm)))  27.2 us
    ppermute x6, waiting for transfers between devices, over_y(): got.append(lax.ppermute(parts[d], 'row', perm))  22.7 us
    all_to_all x2, starting transfers between devices, exchange(): lax.all_to_all(sent, ('row', 'col'), split_axis=0, concat_axis=0, tiled=T...  20.3 us
    unnamed x85, local copies, waits for them, and re-layouts  16.6 us
    all_to_all x1, waiting for transfers between devices, per_device(): lax.all_to_all(y_sum(got_paper, got_author), 'col', split_axis=0, concat_...  10 us
    ppermute x6, starting transfers between devices, over_y(): got.append(lax.ppermute(parts[d], 'row', perm))  10 us
    pallas_call x6, Pallas kernels, join(): pl.pallas_call(functools.partial(join_kernel, n), out_shape=outs, in_spec...  8.81 us
  transfers between devices with their start and end apart: 31, of which 10 were waited for; matrix products, arithmetic and copies ran while one was open for 1% of the time, Pallas kernels for 18%

profile of v3, /device:TPU:0, one launch (start us, length us, event | category | flops | bytes accessed | tf_op | source)
XLA Modules:
  0.0 222.6 jit_solution(2921606760607335133)
XLA Ops:
  2.2 3.3 %fusion.4 = bf16[128,8,768]{2,1,0:T(8,128)(2,1)} fusion(s32[1024]{0:T(1024)S(1)} %eq.15, bf16[256,768]{1,0:T(8,128)(2,1)} %x_paper_ref.1, bf16[256,768]{1,0:T(8,128)(2,1)} %x_author_ref.1), kind=kOutput, calls=%fused_computation.5 | convolution fusion | flops 808189952 | bytes 2363392 | tf_op jit(solution)/shard_map/dot_general | solution.py:22
  5.6 11.6 %all-to-all-start = ((bf16[128,8,768]{2,1,0:T(8,128)(2,1)}), bf16[128,8,768]{2,1,0:T(8,128)(2,1)}, u32[]{:S(2)}, u32[]{:S(2)}) async-start(bf16[128,8,768]{2,1,0:T(8,128)(2,1)} %fusion.4), calls=%async_computation | async-start | bytes 3145728 | tf_op jit(solution)/shard_map/all_to_all | solution.py:152
  17.2 1.0 collective-permute-start
  18.2 2.1 collective-permute-start.1
  20.9 16.3 %collective-permute-done.2.refs_5_ = s32[1,16,256]{2,1,0:T(8,128)S(1)} collective-permute-done((s32[1,16,256]{2,1,0:T(8,128)S(1)}, s32[1,16,256]{2,1,0:T(8,128)S(1)}, u32[]{:S(2)}, u32[]{:S(2)}) %collective-permute-start.2) | collective-permute-done | bytes 16416 | tf_op jit(solution)/shard_map/ppermute | solution.py:61
  37.1 1.0 collective-permute-done.1.refs_3_
  38.2 1.7 collective-permute-start.3
  39.9 2.3 %collective-permute-start.4 = (bf16[256,768]{1,0:T(8,128)(2,1)S(1)}, bf16[256,768]{1,0:T(8,128)(2,1)}, u32[]{:S(2)}, u32[]{:S(2)}) collective-permute-start(bf16[256,768]{1,0:T(8,128)(2,1)S(1)} %get-tuple-element.43.refs_2_), channel_id=1, source_target_pairs={{0,3},{1,2},{2,1},{3,0},{4,7},{5,6},{6,5},{7,4},{8,11},{9,10},{10,... | collective-permute-start | bytes 1179656 | tf_op jit(solution)/shard_map/ppermute | solution.py:61
  43.9 8.0 %cite_table.1.refs_6_.table_ref = bf16[256,4096]{1,0:T(8,128)(2,1)S(1)} custom-call(s32[3]{0:T(128)S(1)} %pad_add_fusion.1.place_ref, s32[256,16]{1,0:T(8,128)S(1)} %copy.21.nbr_ref, bf16[256,768]{1,0:T(8,128)(2,1)S(1)} %get-tuple-element.42.token_ref.refs_0_), custom_call_target="tpu_custom_call" | custom-call | flops 1000000000 | bytes 3000000 | tf_op jit(solution)/shard_map/cite_table/pallas_call | solution.py:105
  51.9 2.3 %join.7 = (bf16[512,768]{1,0:T(8,128)(2,1)}, bf16[512,768]{1,0:T(8,128)(2,1)}, s32[4,16,256]{2,1,0:T(8,128)S(1)}) custom-call(bf16[256,768]{1,0:T(8,128)(2,1)S(1)} %get-tuple-element.42.token_ref.refs_0_, bf16[256,768]{1,0:T(8,128)(2,1)S(1)} %collective-permute-done.3.refs_1_, bf16[256,768]{1,0:T(8,128)(2,1)S(1)} %get-tuple-element.43.refs_2_, ...), custom_call_target="tpu_custom_call" | custom-call | tf_op jit(solution)/shard_map/join/pallas_call | solution.py:46
  54.8 1.0 collective-permute-start.6
  56.4 1.4 copy-done.3
  57.8 1.4 copy-done.4
  59.2 1.0 copy-done.12
  60.2 1.4 copy-done.17
  61.6 1.4 copy-done.18
  63.0 1.0 copy-done.28
  64.1 1.0 copy-done.30
  65.1 6.7 %author_step.1 = (bf16[256,1024]{1,0:T(8,128)(2,1)}, bf16[256,4096]{1,0:T(8,128)(2,1)}, bf16[256,768]{1,0:T(8,128)(2,1)S(1)}, f32[256,768]{1,0:T(8,128)S(1)}, f3...) custom-call(bf16[1024,768]{1,0:T(8,128)(2,1)} %bitcast.9.arrived_ref, ...), custom_call_target="tpu_custom_call" | custom-call | flops 4000000000 | bytes 15000000 | tf_op jit(solution)/shard_map/author_step/pallas_call | solution.py:214
  71.9 1.7 collective-permute-start.8
  73.6 3.8 %collective-permute-done.8.refs_5_ = s32[4,16,256]{2,1,0:T(8,128)S(1)} collective-permute-done((s32[4,16,256]{2,1,0:T(8,128)S(1)}, s32[4,16,256]{2,1,0:T(8,128)S(1)}, u32[]{:S(2)}, u32[]{:S(2)}) %collective-permute-start.8) | collective-permute-done | bytes 65568 | tf_op jit(solution)/shard_map/ppermute | solution.py:61
  77.5 2.1 join.8
  79.6 1.3 collective-permute-start.10
  80.8 1.1 collective-permute-start.9
  81.9 1.0 first_half.2.first_ref
  82.9 1.8 weight_parts.2
  84.8 15.3 %collective-permute-done.10.b1 = bf16[1024,768]{1,0:T(8,128)(2,1)S(1)} collective-permute-done((bf16[1024,768]{1,0:T(8,128)(2,1)S(1)}, bf16[1024,768]{1,0:T(8,128)(2,1)S(1)}, u32[]{:S(2)}, u32[]{:S(2)}) %collective-permute-start.10) | collective-permute-done | bytes 1572896 | tf_op jit(solution)/shard_map/ppermute | solution.py:61
  100.1 2.4 %collective-permute-done.9.b0 = bf16[1024,768]{1,0:T(8,128)(2,1)S(1)} collective-permute-done((bf16[1024,768]{1,0:T(8,128)(2,1)S(1)}, bf16[1024,768]{1,0:T(8,128)(2,1)S(1)}, u32[]{:S(2)}, u32[]{:S(2)}) %collective-permute-start.9) | collective-permute-done | bytes 1572896 | tf_op jit(solution)/shard_map/ppermute | solution.py:61
  102.4 3.2 %paper_step.1 = (bf16[256,1024]{1,0:T(8,128)(2,1)}, bf16[256,1792]{1,0:T(8,128)(2,1)S(1)}, bf16[256,768]{1,0:T(8,128)(2,1)S(1)}) custom-call(bf16[256,4096]{1,0:T(8,128)(2,1)S(1)} %cite_table.1.refs_6_.table_ref, bf16[1024,768]{1,0:T(8,128)(2,1)S(1)} %collective-permute-done.9.b0, bf16[1024,768]{1,0:T(8,128)(2,1)S(1)} %collective-permute-done.10.b1, ...), custom_call_target="tpu_custom_call" | custom-call | flops 3000000000 | bytes 10000000 | tf_op jit(solution)/shard_map/paper_step/pallas_call | solution.py:303
  106.2 2.2 collective-permute-start.14
  108.4 1.7 edge_back.1
  110.2 0.9 copy-done.7
  111.1 2.3 %weight_parts.3 = (bf16[3,96,1024]{2,1,0:T(8,128)(2,1)S(1)}, bf16[3,96,1024]{2,1,0:T(8,128)(2,1)S(1)}, bf16[3,96,1024]{2,1,0:T(8,128)(2,1)S(1)}, bf16[3,96,1024]{2,1,0:T(8,128)(2,1)S(1)}) custom-call(s32[3]{0:T(128)S(1)} %pad_add_fusion.1.place_ref, bf16[256,4096]{1,0:T(8,128)(2,1)S(1)} %copy-done.16, bf16[256,4096]{1,0:T(8,128)(2,1)S(1)} %collective-permute-done.11.refs_1_, ...), custom_call_target="tpu_custom_call" | custom-call | flops 2000000000 | bytes 8000000 | tf_op jit(solution)/shard_map/weight_parts/pallas_call | solution.py:358
  113.4 1.0 join.9
  114.5 1.1 collective-permute-start.17
  115.6 2.3 %fusion.3.refs_4_ = bf16[1024,768]{1,0:T(8,128)(2,1)} fusion(s32[1024]{0:T(1024)S(1)} %eq.15, bf16[256,768]{1,0:T(8,128)(2,1)S(1)} %get-tuple-element.63, bf16[256,768]{1,0:T(8,128)(2,1)S(1)} %get-tuple-element.61), kind=kOutput, calls=%fused_computation.4 | convolution fusion | flops 808189952 | bytes 2363392 | tf_op jit(solution)/shard_map/dot_general | solution.py:22
  117.9 8.7 %all-to-all-start.1 = ((bf16[128,8,768]{2,1,0:T(8,128)(2,1)}), bf16[128,8,768]{2,1,0:T(8,128)(2,1)S(1)}, u32[]{:S(2)}, u32[]{:S(2)}) async-start(bf16[128,8,768]{2,1,0:T(8,128)(2,1)} %bitcast.10), calls=%async_computation.1 | async-start | bytes 3145728 | tf_op jit(solution)/shard_map/all_to_all | solution.py:152
  126.6 1.4 join.10
  128.0 2.3 %collective-permute-start.18 = (bf16[512,768]{1,0:T(8,128)(2,1)S(1)}, bf16[512,768]{1,0:T(8,128)(2,1)S(1)}, u32[]{:S(2)}, u32[]{:S(2)}) collective-permute-start(bf16[512,768]{1,0:T(8,128)(2,1)S(1)} %get-tuple-element.64.token_ref.refs_0_), channel_id=1, source_target_pairs={{0,12},{1,13},{2,14},{3,15},{4,8},{5,9},{6,10},{7,11},{8,4},{9,5},... | collective-permute-start | bytes 2359304 | tf_op jit(solution)/shard_map/ppermute | solution.py:61
  130.5 3.4 %collective-permute-start.12 = (s32[8,16,256]{2,1,0:T(8,128)S(1)}, s32[8,16,256]{2,1,0:T(8,128)S(1)}, u32[]{:S(2)}, u32[]{:S(2)}) collective-permute-start(s32[8,16,256]{2,1,0:T(8,128)S(1)} %copy-done.38), channel_id=1, source_target_pairs={{0,3},{1,2},{2,1},{3,0},{4,7},{5,6},{6,5},{7,4},{8,11},{9,10},{10,... | collective-permute-start | bytes 393224 | tf_op jit(solution)/shard_map/ppermute | solution.py:61
  133.9 1.5 collective-permute-start.25
  135.4 2.8 %collective-permute-start.26 = (bf16[2,96,1024]{2,1,0:T(8,128)(2,1)S(1)}, bf16[2,96,1024]{2,1,0:T(8,128)(2,1)S(1)}, u32[]{:S(2)}, u32[]{:S(2)}) collective-permute-start(bf16[2,96,1024]{2,1,0:T(8,128)(2,1)S(1)} %copy-done.34), channel_id=1, source_target_pairs={{0,64},{16,80},{32,96},{48,112},{64,0},{80,16},{96,32},{112,48},{1... | collective-permute-start | bytes 1179656 | tf_op jit(solution)/shard_map/ppermute | solution.py:164
  138.2 12.2 %collective-permute-done.12.b_ref = s32[8,16,256]{2,1,0:T(8,128)S(1)} collective-permute-done((s32[8,16,256]{2,1,0:T(8,128)S(1)}, s32[8,16,256]{2,1,0:T(8,128)S(1)}, u32[]{:S(2)}, u32[]{:S(2)}) %collective-permute-start.12) | collective-permute-done | bytes 131104 | tf_op jit(solution)/shard_map/ppermute | solution.py:61
  150.5 1.8 collective-permute-start.27
  152.2 4.0 %cited_by_table.1.refs_4_.table_ref = bf16[256,4096]{1,0:T(8,128)(2,1)S(1)} custom-call(s32[3]{0:T(128)S(1)} %pad_add_fusion.1.place_ref, s32[8,16,256]{2,1,0:T(8,128)S(1)} %copy-done.38, s32[8,16,256]{2,1,0:T(8,128)S(1)} %collective-permute-done.12.b_ref, bf16[512,768]{1,0:T(8,128)(2,1)S(1)} %get-tuple-element.64.token_ref.refs_0_), custom_call_target="tpu_custom_call" | custom-call | flops 1000000000 | bytes 3000000 | tf_op jit(solution)/shard_map/cited_by_table/pallas_call | solution.py:131
  156.6 2.3 %collective-permute-start.23 = (bf16[3,96,1024]{2,1,0:T(8,128)(2,1)S(1)}, bf16[3,96,1024]{2,1,0:T(8,128)(2,1)S(1)}, u32[]{:S(2)}, u32[]{:S(2)}) collective-permute-start(bf16[3,96,1024]{2,1,0:T(8,128)(2,1)S(1)} %copy-done.25), channel_id=1, source_target_pairs={{0,64},{16,80},{32,96},{48,112},{64,0},{80,16},{96,32},{112,48},{1... | collective-permute-start | bytes 1769480 | tf_op jit(solution)/shard_map/ppermute | solution.py:164
  158.9 2.0 join.11
  160.9 1.3 collective-permute-start.24
  162.2 1.3 collective-permute-done.26.refs_6_
  163.5 3.5 %collective-permute-start.20 = (bf16[1024,768]{1,0:T(8,128)(2,1)}, bf16[1024,768]{1,0:T(8,128)(2,1)}, u32[]{:S(2)}, u32[]{:S(2)}) collective-permute-start(bf16[1024,768]{1,0:T(8,128)(2,1)} %get-tuple-element.66.b0), channel_id=1, source_target_pairs={{0,3},{1,2},{2,1},{3,0},{4,7},{5,6},{6,5},{7,4},{8,11},{9,10},{10,... | collective-permute-start | bytes 4718600 | tf_op jit(solution)/shard_map/ppermute | solution.py:61
  167.0 9.1 %collective-permute-done.22.refs_1_ = bf16[3,96,1024]{2,1,0:T(8,128)(2,1)S(1)} collective-permute-done((bf16[3,96,1024]{2,1,0:T(8,128)(2,1)S(1)}, bf16[3,96,1024]{2,1,0:T(8,128)(2,1)S(1)}, u32[]{:S(2)}, u32[]{:S(2)}) %collective-permute-start.22) | collective-permute-done | bytes 589856 | tf_op jit(solution)/shard_map/ppermute | solution.py:164
  176.1 12.2 %collective-permute-done.23.refs_2_ = bf16[3,96,1024]{2,1,0:T(8,128)(2,1)S(1)} collective-permute-done((bf16[3,96,1024]{2,1,0:T(8,128)(2,1)S(1)}, bf16[3,96,1024]{2,1,0:T(8,128)(2,1)S(1)}, u32[]{:S(2)}, u32[]{:S(2)}) %collective-permute-start.23) | collective-permute-done | bytes 589856 | tf_op jit(solution)/shard_map/ppermute | solution.py:164
  188.4 1.8 y_sum.1
  190.2 7.3 %all-to-all-start.2 = ((bf16[16,64,512]{2,1,0:T(8,128)(2,1)}), bf16[16,64,512]{2,1,0:T(8,128)(2,1)S(1)}, u32[]{:S(2)}, u32[]{:S(2)}) async-start(bf16[16,64,512]{2,1,0:T(8,128)(2,1)} %y_sum.1), calls=%async_computation.2 | async-start | bytes 2097152 | tf_op jit(solution)/shard_map/all_to_all | solution.py:466
  197.5 1.2 copy-done.6
  198.7 1.1 copy-done.8
  199.8 1.7 edge_add.1
  201.6 0.9 copy-done.20
  202.4 2.9 %first_half.3.first_ref = f32[256,768]{1,0:T(8,128)S(1)} custom-call(bf16[256,4096]{1,0:T(8,128)(2,1)S(1)} %copy-done.1, bf16[1024,768]{1,0:T(8,128)(2,1)} %get-tuple-element.66.b0, bf16[1024,768]{1,0:T(8,128)(2,1)} %get-tuple-element.67.b1), custom_call_target="tpu_custom_call" | custom-call | flops 2000000000 | bytes 5000000 | tf_op jit(solution)/shard_map/first_half/pallas_call | solution.py:235
  205.3 10.0 %all-to-all-done.2.got_ref = bf16[16,64,512]{2,1,0:T(8,128)(2,1)S(1)} async-done(((bf16[16,64,512]{2,1,0:T(8,128)(2,1)}), bf16[16,64,512]{2,1,0:T(8,128)(2,1)S(1)}, u32[]{:S(2)}, u32[]{:S(2)}) %all-to-all-start.2) | async-done | bytes 1048608 | tf_op jit(solution)/shard_map/all_to_all | solution.py:466
  215.4 0.9 last_sum.1
  216.3 1.6 copy-done.2
  217.8 1.1 copy-done.21
  219.0 3.6 %last_half.1 = bf16[256,768]{1,0:T(8,128)(2,1)} custom-call(bf16[256,4096]{1,0:T(8,128)(2,1)S(1)} %copy-done.2, bf16[1024,768]{1,0:T(8,128)(2,1)} %collective-permute-done.20.b0, bf16[1024,768]{1,0:T(8,128)(2,1)} %collective-permute-done.21.b1, f32[256,768]{1,0:T(8,128)S(1)} %first_half.3.first_ref, f32[256,768]{1,0:T(8,128)S(1)} %copy-done.21), custom_call_target="tpu_custom_call" | custom-call | flops 2000000000 | bytes 5000000 | tf_op jit(solution)/shard_map/last_half/pallas_call | solution.py:252
  (115 shorter events, 6.3 us)
Async XLA Ops:
  5.6 11.6 %copy-start.11 = (bf16[256,768]{1,0:T(8,128)(2,1)S(1)}, bf16[256,768]{1,0:T(8,128)(2,1)}, u32[]{:S(2)}) copy-start(bf16[256,768]{1,0:T(8,128)(2,1)} %x_paper_ref.1) | copy-start | bytes 1179652
  5.6 14.7 %copy-start.15 = (s32[256,16]{0,1:T(8,128)S(1)}, s32[256,16]{0,1:T(8,128)}, u32[]{:S(2)}) copy-start(s32[256,16]{0,1:T(8,128)} %param.14) | copy-start | bytes 49156
  5.6 50.9 %all-to-all-start = ((bf16[128,8,768]{2,1,0:T(8,128)(2,1)}), bf16[128,8,768]{2,1,0:T(8,128)(2,1)}, u32[]{:S(2)}, u32[]{:S(2)}) async-start(bf16[128,8,768]{2,1,0:T(8,128)(2,1)} %fusion.4), calls=%async_computation | async-start | bytes 3145728 | tf_op jit(solution)/shard_map/all_to_all | solution.py:152
  17.2 25.2 %copy-start.40 = (s32[1,128,4]{1,2,0:T(4,128)S(1)}, s32[1,128,4]{1,2,0:T(4,128)}, u32[]{:S(2)}) copy-start(s32[1,128,4]{1,2,0:T(4,128)} %param.15) | copy-start | bytes 6148
  17.2 25.5 %copy-start.39 = (s32[1,128,4]{1,2,0:T(4,128)S(1)}, s32[1,128,4]{1,2,0:T(4,128)}, u32[]{:S(2)}) copy-start(s32[1,128,4]{1,2,0:T(4,128)} %param.16) | copy-start | bytes 6148
  17.2 19.9 %collective-permute-start = (bf16[128,768]{1,0:T(8,128)(2,1)S(1)}, bf16[128,768]{1,0:T(8,128)(2,1)S(1)}, u32[]{:S(2)}, u32[]{:S(2)}) collective-permute-start(bf16[128,768]{1,0:T(8,128)(2,1)S(1)} %get-tuple-element.82.refs_0_), channel_id=1, source_target_pairs={{0,4},{1,5},{2,6},{3,7},{4,0},{5,1},{6,2},{7,3},{8,12},{9,13},{10,... | collective-permute-start | bytes 589832 | tf_op jit(solution)/shard_map/ppermute | solution.py:61
  18.2 20.0 %collective-permute-start.1 = (bf16[128,768]{1,0:T(8,128)(2,1)S(1)}, bf16[128,768]{1,0:T(8,128)(2,1)S(1)}, u32[]{:S(2)}, u32[]{:S(2)}) collective-permute-start(bf16[128,768]{1,0:T(8,128)(2,1)S(1)} %get-tuple-element.81.refs_2_), channel_id=1, source_target_pairs={{0,12},{1,13},{2,14},{3,15},{4,8},{5,9},{6,10},{7,11},{8,4},{9,5},... | collective-permute-start | bytes 589832 | tf_op jit(solution)/shard_map/ppermute | solution.py:61
  20.3 16.8 %collective-permute-start.2 = (s32[1,16,256]{2,1,0:T(8,128)S(1)}, s32[1,16,256]{2,1,0:T(8,128)S(1)}, u32[]{:S(2)}, u32[]{:S(2)}) collective-permute-start(s32[1,16,256]{2,1,0:T(8,128)S(1)} %bitcast.16), channel_id=1, source_target_pairs={{0,4},{1,5},{2,6},{3,7},{4,0},{5,1},{6,2},{7,3},{8,12},{9,13},{10,... | collective-permute-start | bytes 49160 | tf_op jit(solution)/shard_map/ppermute | solution.py:61
  38.2 13.7 %collective-permute-start.3 = (bf16[256,768]{1,0:T(8,128)(2,1)S(1)}, bf16[256,768]{1,0:T(8,128)(2,1)S(1)}, u32[]{:S(2)}, u32[]{:S(2)}) collective-permute-start(bf16[256,768]{1,0:T(8,128)(2,1)S(1)} %get-tuple-element.42.token_ref.refs_0_), channel_id=1, source_target_pairs={{0,1},{1,0},{2,3},{3,2},{4,5},{5,4},{6,7},{7,6},{8,9},{9,8},{10,11... | collective-permute-start | bytes 1179656 | tf_op jit(solution)/shard_map/ppermute | solution.py:61
  39.9 12.0 %collective-permute-start.4 = (bf16[256,768]{1,0:T(8,128)(2,1)S(1)}, bf16[256,768]{1,0:T(8,128)(2,1)}, u32[]{:S(2)}, u32[]{:S(2)}) collective-permute-start(bf16[256,768]{1,0:T(8,128)(2,1)S(1)} %get-tuple-element.43.refs_2_), channel_id=1, source_target_pairs={{0,3},{1,2},{2,1},{3,0},{4,7},{5,6},{6,5},{7,4},{8,11},{9,10},{10,... | collective-permute-start | bytes 1179656 | tf_op jit(solution)/shard_map/ppermute | solution.py:61
  43.0 8.9 %collective-permute-start.5 = (s32[2,16,256]{2,1,0:T(8,128)S(1)}, s32[2,16,256]{2,1,0:T(8,128)S(1)}, u32[]{:S(2)}, u32[]{:S(2)}) collective-permute-start(s32[2,16,256]{2,1,0:T(8,128)S(1)} %get-tuple-element.44.refs_4_), channel_id=1, source_target_pairs={{0,1},{1,0},{2,3},{3,2},{4,5},{5,4},{6,7},{7,6},{8,9},{9,8},{10,11... | collective-permute-start | bytes 98312 | tf_op jit(solution)/shard_map/ppermute | solution.py:61
  54.8 22.7 %collective-permute-start.6 = (bf16[512,768]{1,0:T(8,128)(2,1)}, bf16[512,768]{1,0:T(8,128)(2,1)}, u32[]{:S(2)}, u32[]{:S(2)}) collective-permute-start(bf16[512,768]{1,0:T(8,128)(2,1)} %get-tuple-element.45.refs_0_), channel_id=1, source_target_pairs={{0,12},{1,13},{2,14},{3,15},{4,8},{5,9},{6,10},{7,11},{8,4},{9,5},... | collective-permute-start | bytes 2359304 | tf_op jit(solution)/shard_map/ppermute | solution.py:61
  55.8 21.6 %collective-permute-start.7 = (bf16[512,768]{1,0:T(8,128)(2,1)}, bf16[512,768]{1,0:T(8,128)(2,1)}, u32[]{:S(2)}, u32[]{:S(2)}) collective-permute-start(bf16[512,768]{1,0:T(8,128)(2,1)} %get-tuple-element.46.refs_2_), channel_id=1, source_target_pairs={{0,4},{1,5},{2,6},{3,7},{4,0},{5,1},{6,2},{7,3},{8,12},{9,13},{10,... | collective-permute-start | bytes 2359304 | tf_op jit(solution)/shard_map/ppermute | solution.py:61
  56.4 1.4 copy-start.3
  57.8 1.4 copy-start.4
  60.2 1.4 copy-start.17
  61.6 1.4 copy-start.18
  65.1 6.8 %copy-start.14 = (s32[4,16,256]{2,1,0:T(8,128)S(1)}, s32[4,16,256]{2,1,0:T(8,128)}, u32[]{:S(2)}) copy-start(s32[4,16,256]{2,1,0:T(8,128)} %copy-done.13) | copy-start | bytes 196612
  71.8 7.7 %copy-start.5 = (bf16[512,1024]{1,0:T(8,128)(2,1)}, bf16[512,1024]{1,0:T(8,128)(2,1)S(1)}, u32[]{:S(2)}) copy-start(bf16[512,1024]{1,0:T(8,128)(2,1)S(1)} %get-tuple-element.68.adder_ref) | copy-start | bytes 3145732
  71.8 11.1 %collective-permute-start.11 = (bf16[256,4096]{1,0:T(8,128)(2,1)}, bf16[256,4096]{1,0:T(8,128)(2,1)S(1)}, u32[]{:S(2)}, u32[]{:S(2)}) collective-permute-start(bf16[256,4096]{1,0:T(8,128)(2,1)} %get-tuple-element.51.refs_0_), channel_id=1, source_target_pairs={{0,16},{16,0},{32,48},{48,32},{64,80},{80,64},{96,112},{112,96},{1... | collective-permute-start | bytes 6291464 | tf_op jit(solution)/shard_map/ppermute | solution.py:157
  71.9 5.6 %collective-permute-start.8 = (s32[4,16,256]{2,1,0:T(8,128)S(1)}, s32[4,16,256]{2,1,0:T(8,128)S(1)}, u32[]{:S(2)}, u32[]{:S(2)}) collective-permute-start(s32[4,16,256]{2,1,0:T(8,128)S(1)} %copy-done.14), channel_id=1, source_target_pairs={{0,12},{1,13},{2,14},{3,15},{4,8},{5,9},{6,10},{7,11},{8,4},{9,5},... | collective-permute-start | bytes 196616 | tf_op jit(solution)/shard_map/ppermute | solution.py:61
  79.5 3.3 %copy-start.37 = (s32[8,16,256]{2,1,0:T(8,128)}, s32[8,16,256]{2,1,0:T(8,128)S(1)}, u32[]{:S(2)}) copy-start(s32[8,16,256]{2,1,0:T(8,128)S(1)} %get-tuple-element.55.a_ref) | copy-start | bytes 393220
  79.6 20.5 %collective-permute-start.10 = (bf16[1024,768]{1,0:T(8,128)(2,1)S(1)}, bf16[1024,768]{1,0:T(8,128)(2,1)S(1)}, u32[]{:S(2)}, u32[]{:S(2)}) collective-permute-start(bf16[1024,768]{1,0:T(8,128)(2,1)S(1)} %get-tuple-element.49.b1), channel_id=1, source_target_pairs={{0,1},{1,0},{2,3},{3,2},{4,5},{5,4},{6,7},{7,6},{8,9},{9,8},{10,11... | collective-permute-start | bytes 4718600 | tf_op jit(solution)/shard_map/ppermute | solution.py:61
  80.8 2.1 copy-start.16
  80.8 21.6 %collective-permute-start.9 = (bf16[1024,768]{1,0:T(8,128)(2,1)S(1)}, bf16[1024,768]{1,0:T(8,128)(2,1)S(1)}, u32[]{:S(2)}, u32[]{:S(2)}) collective-permute-start(bf16[1024,768]{1,0:T(8,128)(2,1)S(1)} %get-tuple-element.48.b0), channel_id=1, source_target_pairs={{0,3},{1,2},{2,1},{3,0},{4,7},{5,6},{6,5},{7,4},{8,11},{9,10},{10,... | collective-permute-start | bytes 4718600 | tf_op jit(solution)/shard_map/ppermute | solution.py:61
  82.9 19.5 %copy-start.19 = (bf16[768,1024]{1,0:T(8,128)(2,1)S(1)}, bf16[768,1024]{1,0:T(8,128)(2,1)}, u32[]{:S(2)}) copy-start(bf16[768,1024]{1,0:T(8,128)(2,1)} %w_hbm.1) | copy-start | bytes 4718596
  82.9 19.5 %copy-start.29 = (bf16[256,1024]{1,0:T(8,128)(2,1)S(1)}, bf16[256,1024]{1,0:T(8,128)(2,1)}, u32[]{:S(2)}) copy-start(bf16[256,1024]{1,0:T(8,128)(2,1)} %grad_ref.3) | copy-start | bytes 1572868
  84.7 21.0 %copy-start.9 = (bf16[2,96,1024]{2,1,0:T(8,128)(2,1)}, bf16[2,96,1024]{2,1,0:T(8,128)(2,1)S(1)}, u32[]{:S(2)}) copy-start(bf16[2,96,1024]{2,1,0:T(8,128)(2,1)S(1)} %get-tuple-element.52.token_ref.refs_4_) | copy-start | bytes 1179652
  84.7 21.0 %copy-start.31 = (bf16[2,96,1024]{2,1,0:T(8,128)(2,1)}, bf16[2,96,1024]{2,1,0:T(8,128)(2,1)S(1)}, u32[]{:S(2)}) copy-start(bf16[2,96,1024]{2,1,0:T(8,128)(2,1)S(1)} %get-tuple-element.78) | copy-start | bytes 1179652
  84.7 21.0 %copy-start.33 = (bf16[2,96,1024]{2,1,0:T(8,128)(2,1)}, bf16[2,96,1024]{2,1,0:T(8,128)(2,1)S(1)}, u32[]{:S(2)}) copy-start(bf16[2,96,1024]{2,1,0:T(8,128)(2,1)S(1)} %get-tuple-element.77) | copy-start | bytes 1179652
  84.7 21.0 %copy-start.35 = (bf16[2,96,1024]{2,1,0:T(8,128)(2,1)}, bf16[2,96,1024]{2,1,0:T(8,128)(2,1)S(1)}, u32[]{:S(2)}) copy-start(bf16[2,96,1024]{2,1,0:T(8,128)(2,1)S(1)} %get-tuple-element.76) | copy-start | bytes 1179652
  105.7 5.3 %collective-permute-start.15 = (bf16[256,1792]{1,0:T(8,128)(2,1)S(1)}, bf16[256,1792]{1,0:T(8,128)(2,1)S(1)}, u32[]{:S(2)}, u32[]{:S(2)}) collective-permute-start(bf16[256,1792]{1,0:T(8,128)(2,1)S(1)} %get-tuple-element.57.refs_2_.pack_ref), channel_id=1, source_target_pairs={{0,16},{16,0},{32,48},{48,32},{64,80},{80,64},{96,112},{112,96},{1... | collective-permute-start | bytes 2752520 | tf_op jit(solution)/shard_map/ppermute | solution.py:157
  105.9 7.5 %collective-permute-start.13 = (bf16[128,768]{1,0:T(8,128)(2,1)S(1)}, bf16[128,768]{1,0:T(8,128)(2,1)S(1)}, u32[]{:S(2)}, u32[]{:S(2)}) collective-permute-start(bf16[128,768]{1,0:T(8,128)(2,1)S(1)} %get-tuple-element.80.refs_0_), channel_id=1, source_target_pairs={{0,4},{1,5},{2,6},{3,7},{4,0},{5,1},{6,2},{7,3},{8,12},{9,13},{10,... | collective-permute-start | bytes 589832 | tf_op jit(solution)/shard_map/ppermute | solution.py:61
  106.2 7.2 %collective-permute-start.14 = (bf16[128,768]{1,0:T(8,128)(2,1)S(1)}, bf16[128,768]{1,0:T(8,128)(2,1)S(1)}, u32[]{:S(2)}, u32[]{:S(2)}) collective-permute-start(bf16[128,768]{1,0:T(8,128)(2,1)S(1)} %get-tuple-element.79.refs_2_), channel_id=1, source_target_pairs={{0,12},{1,13},{2,14},{3,15},{4,8},{5,9},{6,10},{7,11},{8,4},{9,5},... | collective-permute-start | bytes 589832 | tf_op jit(solution)/shard_map/ppermute | solution.py:61
  113.4 4.5 %copy-start.22 = (bf16[3,96,1024]{2,1,0:T(8,128)(2,1)}, bf16[3,96,1024]{2,1,0:T(8,128)(2,1)S(1)}, u32[]{:S(2)}) copy-start(bf16[3,96,1024]{2,1,0:T(8,128)(2,1)S(1)} %get-tuple-element.75) | copy-start | bytes 1769476
  113.4 4.5 %copy-start.24 = (bf16[3,96,1024]{2,1,0:T(8,128)(2,1)}, bf16[3,96,1024]{2,1,0:T(8,128)(2,1)S(1)}, u32[]{:S(2)}) copy-start(bf16[3,96,1024]{2,1,0:T(8,128)(2,1)S(1)} %get-tuple-element.74) | copy-start | bytes 1769476
  113.4 4.5 %copy-start.26 = (bf16[3,96,1024]{2,1,0:T(8,128)(2,1)}, bf16[3,96,1024]{2,1,0:T(8,128)(2,1)S(1)}, u32[]{:S(2)}) copy-start(bf16[3,96,1024]{2,1,0:T(8,128)(2,1)S(1)} %get-tuple-element.73) | copy-start | bytes 1769476
  114.4 12.1 %collective-permute-start.16 = (bf16[256,768]{1,0:T(8,128)(2,1)}, bf16[256,768]{1,0:T(8,128)(2,1)S(1)}, u32[]{:S(2)}, u32[]{:S(2)}) collective-permute-start(bf16[256,768]{1,0:T(8,128)(2,1)} %get-tuple-element.59.refs_0_), channel_id=1, source_target_pairs={{0,1},{1,0},{2,3},{3,2},{4,5},{5,4},{6,7},{7,6},{8,9},{9,8},{10,11... | collective-permute-start | bytes 1179656 | tf_op jit(solution)/shard_map/ppermute | solution.py:61
  114.5 12.1 %collective-permute-start.17 = (bf16[256,768]{1,0:T(8,128)(2,1)}, bf16[256,768]{1,0:T(8,128)(2,1)}, u32[]{:S(2)}, u32[]{:S(2)}) collective-permute-start(bf16[256,768]{1,0:T(8,128)(2,1)} %get-tuple-element.60.refs_2_), channel_id=1, source_target_pairs={{0,3},{1,2},{2,1},{3,0},{4,7},{5,6},{6,5},{7,4},{8,11},{9,10},{10,... | collective-permute-start | bytes 1179656 | tf_op jit(solution)/shard_map/ppermute | solution.py:61
  117.9 72.3 %all-to-all-start.1 = ((bf16[128,8,768]{2,1,0:T(8,128)(2,1)}), bf16[128,8,768]{2,1,0:T(8,128)(2,1)S(1)}, u32[]{:S(2)}, u32[]{:S(2)}) async-start(bf16[128,8,768]{2,1,0:T(8,128)(2,1)} %bitcast.10), calls=%async_computation.1 | async-start | bytes 3145728 | tf_op jit(solution)/shard_map/all_to_all | solution.py:152
  126.5 4.0 %copy-start.38 = (s32[8,16,256]{2,1,0:T(8,128)S(1)}, s32[8,16,256]{2,1,0:T(8,128)}, u32[]{:S(2)}) copy-start(s32[8,16,256]{2,1,0:T(8,128)} %copy-done.37) | copy-start | bytes 393220
  126.5 7.4 %copy-start.36 = (bf16[2,96,1024]{2,1,0:T(8,128)(2,1)S(1)}, bf16[2,96,1024]{2,1,0:T(8,128)(2,1)}, u32[]{:S(2)}) copy-start(bf16[2,96,1024]{2,1,0:T(8,128)(2,1)} %copy-done.35) | copy-start | bytes 1179652
  126.5 8.9 %copy-start.34 = (bf16[2,96,1024]{2,1,0:T(8,128)(2,1)S(1)}, bf16[2,96,1024]{2,1,0:T(8,128)(2,1)}, u32[]{:S(2)}) copy-start(bf16[2,96,1024]{2,1,0:T(8,128)(2,1)} %copy-done.33) | copy-start | bytes 1179652
  126.6 23.9 %copy-start.32 = (bf16[2,96,1024]{2,1,0:T(8,128)(2,1)S(1)}, bf16[2,96,1024]{2,1,0:T(8,128)(2,1)}, u32[]{:S(2)}) copy-start(bf16[2,96,1024]{2,1,0:T(8,128)(2,1)} %copy-done.31) | copy-start | bytes 1179652
  128.0 28.2 %collective-permute-start.18 = (bf16[512,768]{1,0:T(8,128)(2,1)S(1)}, bf16[512,768]{1,0:T(8,128)(2,1)S(1)}, u32[]{:S(2)}, u32[]{:S(2)}) collective-permute-start(bf16[512,768]{1,0:T(8,128)(2,1)S(1)} %get-tuple-element.64.token_ref.refs_0_), channel_id=1, source_target_pairs={{0,12},{1,13},{2,14},{3,15},{4,8},{5,9},{6,10},{7,11},{8,4},{9,5},... | collective-permute-start | bytes 2359304 | tf_op jit(solution)/shard_map/ppermute | solution.py:61
  130.3 26.3 %collective-permute-start.19 = (bf16[512,768]{1,0:T(8,128)(2,1)S(1)}, bf16[512,768]{1,0:T(8,128)(2,1)S(1)}, u32[]{:S(2)}, u32[]{:S(2)}) collective-permute-start(bf16[512,768]{1,0:T(8,128)(2,1)S(1)} %get-tuple-element.65.refs_2_), channel_id=1, source_target_pairs={{0,4},{1,5},{2,6},{3,7},{4,0},{5,1},{6,2},{7,3},{8,12},{9,13},{10,... | collective-permute-start | bytes 2359304 | tf_op jit(solution)/shard_map/ppermute | solution.py:61
  130.5 19.9 %collective-permute-start.12 = (s32[8,16,256]{2,1,0:T(8,128)S(1)}, s32[8,16,256]{2,1,0:T(8,128)S(1)}, u32[]{:S(2)}, u32[]{:S(2)}) collective-permute-start(s32[8,16,256]{2,1,0:T(8,128)S(1)} %copy-done.38), channel_id=1, source_target_pairs={{0,3},{1,2},{2,1},{3,0},{4,7},{5,6},{6,5},{7,4},{8,11},{9,10},{10,... | collective-permute-start | bytes 393224 | tf_op jit(solution)/shard_map/ppermute | solution.py:61
  133.9 27.0 %collective-permute-start.25 = (bf16[2,96,1024]{2,1,0:T(8,128)(2,1)S(1)}, bf16[2,96,1024]{2,1,0:T(8,128)(2,1)S(1)}, u32[]{:S(2)}, u32[]{:S(2)}) collective-permute-start(bf16[2,96,1024]{2,1,0:T(8,128)(2,1)S(1)} %copy-done.36), channel_id=1, source_target_pairs={{0,32},{16,48},{32,64},{48,80},{64,96},{80,112},{96,0},{112,16},{1... | collective-permute-start | bytes 1179656 | tf_op jit(solution)/shard_map/ppermute | solution.py:164
  135.4 28.1 %collective-permute-start.26 = (bf16[2,96,1024]{2,1,0:T(8,128)(2,1)S(1)}, bf16[2,96,1024]{2,1,0:T(8,128)(2,1)S(1)}, u32[]{:S(2)}, u32[]{:S(2)}) collective-permute-start(bf16[2,96,1024]{2,1,0:T(8,128)(2,1)S(1)} %copy-done.34), channel_id=1, source_target_pairs={{0,64},{16,80},{32,96},{48,112},{64,0},{80,16},{96,32},{112,48},{1... | collective-permute-start | bytes 1179656 | tf_op jit(solution)/shard_map/ppermute | solution.py:164
  150.5 5.8 %copy-start.27 = (bf16[3,96,1024]{2,1,0:T(8,128)(2,1)S(1)}, bf16[3,96,1024]{2,1,0:T(8,128)(2,1)}, u32[]{:S(2)}) copy-start(bf16[3,96,1024]{2,1,0:T(8,128)(2,1)} %copy-done.26) | copy-start | bytes 1769476
  150.5 6.2 %copy-start.25 = (bf16[3,96,1024]{2,1,0:T(8,128)(2,1)S(1)}, bf16[3,96,1024]{2,1,0:T(8,128)(2,1)}, u32[]{:S(2)}) copy-start(bf16[3,96,1024]{2,1,0:T(8,128)(2,1)} %copy-done.24) | copy-start | bytes 1769476
  150.5 16.5 %collective-permute-start.27 = (bf16[2,96,1024]{2,1,0:T(8,128)(2,1)S(1)}, bf16[2,96,1024]{2,1,0:T(8,128)(2,1)S(1)}, u32[]{:S(2)}, u32[]{:S(2)}) collective-permute-start(bf16[2,96,1024]{2,1,0:T(8,128)(2,1)S(1)} %copy-done.32), channel_id=1, source_target_pairs={{0,96},{16,112},{32,0},{48,16},{64,32},{80,48},{96,64},{112,80},{1... | collective-permute-start | bytes 1179656 | tf_op jit(solution)/shard_map/ppermute | solution.py:164
  156.3 4.6 %copy-start = (bf16[256,4096]{1,0:T(8,128)(2,1)}, bf16[256,4096]{1,0:T(8,128)(2,1)S(1)}, u32[]{:S(2)}) copy-start(bf16[256,4096]{1,0:T(8,128)(2,1)S(1)} %cited_by_table.1.refs_4_.table_ref) | copy-start | bytes 6291460
  156.3 19.8 %collective-permute-start.22 = (bf16[3,96,1024]{2,1,0:T(8,128)(2,1)S(1)}, bf16[3,96,1024]{2,1,0:T(8,128)(2,1)S(1)}, u32[]{:S(2)}, u32[]{:S(2)}) collective-permute-start(bf16[3,96,1024]{2,1,0:T(8,128)(2,1)S(1)} %copy-done.27), channel_id=1, source_target_pairs={{0,32},{16,48},{32,64},{48,80},{64,96},{80,112},{96,0},{112,16},{1... | collective-permute-start | bytes 1769480 | tf_op jit(solution)/shard_map/ppermute | solution.py:164
  156.6 4.2 %copy-start.23 = (bf16[3,96,1024]{2,1,0:T(8,128)(2,1)S(1)}, bf16[3,96,1024]{2,1,0:T(8,128)(2,1)}, u32[]{:S(2)}) copy-start(bf16[3,96,1024]{2,1,0:T(8,128)(2,1)} %copy-done.22) | copy-start | bytes 1769476
  156.6 31.7 %copy-start.10 = (bf16[2,96,1024]{2,1,0:T(8,128)(2,1)S(1)}, bf16[2,96,1024]{2,1,0:T(8,128)(2,1)}, u32[]{:S(2)}) copy-start(bf16[2,96,1024]{2,1,0:T(8,128)(2,1)} %copy-done.9) | copy-start | bytes 1179652
  156.6 31.7 %collective-permute-start.23 = (bf16[3,96,1024]{2,1,0:T(8,128)(2,1)S(1)}, bf16[3,96,1024]{2,1,0:T(8,128)(2,1)S(1)}, u32[]{:S(2)}, u32[]{:S(2)}) collective-permute-start(bf16[3,96,1024]{2,1,0:T(8,128)(2,1)S(1)} %copy-done.25), channel_id=1, source_target_pairs={{0,64},{16,80},{32,96},{48,112},{64,0},{80,16},{96,32},{112,48},{1... | collective-permute-start | bytes 1769480 | tf_op jit(solution)/shard_map/ppermute | solution.py:164
  160.9 27.5 %collective-permute-start.24 = (bf16[3,96,1024]{2,1,0:T(8,128)(2,1)S(1)}, bf16[3,96,1024]{2,1,0:T(8,128)(2,1)S(1)}, u32[]{:S(2)}, u32[]{:S(2)}) collective-permute-start(bf16[3,96,1024]{2,1,0:T(8,128)(2,1)S(1)} %copy-done.23), channel_id=1, source_target_pairs={{0,96},{16,112},{32,0},{48,16},{64,32},{80,48},{96,64},{112,80},{1... | collective-permute-start | bytes 1769480 | tf_op jit(solution)/shard_map/ppermute | solution.py:164
  163.5 52.7 %collective-permute-start.20 = (bf16[1024,768]{1,0:T(8,128)(2,1)}, bf16[1024,768]{1,0:T(8,128)(2,1)}, u32[]{:S(2)}, u32[]{:S(2)}) collective-permute-start(bf16[1024,768]{1,0:T(8,128)(2,1)} %get-tuple-element.66.b0), channel_id=1, source_target_pairs={{0,3},{1,2},{2,1},{3,0},{4,7},{5,6},{6,5},{7,4},{8,11},{9,10},{10,... | collective-permute-start | bytes 4718600 | tf_op jit(solution)/shard_map/ppermute | solution.py:61
  167.0 49.2 %collective-permute-start.21 = (bf16[1024,768]{1,0:T(8,128)(2,1)}, bf16[1024,768]{1,0:T(8,128)(2,1)}, u32[]{:S(2)}, u32[]{:S(2)}) collective-permute-start(bf16[1024,768]{1,0:T(8,128)(2,1)} %get-tuple-element.67.b1), channel_id=1, source_target_pairs={{0,1},{1,0},{2,3},{3,2},{4,5},{5,4},{6,7},{7,6},{8,9},{9,8},{10,11... | collective-permute-start | bytes 4718600 | tf_op jit(solution)/shard_map/ppermute | solution.py:61
  190.2 25.2 %all-to-all-start.2 = ((bf16[16,64,512]{2,1,0:T(8,128)(2,1)}), bf16[16,64,512]{2,1,0:T(8,128)(2,1)S(1)}, u32[]{:S(2)}, u32[]{:S(2)}) async-start(bf16[16,64,512]{2,1,0:T(8,128)(2,1)} %y_sum.1), calls=%async_computation.2 | async-start | bytes 2097152 | tf_op jit(solution)/shard_map/all_to_all | solution.py:466
  197.5 1.2 copy-start.6
  199.8 2.6 %copy-start.1 = (bf16[256,4096]{1,0:T(8,128)(2,1)S(1)}, bf16[256,4096]{1,0:T(8,128)(2,1)}, u32[]{:S(2)}) copy-start(bf16[256,4096]{1,0:T(8,128)(2,1)} %copy-done) | copy-start | bytes 6291460
  216.2 1.6 copy-start.2
  (8 other events, 7.7 us)

commit v4 on v3

--- a/solution.py
+++ b/solution.py
@@ -15,6 +15,7 @@
 CYCLE = (4, 1, 12, 3)
 IN_VMEM = pl.BlockSpec(memory_space=pltpu.VMEM)
 ANYWHERE = pl.BlockSpec(memory_space=pl.ANY)
+IN_HBM = pl.BlockSpec(memory_space=pltpu.HBM)
 IN_SMEM = pl.BlockSpec(memory_space=pltpu.SMEM)
 
 
@@ -144,13 +145,31 @@
     pick = jnp.concatenate([write_src, jnp.where(write_dst >= 0, write_dst + 256, -1)], axis=1)
     into_paper = jnp.concatenate([write_dst, none], axis=1)
     into_author = jnp.concatenate([none, write_src], axis=1)
-    return pick.reshape(-1), into_paper.reshape(1, -1), into_author.reshape(1, -1)
+    return pick.reshape(1, -1), into_paper.reshape(1, -1), into_author.reshape(1, -1)
 
 
 def exchange(rows):
     sent = rows.reshape(128, 8, rows.shape[-1])
     got = lax.all_to_all(sent, ("row", "col"), split_axis=0, concat_axis=0, tiled=True)
     return got.reshape(1024, rows.shape[-1])
+
+
+def pick_kernel(pick_ref, a_ref, b_ref, token_ref, out_ref):
+    hit = jnp.where(lax.broadcasted_iota(I32, (512, 1024), 0) == pick_ref[...], 1.0, 0.0).astype(BF)
+    rows = dot(hit[:256], a_ref[...], ((0,), (0,))) + dot(hit[256:], b_ref[...], ((0,), (0,)))
+    out_ref[...] = rows.astype(BF)
+
+
+def pick_rows(pick, authors, papers, token):
+    return pl.pallas_call(
+        pick_kernel,
+        out_shape=shape((1024, 768), BF),
+        in_specs=[IN_VMEM] * 3 + [ANYWHERE],
+        out_specs=IN_VMEM,
+        compiler_params=params(16),
+        cost_estimate=pl.CostEstimate(flops=10**9, bytes_accessed=3 * 10**6, transcendentals=0),
+        name="pick_rows",
+    )(pick, authors, papers, token)
 
 
 def other_core(value):
@@ -171,15 +190,14 @@
 
 
 def author_kernel(
-    arrived_ref, into_paper_ref, into_author_ref, x_author_ref, x_paper_ref, grad_ref,
-    w_sa_hbm, w_wn_hbm, w_sp_hbm, w_wr_hbm,
-    out_ref, pack_ref, dz_ref, dx_ref, pre_ref, adder_ref, cnt_ref,
-    w_sa, w_wn, w_sp, w_wr, sems,
+    arrived_ref, into_paper_ref, into_author_ref, *refs
 ):
-    copies = []
-    for i, (a, b) in enumerate(((w_sa_hbm, w_sa), (w_wn_hbm, w_wn), (w_sp_hbm, w_sp), (w_wr_hbm, w_wr))):
-        copies.append(pltpu.make_async_copy(a, b, sems.at[i]))
-        copies[-1].start()
+    sources, outs, held, sems = refs[:7], refs[7:14], refs[14:21], refs[21]
+    out_ref, pack_ref, dz_ref, dx_ref, pre_ref, adder_ref, cnt_ref = outs
+    x_author_ref, x_paper_ref, grad_ref, w_sa, w_wn, w_sp, w_wr = held
+    copies = [pltpu.make_async_copy(a, b, sems.at[i]) for i, (a, b) in enumerate(zip(sources, held))]
+    for i in (0, 3, 4, 2, 1, 5, 6):
+        copies[i].start()
     ids = lax.broadcasted_iota(I32, (256, 1024), 0)
     means = []
     for i, ref in enumerate((into_paper_ref, into_author_ref)):
@@ -190,12 +208,15 @@
         adder_ref[pl.ds(256 * i, 256), :] = hit
         means.append((dot(hit, arrived_ref[...]) / cnt).astype(BF))
     written, authored = means
-    x_author, x_paper = x_author_ref[...], x_paper_ref[...]
-    copies[0].wait()
-    copies[1].wait()
+    for i in (0, 3, 4):
+        copies[i].wait()
+    x_author = x_author_ref[...]
     pre = dot(x_author, w_sa[...]) + dot(authored, w_wn[...])
     out, slope = silu_and_slope(pre)
     out_ref[...] = out
+    copies[2].wait()
+    copies[1].wait()
+    x_paper = x_paper_ref[...]
     dpre = (grad_ref[...].astype(F32) * slope).astype(BF)
     pack_ref[:, pl.ds(0, 768)] = x_author
     pack_ref[:, pl.ds(768, 768)] = authored
@@ -204,8 +225,8 @@
     pack_ref[:, pl.ds(3072, 1024)] = dpre
     dz_ref[...] = (dot(dpre, w_wn[...], ((1,), (1,))) / cnt_ref[pl.ds(256, 256), pl.ds(0, 1)]).astype(BF)
     dx_ref[...] = dot(dpre, w_sa[...], ((1,), (1,)))
-    copies[2].wait()
-    copies[3].wait()
+    copies[5].wait()
+    copies[6].wait()
     pre_ref[...] = dot(x_paper, w_sp[...]) + dot(written, w_wr[...])
 
 
@@ -217,9 +238,10 @@
             shape((256, 1024), BF), shape((256, 4096), BF), shape((256, 768), BF), shape((256, 768), F32),
             shape((256, 1024), F32), shape((512, 1024), BF), shape((512, 128), F32),
         ],
-        in_specs=[IN_VMEM] * 6 + [ANYWHERE] * 4,
+        in_specs=[IN_VMEM] * 3 + [IN_HBM] * 7,
         out_specs=[IN_VMEM] * 7,
-        scratch_shapes=[weight] * 4 + [pltpu.SemaphoreType.DMA((4,))],
+        scratch_shapes=[pltpu.VMEM((256, 768), BF)] * 2 + [pltpu.VMEM((256, 1024), BF)] + [weight] * 4
+        + [pltpu.SemaphoreType.DMA((7,))],
         compiler_params=params(40),
         cost_estimate=pl.CostEstimate(flops=4 * 10**9, bytes_accessed=15 * 10**6, transcendentals=0),
         name="author_step",
@@ -279,11 +301,12 @@
 
 
 def paper_kernel(
-    table_ref, b0, b1, first_ref, nbr_ref, pre_ref, grad_ref, w_hbm, token_ref,
-    out_ref, pack_ref, dz_ref, w_ref, sem,
+    table_ref, b0, b1, first_ref, nbr_ref, pre_ref, grad_hbm, w_hbm, token_ref,
+    out_ref, pack_ref, dz_ref, grad_ref, w_ref, sems,
 ):
-    copy = pltpu.make_async_copy(w_hbm, w_ref, sem)
-    copy.start()
+    copies = [pltpu.make_async_copy(w_hbm, w_ref, sems.at[0]), pltpu.make_async_copy(grad_hbm, grad_ref, sems.at[1])]
+    for copy in copies:
+        copy.start()
     total = first_ref[...]
     for h, block in enumerate((b0, b1)):
         total = total + dot(table_ref[:, pl.ds(h * 2048 + 1024, 1024)], block[...])
@@ -291,9 +314,10 @@
     cnt = jnp.maximum(cnt, 1.0)
     cited = (total / cnt).astype(BF)
     pack_ref[:, pl.ds(0, 768)] = cited
-    copy.wait()
+    copies[0].wait()
     out, slope = silu_and_slope(pre_ref[...] + dot(cited, w_ref[...]))
     out_ref[...] = out
+    copies[1].wait()
     dpre = (grad_ref[...].astype(F32) * slope).astype(BF)
     pack_ref[:, pl.ds(768, 1024)] = dpre
     dz_ref[...] = (dot(dpre, w_ref[...], ((1,), (1,))) / cnt).astype(BF)
@@ -303,9 +327,9 @@
     return pl.pallas_call(
         paper_kernel,
         out_shape=[shape((256, 1024), BF), shape((256, 1792), BF), shape((256, 768), BF)],
-        in_specs=[IN_VMEM] * 7 + [ANYWHERE] * 2,
+        in_specs=[IN_VMEM] * 6 + [IN_HBM] * 2 + [ANYWHERE],
         out_specs=[IN_VMEM] * 3,
-        scratch_shapes=[pltpu.VMEM((768, 1024), BF), pltpu.SemaphoreType.DMA],
+        scratch_shapes=[pltpu.VMEM((256, 1024), BF), pltpu.VMEM((768, 1024), BF), pltpu.SemaphoreType.DMA((2,))],
         compiler_params=params(32),
         cost_estimate=pl.CostEstimate(flops=3 * 10**9, bytes_accessed=10 * 10**6, transcendentals=0),
         name="paper_step",
@@ -327,7 +351,7 @@
     return pl.pallas_call(
         edge_back_kernel,
         out_shape=[shape((256, 768), BF), shape((256, 768), F32)],
-        in_specs=[IN_VMEM, IN_VMEM, ANYWHERE, ANYWHERE],
+        in_specs=[IN_VMEM, IN_VMEM, IN_HBM, IN_HBM],
         out_specs=[IN_VMEM] * 2,
         scratch_shapes=[pltpu.VMEM((768, 1024), BF)] * 2 + [pltpu.SemaphoreType.DMA((2,))],
         compiler_params=params(16),
@@ -394,7 +418,7 @@
     )(*paper, *author)
 
 
-def last_sum_kernel(got_ref, out_ref):
+def last_sum_kernel(got_ref, token_ref, out_ref):
     total = got_ref[0].astype(F32)
     for j in range(1, 16):
         total = total + got_ref[j].astype(F32)
@@ -403,15 +427,15 @@
         out_ref[m] = total[:, 96 * m : 96 * m + 96]
 
 
-def last_sum(got):
+def last_sum(got, token):
     return pl.pallas_call(
         last_sum_kernel,
         out_shape=shape((5, 64, 96), F32),
-        in_specs=[IN_VMEM],
+        in_specs=[IN_VMEM, ANYWHERE],
         out_specs=IN_VMEM,
         compiler_params=params(8),
         name="last_sum",
-    )(got)
+    )(got, token)
 
 
 def per_device(
@@ -425,13 +449,11 @@
     parts = join(travel(parts, 0))
 
     pick, into_paper, into_author = edge_lists(write_src[0], write_dst[0])
-    picker = (pick[:, None] == lax.iota(I32, 512)[None, :]).astype(BF)
-    rows = dot(picker, jnp.concatenate([x_author, x_paper], axis=0)).astype(BF)
-    arrived = exchange(rows)
+    arrived = exchange(pick_rows(pick, x_author, x_paper, parts[0]))
+    parts = join(travel(parts, 1))
 
     table = cite_table(place, cite_nbr, parts[0])
-    parts = join(travel(parts, 1), (table,))
-    parts = join(travel(parts, 2))
+    parts = join(travel(parts, 2), (table,))
     pairs = travel(parts, 3)
     cite_first = first_half(table, [pair[0] for pair in pairs[:2]])
 
@@ -453,21 +475,21 @@
         place, [pack_a, pack_a_other, pack_p, pack_p_other],
         [(0, 1, 1536), (2, 3, 0), (0, 1, 2304)], (2, 3, 768),
     )
-    parts = join(back_pairs, (parts_paper[0],))
+    rows = pick_rows(pick, dz_written, dz_write, dz_cite)
+    parts = join(back_pairs, (parts_paper[0], rows, pairs[2][1], *got_author[1:]))
     got_paper = over_y(parts_paper)
-    rows = dot(picker, jnp.concatenate([dz_written, dz_write], axis=0)).astype(BF)
-    parts = join(travel(parts, 1), (rows,))
     back = exchange(rows)
+    parts = join(travel(parts, 1))
     back_table = cited_by_table(place, pairs[2][0], pairs[2][1], parts[0])
-    parts = join(travel(parts, 2), (back_table,))
+    parts = join(travel(parts, 2), (back_table, *got_paper[1:]))
     back_pairs = travel(parts, 3)
     back_first = first_half(back_table, [pair[0] for pair in back_pairs])
 
     got = lax.all_to_all(y_sum(got_paper, got_author), "col", split_axis=0, concat_axis=0, tiled=True)
-    dweights = last_sum(got).transpose(0, 2, 1)
 
     dx_author, dx_paper_own = edge_add(adder, back, dx_author_own, dx_paper_own)
     dx_paper = last_half(back_table, [pair[1] for pair in back_pairs], back_first, dx_paper_own)
+    dweights = last_sum(got, dx_paper).transpose(0, 2, 1)
     return (out_paper, out_author, dx_paper, dx_author, dweights)
 
 

time: 223 us -> 245 us (1.099)
  local copies, waits for them, and re-layouts: 17.1 us -> 29.6 us
  waiting for transfers between devices: 83.8 us -> 93.3 us
  Pallas kernels: 48.5 us -> 56.2 us
  matrix products: 5.61 us -> 0 us
  starting transfers between devices: 64.9 us -> 61.9 us
    ppermute x6, waiting for transfers between devices: 22.7 us -> 38.4 us  [over_y(): got.append(lax.ppermute(parts[d], 'row', perm))]
    all_to_all x1, waiting for transfers between devices: 10 us -> 0.01 us  [per_device(): lax.all_to_all(y_sum(got_paper, got_author), 'col', split_axis=0, concat_...]
    dot_general x2 -> x0, matrix products: 5.61 us -> none  [dot(): return lax.dot_general(a, b, (dims, ((), ())), preferred_element_type=F32)]
    unnamed x85 -> x103, local copies, waits for them, and re-layouts: 16.6 us -> 22.2 us
    pallas_call x0 -> x2, Pallas kernels: none -> 4.4 us  [pick_rows(): pl.pallas_call(pick_kernel, out_shape=shape((1024, 768), BF), in_specs=[I...]
    ppermute x20, waiting for transfers between devices: 51.1 us -> 54.9 us  [travel(): pairs.append((part, lax.ppermute(part, ('row', 'col'), perm)))]
    all_to_all x2, starting transfers between devices: 20.3 us -> 17.1 us  [exchange(): lax.all_to_all(sent, ('row', 'col'), split_axis=0, concat_axis=0, tiled=T...]
  transfers between devices with their start and end apart: 31 -> 31, of which waited for: 10 -> 13; matrix products, arithmetic and copies ran while one was open for 1% -> 4% of each run, Pallas kernels for 18% -> 20%
where the time goes in v4:
time: 245 us; the launch traced here: 244 us
  waiting for transfers between devices  93.3 us (38%)
  starting transfers between devices  61.9 us (25%)
  Pallas kernels  56.2 us (23%)
  local copies, waits for them, and re-layouts  29.6 us (12%)
    ppermute x20, waiting for transfers between devices, travel(): pairs.append((part, lax.ppermute(part, ('row', 'col'), perm)))  54.9 us
    ppermute x6, waiting for transfers between devices, over_y(): got.append(lax.ppermute(parts[d], 'row', perm))  38.4 us
    ppermute x20, starting transfers between devices, travel(): pairs.append((part, lax.ppermute(part, ('row', 'col'), perm)))  28.3 us
    unnamed x103, local copies, waits for them, and re-layouts  22.2 us
    all_to_all x2, starting transfers between devices, exchange(): lax.all_to_all(sent, ('row', 'col'), split_axis=0, concat_axis=0, tiled=T...  17.1 us
    ppermute x6, starting transfers between devices, over_y(): got.append(lax.ppermute(parts[d], 'row', perm))  10.5 us
    pallas_call x6, Pallas kernels, join(): pl.pallas_call(functools.partial(join_kernel, n), out_shape=outs, in_spec...  9.46 us
    pallas_call x1, Pallas kernels, cite_table(): pl.pallas_call(table_kernel, out_shape=shape((256, 4096), BF), in_specs=[...  8.03 us
  transfers between devices with their start and end apart: 31, of which 13 were waited for; matrix products, arithmetic and copies ran while one was open for 4% of the time, Pallas kernels for 20%

profile of v4, /device:TPU:0, one launch (start us, length us, event | category | flops | bytes accessed | tf_op | source)
XLA Modules:
  0.0 243.6 jit_solution(11911693607531589138)
XLA Ops:
  0.7 1.1 fusion.1
  1.8 1.7 collective-permute-start
  3.4 2.1 collective-permute-start.1
  7.7 1.8 collective-permute-done.2.refs_5_
  11.8 2.2 pick_rows.2
  14.1 10.6 %all-to-all-start = ((bf16[128,8,768]{2,1,0:T(8,128)(2,1)}), bf16[128,8,768]{2,1,0:T(8,128)(2,1)}, u32[]{:S(2)}, u32[]{:S(2)}) async-start(bf16[128,8,768]{2,1,0:T(8,128)(2,1)} %bitcast.8), calls=%async_computation | async-start | bytes 3145728 | tf_op jit(solution)/shard_map/all_to_all | solution.py:153
  24.7 1.1 collective-permute-start.3
  25.8 2.3 collective-permute-start.4
  29.7 1.6 concatenate.11.clone
  31.3 1.5 reshape.39.into_author_ref
  33.5 1.5 concatenate.10.clone
  35.0 1.5 reshape.38.into_paper_ref
  36.5 11.5 %collective-permute-done.5.refs_5_ = s32[2,16,256]{2,1,0:T(8,128)} collective-permute-done((s32[2,16,256]{2,1,0:T(8,128)}, s32[2,16,256]{2,1,0:T(8,128)}, u32[]{:S(2)}, u32[]{:S(2)}) %collective-permute-start.5) | collective-permute-done | bytes 32800 | tf_op jit(solution)/shard_map/ppermute | solution.py:62
  48.0 1.5 collective-permute-done.4.refs_3_
  49.5 1.0 copy-done.15
  50.5 1.0 copy-done.17
  52.3 2.4 join.7
  55.3 2.4 collective-permute-start.6
  59.0 1.4 copy-done.32
  60.4 1.4 copy-done.33
  61.8 1.0 copy-done.38
  62.9 1.0 copy-done.41
  63.9 7.3 %author_step.1 = (bf16[256,1024]{1,0:T(8,128)(2,1)}, bf16[256,4096]{1,0:T(8,128)(2,1)}, bf16[256,768]{1,0:T(8,128)(2,1)S(1)}, f32[256,768]{1,0:T(8,128)S(1)}, f3...) custom-call(bf16[1024,768]{1,0:T(8,128)(2,1)} %bitcast.9.arrived_ref, ...), custom_call_target="tpu_custom_call" | custom-call | flops 4000000000 | bytes 15000000 | tf_op jit(solution)/shard_map/author_step/pallas_call | solution.py:235
  75.6 1.3 collective-permute-start.8
  76.9 8.0 %cite_table.1.refs_6_.table_ref = bf16[256,4096]{1,0:T(8,128)(2,1)S(1)} custom-call(s32[3]{0:T(128)S(1)} %pad_add_fusion.1.place_ref, s32[256,16]{1,0:T(8,128)S(1)} %copy.22.nbr_ref, bf16[512,768]{1,0:T(8,128)(2,1)} %get-tuple-element.45.token_ref.refs_0_), custom_call_target="tpu_custom_call" | custom-call | flops 1000000000 | bytes 3000000 | tf_op jit(solution)/shard_map/cite_table/pallas_call | solution.py:106
  85.0 2.1 join.8
  87.7 1.8 collective-permute-start.9
  90.6 3.0 %weight_parts.2 = (bf16[2,96,1024]{2,1,0:T(8,128)(2,1)S(1)}, bf16[2,96,1024]{2,1,0:T(8,128)(2,1)S(1)}, bf16[2,96,1024]{2,1,0:T(8,128)(2,1)S(1)}, bf16[2,96,1024]{2,1,0:T(8,128)(2,1)S(1)}) custom-call(s32[3]{0:T(128)S(1)} %pad_add_fusion.1.place_ref, bf16[256,4096]{1,0:T(8,128)(2,1)S(1)} %copy-done.31, bf16[256,4096]{1,0:T(8,128)(2,1)} %collective-permute-done.11.refs_1_), custom_call_target="tpu_custom_call" | custom-call | flops 2000000000 | bytes 8000000 | tf_op jit(solution)/shard_map/weight_parts/pallas_call | solution.py:382
  93.6 14.0 %collective-permute-done.10.b1 = bf16[1024,768]{1,0:T(8,128)(2,1)S(1)} collective-permute-done((bf16[1024,768]{1,0:T(8,128)(2,1)S(1)}, bf16[1024,768]{1,0:T(8,128)(2,1)S(1)}, u32[]{:S(2)}, u32[]{:S(2)}) %collective-permute-start.10) | collective-permute-done | bytes 1572896 | tf_op jit(solution)/shard_map/ppermute | solution.py:62
  107.5 1.8 collective-permute-done.9.b0
  109.4 3.2 %paper_step.1 = (bf16[256,1024]{1,0:T(8,128)(2,1)}, bf16[256,1792]{1,0:T(8,128)(2,1)S(1)}, bf16[256,768]{1,0:T(8,128)(2,1)S(1)}) custom-call(bf16[256,4096]{1,0:T(8,128)(2,1)S(1)} %cite_table.1.refs_6_.table_ref, bf16[1024,768]{1,0:T(8,128)(2,1)S(1)} %collective-permute-done.9.b0, bf16[1024,768]{1,0:T(8,128)(2,1)S(1)} %collective-permute-done.10.b1, ...), custom_call_target="tpu_custom_call" | custom-call | flops 3000000000 | bytes 10000000 | tf_op jit(solution)/shard_map/paper_step/pallas_call | solution.py:327
  112.7 1.9 collective-permute-start.12
  114.6 1.1 collective-permute-start.16
  115.7 2.7 %collective-permute-start.17 = (bf16[2,96,1024]{2,1,0:T(8,128)(2,1)S(1)}, bf16[2,96,1024]{2,1,0:T(8,128)(2,1)S(1)}, u32[]{:S(2)}, u32[]{:S(2)}) collective-permute-start(bf16[2,96,1024]{2,1,0:T(8,128)(2,1)S(1)} %get-tuple-element.63), channel_id=1, source_target_pairs={{0,64},{16,80},{32,96},{48,112},{64,0},{80,16},{96,32},{112,48},{1... | collective-permute-start | bytes 1179656 | tf_op jit(solution)/shard_map/ppermute | solution.py:183
  118.4 1.5 collective-permute-start.18
  120.0 1.8 edge_back.1
  123.2 2.6 %collective-permute-start.14 = (bf16[128,768]{1,0:T(8,128)(2,1)S(1)}, bf16[128,768]{1,0:T(8,128)(2,1)S(1)}, u32[]{:S(2)}, u32[]{:S(2)}) collective-permute-start(bf16[128,768]{1,0:T(8,128)(2,1)S(1)} %get-tuple-element.79.refs_2_), channel_id=1, source_target_pairs={{0,12},{1,13},{2,14},{3,15},{4,8},{5,9},{6,10},{7,11},{8,4},{9,5},... | collective-permute-start | bytes 589832 | tf_op jit(solution)/shard_map/ppermute | solution.py:62
  125.8 2.2 pick_rows.3.refs_5_
  128.0 3.3 %weight_parts.3 = (bf16[3,96,1024]{2,1,0:T(8,128)(2,1)S(1)}, bf16[3,96,1024]{2,1,0:T(8,128)(2,1)S(1)}, bf16[3,96,1024]{2,1,0:T(8,128)(2,1)S(1)}, bf16[3,96,1024]{2,1,0:T(8,128)(2,1)S(1)}) custom-call(s32[3]{0:T(128)S(1)} %pad_add_fusion.1.place_ref, bf16[256,4096]{1,0:T(8,128)(2,1)S(1)} %copy-done.31, bf16[256,4096]{1,0:T(8,128)(2,1)} %collective-permute-done.11.refs_1_, ...), custom_call_target="tpu_custom_call" | custom-call | flops 2000000000 | bytes 8000000 | tf_op jit(solution)/shard_map/weight_parts/pallas_call | solution.py:382
  131.5 3.5 %collective-permute-done.17.refs_8_.refs_6_ = bf16[2,96,1024]{2,1,0:T(8,128)(2,1)S(1)} collective-permute-done((bf16[2,96,1024]{2,1,0:T(8,128)(2,1)S(1)}, bf16[2,96,1024]{2,1,0:T(8,128)(2,1)S(1)}, u32[]{:S(2)}, u32[]{:S(2)}) %collective-permute-start.17) | collective-permute-done | bytes 393248 | tf_op jit(solution)/shard_map/ppermute | solution.py:183
  135.6 1.3 collective-permute-start.20
  136.9 6.0 %collective-permute-done.19.refs_1_ = bf16[256,768]{1,0:T(8,128)(2,1)S(1)} collective-permute-done((bf16[256,768]{1,0:T(8,128)(2,1)S(1)}, bf16[256,768]{1,0:T(8,128)(2,1)S(1)}, u32[]{:S(2)}, u32[]{:S(2)}) %collective-permute-start.19) | collective-permute-done | bytes 393248 | tf_op jit(solution)/shard_map/ppermute | solution.py:62
  142.9 1.6 collective-permute-done.20.refs_3_
  144.6 1.2 join.10
  145.8 2.3 collective-permute-start.21
  149.0 6.5 %all-to-all-start.1 = ((bf16[128,8,768]{2,1,0:T(8,128)(2,1)}), bf16[128,8,768]{2,1,0:T(8,128)(2,1)S(1)}, u32[]{:S(2)}, u32[]{:S(2)}) async-start(bf16[128,8,768]{2,1,0:T(8,128)(2,1)} %bitcast.10), calls=%async_computation.1 | async-start | bytes 3145728 | tf_op jit(solution)/shard_map/all_to_all | solution.py:153
  155.5 1.0 collective-permute-start.23
  156.5 2.7 %collective-permute-start.24 = (bf16[3,96,1024]{2,1,0:T(8,128)(2,1)}, bf16[3,96,1024]{2,1,0:T(8,128)(2,1)S(1)}, u32[]{:S(2)}, u32[]{:S(2)}) collective-permute-start(bf16[3,96,1024]{2,1,0:T(8,128)(2,1)} %copy-done.36), channel_id=1, source_target_pairs={{0,64},{16,80},{32,96},{48,112},{64,0},{80,16},{96,32},{112,48},{1... | collective-permute-start | bytes 1769480 | tf_op jit(solution)/shard_map/ppermute | solution.py:183
  159.2 1.4 collective-permute-start.25
  161.5 4.0 %cited_by_table.1.refs_4_.table_ref = bf16[256,4096]{1,0:T(8,128)(2,1)S(1)} custom-call(s32[3]{0:T(128)S(1)} %pad_add_fusion.1.place_ref, s32[8,16,256]{2,1,0:T(8,128)S(1)} %copy-done.43, s32[8,16,256]{2,1,0:T(8,128)S(1)} %collective-permute-done.12.refs_6_.b_ref, bf16[512,768]{1,0:T(8,128)(2,1)} %get-tuple-element.67.token_ref.refs_0_), custom_call_target="tpu_custom_call" | custom-call | flops 1000000000 | bytes 3000000 | tf_op jit(solution)/shard_map/cited_by_table/pallas_call | solution.py:132
  165.6 22.2 %collective-permute-done.23.refs_5_.refs_1_ = bf16[3,96,1024]{2,1,0:T(8,128)(2,1)S(1)} collective-permute-done((bf16[3,96,1024]{2,1,0:T(8,128)(2,1)}, bf16[3,96,1024]{2,1,0:T(8,128)(2,1)S(1)}, u32[]{:S(2)}, u32[]{:S(2)}) %collective-permute-start.23) | collective-permute-done | bytes 589856 | tf_op jit(solution)/shard_map/ppermute | solution.py:183
  187.8 12.7 %collective-permute-done.24.refs_6_.refs_2_ = bf16[3,96,1024]{2,1,0:T(8,128)(2,1)S(1)} collective-permute-done((bf16[3,96,1024]{2,1,0:T(8,128)(2,1)}, bf16[3,96,1024]{2,1,0:T(8,128)(2,1)S(1)}, u32[]{:S(2)}, u32[]{:S(2)}) %collective-permute-start.24) | collective-permute-done | bytes 589856 | tf_op jit(solution)/shard_map/ppermute | solution.py:183
  200.4 3.7 %join.11 = (bf16[1024,768]{1,0:T(8,128)(2,1)}, bf16[1024,768]{1,0:T(8,128)(2,1)}) custom-call(bf16[512,768]{1,0:T(8,128)(2,1)} %get-tuple-element.67.token_ref.refs_0_, bf16[512,768]{1,0:T(8,128)(2,1)} %collective-permute-done.21.refs_1_, bf16[512,768]{1,0:T(8,128)(2,1)} %get-tuple-element.68.refs_2_, bf16[512,768]{1,0:T(8,128)(2,1)} %collective-permute-done.22.refs_3_, ...), custom_call_target="tpu_custom_call" | custom-call | tf_op jit(solution)/shard_map/join/pallas_call | solution.py:47
  204.1 3.5 %collective-permute-start.26 = (bf16[1024,768]{1,0:T(8,128)(2,1)}, bf16[1024,768]{1,0:T(8,128)(2,1)}, u32[]{:S(2)}, u32[]{:S(2)}) collective-permute-start(bf16[1024,768]{1,0:T(8,128)(2,1)} %get-tuple-element.72.b0), channel_id=1, source_target_pairs={{0,3},{1,2},{2,1},{3,0},{4,7},{5,6},{6,5},{7,4},{8,11},{9,10},{10,... | collective-permute-start | bytes 4718600 | tf_op jit(solution)/shard_map/ppermute | solution.py:62
  207.6 1.8 y_sum.1
  209.4 6.0 %all-to-all-start.2 = ((bf16[16,64,512]{2,1,0:T(8,128)(2,1)}), bf16[16,64,512]{2,1,0:T(8,128)(2,1)S(1)}, u32[]{:S(2)}, u32[]{:S(2)}) async-start(bf16[16,64,512]{2,1,0:T(8,128)(2,1)} %y_sum.1), calls=%async_computation.2 | async-start | bytes 2097152 | tf_op jit(solution)/shard_map/all_to_all | solution.py:488
  215.3 1.2 copy-done.6
  216.6 1.1 copy-done.10
  217.7 1.7 edge_add.1
  219.4 2.9 %first_half.3.first_ref = f32[256,768]{1,0:T(8,128)S(1)} custom-call(bf16[256,4096]{1,0:T(8,128)(2,1)S(1)} %copy-done.1, bf16[1024,768]{1,0:T(8,128)(2,1)} %get-tuple-element.72.b0, bf16[1024,768]{1,0:T(8,128)(2,1)} %get-tuple-element.73.b1), custom_call_target="tpu_custom_call" | custom-call | flops 2000000000 | bytes 5000000 | tf_op jit(solution)/shard_map/first_half/pallas_call | solution.py:257
  222.3 9.6 %collective-permute-done.26.b0 = bf16[1024,768]{1,0:T(8,128)(2,1)} collective-permute-done((bf16[1024,768]{1,0:T(8,128)(2,1)}, bf16[1024,768]{1,0:T(8,128)(2,1)}, u32[]{:S(2)}, u32[]{:S(2)}) %collective-permute-start.26) | collective-permute-done | bytes 1572896 | tf_op jit(solution)/shard_map/ppermute | solution.py:62
  231.9 6.2 %collective-permute-done.27.b1 = bf16[1024,768]{1,0:T(8,128)(2,1)} collective-permute-done((bf16[1024,768]{1,0:T(8,128)(2,1)}, bf16[1024,768]{1,0:T(8,128)(2,1)}, u32[]{:S(2)}, u32[]{:S(2)}) %collective-permute-start.27) | collective-permute-done | bytes 1572896 | tf_op jit(solution)/shard_map/ppermute | solution.py:62
  238.1 3.6 %last_half.1.token_ref = bf16[256,768]{1,0:T(8,128)(2,1)} custom-call(bf16[256,4096]{1,0:T(8,128)(2,1)S(1)} %copy-done.1, bf16[1024,768]{1,0:T(8,128)(2,1)} %collective-permute-done.26.b0, bf16[1024,768]{1,0:T(8,128)(2,1)} %collective-permute-done.27.b1, f32[256,768]{1,0:T(8,128)S(1)} %first_half.3.first_ref, f32[256,768]{1,0:T(8,128)S(1)} %get-tuple-element.77.own_ref), custom_call_target="tpu_custom_call" | custom-call | flops 2000000000 | bytes 5000000 | tf_op jit(solution)/shard_map/last_half/pallas_call | solution.py:274
  241.8 1.0 copy-done.18
  (133 shorter events, 20.7 us)
Async XLA Ops:
  0.6 11.2 %copy-start.13 = (bf16[256,768]{1,0:T(8,128)(2,1)S(1)}, bf16[256,768]{1,0:T(8,128)(2,1)}, u32[]{:S(2)}) copy-start(bf16[256,768]{1,0:T(8,128)(2,1)} %refs_1_.1) | copy-start | bytes 1179652
  0.6 11.2 %copy-start.40 = (bf16[256,768]{1,0:T(8,128)(2,1)S(1)}, bf16[256,768]{1,0:T(8,128)(2,1)}, u32[]{:S(2)}) copy-start(bf16[256,768]{1,0:T(8,128)(2,1)} %refs_0_.1) | copy-start | bytes 1179652
  1.8 7.7 %collective-permute-start = (bf16[128,768]{1,0:T(8,128)(2,1)S(1)}, bf16[128,768]{1,0:T(8,128)(2,1)S(1)}, u32[]{:S(2)}, u32[]{:S(2)}) collective-permute-start(bf16[128,768]{1,0:T(8,128)(2,1)S(1)} %get-tuple-element.82.refs_0_), channel_id=1, source_target_pairs={{0,4},{1,5},{2,6},{3,7},{4,0},{5,1},{6,2},{7,3},{8,12},{9,13},{10,... | collective-permute-start | bytes 589832 | tf_op jit(solution)/shard_map/ppermute | solution.py:62
  3.4 6.9 %collective-permute-start.1 = (bf16[128,768]{1,0:T(8,128)(2,1)S(1)}, bf16[128,768]{1,0:T(8,128)(2,1)S(1)}, u32[]{:S(2)}, u32[]{:S(2)}) collective-permute-start(bf16[128,768]{1,0:T(8,128)(2,1)S(1)} %get-tuple-element.81.refs_2_), channel_id=1, source_target_pairs={{0,12},{1,13},{2,14},{3,15},{4,8},{5,9},{6,10},{7,11},{8,4},{9,5},... | collective-permute-start | bytes 589832 | tf_op jit(solution)/shard_map/ppermute | solution.py:62
  5.5 3.9 %collective-permute-start.2 = (s32[1,16,256]{2,1,0:T(8,128)}, s32[1,16,256]{2,1,0:T(8,128)S(1)}, u32[]{:S(2)}, u32[]{:S(2)}) collective-permute-start(s32[1,16,256]{2,1,0:T(8,128)} %bitcast.15), channel_id=1, source_target_pairs={{0,4},{1,5},{2,6},{3,7},{4,0},{5,1},{6,2},{7,3},{8,12},{9,13},{10,... | collective-permute-start | bytes 49160 | tf_op jit(solution)/shard_map/ppermute | solution.py:62
  7.7 6.3 %copy-start.27 = (s32[1,1024]{1,0:T(1,128)}, s32[1,1024]{1,0:T(1,128)S(1)}, u32[]{:S(2)}) copy-start(s32[1,1024]{1,0:T(1,128)S(1)} %reshape.35.pick_ref) | copy-start | bytes 12292
  11.8 2.2 copy-start.25
  11.8 2.2 copy-start.14
  14.0 14.9 %copy-start.49 = (s32[1,128,4]{1,2,0:T(4,128)S(1)}, s32[1,128,4]{1,2,0:T(4,128)}, u32[]{:S(2)}) copy-start(s32[1,128,4]{1,2,0:T(4,128)} %param.15) | copy-start | bytes 6148
  14.0 18.7 %copy-start.48 = (s32[1,128,4]{1,2,0:T(4,128)S(1)}, s32[1,128,4]{1,2,0:T(4,128)}, u32[]{:S(2)}) copy-start(s32[1,128,4]{1,2,0:T(4,128)} %param.16) | copy-start | bytes 6148
  14.0 43.6 %copy-start.3 = (bf16[768,1024]{1,0:T(8,128)(2,1)S(1)}, bf16[768,1024]{1,0:T(8,128)(2,1)}, u32[]{:S(2)}) copy-start(bf16[768,1024]{1,0:T(8,128)(2,1)} %w_wr_hbm.1) | copy-start | bytes 4718596
  14.1 43.6 %all-to-all-start = ((bf16[128,8,768]{2,1,0:T(8,128)(2,1)}), bf16[128,8,768]{2,1,0:T(8,128)(2,1)}, u32[]{:S(2)}, u32[]{:S(2)}) async-start(bf16[128,8,768]{2,1,0:T(8,128)(2,1)} %bitcast.8), calls=%async_computation | async-start | bytes 3145728 | tf_op jit(solution)/shard_map/all_to_all | solution.py:153
  24.7 33.0 %copy-start.2 = (bf16[768,1024]{1,0:T(8,128)(2,1)S(1)}, bf16[768,1024]{1,0:T(8,128)(2,1)}, u32[]{:S(2)}) copy-start(bf16[768,1024]{1,0:T(8,128)(2,1)} %w_sp_hbm.1) | copy-start | bytes 4718596
  24.7 23.3 %collective-permute-start.3 = (bf16[256,768]{1,0:T(8,128)(2,1)}, bf16[256,768]{1,0:T(8,128)(2,1)}, u32[]{:S(2)}, u32[]{:S(2)}) collective-permute-start(bf16[256,768]{1,0:T(8,128)(2,1)} %copy-done.14), channel_id=1, source_target_pairs={{0,1},{1,0},{2,3},{3,2},{4,5},{5,4},{6,7},{7,6},{8,9},{9,8},{10,11... | collective-permute-start | bytes 1179656 | tf_op jit(solution)/shard_map/ppermute | solution.py:62
  25.8 23.7 %collective-permute-start.4 = (bf16[256,768]{1,0:T(8,128)(2,1)}, bf16[256,768]{1,0:T(8,128)(2,1)}, u32[]{:S(2)}, u32[]{:S(2)}) collective-permute-start(bf16[256,768]{1,0:T(8,128)(2,1)} %copy-done.16), channel_id=1, source_target_pairs={{0,3},{1,2},{2,1},{3,0},{4,7},{5,6},{6,5},{7,4},{8,11},{9,10},{10,... | collective-permute-start | bytes 1179656 | tf_op jit(solution)/shard_map/ppermute | solution.py:62
  28.1 19.9 %collective-permute-start.5 = (s32[2,16,256]{2,1,0:T(8,128)}, s32[2,16,256]{2,1,0:T(8,128)}, u32[]{:S(2)}, u32[]{:S(2)}) collective-permute-start(s32[2,16,256]{2,1,0:T(8,128)} %copy-done.25), channel_id=1, source_target_pairs={{0,1},{1,0},{2,3},{3,2},{4,5},{5,4},{6,7},{7,6},{8,9},{9,8},{10,11... | collective-permute-start | bytes 98312 | tf_op jit(solution)/shard_map/ppermute | solution.py:62
  55.3 29.7 %collective-permute-start.6 = (bf16[512,768]{1,0:T(8,128)(2,1)}, bf16[512,768]{1,0:T(8,128)(2,1)}, u32[]{:S(2)}, u32[]{:S(2)}) collective-permute-start(bf16[512,768]{1,0:T(8,128)(2,1)} %get-tuple-element.45.token_ref.refs_0_), channel_id=1, source_target_pairs={{0,12},{1,13},{2,14},{3,15},{4,8},{5,9},{6,10},{7,11},{8,4},{9,5},... | collective-permute-start | bytes 2359304 | tf_op jit(solution)/shard_map/ppermute | solution.py:62
  57.6 27.3 %collective-permute-start.7 = (bf16[512,768]{1,0:T(8,128)(2,1)}, bf16[512,768]{1,0:T(8,128)(2,1)}, u32[]{:S(2)}, u32[]{:S(2)}) collective-permute-start(bf16[512,768]{1,0:T(8,128)(2,1)} %get-tuple-element.46.refs_2_), channel_id=1, source_target_pairs={{0,4},{1,5},{2,6},{3,7},{4,0},{5,1},{6,2},{7,3},{8,12},{9,13},{10,... | collective-permute-start | bytes 2359304 | tf_op jit(solution)/shard_map/ppermute | solution.py:62
  59.0 1.4 copy-start.32
  60.4 1.4 copy-start.33
  61.8 1.0 copy-start.38
  63.9 11.6 %copy-start.24 = (s32[256,16]{0,1:T(8,128)S(1)}, s32[256,16]{0,1:T(8,128)}, u32[]{:S(2)}) copy-start(s32[256,16]{0,1:T(8,128)} %param.14) | copy-start | bytes 49156
  75.4 15.1 %collective-permute-start.11 = (bf16[256,4096]{1,0:T(8,128)(2,1)}, bf16[256,4096]{1,0:T(8,128)(2,1)}, u32[]{:S(2)}, u32[]{:S(2)}) collective-permute-start(bf16[256,4096]{1,0:T(8,128)(2,1)} %get-tuple-element.51.refs_0_), channel_id=1, source_target_pairs={{0,16},{16,0},{32,48},{48,32},{64,80},{80,64},{96,112},{112,96},{1... | collective-permute-start | bytes 6291464 | tf_op jit(solution)/shard_map/ppermute | solution.py:176
  75.6 9.3 %copy-start.22 = (s32[4,16,256]{2,1,0:T(8,128)S(1)}, s32[4,16,256]{2,1,0:T(8,128)}, u32[]{:S(2)}) copy-start(s32[4,16,256]{2,1,0:T(8,128)} %copy-done.21) | copy-start | bytes 196612
  75.6 9.3 %collective-permute-start.8 = (s32[4,16,256]{2,1,0:T(8,128)}, s32[4,16,256]{2,1,0:T(8,128)S(1)}, u32[]{:S(2)}, u32[]{:S(2)}) collective-permute-start(s32[4,16,256]{2,1,0:T(8,128)} %copy-done.21), channel_id=1, source_target_pairs={{0,12},{1,13},{2,14},{3,15},{4,8},{5,9},{6,10},{7,11},{8,4},{9,5},... | collective-permute-start | bytes 196616 | tf_op jit(solution)/shard_map/ppermute | solution.py:62
  87.0 25.6 %copy-start.42 = (s32[8,16,256]{2,1,0:T(8,128)}, s32[8,16,256]{2,1,0:T(8,128)S(1)}, u32[]{:S(2)}) copy-start(s32[8,16,256]{2,1,0:T(8,128)S(1)} %get-tuple-element.55.a_ref) | copy-start | bytes 393220
  87.0 20.5 %collective-permute-start.10 = (bf16[1024,768]{1,0:T(8,128)(2,1)S(1)}, bf16[1024,768]{1,0:T(8,128)(2,1)S(1)}, u32[]{:S(2)}, u32[]{:S(2)}) collective-permute-start(bf16[1024,768]{1,0:T(8,128)(2,1)S(1)} %get-tuple-element.49.b1), channel_id=1, source_target_pairs={{0,1},{1,0},{2,3},{3,2},{4,5},{5,4},{6,7},{7,6},{8,9},{9,8},{10,11... | collective-permute-start | bytes 4718600 | tf_op jit(solution)/shard_map/ppermute | solution.py:62
  87.7 2.9 %copy-start.31 = (bf16[256,4096]{1,0:T(8,128)(2,1)S(1)}, bf16[256,4096]{1,0:T(8,128)(2,1)}, u32[]{:S(2)}) copy-start(bf16[256,4096]{1,0:T(8,128)(2,1)} %get-tuple-element.51.refs_0_) | copy-start | bytes 6291460
  87.7 21.6 %collective-permute-start.9 = (bf16[1024,768]{1,0:T(8,128)(2,1)S(1)}, bf16[1024,768]{1,0:T(8,128)(2,1)S(1)}, u32[]{:S(2)}, u32[]{:S(2)}) collective-permute-start(bf16[1024,768]{1,0:T(8,128)(2,1)S(1)} %get-tuple-element.48.b0), channel_id=1, source_target_pairs={{0,3},{1,2},{2,1},{3,0},{4,7},{5,6},{6,5},{7,4},{8,11},{9,10},{10,... | collective-permute-start | bytes 4718600 | tf_op jit(solution)/shard_map/ppermute | solution.py:62
  90.5 18.8 %copy-start.34 = (bf16[768,1024]{1,0:T(8,128)(2,1)S(1)}, bf16[768,1024]{1,0:T(8,128)(2,1)}, u32[]{:S(2)}) copy-start(bf16[768,1024]{1,0:T(8,128)(2,1)} %w_hbm.1) | copy-start | bytes 4718596
  90.5 18.8 %copy-start.39 = (bf16[256,1024]{1,0:T(8,128)(2,1)S(1)}, bf16[256,1024]{1,0:T(8,128)(2,1)}, u32[]{:S(2)}) copy-start(bf16[256,1024]{1,0:T(8,128)(2,1)} %grad_hbm.1) | copy-start | bytes 1572868
  90.5 18.8 %copy-start.45 = (f32[256,1024]{1,0:T(8,128)S(1)}, f32[256,1024]{1,0:T(8,128)}, u32[]{:S(2)}) copy-start(f32[256,1024]{1,0:T(8,128)} %copy-done.44) | copy-start | bytes 3145732
  93.5 19.0 %copy-start.11 = (bf16[2,96,1024]{2,1,0:T(8,128)(2,1)}, bf16[2,96,1024]{2,1,0:T(8,128)(2,1)S(1)}, u32[]{:S(2)}) copy-start(bf16[2,96,1024]{2,1,0:T(8,128)(2,1)S(1)} %get-tuple-element.52.token_ref.refs_4_) | copy-start | bytes 1179652
  109.3 10.6 %copy-start.4 = (bf16[768,1024]{1,0:T(8,128)(2,1)S(1)}, bf16[768,1024]{1,0:T(8,128)(2,1)}, u32[]{:S(2)}) copy-start(bf16[768,1024]{1,0:T(8,128)(2,1)} %w_wr_hbm.1) | copy-start | bytes 4718596
  109.4 10.6 %copy-start.20 = (f32[512,128]{1,0:T(8,128)S(1)}, f32[512,128]{1,0:T(8,128)}, u32[]{:S(2)}) copy-start(f32[512,128]{1,0:T(8,128)} %copy-done.19) | copy-start | bytes 786436
  112.6 10.6 %collective-permute-start.15 = (bf16[256,1792]{1,0:T(8,128)(2,1)S(1)}, bf16[256,1792]{1,0:T(8,128)(2,1)S(1)}, u32[]{:S(2)}, u32[]{:S(2)}) collective-permute-start(bf16[256,1792]{1,0:T(8,128)(2,1)S(1)} %get-tuple-element.57.refs_2_.pack_ref), channel_id=1, source_target_pairs={{0,16},{16,0},{32,48},{48,32},{64,80},{80,64},{96,112},{112,96},{1... | collective-permute-start | bytes 2752520 | tf_op jit(solution)/shard_map/ppermute | solution.py:176
  112.7 10.0 %collective-permute-start.12 = (s32[8,16,256]{2,1,0:T(8,128)S(1)}, s32[8,16,256]{2,1,0:T(8,128)S(1)}, u32[]{:S(2)}, u32[]{:S(2)}) collective-permute-start(s32[8,16,256]{2,1,0:T(8,128)S(1)} %get-tuple-element.55.a_ref), channel_id=1, source_target_pairs={{0,3},{1,2},{2,1},{3,0},{4,7},{5,6},{6,5},{7,4},{8,11},{9,10},{10,... | collective-permute-start | bytes 393224 | tf_op jit(solution)/shard_map/ppermute | solution.py:62
  114.6 16.9 %collective-permute-start.16 = (bf16[2,96,1024]{2,1,0:T(8,128)(2,1)S(1)}, bf16[2,96,1024]{2,1,0:T(8,128)(2,1)S(1)}, u32[]{:S(2)}, u32[]{:S(2)}) collective-permute-start(bf16[2,96,1024]{2,1,0:T(8,128)(2,1)S(1)} %get-tuple-element.62), channel_id=1, source_target_pairs={{0,32},{16,48},{32,64},{48,80},{64,96},{80,112},{96,0},{112,16},{1... | collective-permute-start | bytes 1179656 | tf_op jit(solution)/shard_map/ppermute | solution.py:183
  115.7 19.3 %collective-permute-start.17 = (bf16[2,96,1024]{2,1,0:T(8,128)(2,1)S(1)}, bf16[2,96,1024]{2,1,0:T(8,128)(2,1)S(1)}, u32[]{:S(2)}, u32[]{:S(2)}) collective-permute-start(bf16[2,96,1024]{2,1,0:T(8,128)(2,1)S(1)} %get-tuple-element.63), channel_id=1, source_target_pairs={{0,64},{16,80},{32,96},{48,112},{64,0},{80,16},{96,32},{112,48},{1... | collective-permute-start | bytes 1179656 | tf_op jit(solution)/shard_map/ppermute | solution.py:183
  118.4 16.6 %collective-permute-start.18 = (bf16[2,96,1024]{2,1,0:T(8,128)(2,1)S(1)}, bf16[2,96,1024]{2,1,0:T(8,128)(2,1)S(1)}, u32[]{:S(2)}, u32[]{:S(2)}) collective-permute-start(bf16[2,96,1024]{2,1,0:T(8,128)(2,1)S(1)} %get-tuple-element.64), channel_id=1, source_target_pairs={{0,96},{16,112},{32,0},{48,16},{64,32},{80,48},{96,64},{112,80},{1... | collective-permute-start | bytes 1179656 | tf_op jit(solution)/shard_map/ppermute | solution.py:183
  119.9 5.9 %copy-start.28 = (s32[1,1024]{1,0:T(1,128)S(1)}, s32[1,1024]{1,0:T(1,128)}, u32[]{:S(2)}) copy-start(s32[1,1024]{1,0:T(1,128)} %copy-done.27) | copy-start | bytes 12292
  120.0 5.9 %copy-start.47 = (bf16[256,768]{1,0:T(8,128)(2,1)S(1)}, bf16[256,768]{1,0:T(8,128)(2,1)}, u32[]{:S(2)}) copy-start(bf16[256,768]{1,0:T(8,128)(2,1)} %copy-done.46) | copy-start | bytes 1179652
  122.6 8.8 %collective-permute-start.13 = (bf16[128,768]{1,0:T(8,128)(2,1)S(1)}, bf16[128,768]{1,0:T(8,128)(2,1)S(1)}, u32[]{:S(2)}, u32[]{:S(2)}) collective-permute-start(bf16[128,768]{1,0:T(8,128)(2,1)S(1)} %get-tuple-element.80.refs_0_), channel_id=1, source_target_pairs={{0,4},{1,5},{2,6},{3,7},{4,0},{5,1},{6,2},{7,3},{8,12},{9,13},{10,... | collective-permute-start | bytes 589832 | tf_op jit(solution)/shard_map/ppermute | solution.py:62
  123.2 8.2 %collective-permute-start.14 = (bf16[128,768]{1,0:T(8,128)(2,1)S(1)}, bf16[128,768]{1,0:T(8,128)(2,1)S(1)}, u32[]{:S(2)}, u32[]{:S(2)}) collective-permute-start(bf16[128,768]{1,0:T(8,128)(2,1)S(1)} %get-tuple-element.79.refs_2_), channel_id=1, source_target_pairs={{0,12},{1,13},{2,14},{3,15},{4,8},{5,9},{6,10},{7,11},{8,4},{9,5},... | collective-permute-start | bytes 589832 | tf_op jit(solution)/shard_map/ppermute | solution.py:62
  131.4 3.6 %copy-start.35 = (bf16[3,96,1024]{2,1,0:T(8,128)(2,1)}, bf16[3,96,1024]{2,1,0:T(8,128)(2,1)S(1)}, u32[]{:S(2)}) copy-start(bf16[3,96,1024]{2,1,0:T(8,128)(2,1)S(1)} %get-tuple-element.71) | copy-start | bytes 1769476
  131.4 3.6 %copy-start.36 = (bf16[3,96,1024]{2,1,0:T(8,128)(2,1)}, bf16[3,96,1024]{2,1,0:T(8,128)(2,1)S(1)}, u32[]{:S(2)}) copy-start(bf16[3,96,1024]{2,1,0:T(8,128)(2,1)S(1)} %get-tuple-element.70) | copy-start | bytes 1769476
  131.4 3.6 %copy-start.37 = (bf16[3,96,1024]{2,1,0:T(8,128)(2,1)}, bf16[3,96,1024]{2,1,0:T(8,128)(2,1)S(1)}, u32[]{:S(2)}) copy-start(bf16[3,96,1024]{2,1,0:T(8,128)(2,1)S(1)} %get-tuple-element.69) | copy-start | bytes 1769476
  135.1 7.9 %collective-permute-start.19 = (bf16[256,768]{1,0:T(8,128)(2,1)S(1)}, bf16[256,768]{1,0:T(8,128)(2,1)S(1)}, u32[]{:S(2)}, u32[]{:S(2)}) collective-permute-start(bf16[256,768]{1,0:T(8,128)(2,1)S(1)} %get-tuple-element.65.refs_0_), channel_id=1, source_target_pairs={{0,1},{1,0},{2,3},{3,2},{4,5},{5,4},{6,7},{7,6},{8,9},{9,8},{10,11... | collective-permute-start | bytes 1179656 | tf_op jit(solution)/shard_map/ppermute | solution.py:62
  135.6 9.0 %collective-permute-start.20 = (bf16[256,768]{1,0:T(8,128)(2,1)S(1)}, bf16[256,768]{1,0:T(8,128)(2,1)S(1)}, u32[]{:S(2)}, u32[]{:S(2)}) collective-permute-start(bf16[256,768]{1,0:T(8,128)(2,1)S(1)} %get-tuple-element.66.refs_2_), channel_id=1, source_target_pairs={{0,3},{1,2},{2,1},{3,0},{4,7},{5,6},{6,5},{7,4},{8,11},{9,10},{10,... | collective-permute-start | bytes 1179656 | tf_op jit(solution)/shard_map/ppermute | solution.py:62
  145.8 54.6 %collective-permute-start.21 = (bf16[512,768]{1,0:T(8,128)(2,1)}, bf16[512,768]{1,0:T(8,128)(2,1)}, u32[]{:S(2)}, u32[]{:S(2)}) collective-permute-start(bf16[512,768]{1,0:T(8,128)(2,1)} %get-tuple-element.67.token_ref.refs_0_), channel_id=1, source_target_pairs={{0,12},{1,13},{2,14},{3,15},{4,8},{5,9},{6,10},{7,11},{8,4},{9,5},... | collective-permute-start | bytes 2359304 | tf_op jit(solution)/shard_map/ppermute | solution.py:62
  148.1 52.3 %collective-permute-start.22 = (bf16[512,768]{1,0:T(8,128)(2,1)}, bf16[512,768]{1,0:T(8,128)(2,1)}, u32[]{:S(2)}, u32[]{:S(2)}) collective-permute-start(bf16[512,768]{1,0:T(8,128)(2,1)} %get-tuple-element.68.refs_2_), channel_id=1, source_target_pairs={{0,4},{1,5},{2,6},{3,7},{4,0},{5,1},{6,2},{7,3},{8,12},{9,13},{10,... | collective-permute-start | bytes 2359304 | tf_op jit(solution)/shard_map/ppermute | solution.py:62
  149.0 60.4 %all-to-all-start.1 = ((bf16[128,8,768]{2,1,0:T(8,128)(2,1)}), bf16[128,8,768]{2,1,0:T(8,128)(2,1)S(1)}, u32[]{:S(2)}, u32[]{:S(2)}) async-start(bf16[128,8,768]{2,1,0:T(8,128)(2,1)} %bitcast.10), calls=%async_computation.1 | async-start | bytes 3145728 | tf_op jit(solution)/shard_map/all_to_all | solution.py:153
  155.5 32.3 %collective-permute-start.23 = (bf16[3,96,1024]{2,1,0:T(8,128)(2,1)}, bf16[3,96,1024]{2,1,0:T(8,128)(2,1)S(1)}, u32[]{:S(2)}, u32[]{:S(2)}) collective-permute-start(bf16[3,96,1024]{2,1,0:T(8,128)(2,1)} %copy-done.37), channel_id=1, source_target_pairs={{0,32},{16,48},{32,64},{48,80},{64,96},{80,112},{96,0},{112,16},{1... | collective-permute-start | bytes 1769480 | tf_op jit(solution)/shard_map/ppermute | solution.py:183
  156.5 43.9 %collective-permute-start.24 = (bf16[3,96,1024]{2,1,0:T(8,128)(2,1)}, bf16[3,96,1024]{2,1,0:T(8,128)(2,1)S(1)}, u32[]{:S(2)}, u32[]{:S(2)}) collective-permute-start(bf16[3,96,1024]{2,1,0:T(8,128)(2,1)} %copy-done.36), channel_id=1, source_target_pairs={{0,64},{16,80},{32,96},{48,112},{64,0},{80,16},{96,32},{112,48},{1... | collective-permute-start | bytes 1769480 | tf_op jit(solution)/shard_map/ppermute | solution.py:183
  159.2 41.2 %collective-permute-start.25 = (bf16[3,96,1024]{2,1,0:T(8,128)(2,1)}, bf16[3,96,1024]{2,1,0:T(8,128)(2,1)S(1)}, u32[]{:S(2)}, u32[]{:S(2)}) collective-permute-start(bf16[3,96,1024]{2,1,0:T(8,128)(2,1)} %copy-done.35), channel_id=1, source_target_pairs={{0,96},{16,112},{32,0},{48,16},{64,32},{80,48},{96,64},{112,80},{1... | collective-permute-start | bytes 1769480 | tf_op jit(solution)/shard_map/ppermute | solution.py:183
  165.6 38.6 %copy-start = (bf16[256,4096]{1,0:T(8,128)(2,1)}, bf16[256,4096]{1,0:T(8,128)(2,1)S(1)}, u32[]{:S(2)}) copy-start(bf16[256,4096]{1,0:T(8,128)(2,1)S(1)} %cited_by_table.1.refs_4_.table_ref) | copy-start | bytes 6291460
  165.6 42.0 %copy-start.12 = (bf16[2,96,1024]{2,1,0:T(8,128)(2,1)S(1)}, bf16[2,96,1024]{2,1,0:T(8,128)(2,1)}, u32[]{:S(2)}) copy-start(bf16[2,96,1024]{2,1,0:T(8,128)(2,1)} %copy-done.11) | copy-start | bytes 1179652
  204.1 27.8 %collective-permute-start.26 = (bf16[1024,768]{1,0:T(8,128)(2,1)}, bf16[1024,768]{1,0:T(8,128)(2,1)}, u32[]{:S(2)}, u32[]{:S(2)}) collective-permute-start(bf16[1024,768]{1,0:T(8,128)(2,1)} %get-tuple-element.72.b0), channel_id=1, source_target_pairs={{0,3},{1,2},{2,1},{3,0},{4,7},{5,6},{6,5},{7,4},{8,11},{9,10},{10,... | collective-permute-start | bytes 4718600 | tf_op jit(solution)/shard_map/ppermute | solution.py:62
  207.6 30.6 %collective-permute-start.27 = (bf16[1024,768]{1,0:T(8,128)(2,1)}, bf16[1024,768]{1,0:T(8,128)(2,1)}, u32[]{:S(2)}, u32[]{:S(2)}) collective-permute-start(bf16[1024,768]{1,0:T(8,128)(2,1)} %get-tuple-element.73.b1), channel_id=1, source_target_pairs={{0,1},{1,0},{2,3},{3,2},{4,5},{5,4},{6,7},{7,6},{8,9},{9,8},{10,11... | collective-permute-start | bytes 4718600 | tf_op jit(solution)/shard_map/ppermute | solution.py:62
  209.4 6.0 %copy-start.8 = (f32[256,768]{1,0:T(8,128)S(1)}, f32[256,768]{1,0:T(8,128)}, u32[]{:S(2)}) copy-start(f32[256,768]{1,0:T(8,128)} %copy-done.7) | copy-start | bytes 2359300
  209.4 32.4 %all-to-all-start.2 = ((bf16[16,64,512]{2,1,0:T(8,128)(2,1)}), bf16[16,64,512]{2,1,0:T(8,128)(2,1)S(1)}, u32[]{:S(2)}, u32[]{:S(2)}) async-start(bf16[16,64,512]{2,1,0:T(8,128)(2,1)} %y_sum.1), calls=%async_computation.2 | async-start | bytes 2097152 | tf_op jit(solution)/shard_map/all_to_all | solution.py:488
  215.3 1.2 copy-start.6
  216.6 1.1 copy-start.10
  217.7 1.7 copy-start.1
  (17 other events, 14.3 us)

commit v5 on v4

--- a/solution.py
+++ b/solution.py
@@ -110,7 +110,7 @@
         out_specs=IN_VMEM,
         scratch_shapes=[pltpu.VMEM((256, 2048), I16)],
         compiler_params=params(16),
-        cost_estimate=pl.CostEstimate(flops=10**9, bytes_accessed=3 * 10**6, transcendentals=0),
+        cost_estimate=pl.CostEstimate(flops=1, bytes_accessed=1, transcendentals=0),
         name="cite_table",
     )(place, nbr, token)
 
@@ -135,7 +135,7 @@
         in_specs=[IN_SMEM, IN_VMEM, IN_VMEM, ANYWHERE],
         out_specs=IN_VMEM,
         compiler_params=params(16),
-        cost_estimate=pl.CostEstimate(flops=10**9, bytes_accessed=3 * 10**6, transcendentals=0),
+        cost_estimate=pl.CostEstimate(flops=1, bytes_accessed=1, transcendentals=0),
         name="cited_by_table",
     )(place, a, b, token)
 
@@ -167,7 +167,7 @@
         in_specs=[IN_VMEM] * 3 + [ANYWHERE],
         out_specs=IN_VMEM,
         compiler_params=params(16),
-        cost_estimate=pl.CostEstimate(flops=10**9, bytes_accessed=3 * 10**6, transcendentals=0),
+        cost_estimate=pl.CostEstimate(flops=1, bytes_accessed=1, transcendentals=0),
         name="pick_rows",
     )(pick, authors, papers, token)
 
@@ -192,8 +192,8 @@
 def author_kernel(
     arrived_ref, into_paper_ref, into_author_ref, *refs
 ):
-    sources, outs, held, sems = refs[:7], refs[7:14], refs[14:21], refs[21]
-    out_ref, pack_ref, dz_ref, dx_ref, pre_ref, adder_ref, cnt_ref = outs
+    sources, outs, held, sems = refs[:7], refs[8:17], refs[17:24], refs[24]
+    out_ref, authored_ref, written_ref, dpre_ref, dz_ref, dx_ref, pre_ref, adder_ref, cnt_ref = outs
     x_author_ref, x_paper_ref, grad_ref, w_sa, w_wn, w_sp, w_wr = held
     copies = [pltpu.make_async_copy(a, b, sems.at[i]) for i, (a, b) in enumerate(zip(sources, held))]
     for i in (0, 3, 4, 2, 1, 5, 6):
@@ -218,11 +218,9 @@
     copies[1].wait()
     x_paper = x_paper_ref[...]
     dpre = (grad_ref[...].astype(F32) * slope).astype(BF)
-    pack_ref[:, pl.ds(0, 768)] = x_author
-    pack_ref[:, pl.ds(768, 768)] = authored
-    pack_ref[:, pl.ds(1536, 768)] = x_paper
-    pack_ref[:, pl.ds(2304, 768)] = written
-    pack_ref[:, pl.ds(3072, 1024)] = dpre
+    authored_ref[...] = authored
+    written_ref[...] = written
+    dpre_ref[...] = dpre
     dz_ref[...] = (dot(dpre, w_wn[...], ((1,), (1,))) / cnt_ref[pl.ds(256, 256), pl.ds(0, 1)]).astype(BF)
     dx_ref[...] = dot(dpre, w_sa[...], ((1,), (1,)))
     copies[5].wait()
@@ -230,22 +228,23 @@
     pre_ref[...] = dot(x_paper, w_sp[...]) + dot(written, w_wr[...])
 
 
-def author_step(arrived, into_paper, into_author, x_author, x_paper, grad, w_sa, w_wn, w_sp, w_wr):
+def author_step(arrived, into_paper, into_author, x_author, x_paper, grad, w_sa, w_wn, w_sp, w_wr, token):
     weight = pltpu.VMEM((768, 1024), BF)
     return pl.pallas_call(
         author_kernel,
         out_shape=[
-            shape((256, 1024), BF), shape((256, 4096), BF), shape((256, 768), BF), shape((256, 768), F32),
+            shape((256, 1024), BF), shape((256, 768), BF), shape((256, 768), BF), shape((256, 1024), BF),
+            shape((256, 768), BF), shape((256, 768), F32),
             shape((256, 1024), F32), shape((512, 1024), BF), shape((512, 128), F32),
         ],
-        in_specs=[IN_VMEM] * 3 + [IN_HBM] * 7,
-        out_specs=[IN_VMEM] * 7,
+        in_specs=[IN_VMEM] * 3 + [IN_HBM] * 7 + [ANYWHERE],
+        out_specs=[IN_VMEM] * 9,
         scratch_shapes=[pltpu.VMEM((256, 768), BF)] * 2 + [pltpu.VMEM((256, 1024), BF)] + [weight] * 4
         + [pltpu.SemaphoreType.DMA((7,))],
-        compiler_params=params(40),
-        cost_estimate=pl.CostEstimate(flops=4 * 10**9, bytes_accessed=15 * 10**6, transcendentals=0),
+        compiler_params=params(58),
+        cost_estimate=pl.CostEstimate(flops=1, bytes_accessed=1, transcendentals=0),
         name="author_step",
-    )(arrived, into_paper, into_author, x_author, x_paper, grad, w_sa, w_wn, w_sp, w_wr)
+    )(arrived, into_paper, into_author, x_author, x_paper, grad, w_sa, w_wn, w_sp, w_wr, token)
 
 
 def first_kernel(table_ref, b0, b1, out_ref):
@@ -260,7 +259,7 @@
         in_specs=[IN_VMEM] * 3,
         out_specs=IN_VMEM,
         compiler_params=params(24),
-        cost_estimate=pl.CostEstimate(flops=2 * 10**9, bytes_accessed=5 * 10**6, transcendentals=0),
+        cost_estimate=pl.CostEstimate(flops=1, bytes_accessed=1, transcendentals=0),
         name="first_half",
     )(table, *blocks)
 
@@ -277,7 +276,7 @@
         in_specs=[IN_VMEM] * 5,
         out_specs=IN_VMEM,
         compiler_params=params(24),
-        cost_estimate=pl.CostEstimate(flops=2 * 10**9, bytes_accessed=5 * 10**6, transcendentals=0),
+        cost_estimate=pl.CostEstimate(flops=1, bytes_accessed=1, transcendentals=0),
         name="last_half",
     )(table, *blocks, first, own)
 
@@ -295,13 +294,13 @@
         in_specs=[IN_VMEM] * 4,
         out_specs=[IN_VMEM] * 2,
         compiler_params=params(16),
-        cost_estimate=pl.CostEstimate(flops=10**9, bytes_accessed=5 * 10**6, transcendentals=0),
+        cost_estimate=pl.CostEstimate(flops=1, bytes_accessed=1, transcendentals=0),
         name="edge_add",
     )(adder, back, author, paper)
 
 
 def paper_kernel(
-    table_ref, b0, b1, first_ref, nbr_ref, pre_ref, grad_hbm, w_hbm, token_ref,
+    table_ref, b0, b1, first_ref, nbr_ref, pre_ref, grad_hbm, w_hbm, token_a, token_b, token_c,
     out_ref, pack_ref, dz_ref, grad_ref, w_ref, sems,
 ):
     copies = [pltpu.make_async_copy(w_hbm, w_ref, sems.at[0]), pltpu.make_async_copy(grad_hbm, grad_ref, sems.at[1])]
@@ -323,17 +322,17 @@
     dz_ref[...] = (dot(dpre, w_ref[...], ((1,), (1,))) / cnt).astype(BF)
 
 
-def paper_step(table, blocks, first, nbr, pre, grad, w_cite, token):
+def paper_step(table, blocks, first, nbr, pre, grad, w_cite, *tokens):
     return pl.pallas_call(
         paper_kernel,
         out_shape=[shape((256, 1024), BF), shape((256, 1792), BF), shape((256, 768), BF)],
-        in_specs=[IN_VMEM] * 6 + [IN_HBM] * 2 + [ANYWHERE],
+        in_specs=[IN_VMEM] * 6 + [IN_HBM] * 2 + [ANYWHERE] * 3,
         out_specs=[IN_VMEM] * 3,
         scratch_shapes=[pltpu.VMEM((256, 1024), BF), pltpu.VMEM((768, 1024), BF), pltpu.SemaphoreType.DMA((2,))],
         compiler_params=params(32),
-        cost_estimate=pl.CostEstimate(flops=3 * 10**9, bytes_accessed=10 * 10**6, transcendentals=0),
+        cost_estimate=pl.CostEstimate(flops=1, bytes_accessed=1, transcendentals=0),
         name="paper_step",
-    )(table, *blocks, first, nbr, pre, grad, w_cite, token)
+    )(table, *blocks, first, nbr, pre, grad, w_cite, *tokens)
 
 
 def edge_back_kernel(pack_ref, cnt_ref, w_wr_hbm, w_sp_hbm, dz_ref, dx_ref, w_wr, w_sp, sems):
@@ -347,7 +346,7 @@
     dx_ref[...] = dot(dpre, w_sp[...], ((1,), (1,)))
 
 
-def edge_back(pack, cnt, w_write, w_self):
+def edge_back(dpre, cnt, w_write, w_self):
     return pl.pallas_call(
         edge_back_kernel,
         out_shape=[shape((256, 768), BF), shape((256, 768), F32)],
@@ -355,87 +354,130 @@
         out_specs=[IN_VMEM] * 2,
         scratch_shapes=[pltpu.VMEM((768, 1024), BF)] * 2 + [pltpu.SemaphoreType.DMA((2,))],
         compiler_params=params(16),
-        cost_estimate=pl.CostEstimate(flops=10**9, bytes_accessed=5 * 10**6, transcendentals=0),
+        cost_estimate=pl.CostEstimate(flops=1, bytes_accessed=1, transcendentals=0),
         name="edge_back",
-    )(pack, cnt, w_write, w_self)
-
-
-def weight_kernel(lefts, right, place_ref, *refs):
-    ins, outs, turned = refs[:-5], refs[-5:-1], refs[-1]
+    )(dpre, cnt, w_write, w_self)
+
+
+def weight_kernel(n, cuts, place_ref, *refs):
+    outs, turned = refs[-4 * cuts - 1 : -1] if cuts else refs[-2:-1], refs[-1]
     core, y = place_ref[1], place_ref[2]
-    own, other, lane = right
-    dpre = jnp.concatenate([ins[own][:, pl.ds(lane, 1024)], ins[other][:, pl.ds(lane, 1024)]], axis=0)
-    for i, (own, other, lane) in enumerate(lefts):
-        for k, ref in enumerate((ins[own], ins[other])):
-            turned[i, :, pl.ds(256 * k, 256)] = ref[:, pl.ds(lane, 768)].T
+    dpre = jnp.concatenate([ref[:, pl.ds(ref.shape[1] - 1024, 1024)] for ref in refs[:2]], axis=0)
+    wide = 1024 // max(cuts, 1)
+    for i in range(n):
+        for k in range(2):
+            turned[i, :, pl.ds(256 * k, 256)] = refs[2 + 2 * i + k][:, pl.ds(0, 768)].T
         rows = []
         for d in range(4):
-            start = pl.multiple_of((2 * ((y + d) & 3) + core) * 96, 32)
+            ahead = ((y + d) & 3) if cuts else d
+            start = pl.multiple_of((2 * ahead + core) * 96, 32)
             rows.append(turned[i, pl.ds(start, 96), :])
         product = dot(jnp.concatenate(rows, axis=0), dpre).astype(BF)
-        for d in range(4):
-            outs[d][i] = product[96 * d : 96 * d + 96]
-
-
-def weight_parts(place, arrays, lefts, right):
+        if not cuts:
+            for d in range(4):
+                outs[0][d, i] = product[96 * d : 96 * d + 96]
+        for j in range(cuts):
+            for d in range(4):
+                outs[4 * j + d][i] = product[96 * d : 96 * d + 96, wide * j : wide * j + wide]
+
+
+def weight_parts(place, dpre, lefts, token, cuts):
     n = len(lefts)
-    return pl.pallas_call(
-        functools.partial(weight_kernel, lefts, right),
-        out_shape=[shape((n, 96, 1024), BF)] * 4,
-        in_specs=[IN_SMEM] + [IN_VMEM] * len(arrays),
+    outs = pl.pallas_call(
+        functools.partial(weight_kernel, n, cuts),
+        out_shape=[shape((n, 96, 1024 // cuts), BF)] * (4 * cuts) if cuts else [shape((4, n, 96, 1024), BF)],
+        in_specs=[IN_SMEM] + [IN_VMEM] * (2 + 2 * n) + [ANYWHERE],
+        out_specs=[IN_VMEM] * max(4 * cuts, 1),
+        scratch_shapes=[pltpu.VMEM((n, 768, 512), BF)],
+        compiler_params=params(24),
+        cost_estimate=pl.CostEstimate(flops=1, bytes_accessed=1, transcendentals=0),
+        name="weight_parts",
+    )(place, *dpre, *[v for pair in lefts for v in pair], token)
+    return [outs[4 * j : 4 * j + 4] for j in range(cuts)] if cuts else outs
+
+
+def y_sum_kernel(place_ref, *refs):
+    left, right, authors, outs, stack = refs[:4], refs[4:8], refs[8], refs[9:13], refs[13]
+    for group, first, rows, lane, wide in ((left, 0, 3, 0, 512), (right, 0, 3, 512, 512), (authors, 3, 2, 0, 1024)):
+        for i in range(rows):
+            part = (lambda y: group[y, i]) if first else (lambda y: group[y][i])
+            total = part(0).astype(F32)
+            for y in range(1, 4):
+                total = total + part(y).astype(F32)
+            stack[pl.ds(96 * (first + i), 96), pl.ds(lane, wide)] = total
+    stack[pl.ds(480, 32), :] = jnp.zeros((32, 1024), F32)
+    x = place_ref[0] >> 2
+    for d in range(4):
+        start = pl.multiple_of(((x + d) & 3) * 256, 256)
+        outs[d][...] = stack[:, pl.ds(start, 256)].T.astype(BF)
+
+
+def y_sum(place, left, right, author):
+    return pl.pallas_call(
+        y_sum_kernel,
+        out_shape=[shape((256, 512), BF)] * 4,
+        in_specs=[IN_SMEM] + [IN_VMEM] * 9,
         out_specs=[IN_VMEM] * 4,
-        scratch_shapes=[pltpu.VMEM((n, 768, 512), BF)],
-        compiler_params=params(32),
-        cost_estimate=pl.CostEstimate(flops=2 * 10**9, bytes_accessed=8 * 10**6, transcendentals=0),
-        name="weight_parts",
-    )(place, *arrays)
-
-
-def y_sum_kernel(*refs):
-    papers, authors, out_ref, stack = refs[:4], refs[4:8], refs[8], refs[9]
-    for m in range(5):
-        group, i = (papers, m) if m < 3 else (authors, m - 3)
-        total = group[0][i].astype(F32)
-        for y in range(1, 4):
-            total = total + group[y][i].astype(F32)
-        stack[pl.ds(96 * m, 96), :] = total
-    stack[pl.ds(480, 32), :] = jnp.zeros((32, 1024), F32)
-    for j in range(0, 16, 2):
-        turned = stack[:, pl.ds(64 * j, 128)].T.astype(BF)
-        out_ref[j] = turned[:64]
-        out_ref[j + 1] = turned[64:]
-
-
-def y_sum(paper, author):
-    return pl.pallas_call(
-        y_sum_kernel,
-        out_shape=shape((16, 64, 512), BF),
-        in_specs=[IN_VMEM] * 8,
-        out_specs=IN_VMEM,
         scratch_shapes=[pltpu.VMEM((512, 1024), F32)],
         compiler_params=params(20),
+        cost_estimate=pl.CostEstimate(flops=1, bytes_accessed=1, transcendentals=0),
         name="y_sum",
-    )(*paper, *author)
-
-
-def last_sum_kernel(got_ref, token_ref, out_ref):
-    total = got_ref[0].astype(F32)
-    for j in range(1, 16):
-        total = total + got_ref[j].astype(F32)
+    )(place, *left, *right, author)
+
+
+def x_sum_kernel(place_ref, token_a, token_b, *refs):
+    total = refs[0][...].astype(F32)
+    for ref in refs[1:4]:
+        total = total + ref[...].astype(F32)
+    refs[8][...] = total
+    z = place_ref[0] & 3
+    for d in range(4):
+        refs[4 + d][...] = refs[8][pl.ds(pl.multiple_of(((z + d) & 3) * 64, 64), 64), :]
+
+
+def x_sum(place, got, *tokens):
+    return pl.pallas_call(
+        x_sum_kernel,
+        out_shape=[shape((64, 512), F32)] * 4,
+        in_specs=[IN_SMEM, ANYWHERE, ANYWHERE] + [IN_VMEM] * 4,
+        out_specs=[IN_VMEM] * 4,
+        scratch_shapes=[pltpu.VMEM((256, 512), F32)],
+        compiler_params=params(8),
+        cost_estimate=pl.CostEstimate(flops=1, bytes_accessed=1, transcendentals=0),
+        name="x_sum",
+    )(place, *tokens, *got)
+
+
+def over_col(parts, step):
+    got = [parts[0]]
+    for d in range(1, 4):
+        perm = []
+        for c in range(16):
+            x, z = c >> 2, c & 3
+            perm.append((c, ((x + d) % 4) * 4 + z if step == 4 else x * 4 + (z + d) % 4))
+        got.append(lax.ppermute(parts[d], "col", perm))
+    return got
+
+
+def last_sum_kernel(*refs):
+    total = refs[0][...]
+    for ref in refs[1:4]:
+        total = total + ref[...]
     total = total * (32768.0 ** -0.5)
     for m in range(5):
-        out_ref[m] = total[:, 96 * m : 96 * m + 96]
-
-
-def last_sum(got, token):
+        refs[-1][m] = total[:, 96 * m : 96 * m + 96]
+
+
+def last_sum(got):
     return pl.pallas_call(
         last_sum_kernel,
         out_shape=shape((5, 64, 96), F32),
-        in_specs=[IN_VMEM, ANYWHERE],
+        in_specs=[IN_VMEM] * 4,
         out_specs=IN_VMEM,
         compiler_params=params(8),
+        cost_estimate=pl.CostEstimate(flops=1, bytes_accessed=1, transcendentals=0),
         name="last_sum",
-    )(got, token)
+    )(*got)
 
 
 def per_device(
@@ -445,51 +487,67 @@
     row = lax.axis_index("row")
     place = jnp.stack([lax.axis_index("col"), row & 1, row >> 1]).astype(I32)
 
-    parts = [x_paper[:128], x_paper[128:], cite_nbr.T.reshape(1, 16, 256)]
-    parts = join(travel(parts, 0))
+    lists = [cite_nbr.T.reshape(1, 16, 256)]
+    pairs = travel([x_paper[:128], x_paper[128:]], 0)
+    lists = travel(lists, 0)
 
     pick, into_paper, into_author = edge_lists(write_src[0], write_dst[0])
-    arrived = exchange(pick_rows(pick, x_author, x_paper, parts[0]))
-    parts = join(travel(parts, 1))
-
+    arrived = exchange(pick_rows(pick, x_author, x_paper, lists[0][1]))
+    parts = join(pairs)
+    pairs = travel(parts, 1)
+    lists = travel(join(lists), 1)
+    x_author_pair = (x_author, other_core(x_author))
+    x_paper_pair = (x_paper, other_core(x_paper))
+
+    parts = join(pairs, (lists[0][1],))
     table = cite_table(place, cite_nbr, parts[0])
     parts = join(travel(parts, 2), (table,))
     pairs = travel(parts, 3)
-    cite_first = first_half(table, [pair[0] for pair in pairs[:2]])
-
-    out_author, pack_a, dz_written, dx_author_own, pre_paper, adder, cnt = author_step(
+    lists = travel(join(lists), 2)
+    cite_first = first_half(table, [pair[0] for pair in pairs])
+
+    out_author, authored, written, dpre_author, dz_written, dx_author_own, pre_paper, adder, cnt = author_step(
         arrived, into_paper, into_author, x_author, x_paper, grad_author,
-        w_self_author, w_written, w_self_paper, w_write,
+        w_self_author, w_written, w_self_paper, w_write, parts[0],
     )
-    pack_a_other = other_core(pack_a)
-    parts_author = weight_parts(place, [pack_a, pack_a_other], [(0, 1, 0), (0, 1, 768)], (0, 1, 3072))
-    got_author = over_y(parts_author)
-
-    out_paper, pack_p, dz_cite = paper_step(
-        table, [pair[1] for pair in pairs[:2]], cite_first, cite_nbr, pre_paper, grad_paper, w_cite, parts_author[0]
+    (parts_author,) = weight_parts(
+        place, (dpre_author, other_core(dpre_author)),
+        [x_author_pair, (authored, other_core(authored))], table, 0,
     )
-    pack_p_other = other_core(pack_p)
+    got_author = lax.all_to_all(
+        parts_author, "row", split_axis=0, concat_axis=0, tiled=True,
+        axis_index_groups=[[0, 2, 4, 6], [1, 3, 5, 7]],
+    )
+    written_pair = (written, other_core(written))
+
+    out_paper, pack, dz_cite = paper_step(
+        table, [pair[1] for pair in pairs], cite_first, cite_nbr, pre_paper, grad_paper, w_cite,
+        parts_author, lists[0][1], authored,
+    )
     back_pairs = travel([dz_cite[:128], dz_cite[128:]], 0)
-    dz_write, dx_paper_own = edge_back(pack_p, cnt, w_write, w_self_paper)
-    parts_paper = weight_parts(
-        place, [pack_a, pack_a_other, pack_p, pack_p_other],
-        [(0, 1, 1536), (2, 3, 0), (0, 1, 2304)], (2, 3, 768),
+    dz_write, dx_paper_own = edge_back(pack, cnt, w_write, w_self_paper)
+    pack_other = other_core(pack)
+    left, right = weight_parts(
+        place, (pack, pack_other), [x_paper_pair, (pack, pack_other), written_pair], dz_write, 2,
     )
-    rows = pick_rows(pick, dz_written, dz_write, dz_cite)
-    parts = join(back_pairs, (parts_paper[0], rows, pairs[2][1], *got_author[1:]))
-    got_paper = over_y(parts_paper)
+    lists = travel(join(lists), 3)[0]
+    parts = join(back_pairs, (left[0], lists[1], got_author))
+    pairs = travel(parts, 1)
+    left = over_y(left)
+    rows = pick_rows(pick, dz_written, dz_write, parts[0])
     back = exchange(rows)
-    parts = join(travel(parts, 1))
-    back_table = cited_by_table(place, pairs[2][0], pairs[2][1], parts[0])
-    parts = join(travel(parts, 2), (back_table, *got_paper[1:]))
+    parts = join(pairs, left[1:])
+    right = over_y(right)
+    back_table = cited_by_table(place, lists[0], lists[1], parts[0])
+    parts = join(travel(parts, 2), (back_table, *right[1:]))
+    dx_author, dx_paper_own = edge_add(adder, back, dx_author_own, dx_paper_own)
     back_pairs = travel(parts, 3)
     back_first = first_half(back_table, [pair[0] for pair in back_pairs])
 
-    got = lax.all_to_all(y_sum(got_paper, got_author), "col", split_axis=0, concat_axis=0, tiled=True)
-
-    dx_author, dx_paper_own = edge_add(adder, back, dx_author_own, dx_paper_own)
+    got = over_col(y_sum(place, left, right, got_author), 4)
+    got = over_col(x_sum(place, got, back_first, dx_author), 1)
     dx_paper = last_half(back_table, [pair[1] for pair in back_pairs], back_first, dx_paper_own)
-    dweights = last_sum(got, dx_paper).transpose(0, 2, 1)
+    dweights = last_sum(got).transpose(0, 2, 1)
     return (out_paper, out_author, dx_paper, dx_author, dweights)
 
 

time: 245 us -> 204 us (0.83)
  the two profiles are of different devices: /device:TPU:0 before, /device:TPU:1 now
where the time goes in v5:
time: 204 us; the launch traced here: 203 us
  starting transfers between devices  68.6 us (34%)
  Pallas kernels  64.2 us (31%)
  waiting for transfers between devices  53.9 us (26%)
  local copies, waits for them, and re-layouts  14.9 us (7%)
    ppermute x20, starting transfers between devices, travel(): pairs.append((part, lax.ppermute(part, ('row', 'col'), perm)))  22.9 us
    all_to_all x2, starting transfers between devices, exchange(): lax.all_to_all(sent, ('row', 'col'), split_axis=0, concat_axis=0, tiled=T...  20.4 us
    ppermute x6, waiting for transfers between devices, over_col(): got.append(lax.ppermute(parts[d], 'col', perm))  19.8 us
    unnamed x81, local copies, waits for them, and re-layouts  12.1 us
    ppermute x20, waiting for transfers between devices, travel(): pairs.append((part, lax.ppermute(part, ('row', 'col'), perm)))  11.3 us
    ppermute x6, waiting for transfers between devices, over_y(): got.append(lax.ppermute(parts[d], 'row', perm))  10 us
    ppermute x6, starting transfers between devices, over_y(): got.append(lax.ppermute(parts[d], 'row', perm))  9.56 us
    pallas_call x9, Pallas kernels, join(): pl.pallas_call(functools.partial(join_kernel, n), out_shape=outs, in_spec...  9.53 us
  transfers between devices with their start and end apart: 41, of which 17 were waited for; matrix products, arithmetic and copies ran while one was open for 1% of the time, Pallas kernels for 29%

profile of v5, /device:TPU:1, one launch (start us, length us, event | category | flops | bytes accessed | tf_op | source)
XLA Modules:
  0.0 202.9 jit_solution(15852428850071390323)
XLA Ops:
  0.7 1.1 fusion.1
  1.8 2.5 %collective-permute-start = (bf16[128,768]{1,0:T(8,128)(2,1)S(1)}, bf16[128,768]{1,0:T(8,128)(2,1)S(1)}, u32[]{:S(2)}, u32[]{:S(2)}) collective-permute-start(bf16[128,768]{1,0:T(8,128)(2,1)S(1)} %get-tuple-element.96.refs_0_), channel_id=1, source_target_pairs={{0,4},{1,5},{2,6},{3,7},{4,0},{5,1},{6,2},{7,3},{8,12},{9,13},{10,... | collective-permute-start | bytes 589832 | tf_op jit(solution)/shard_map/ppermute | solution.py:62
  4.4 2.2 %collective-permute-start.1 = (bf16[128,768]{1,0:T(8,128)(2,1)S(1)}, bf16[128,768]{1,0:T(8,128)(2,1)S(1)}, u32[]{:S(2)}, u32[]{:S(2)}) collective-permute-start(bf16[128,768]{1,0:T(8,128)(2,1)S(1)} %get-tuple-element.95.refs_2_), channel_id=1, source_target_pairs={{0,12},{1,13},{2,14},{3,15},{4,8},{5,9},{6,10},{7,11},{8,4},{9,5},... | collective-permute-start | bytes 589832 | tf_op jit(solution)/shard_map/ppermute | solution.py:62
  6.6 1.1 collective-permute-done.refs_1_
  7.7 2.7 %collective-permute-done.1.refs_3_ = bf16[128,768]{1,0:T(8,128)(2,1)S(1)} collective-permute-done((bf16[128,768]{1,0:T(8,128)(2,1)S(1)}, bf16[128,768]{1,0:T(8,128)(2,1)S(1)}, u32[]{:S(2)}, u32[]{:S(2)}) %collective-permute-start.1) | collective-permute-done | bytes 196640 | tf_op jit(solution)/shard_map/ppermute | solution.py:62
  10.4 2.6 %collective-permute-start.2 = (bf16[256,768]{1,0:T(8,128)(2,1)S(1)}, bf16[256,768]{1,0:T(8,128)(2,1)S(1)}, u32[]{:S(2)}, u32[]{:S(2)}) collective-permute-start(bf16[256,768]{1,0:T(8,128)(2,1)S(1)} %get-tuple-element.49.refs_0_), channel_id=1, source_target_pairs={{0,1},{1,0},{2,3},{3,2},{4,5},{5,4},{6,7},{7,6},{8,9},{9,8},{10,11... | collective-permute-start | bytes 1179656 | tf_op jit(solution)/shard_map/ppermute | solution.py:62
  13.3 2.7 %collective-permute-done.4.refs_1_.token_ref = s32[1,16,256]{2,1,0:T(8,128)S(1)} collective-permute-done((s32[1,16,256]{2,1,0:T(8,128)S(1)}, s32[1,16,256]{2,1,0:T(8,128)S(1)}, u32[]{:S(2)}, u32[]{:S(2)}) %collective-permute-start.4) | collective-permute-done | bytes 16416 | tf_op jit(solution)/shard_map/ppermute | solution.py:62
  16.1 4.2 %collective-permute-done.5.refs_4_.refs_1_ = s32[2,16,256]{2,1,0:T(8,128)S(1)} collective-permute-done((s32[2,16,256]{2,1,0:T(8,128)S(1)}, s32[2,16,256]{2,1,0:T(8,128)S(1)}, u32[]{:S(2)}, u32[]{:S(2)}) %collective-permute-start.5) | collective-permute-done | bytes 32800 | tf_op jit(solution)/shard_map/ppermute | solution.py:62
  20.3 1.3 join.11
  21.5 2.1 %collective-permute-start.6 = (bf16[512,768]{1,0:T(8,128)(2,1)}, bf16[512,768]{1,0:T(8,128)(2,1)}, u32[]{:S(2)}, u32[]{:S(2)}) collective-permute-start(bf16[512,768]{1,0:T(8,128)(2,1)} %get-tuple-element.51.token_ref.refs_0_), channel_id=1, source_target_pairs={{0,12},{1,13},{2,14},{3,15},{4,8},{5,9},{6,10},{7,11},{8,4},{9,5},... | collective-permute-start | bytes 2359304 | tf_op jit(solution)/shard_map/ppermute | solution.py:62
  23.8 2.2 %pick_rows.2 = bf16[1024,768]{1,0:T(8,128)(2,1)} custom-call(s32[1,1024]{1,0:T(1,128)S(1)} %reshape.35.pick_ref, bf16[256,768]{1,0:T(8,128)(2,1)S(1)} %copy-done.6, bf16[256,768]{1,0:T(8,128)(2,1)S(1)} %copy-done.2, s32[1,16,256]{2,1,0:T(8,128)S(1)} %collective-permute-done.4.refs_1_.token_ref), custom_call_target="tpu_custom_call" | custom-call | flops 1 | bytes 1 | tf_op jit(solution)/shard_map/pick_rows/pallas_call | solution.py:164
  26.0 11.0 %all-to-all-start = ((bf16[128,8,768]{2,1,0:T(8,128)(2,1)}), bf16[128,8,768]{2,1,0:T(8,128)(2,1)}, u32[]{:S(2)}, u32[]{:S(2)}) async-start(bf16[128,8,768]{2,1,0:T(8,128)(2,1)} %bitcast.8), calls=%async_computation | async-start | bytes 3145728 | tf_op jit(solution)/shard_map/all_to_all | solution.py:153
  37.2 8.0 %cite_table.1.refs_4_.table_ref.refs_6_ = bf16[256,4096]{1,0:T(8,128)(2,1)S(1)} custom-call(s32[3]{0:T(128)S(1)} %pad_add_fusion.1.place_ref, s32[256,16]{1,0:T(8,128)S(1)} %copy.22.nbr_ref, bf16[512,768]{1,0:T(8,128)(2,1)} %get-tuple-element.51.token_ref.refs_0_), custom_call_target="tpu_custom_call" | custom-call | flops 1 | bytes 1 | tf_op jit(solution)/shard_map/cite_table/pallas_call | solution.py:106
  45.3 3.6 %join.12 = (bf16[1024,768]{1,0:T(8,128)(2,1)}, bf16[1024,768]{1,0:T(8,128)(2,1)}) custom-call(bf16[512,768]{1,0:T(8,128)(2,1)} %get-tuple-element.51.token_ref.refs_0_, bf16[512,768]{1,0:T(8,128)(2,1)} %collective-permute-done.6.refs_1_, bf16[512,768]{1,0:T(8,128)(2,1)} %get-tuple-element.52.refs_2_, bf16[512,768]{1,0:T(8,128)(2,1)} %collective-permute-done.7.refs_3_, ...), custom_call_target="tpu_custom_call" | custom-call | tf_op jit(solution)/shard_map/join/pallas_call | solution.py:47
  48.9 1.4 collective-permute-start.8
  50.3 1.8 collective-permute-start.9
  53.8 7.4 %all-to-all-done = bf16[128,8,768]{2,1,0:T(8,128)(2,1)} async-done(((bf16[128,8,768]{2,1,0:T(8,128)(2,1)}), bf16[128,8,768]{2,1,0:T(8,128)(2,1)}, u32[]{:S(2)}, u32[]{:S(2)}) %all-to-all-start) | async-done | bytes 1572896 | tf_op jit(solution)/shard_map/all_to_all | solution.py:153
  61.2 8.3 %author_step.1 = (bf16[256,1024]{1,0:T(8,128)(2,1)}, bf16[256,768]{1,0:T(8,128)(2,1)}, bf16[256,768]{1,0:T(8,128)(2,1)}, bf16[256,1024]{1,0:T(8,128)(2,1)}, bf16...) custom-call(bf16[1024,768]{1,0:T(8,128)(2,1)} %bitcast.9.arrived_ref, ...), custom_call_target="tpu_custom_call" | custom-call | flops 1 | bytes 1 | tf_op jit(solution)/shard_map/author_step/pallas_call | solution.py:233
  69.5 1.2 collective-permute-start.10
  71.2 2.1 %collective-permute-done.11.refs_3_ = bf16[256,768]{1,0:T(8,128)(2,1)S(1)} collective-permute-done((bf16[256,768]{1,0:T(8,128)(2,1)S(1)}, bf16[256,768]{1,0:T(8,128)(2,1)S(1)}, u32[]{:S(2)}, u32[]{:S(2)}) %collective-permute-start.11) | collective-permute-done | bytes 393248 | tf_op jit(solution)/shard_map/ppermute | solution.py:176
  73.5 1.0 copy-done.8
  74.5 1.0 copy-done.21
  75.6 1.8 weight_parts.2.token_a
  77.4 1.2 copy-done
  78.6 4.3 %all-to-all-start.1 = ((bf16[4,2,96,1024]{3,2,1,0:T(8,128)(2,1)}), bf16[4,2,96,1024]{3,2,1,0:T(8,128)(2,1)}, u32[]{:S(2)}, u32[]{:S(2)}) async-start(bf16[4,2,96,1024]{3,2,1,0:T(8,128)(2,1)} %copy-done), calls=%async_computation.1 | async-start | bytes 3145728 | tf_op jit(solution)/shard_map/all_to_all | solution.py:517
  83.0 1.1 collective-permute-start.13
  84.1 3.2 %first_half.2.first_ref = f32[256,768]{1,0:T(8,128)S(1)} custom-call(bf16[256,4096]{1,0:T(8,128)(2,1)S(1)} %cite_table.1.refs_4_.table_ref.refs_6_, bf16[1024,768]{1,0:T(8,128)(2,1)} %get-tuple-element.53.b0.refs_7_, bf16[1024,768]{1,0:T(8,128)(2,1)} %get-tuple-element.54.b1), custom_call_target="tpu_custom_call" | custom-call | flops 1 | bytes 1 | tf_op jit(solution)/shard_map/first_half/pallas_call | solution.py:256
  88.1 5.2 %paper_step.1 = (bf16[256,1024]{1,0:T(8,128)(2,1)}, bf16[256,1792]{1,0:T(8,128)(2,1)S(1)}, bf16[256,768]{1,0:T(8,128)(2,1)S(1)}) custom-call(bf16[256,4096]{1,0:T(8,128)(2,1)S(1)} %cite_table.1.refs_4_.table_ref.refs_6_, bf16[1024,768]{1,0:T(8,128)(2,1)} %collective-permute-done.8.b0, bf16[1024,768]{1,0:T(8,128)(2,1)} %collective-permute-done.9.b1, ...), custom_call_target="tpu_custom_call" | custom-call | flops 1 | bytes 1 | tf_op jit(solution)/shard_map/paper_step/pallas_call | solution.py:326
  93.3 1.2 collective-permute-start.17
  97.2 1.8 edge_back.1
  99.0 3.2 %weight_parts.3 = (bf16[3,96,512]{2,1,0:T(8,128)(2,1)S(1)}, bf16[3,96,512]{2,1,0:T(8,128)(2,1)}, bf16[3,96,512]{2,1,0:T(8,128)(2,1)S(1)}, bf16[3,96,512]{2,1,0:T...) custom-call(s32[3]{0:T(128)S(1)} %pad_add_fusion.1.place_ref, ...), custom_call_target="tpu_custom_call" | custom-call | flops 1 | bytes 1 | tf_op jit(solution)/shard_map/weight_parts/pallas_call | solution.py:386
  103.7 1.0 collective-permute-start.20
  105.6 1.7 collective-permute-start.22
  107.3 2.4 %collective-permute-start.23 = (bf16[3,96,512]{2,1,0:T(8,128)(2,1)S(1)}, bf16[3,96,512]{2,1,0:T(8,128)(2,1)S(1)}, u32[]{:S(2)}, u32[]{:S(2)}) collective-permute-start(bf16[3,96,512]{2,1,0:T(8,128)(2,1)S(1)} %copy-done.36), channel_id=1, source_target_pairs={{0,64},{16,80},{32,96},{48,112},{64,0},{80,16},{96,32},{112,48},{1... | collective-permute-start | bytes 884744 | tf_op jit(solution)/shard_map/ppermute | solution.py:183
  109.7 1.2 collective-permute-start.24
  110.8 2.8 %collective-permute-done.22.refs_4_.refs_1_ = bf16[3,96,512]{2,1,0:T(8,128)(2,1)S(1)} collective-permute-done((bf16[3,96,512]{2,1,0:T(8,128)(2,1)}, bf16[3,96,512]{2,1,0:T(8,128)(2,1)S(1)}, u32[]{:S(2)}, u32[]{:S(2)}) %collective-permute-start.22) | collective-permute-done | bytes 294944 | tf_op jit(solution)/shard_map/ppermute | solution.py:183
  113.6 7.3 %collective-permute-done.23.refs_5_.refs_2_ = bf16[3,96,512]{2,1,0:T(8,128)(2,1)S(1)} collective-permute-done((bf16[3,96,512]{2,1,0:T(8,128)(2,1)S(1)}, bf16[3,96,512]{2,1,0:T(8,128)(2,1)S(1)}, u32[]{:S(2)}, u32[]{:S(2)}) %collective-permute-start.23) | collective-permute-done | bytes 294944 | tf_op jit(solution)/shard_map/ppermute | solution.py:183
  120.9 1.1 join.16
  122.0 2.6 %collective-permute-start.25 = (bf16[512,768]{1,0:T(8,128)(2,1)S(1)}, bf16[512,768]{1,0:T(8,128)(2,1)}, u32[]{:S(2)}, u32[]{:S(2)}) collective-permute-start(bf16[512,768]{1,0:T(8,128)(2,1)S(1)} %get-tuple-element.71.token_ref.refs_0_), channel_id=1, source_target_pairs={{0,12},{1,13},{2,14},{3,15},{4,8},{5,9},{6,10},{7,11},{8,4},{9,5},... | collective-permute-start | bytes 2359304 | tf_op jit(solution)/shard_map/ppermute | solution.py:62
  124.6 1.4 collective-permute-start.27
  125.9 2.9 %collective-permute-start.28 = (bf16[3,96,512]{2,1,0:T(8,128)(2,1)}, bf16[3,96,512]{2,1,0:T(8,128)(2,1)}, u32[]{:S(2)}, u32[]{:S(2)}) collective-permute-start(bf16[3,96,512]{2,1,0:T(8,128)(2,1)} %get-tuple-element.74), channel_id=1, source_target_pairs={{0,64},{16,80},{32,96},{48,112},{64,0},{80,16},{96,32},{112,48},{1... | collective-permute-start | bytes 884744 | tf_op jit(solution)/shard_map/ppermute | solution.py:183
  128.9 2.2 %pick_rows.3 = bf16[1024,768]{1,0:T(8,128)(2,1)} custom-call(s32[1,1024]{1,0:T(1,128)S(1)} %reshape.35.pick_ref, bf16[256,768]{1,0:T(8,128)(2,1)S(1)} %copy-done.28, bf16[256,768]{1,0:T(8,128)(2,1)S(1)} %get-tuple-element.64.refs_8_.b_ref, bf16[256,768]{1,0:T(8,128)(2,1)S(1)} %get-tuple-element.66.refs_0_.token_ref), custom_call_target="tpu_custom_call" | custom-call | flops 1 | bytes 1 | tf_op jit(solution)/shard_map/pick_rows/pallas_call | solution.py:164
  131.0 9.4 %all-to-all-start.2 = ((bf16[128,8,768]{2,1,0:T(8,128)(2,1)}), bf16[128,8,768]{2,1,0:T(8,128)(2,1)}, u32[]{:S(2)}, u32[]{:S(2)}) async-start(bf16[128,8,768]{2,1,0:T(8,128)(2,1)} %bitcast.10), calls=%async_computation.2 | async-start | bytes 3145728 | tf_op jit(solution)/shard_map/all_to_all | solution.py:153
  142.2 4.0 %cited_by_table.1.refs_4_.table_ref = bf16[256,4096]{1,0:T(8,128)(2,1)S(1)} custom-call(s32[3]{0:T(128)S(1)} %pad_add_fusion.1.place_ref, s32[8,16,256]{2,1,0:T(8,128)S(1)} %copy-done.25, s32[8,16,256]{2,1,0:T(8,128)S(1)} %copy-done.23, bf16[512,768]{1,0:T(8,128)(2,1)S(1)} %get-tuple-element.71.token_ref.refs_0_), custom_call_target="tpu_custom_call" | custom-call | flops 1 | bytes 1 | tf_op jit(solution)/shard_map/cited_by_table/pallas_call | solution.py:132
  146.3 3.5 %join.17 = (bf16[1024,768]{1,0:T(8,128)(2,1)}, bf16[1024,768]{1,0:T(8,128)(2,1)}) custom-call(bf16[512,768]{1,0:T(8,128)(2,1)S(1)} %get-tuple-element.71.token_ref.refs_0_, bf16[512,768]{1,0:T(8,128)(2,1)} %collective-permute-done.25.refs_1_, bf16[512,768]{1,0:T(8,128)(2,1)} %get-tuple-element.72.refs_2_, bf16[512,768]{1,0:T(8,128)(2,1)} %collective-permute-done.26.refs_3_, ...), custom_call_target="tpu_custom_call" | custom-call | tf_op jit(solution)/shard_map/join/pallas_call | solution.py:47
  149.8 1.4 collective-permute-start.30
  151.2 1.8 collective-permute-start.31
  153.0 3.2 %y_sum.1 = (bf16[256,512]{1,0:T(8,128)(2,1)S(1)}, bf16[256,512]{1,0:T(8,128)(2,1)}, bf16[256,512]{1,0:T(8,128)(2,1)}, bf16[256,512]{1,0:T(8,128)(2,1)}) custom-call(s32[3]{0:T(128)S(1)} %pad_add_fusion.1.place_ref, bf16[3,96,512]{2,1,0:T(8,128)(2,1)S(1)} %copy-done.14, bf16[3,96,512]{2,1,0:T(8,128)(2,1)S(1)} %collective-permute-done.22.refs_4_.refs_1_, ...), custom_call_target="tpu_custom_call" | custom-call | flops 1 | bytes 1 | tf_op jit(solution)/shard_map/y_sum/pallas_call | solution.py:416
  157.2 1.9 collective-permute-start.33
  159.6 2.9 %first_half.3.first_ref.token_a = f32[256,768]{1,0:T(8,128)S(1)} custom-call(bf16[256,4096]{1,0:T(8,128)(2,1)S(1)} %cited_by_table.1.refs_4_.table_ref, bf16[1024,768]{1,0:T(8,128)(2,1)} %get-tuple-element.76.b0, bf16[1024,768]{1,0:T(8,128)(2,1)} %get-tuple-element.77.b1), custom_call_target="tpu_custom_call" | custom-call | flops 1 | bytes 1 | tf_op jit(solution)/shard_map/first_half/pallas_call | solution.py:256
  162.5 2.0 %all-to-all-done.2 = bf16[128,8,768]{2,1,0:T(8,128)(2,1)} async-done(((bf16[128,8,768]{2,1,0:T(8,128)(2,1)}), bf16[128,8,768]{2,1,0:T(8,128)(2,1)}, u32[]{:S(2)}, u32[]{:S(2)}) %all-to-all-start.2) | async-done | bytes 1572896 | tf_op jit(solution)/shard_map/all_to_all | solution.py:153
  164.5 1.2 copy-done.15
  165.7 1.1 copy-done.17
  166.9 1.1 copy-done.19
  168.0 3.2 %edge_add.1 = (bf16[256,768]{1,0:T(8,128)(2,1)}, f32[256,768]{1,0:T(8,128)S(1)}) custom-call(bf16[512,1024]{1,0:T(8,128)(2,1)S(1)} %copy-done.15, bf16[1024,768]{1,0:T(8,128)(2,1)} %bitcast.11.back_ref, f32[256,768]{1,0:T(8,128)S(1)} %copy-done.17, f32[256,768]{1,0:T(8,128)S(1)} %copy-done.19), custom_call_target="tpu_custom_call" | custom-call | flops 1 | bytes 1 | tf_op jit(solution)/shard_map/edge_add/pallas_call | solution.py:291
  171.2 14.1 %collective-permute-done.32.refs_1_ = bf16[256,512]{1,0:T(8,128)(2,1)S(1)} collective-permute-done((bf16[256,512]{1,0:T(8,128)(2,1)}, bf16[256,512]{1,0:T(8,128)(2,1)S(1)}, u32[]{:S(2)}, u32[]{:S(2)}) %collective-permute-start.32) | collective-permute-done | bytes 262176 | tf_op jit(solution)/shard_map/ppermute | solution.py:458
  185.3 2.8 %collective-permute-done.33.refs_2_ = bf16[256,512]{1,0:T(8,128)(2,1)S(1)} collective-permute-done((bf16[256,512]{1,0:T(8,128)(2,1)}, bf16[256,512]{1,0:T(8,128)(2,1)S(1)}, u32[]{:S(2)}, u32[]{:S(2)}) %collective-permute-start.33) | collective-permute-done | bytes 262176 | tf_op jit(solution)/shard_map/ppermute | solution.py:458
  188.1 1.0 copy-done.27
  189.1 1.2 x_sum.1
  190.3 1.4 collective-permute-start.35
  191.7 2.9 %collective-permute-start.36 = (f32[64,512]{1,0:T(8,128)S(1)}, f32[64,512]{1,0:T(8,128)S(1)}, u32[]{:S(2)}, u32[]{:S(2)}) collective-permute-start(f32[64,512]{1,0:T(8,128)S(1)} %get-tuple-element.91), channel_id=1, source_target_pairs={{0,2},{1,3},{2,0},{3,1},{4,6},{5,7},{6,4},{7,5},{8,10},{9,11},{10,... | collective-permute-start | bytes 393224 | tf_op jit(solution)/shard_map/ppermute | solution.py:458
  194.6 0.9 collective-permute-start.37
  195.8 2.6 %collective-permute-done.36.refs_2_ = f32[64,512]{1,0:T(8,128)S(1)} collective-permute-done((f32[64,512]{1,0:T(8,128)S(1)}, f32[64,512]{1,0:T(8,128)S(1)}, u32[]{:S(2)}, u32[]{:S(2)}) %collective-permute-start.36) | collective-permute-done | bytes 131104 | tf_op jit(solution)/shard_map/ppermute | solution.py:458
  199.3 3.6 %last_half.1 = bf16[256,768]{1,0:T(8,128)(2,1)} custom-call(bf16[256,4096]{1,0:T(8,128)(2,1)S(1)} %cited_by_table.1.refs_4_.table_ref, bf16[1024,768]{1,0:T(8,128)(2,1)} %collective-permute-done.30.b0, bf16[1024,768]{1,0:T(8,128)(2,1)} %collective-permute-done.31.b1, f32[256,768]{1,0:T(8,128)S(1)} %first_half.3.first_ref.token_a, ...), custom_call_target="tpu_custom_call" | custom-call | flops 1 | bytes 1 | tf_op jit(solution)/shard_map/last_half/pallas_call | solution.py:273
  (135 shorter events, 13.6 us)
Async XLA Ops:
  0.6 23.2 %copy-start.2 = (bf16[256,768]{1,0:T(8,128)(2,1)S(1)}, bf16[256,768]{1,0:T(8,128)(2,1)}, u32[]{:S(2)}) copy-start(bf16[256,768]{1,0:T(8,128)(2,1)} %refs_2_.5) | copy-start | bytes 1179652
  0.6 12.4 %copy-start.34 = (s32[256,16]{0,1:T(8,128)S(1)}, s32[256,16]{0,1:T(8,128)}, u32[]{:S(2)}) copy-start(s32[256,16]{0,1:T(8,128)} %param.14) | copy-start | bytes 49156
  0.7 15.4 %copy-start.37 = (s32[1,128,4]{1,2,0:T(4,128)S(1)}, s32[1,128,4]{1,2,0:T(4,128)}, u32[]{:S(2)}) copy-start(s32[1,128,4]{1,2,0:T(4,128)} %param.16) | copy-start | bytes 6148
  0.7 22.9 %copy-start.38 = (s32[1,128,4]{1,2,0:T(4,128)S(1)}, s32[1,128,4]{1,2,0:T(4,128)}, u32[]{:S(2)}) copy-start(s32[1,128,4]{1,2,0:T(4,128)} %param.15) | copy-start | bytes 6148
  0.7 23.1 %copy-start.6 = (bf16[256,768]{1,0:T(8,128)(2,1)S(1)}, bf16[256,768]{1,0:T(8,128)(2,1)}, u32[]{:S(2)}) copy-start(bf16[256,768]{1,0:T(8,128)(2,1)} %refs_2_.4) | copy-start | bytes 1179652
  1.8 5.9 %collective-permute-start = (bf16[128,768]{1,0:T(8,128)(2,1)S(1)}, bf16[128,768]{1,0:T(8,128)(2,1)S(1)}, u32[]{:S(2)}, u32[]{:S(2)}) collective-permute-start(bf16[128,768]{1,0:T(8,128)(2,1)S(1)} %get-tuple-element.96.refs_0_), channel_id=1, source_target_pairs={{0,4},{1,5},{2,6},{3,7},{4,0},{5,1},{6,2},{7,3},{8,12},{9,13},{10,... | collective-permute-start | bytes 589832 | tf_op jit(solution)/shard_map/ppermute | solution.py:62
  4.4 6.0 %collective-permute-start.1 = (bf16[128,768]{1,0:T(8,128)(2,1)S(1)}, bf16[128,768]{1,0:T(8,128)(2,1)S(1)}, u32[]{:S(2)}, u32[]{:S(2)}) collective-permute-start(bf16[128,768]{1,0:T(8,128)(2,1)S(1)} %get-tuple-element.95.refs_2_), channel_id=1, source_target_pairs={{0,12},{1,13},{2,14},{3,15},{4,8},{5,9},{6,10},{7,11},{8,4},{9,5},... | collective-permute-start | bytes 589832 | tf_op jit(solution)/shard_map/ppermute | solution.py:62
  10.4 9.8 %collective-permute-start.2 = (bf16[256,768]{1,0:T(8,128)(2,1)S(1)}, bf16[256,768]{1,0:T(8,128)(2,1)S(1)}, u32[]{:S(2)}, u32[]{:S(2)}) collective-permute-start(bf16[256,768]{1,0:T(8,128)(2,1)S(1)} %get-tuple-element.49.refs_0_), channel_id=1, source_target_pairs={{0,1},{1,0},{2,3},{3,2},{4,5},{5,4},{6,7},{7,6},{8,9},{9,8},{10,11... | collective-permute-start | bytes 1179656 | tf_op jit(solution)/shard_map/ppermute | solution.py:62
  13.0 7.3 %collective-permute-start.3 = (bf16[256,768]{1,0:T(8,128)(2,1)S(1)}, bf16[256,768]{1,0:T(8,128)(2,1)S(1)}, u32[]{:S(2)}, u32[]{:S(2)}) collective-permute-start(bf16[256,768]{1,0:T(8,128)(2,1)S(1)} %get-tuple-element.50.refs_2_), channel_id=1, source_target_pairs={{0,3},{1,2},{2,1},{3,0},{4,7},{5,6},{6,5},{7,4},{8,11},{9,10},{10,... | collective-permute-start | bytes 1179656 | tf_op jit(solution)/shard_map/ppermute | solution.py:62
  13.0 3.0 %collective-permute-start.4 = (s32[1,16,256]{2,1,0:T(8,128)S(1)}, s32[1,16,256]{2,1,0:T(8,128)S(1)}, u32[]{:S(2)}, u32[]{:S(2)}) collective-permute-start(s32[1,16,256]{2,1,0:T(8,128)S(1)} %bitcast.14), channel_id=1, source_target_pairs={{0,4},{1,5},{2,6},{3,7},{4,0},{5,1},{6,2},{7,3},{8,12},{9,13},{10,... | collective-permute-start | bytes 49160 | tf_op jit(solution)/shard_map/ppermute | solution.py:62
  16.0 4.3 %collective-permute-start.5 = (s32[2,16,256]{2,1,0:T(8,128)S(1)}, s32[2,16,256]{2,1,0:T(8,128)S(1)}, u32[]{:S(2)}, u32[]{:S(2)}) collective-permute-start(s32[2,16,256]{2,1,0:T(8,128)S(1)} %join.10.refs_0_), channel_id=1, source_target_pairs={{0,1},{1,0},{2,3},{3,2},{4,5},{5,4},{6,7},{7,6},{8,9},{9,8},{10,11... | collective-permute-start | bytes 98312 | tf_op jit(solution)/shard_map/ppermute | solution.py:62
  21.5 23.7 %collective-permute-start.6 = (bf16[512,768]{1,0:T(8,128)(2,1)}, bf16[512,768]{1,0:T(8,128)(2,1)}, u32[]{:S(2)}, u32[]{:S(2)}) collective-permute-start(bf16[512,768]{1,0:T(8,128)(2,1)} %get-tuple-element.51.token_ref.refs_0_), channel_id=1, source_target_pairs={{0,12},{1,13},{2,14},{3,15},{4,8},{5,9},{6,10},{7,11},{8,4},{9,5},... | collective-permute-start | bytes 2359304 | tf_op jit(solution)/shard_map/ppermute | solution.py:62
  23.6 21.7 %collective-permute-start.7 = (bf16[512,768]{1,0:T(8,128)(2,1)}, bf16[512,768]{1,0:T(8,128)(2,1)}, u32[]{:S(2)}, u32[]{:S(2)}) collective-permute-start(bf16[512,768]{1,0:T(8,128)(2,1)} %get-tuple-element.52.refs_2_), channel_id=1, source_target_pairs={{0,4},{1,5},{2,6},{3,7},{4,0},{5,1},{6,2},{7,3},{8,12},{9,13},{10,... | collective-permute-start | bytes 2359304 | tf_op jit(solution)/shard_map/ppermute | solution.py:62
  26.0 35.1 %all-to-all-start = ((bf16[128,8,768]{2,1,0:T(8,128)(2,1)}), bf16[128,8,768]{2,1,0:T(8,128)(2,1)}, u32[]{:S(2)}, u32[]{:S(2)}) async-start(bf16[128,8,768]{2,1,0:T(8,128)(2,1)} %bitcast.8), calls=%async_computation | async-start | bytes 3145728 | tf_op jit(solution)/shard_map/all_to_all | solution.py:153
  48.9 39.0 %collective-permute-start.8 = (bf16[1024,768]{1,0:T(8,128)(2,1)}, bf16[1024,768]{1,0:T(8,128)(2,1)}, u32[]{:S(2)}, u32[]{:S(2)}) collective-permute-start(bf16[1024,768]{1,0:T(8,128)(2,1)} %get-tuple-element.53.b0.refs_7_), channel_id=1, source_target_pairs={{0,3},{1,2},{2,1},{3,0},{4,7},{5,6},{6,5},{7,4},{8,11},{9,10},{10,... | collective-permute-start | bytes 4718600 | tf_op jit(solution)/shard_map/ppermute | solution.py:62
  50.3 37.7 %collective-permute-start.9 = (bf16[1024,768]{1,0:T(8,128)(2,1)}, bf16[1024,768]{1,0:T(8,128)(2,1)}, u32[]{:S(2)}, u32[]{:S(2)}) collective-permute-start(bf16[1024,768]{1,0:T(8,128)(2,1)} %get-tuple-element.54.b1), channel_id=1, source_target_pairs={{0,1},{1,0},{2,3},{3,2},{4,5},{5,4},{6,7},{7,6},{8,9},{9,8},{10,11... | collective-permute-start | bytes 4718600 | tf_op jit(solution)/shard_map/ppermute | solution.py:62
  61.2 9.5 %copy-start.7 = (bf16[256,768]{1,0:T(8,128)(2,1)S(1)}, bf16[256,768]{1,0:T(8,128)(2,1)}, u32[]{:S(2)}) copy-start(bf16[256,768]{1,0:T(8,128)(2,1)} %refs_2_.4) | copy-start | bytes 1179652
  69.5 4.1 %collective-permute-start.10 = (bf16[256,1024]{1,0:T(8,128)(2,1)}, bf16[256,1024]{1,0:T(8,128)(2,1)S(1)}, u32[]{:S(2)}, u32[]{:S(2)}) collective-permute-start(bf16[256,1024]{1,0:T(8,128)(2,1)} %get-tuple-element.56.refs_0_), channel_id=1, source_target_pairs={{0,16},{16,0},{32,48},{48,32},{64,80},{80,64},{96,112},{112,96},{1... | collective-permute-start | bytes 1572872 | tf_op jit(solution)/shard_map/ppermute | solution.py:176
  70.7 2.7 %collective-permute-start.11 = (bf16[256,768]{1,0:T(8,128)(2,1)S(1)}, bf16[256,768]{1,0:T(8,128)(2,1)S(1)}, u32[]{:S(2)}, u32[]{:S(2)}) collective-permute-start(bf16[256,768]{1,0:T(8,128)(2,1)S(1)} %copy-done.7), channel_id=1, source_target_pairs={{0,16},{16,0},{32,48},{48,32},{64,80},{80,64},{96,112},{112,96},{1... | collective-permute-start | bytes 1179656 | tf_op jit(solution)/shard_map/ppermute | solution.py:176
  70.8 2.8 %collective-permute-start.12 = (bf16[256,768]{1,0:T(8,128)(2,1)}, bf16[256,768]{1,0:T(8,128)(2,1)S(1)}, u32[]{:S(2)}, u32[]{:S(2)}) collective-permute-start(bf16[256,768]{1,0:T(8,128)(2,1)} %get-tuple-element.57.refs_4_.token_c), channel_id=1, source_target_pairs={{0,16},{16,0},{32,48},{48,32},{64,80},{80,64},{96,112},{112,96},{1... | collective-permute-start | bytes 1179656 | tf_op jit(solution)/shard_map/ppermute | solution.py:176
  78.6 25.1 %all-to-all-start.1 = ((bf16[4,2,96,1024]{3,2,1,0:T(8,128)(2,1)}), bf16[4,2,96,1024]{3,2,1,0:T(8,128)(2,1)}, u32[]{:S(2)}, u32[]{:S(2)}) async-start(bf16[4,2,96,1024]{3,2,1,0:T(8,128)(2,1)} %copy-done), calls=%async_computation.1 | async-start | bytes 3145728 | tf_op jit(solution)/shard_map/all_to_all | solution.py:517
  82.9 5.1 %copy-start.1 = (bf16[4,2,96,1024]{3,2,1,0:T(8,128)(2,1)S(1)}, bf16[4,2,96,1024]{3,2,1,0:T(8,128)(2,1)}, u32[]{:S(2)}) copy-start(bf16[4,2,96,1024]{3,2,1,0:T(8,128)(2,1)} %copy-done) | copy-start | bytes 4718596
  82.9 5.0 %copy-start.9 = (bf16[256,768]{1,0:T(8,128)(2,1)S(1)}, bf16[256,768]{1,0:T(8,128)(2,1)}, u32[]{:S(2)}) copy-start(bf16[256,768]{1,0:T(8,128)(2,1)} %get-tuple-element.57.refs_4_.token_c) | copy-start | bytes 1179652
  82.9 5.0 %copy-start.10 = (bf16[768,1024]{1,0:T(8,128)(2,1)S(1)}, bf16[768,1024]{1,0:T(8,128)(2,1)}, u32[]{:S(2)}) copy-start(bf16[768,1024]{1,0:T(8,128)(2,1)} %w_hbm.1) | copy-start | bytes 4718596
  83.0 5.0 %copy-start.16 = (f32[256,1024]{1,0:T(8,128)S(1)}, f32[256,1024]{1,0:T(8,128)}, u32[]{:S(2)}) copy-start(f32[256,1024]{1,0:T(8,128)} %get-tuple-element.55.pre_ref) | copy-start | bytes 3145732
  83.0 5.0 %copy-start.20 = (bf16[256,1024]{1,0:T(8,128)(2,1)S(1)}, bf16[256,1024]{1,0:T(8,128)(2,1)}, u32[]{:S(2)}) copy-start(bf16[256,1024]{1,0:T(8,128)(2,1)} %grad_hbm.1) | copy-start | bytes 1572868
  83.0 5.0 %collective-permute-start.13 = (s32[4,16,256]{2,1,0:T(8,128)S(1)}, s32[4,16,256]{2,1,0:T(8,128)S(1)}, u32[]{:S(2)}, u32[]{:S(2)}) collective-permute-start(s32[4,16,256]{2,1,0:T(8,128)S(1)} %join.13.refs_0_), channel_id=1, source_target_pairs={{0,12},{1,13},{2,14},{3,15},{4,8},{5,9},{6,10},{7,11},{8,4},{9,5},... | collective-permute-start | bytes 196616 | tf_op jit(solution)/shard_map/ppermute | solution.py:62
  88.0 6.5 %copy-start.3 = (bf16[256,768]{1,0:T(8,128)(2,1)S(1)}, bf16[256,768]{1,0:T(8,128)(2,1)}, u32[]{:S(2)}) copy-start(bf16[256,768]{1,0:T(8,128)(2,1)} %refs_2_.5) | copy-start | bytes 1179652
  88.0 6.6 %copy-start.26 = (bf16[256,768]{1,0:T(8,128)(2,1)S(1)}, bf16[256,768]{1,0:T(8,128)(2,1)}, u32[]{:S(2)}) copy-start(bf16[256,768]{1,0:T(8,128)(2,1)} %get-tuple-element.62.refs_6_) | copy-start | bytes 1179652
  88.0 9.1 %copy-start.4 = (bf16[768,1024]{1,0:T(8,128)(2,1)S(1)}, bf16[768,1024]{1,0:T(8,128)(2,1)}, u32[]{:S(2)}) copy-start(bf16[768,1024]{1,0:T(8,128)(2,1)} %w_sp_hbm.1) | copy-start | bytes 4718596
  88.1 9.1 %copy-start.5 = (bf16[768,1024]{1,0:T(8,128)(2,1)S(1)}, bf16[768,1024]{1,0:T(8,128)(2,1)}, u32[]{:S(2)}) copy-start(bf16[768,1024]{1,0:T(8,128)(2,1)} %w_wr_hbm.1) | copy-start | bytes 4718596
  88.1 9.1 %copy-start.31 = (f32[512,128]{1,0:T(8,128)S(1)}, f32[512,128]{1,0:T(8,128)}, u32[]{:S(2)}) copy-start(f32[512,128]{1,0:T(8,128)} %get-tuple-element.63.cnt_ref) | copy-start | bytes 786436
  93.3 5.7 %collective-permute-start.17 = (bf16[256,1792]{1,0:T(8,128)(2,1)S(1)}, bf16[256,1792]{1,0:T(8,128)(2,1)S(1)}, u32[]{:S(2)}, u32[]{:S(2)}) collective-permute-start(bf16[256,1792]{1,0:T(8,128)(2,1)S(1)} %get-tuple-element.61.pack_ref.refs_0_.refs_4_), channel_id=1, source_target_pairs={{0,16},{16,0},{32,48},{48,32},{64,80},{80,64},{96,112},{112,96},{1... | collective-permute-start | bytes 2752520 | tf_op jit(solution)/shard_map/ppermute | solution.py:176
  94.5 2.7 %collective-permute-start.18 = (bf16[256,768]{1,0:T(8,128)(2,1)S(1)}, bf16[256,768]{1,0:T(8,128)(2,1)S(1)}, u32[]{:S(2)}, u32[]{:S(2)}) collective-permute-start(bf16[256,768]{1,0:T(8,128)(2,1)S(1)} %copy-done.3), channel_id=1, source_target_pairs={{0,16},{16,0},{32,48},{48,32},{64,80},{80,64},{96,112},{112,96},{1... | collective-permute-start | bytes 1179656 | tf_op jit(solution)/shard_map/ppermute | solution.py:176
  94.6 4.4 %collective-permute-start.19 = (bf16[256,768]{1,0:T(8,128)(2,1)S(1)}, bf16[256,768]{1,0:T(8,128)(2,1)S(1)}, u32[]{:S(2)}, u32[]{:S(2)}) collective-permute-start(bf16[256,768]{1,0:T(8,128)(2,1)S(1)} %copy-done.26), channel_id=1, source_target_pairs={{0,16},{16,0},{32,48},{48,32},{64,80},{80,64},{96,112},{112,96},{1... | collective-permute-start | bytes 1179656 | tf_op jit(solution)/shard_map/ppermute | solution.py:176
  95.0 8.6 %collective-permute-start.15 = (bf16[128,768]{1,0:T(8,128)(2,1)S(1)}, bf16[128,768]{1,0:T(8,128)(2,1)S(1)}, u32[]{:S(2)}, u32[]{:S(2)}) collective-permute-start(bf16[128,768]{1,0:T(8,128)(2,1)S(1)} %get-tuple-element.94.refs_0_), channel_id=1, source_target_pairs={{0,4},{1,5},{2,6},{3,7},{4,0},{5,1},{6,2},{7,3},{8,12},{9,13},{10,... | collective-permute-start | bytes 589832 | tf_op jit(solution)/shard_map/ppermute | solution.py:62
  96.0 7.7 %collective-permute-start.16 = (bf16[128,768]{1,0:T(8,128)(2,1)S(1)}, bf16[128,768]{1,0:T(8,128)(2,1)S(1)}, u32[]{:S(2)}, u32[]{:S(2)}) collective-permute-start(bf16[128,768]{1,0:T(8,128)(2,1)S(1)} %get-tuple-element.93.refs_2_), channel_id=1, source_target_pairs={{0,12},{1,13},{2,14},{3,15},{4,8},{5,9},{6,10},{7,11},{8,4},{9,5},... | collective-permute-start | bytes 589832 | tf_op jit(solution)/shard_map/ppermute | solution.py:62
  97.2 6.5 %collective-permute-start.14 = (s32[8,16,256]{2,1,0:T(8,128)S(1)}, s32[8,16,256]{2,1,0:T(8,128)S(1)}, u32[]{:S(2)}, u32[]{:S(2)}) collective-permute-start(s32[8,16,256]{2,1,0:T(8,128)S(1)} %join.14.a_ref), channel_id=1, source_target_pairs={{0,3},{1,2},{2,1},{3,0},{4,7},{5,6},{6,5},{7,4},{8,11},{9,10},{10,... | collective-permute-start | bytes 393224 | tf_op jit(solution)/shard_map/ppermute | solution.py:62
  103.6 18.3 %copy-start.13 = (bf16[3,96,512]{2,1,0:T(8,128)(2,1)}, bf16[3,96,512]{2,1,0:T(8,128)(2,1)S(1)}, u32[]{:S(2)}) copy-start(bf16[3,96,512]{2,1,0:T(8,128)(2,1)S(1)} %get-tuple-element.65.refs_4_.refs_0_) | copy-start | bytes 884740
  103.6 18.3 %copy-start.22 = (s32[8,16,256]{2,1,0:T(8,128)}, s32[8,16,256]{2,1,0:T(8,128)S(1)}, u32[]{:S(2)}) copy-start(s32[8,16,256]{2,1,0:T(8,128)S(1)} %collective-permute-done.14.refs_5_.b_ref) | copy-start | bytes 393220
  103.7 25.1 %copy-start.28 = (bf16[256,768]{1,0:T(8,128)(2,1)S(1)}, bf16[256,768]{1,0:T(8,128)(2,1)}, u32[]{:S(2)}) copy-start(bf16[256,768]{1,0:T(8,128)(2,1)} %get-tuple-element.79.a_ref) | copy-start | bytes 1179652
  103.7 17.1 %collective-permute-start.20 = (bf16[256,768]{1,0:T(8,128)(2,1)S(1)}, bf16[256,768]{1,0:T(8,128)(2,1)S(1)}, u32[]{:S(2)}, u32[]{:S(2)}) collective-permute-start(bf16[256,768]{1,0:T(8,128)(2,1)S(1)} %get-tuple-element.66.refs_0_.token_ref), channel_id=1, source_target_pairs={{0,1},{1,0},{2,3},{3,2},{4,5},{5,4},{6,7},{7,6},{8,9},{9,8},{10,11... | collective-permute-start | bytes 1179656 | tf_op jit(solution)/shard_map/ppermute | solution.py:62
  104.8 16.1 %collective-permute-start.21 = (bf16[256,768]{1,0:T(8,128)(2,1)S(1)}, bf16[256,768]{1,0:T(8,128)(2,1)S(1)}, u32[]{:S(2)}, u32[]{:S(2)}) collective-permute-start(bf16[256,768]{1,0:T(8,128)(2,1)S(1)} %get-tuple-element.67.refs_2_), channel_id=1, source_target_pairs={{0,3},{1,2},{2,1},{3,0},{4,7},{5,6},{6,5},{7,4},{8,11},{9,10},{10,... | collective-permute-start | bytes 1179656 | tf_op jit(solution)/shard_map/ppermute | solution.py:62
  105.6 8.0 %collective-permute-start.22 = (bf16[3,96,512]{2,1,0:T(8,128)(2,1)}, bf16[3,96,512]{2,1,0:T(8,128)(2,1)S(1)}, u32[]{:S(2)}, u32[]{:S(2)}) collective-permute-start(bf16[3,96,512]{2,1,0:T(8,128)(2,1)} %get-tuple-element.68), channel_id=1, source_target_pairs={{0,32},{16,48},{32,64},{48,80},{64,96},{80,112},{96,0},{112,16},{1... | collective-permute-start | bytes 884744 | tf_op jit(solution)/shard_map/ppermute | solution.py:183
  107.3 13.6 %collective-permute-start.23 = (bf16[3,96,512]{2,1,0:T(8,128)(2,1)S(1)}, bf16[3,96,512]{2,1,0:T(8,128)(2,1)S(1)}, u32[]{:S(2)}, u32[]{:S(2)}) collective-permute-start(bf16[3,96,512]{2,1,0:T(8,128)(2,1)S(1)} %copy-done.36), channel_id=1, source_target_pairs={{0,64},{16,80},{32,96},{48,112},{64,0},{80,16},{96,32},{112,48},{1... | collective-permute-start | bytes 884744 | tf_op jit(solution)/shard_map/ppermute | solution.py:183
  109.7 11.2 %collective-permute-start.24 = (bf16[3,96,512]{2,1,0:T(8,128)(2,1)S(1)}, bf16[3,96,512]{2,1,0:T(8,128)(2,1)S(1)}, u32[]{:S(2)}, u32[]{:S(2)}) collective-permute-start(bf16[3,96,512]{2,1,0:T(8,128)(2,1)S(1)} %get-tuple-element.70), channel_id=1, source_target_pairs={{0,96},{16,112},{32,0},{48,16},{64,32},{80,48},{96,64},{112,80},{1... | collective-permute-start | bytes 884744 | tf_op jit(solution)/shard_map/ppermute | solution.py:183
  122.0 24.3 %collective-permute-start.25 = (bf16[512,768]{1,0:T(8,128)(2,1)S(1)}, bf16[512,768]{1,0:T(8,128)(2,1)}, u32[]{:S(2)}, u32[]{:S(2)}) collective-permute-start(bf16[512,768]{1,0:T(8,128)(2,1)S(1)} %get-tuple-element.71.token_ref.refs_0_), channel_id=1, source_target_pairs={{0,12},{1,13},{2,14},{3,15},{4,8},{5,9},{6,10},{7,11},{8,4},{9,5},... | collective-permute-start | bytes 2359304 | tf_op jit(solution)/shard_map/ppermute | solution.py:62
  124.6 21.7 %collective-permute-start.26 = (bf16[512,768]{1,0:T(8,128)(2,1)}, bf16[512,768]{1,0:T(8,128)(2,1)}, u32[]{:S(2)}, u32[]{:S(2)}) collective-permute-start(bf16[512,768]{1,0:T(8,128)(2,1)} %get-tuple-element.72.refs_2_), channel_id=1, source_target_pairs={{0,4},{1,5},{2,6},{3,7},{4,0},{5,1},{6,2},{7,3},{8,12},{9,13},{10,... | collective-permute-start | bytes 2359304 | tf_op jit(solution)/shard_map/ppermute | solution.py:62
  124.6 21.7 %collective-permute-start.27 = (bf16[3,96,512]{2,1,0:T(8,128)(2,1)}, bf16[3,96,512]{2,1,0:T(8,128)(2,1)}, u32[]{:S(2)}, u32[]{:S(2)}) collective-permute-start(bf16[3,96,512]{2,1,0:T(8,128)(2,1)} %get-tuple-element.73), channel_id=1, source_target_pairs={{0,32},{16,48},{32,64},{48,80},{64,96},{80,112},{96,0},{112,16},{1... | collective-permute-start | bytes 884744 | tf_op jit(solution)/shard_map/ppermute | solution.py:183
  125.9 20.3 %collective-permute-start.28 = (bf16[3,96,512]{2,1,0:T(8,128)(2,1)}, bf16[3,96,512]{2,1,0:T(8,128)(2,1)}, u32[]{:S(2)}, u32[]{:S(2)}) collective-permute-start(bf16[3,96,512]{2,1,0:T(8,128)(2,1)} %get-tuple-element.74), channel_id=1, source_target_pairs={{0,64},{16,80},{32,96},{48,112},{64,0},{80,16},{96,32},{112,48},{1... | collective-permute-start | bytes 884744 | tf_op jit(solution)/shard_map/ppermute | solution.py:183
  128.9 17.4 %collective-permute-start.29 = (bf16[3,96,512]{2,1,0:T(8,128)(2,1)}, bf16[3,96,512]{2,1,0:T(8,128)(2,1)}, u32[]{:S(2)}, u32[]{:S(2)}) collective-permute-start(bf16[3,96,512]{2,1,0:T(8,128)(2,1)} %get-tuple-element.75), channel_id=1, source_target_pairs={{0,96},{16,112},{32,0},{48,16},{64,32},{80,48},{96,64},{112,80},{1... | collective-permute-start | bytes 884744 | tf_op jit(solution)/shard_map/ppermute | solution.py:183
  131.0 33.5 %all-to-all-start.2 = ((bf16[128,8,768]{2,1,0:T(8,128)(2,1)}), bf16[128,8,768]{2,1,0:T(8,128)(2,1)}, u32[]{:S(2)}, u32[]{:S(2)}) async-start(bf16[128,8,768]{2,1,0:T(8,128)(2,1)} %bitcast.10), calls=%async_computation.2 | async-start | bytes 3145728 | tf_op jit(solution)/shard_map/all_to_all | solution.py:153
  146.2 6.7 %copy-start.12 = (bf16[3,96,512]{2,1,0:T(8,128)(2,1)S(1)}, bf16[3,96,512]{2,1,0:T(8,128)(2,1)}, u32[]{:S(2)}) copy-start(bf16[3,96,512]{2,1,0:T(8,128)(2,1)} %copy-done.11) | copy-start | bytes 884740
  146.2 6.7 %copy-start.14 = (bf16[3,96,512]{2,1,0:T(8,128)(2,1)S(1)}, bf16[3,96,512]{2,1,0:T(8,128)(2,1)}, u32[]{:S(2)}) copy-start(bf16[3,96,512]{2,1,0:T(8,128)(2,1)} %copy-done.13) | copy-start | bytes 884740
  146.3 6.7 %copy-start.30 = (bf16[3,96,512]{2,1,0:T(8,128)(2,1)S(1)}, bf16[3,96,512]{2,1,0:T(8,128)(2,1)}, u32[]{:S(2)}) copy-start(bf16[3,96,512]{2,1,0:T(8,128)(2,1)} %copy-done.29) | copy-start | bytes 884740
  149.8 49.5 %collective-permute-start.30 = (bf16[1024,768]{1,0:T(8,128)(2,1)}, bf16[1024,768]{1,0:T(8,128)(2,1)}, u32[]{:S(2)}, u32[]{:S(2)}) collective-permute-start(bf16[1024,768]{1,0:T(8,128)(2,1)} %get-tuple-element.76.b0), channel_id=1, source_target_pairs={{0,3},{1,2},{2,1},{3,0},{4,7},{5,6},{6,5},{7,4},{8,11},{9,10},{10,... | collective-permute-start | bytes 4718600 | tf_op jit(solution)/shard_map/ppermute | solution.py:62
  151.2 48.1 %collective-permute-start.31 = (bf16[1024,768]{1,0:T(8,128)(2,1)}, bf16[1024,768]{1,0:T(8,128)(2,1)}, u32[]{:S(2)}, u32[]{:S(2)}) collective-permute-start(bf16[1024,768]{1,0:T(8,128)(2,1)} %get-tuple-element.77.b1), channel_id=1, source_target_pairs={{0,1},{1,0},{2,3},{3,2},{4,5},{5,4},{6,7},{7,6},{8,9},{9,8},{10,11... | collective-permute-start | bytes 4718600 | tf_op jit(solution)/shard_map/ppermute | solution.py:62
  156.9 28.4 %collective-permute-start.32 = (bf16[256,512]{1,0:T(8,128)(2,1)}, bf16[256,512]{1,0:T(8,128)(2,1)S(1)}, u32[]{:S(2)}, u32[]{:S(2)}) collective-permute-start(bf16[256,512]{1,0:T(8,128)(2,1)} %get-tuple-element.86), channel_id=1, source_target_pairs={{0,4},{1,5},{2,6},{3,7},{4,8},{5,9},{6,10},{7,11},{8,12},{9,13},{1... | collective-permute-start | bytes 786440 | tf_op jit(solution)/shard_map/ppermute | solution.py:458
  157.2 30.9 %collective-permute-start.33 = (bf16[256,512]{1,0:T(8,128)(2,1)}, bf16[256,512]{1,0:T(8,128)(2,1)S(1)}, u32[]{:S(2)}, u32[]{:S(2)}) collective-permute-start(bf16[256,512]{1,0:T(8,128)(2,1)} %get-tuple-element.87), channel_id=1, source_target_pairs={{0,8},{1,9},{2,10},{3,11},{4,12},{5,13},{6,14},{7,15},{8,0},{9,1},... | collective-permute-start | bytes 786440 | tf_op jit(solution)/shard_map/ppermute | solution.py:458
  159.0 29.1 %collective-permute-start.34 = (bf16[256,512]{1,0:T(8,128)(2,1)}, bf16[256,512]{1,0:T(8,128)(2,1)}, u32[]{:S(2)}, u32[]{:S(2)}) collective-permute-start(bf16[256,512]{1,0:T(8,128)(2,1)} %get-tuple-element.88), channel_id=1, source_target_pairs={{0,12},{1,13},{2,14},{3,15},{4,0},{5,1},{6,2},{7,3},{8,4},{9,5},{1... | collective-permute-start | bytes 786440 | tf_op jit(solution)/shard_map/ppermute | solution.py:458
  168.0 20.1 %copy-start.33 = (bf16[256,512]{1,0:T(8,128)(2,1)S(1)}, bf16[256,512]{1,0:T(8,128)(2,1)}, u32[]{:S(2)}) copy-start(bf16[256,512]{1,0:T(8,128)(2,1)} %copy-done.32) | copy-start | bytes 786436
  190.3 5.5 %collective-permute-start.35 = (f32[64,512]{1,0:T(8,128)S(1)}, f32[64,512]{1,0:T(8,128)S(1)}, u32[]{:S(2)}, u32[]{:S(2)}) collective-permute-start(f32[64,512]{1,0:T(8,128)S(1)} %get-tuple-element.90), channel_id=1, source_target_pairs={{0,1},{1,2},{2,3},{3,0},{4,5},{5,6},{6,7},{7,4},{8,9},{9,10},{10,1... | collective-permute-start | bytes 393224 | tf_op jit(solution)/shard_map/ppermute | solution.py:458
  191.7 6.7 %collective-permute-start.36 = (f32[64,512]{1,0:T(8,128)S(1)}, f32[64,512]{1,0:T(8,128)S(1)}, u32[]{:S(2)}, u32[]{:S(2)}) collective-permute-start(f32[64,512]{1,0:T(8,128)S(1)} %get-tuple-element.91), channel_id=1, source_target_pairs={{0,2},{1,3},{2,0},{3,1},{4,6},{5,7},{6,4},{7,5},{8,10},{9,11},{10,... | collective-permute-start | bytes 393224 | tf_op jit(solution)/shard_map/ppermute | solution.py:458
  194.6 3.8 %collective-permute-start.37 = (f32[64,512]{1,0:T(8,128)S(1)}, f32[64,512]{1,0:T(8,128)S(1)}, u32[]{:S(2)}, u32[]{:S(2)}) collective-permute-start(f32[64,512]{1,0:T(8,128)S(1)} %get-tuple-element.92), channel_id=1, source_target_pairs={{0,3},{1,0},{2,1},{3,2},{4,7},{5,4},{6,5},{7,6},{8,11},{9,8},{10,9... | collective-permute-start | bytes 393224 | tf_op jit(solution)/shard_map/ppermute | solution.py:458
  (16 other events, 22.3 us)

commit v6 on v5

--- a/solution.py
+++ b/solution.py
@@ -397,7 +397,7 @@
 
 
 def y_sum_kernel(place_ref, *refs):
-    left, right, authors, outs, stack = refs[:4], refs[4:8], refs[8], refs[9:13], refs[13]
+    left, right, authors, outs, stack, turned = refs[:4], refs[4:8], refs[8], refs[9:13], refs[13], refs[14]
     for group, first, rows, lane, wide in ((left, 0, 3, 0, 512), (right, 0, 3, 512, 512), (authors, 3, 2, 0, 1024)):
         for i in range(rows):
             part = (lambda y: group[y, i]) if first else (lambda y: group[y][i])
@@ -406,10 +406,12 @@
                 total = total + part(y).astype(F32)
             stack[pl.ds(96 * (first + i), 96), pl.ds(lane, wide)] = total
     stack[pl.ds(480, 32), :] = jnp.zeros((32, 1024), F32)
-    x = place_ref[0] >> 2
+    turned[...] = stack[...].T.astype(BF)
+    core, x, z = place_ref[1], place_ref[0] >> 2, place_ref[0] & 3
     for d in range(4):
-        start = pl.multiple_of(((x + d) & 3) * 256, 256)
-        outs[d][...] = stack[:, pl.ds(start, 256)].T.astype(BF)
+        for j in range(4):
+            start = jnp.where(core == 0, ((x + d) & 3) * 256 + j * 64, j * 256 + ((z + d) & 3) * 64)
+            outs[d][pl.ds(64 * j, 64), :] = turned[pl.ds(pl.multiple_of(start, 64), 64), :]
 
 
 def y_sum(place, left, right, author):
@@ -418,7 +420,7 @@
         out_shape=[shape((256, 512), BF)] * 4,
         in_specs=[IN_SMEM] + [IN_VMEM] * 9,
         out_specs=[IN_VMEM] * 4,
-        scratch_shapes=[pltpu.VMEM((512, 1024), F32)],
+        scratch_shapes=[pltpu.VMEM((512, 1024), F32), pltpu.VMEM((1024, 512), BF)],
         compiler_params=params(20),
         cost_estimate=pl.CostEstimate(flops=1, bytes_accessed=1, transcendentals=0),
         name="y_sum",
@@ -430,9 +432,9 @@
     for ref in refs[1:4]:
         total = total + ref[...].astype(F32)
     refs[8][...] = total
-    z = place_ref[0] & 3
+    at = jnp.where(place_ref[1] == 0, place_ref[0] & 3, place_ref[0] >> 2)
     for d in range(4):
-        refs[4 + d][...] = refs[8][pl.ds(pl.multiple_of(((z + d) & 3) * 64, 64), 64), :]
+        refs[4 + d][...] = refs[8][pl.ds(pl.multiple_of(((at + d) & 3) * 64, 64), 64), :]
 
 
 def x_sum(place, got, *tokens):
@@ -448,14 +450,16 @@
     )(place, *tokens, *got)
 
 
-def over_col(parts, step):
+def over_col(parts, stage):
     got = [parts[0]]
     for d in range(1, 4):
         perm = []
-        for c in range(16):
-            x, z = c >> 2, c & 3
-            perm.append((c, ((x + d) % 4) * 4 + z if step == 4 else x * 4 + (z + d) % 4))
-        got.append(lax.ppermute(parts[d], "col", perm))
+        for r in range(8):
+            for c in range(16):
+                x, z = c >> 2, c & 3
+                to = ((x + d) % 4) * 4 + z if (r & 1) == stage else x * 4 + (z + d) % 4
+                perm.append((r * 16 + c, r * 16 + to))
+        got.append(lax.ppermute(parts[d], ("row", "col"), perm))
     return got
 
 
@@ -544,7 +548,7 @@
     back_pairs = travel(parts, 3)
     back_first = first_half(back_table, [pair[0] for pair in back_pairs])
 
-    got = over_col(y_sum(place, left, right, got_author), 4)
+    got = over_col(y_sum(place, left, right, got_author), 0)
     got = over_col(x_sum(place, got, back_first, dx_author), 1)
     dx_paper = last_half(back_table, [pair[1] for pair in back_pairs], back_first, dx_paper_own)
     dweights = last_sum(got).transpose(0, 2, 1)

time: 204 us -> 192 us (0.941)
  the two profiles are of different devices: /device:TPU:1 before, /device:TPU:0 now
where the time goes in v6:
time: 192 us; the launch traced here: 191 us
  starting transfers between devices  67.3 us (35%)
  Pallas kernels  64.3 us (33%)
  waiting for transfers between devices  43.3 us (23%)
  local copies, waits for them, and re-layouts  14.9 us (8%)
    ppermute x20, starting transfers between devices, travel(): pairs.append((part, lax.ppermute(part, ('row', 'col'), perm)))  24.9 us
    all_to_all x2, starting transfers between devices, exchange(): lax.all_to_all(sent, ('row', 'col'), split_axis=0, concat_axis=0, tiled=T...  15 us
    ppermute x20, waiting for transfers between devices, travel(): pairs.append((part, lax.ppermute(part, ('row', 'col'), perm)))  13.8 us
    unnamed x81, local copies, waits for them, and re-layouts  12.1 us
    ppermute x6, starting transfers between devices, over_y(): got.append(lax.ppermute(parts[d], 'row', perm))  11.2 us
    ppermute x6, starting transfers between devices, over_col(): got.append(lax.ppermute(parts[d], ('row', 'col'), perm))  10.5 us
    ppermute x6, waiting for transfers between devices, over_y(): got.append(lax.ppermute(parts[d], 'row', perm))  10.1 us
    pallas_call x9, Pallas kernels, join(): pl.pallas_call(functools.partial(join_kernel, n), out_shape=outs, in_spec...  9.53 us
  transfers between devices with their start and end apart: 41, of which 14 were waited for; matrix products, arithmetic and copies ran while one was open for 1% of the time, Pallas kernels for 30%

profile of v6, /device:TPU:0, one launch (start us, length us, event | category | flops | bytes accessed | tf_op | source)
XLA Modules:
  0.0 191.2 jit_solution(14830715414084433085)
XLA Ops:
  0.7 1.1 fusion.1
  1.8 1.7 collective-permute-start
  3.5 2.1 %collective-permute-start.1 = (bf16[128,768]{1,0:T(8,128)(2,1)S(1)}, bf16[128,768]{1,0:T(8,128)(2,1)S(1)}, u32[]{:S(2)}, u32[]{:S(2)}) collective-permute-start(bf16[128,768]{1,0:T(8,128)(2,1)S(1)} %get-tuple-element.95.refs_2_), channel_id=1, source_target_pairs={{0,12},{1,13},{2,14},{3,15},{4,8},{5,9},{6,10},{7,11},{8,4},{9,5},... | collective-permute-start | bytes 589832 | tf_op jit(solution)/shard_map/ppermute | solution.py:62
  5.6 2.0 %collective-permute-done.refs_1_ = bf16[128,768]{1,0:T(8,128)(2,1)S(1)} collective-permute-done((bf16[128,768]{1,0:T(8,128)(2,1)S(1)}, bf16[128,768]{1,0:T(8,128)(2,1)S(1)}, u32[]{:S(2)}, u32[]{:S(2)}) %collective-permute-start) | collective-permute-done | bytes 196640 | tf_op jit(solution)/shard_map/ppermute | solution.py:62
  7.6 2.8 %collective-permute-done.1.refs_3_ = bf16[128,768]{1,0:T(8,128)(2,1)S(1)} collective-permute-done((bf16[128,768]{1,0:T(8,128)(2,1)S(1)}, bf16[128,768]{1,0:T(8,128)(2,1)S(1)}, u32[]{:S(2)}, u32[]{:S(2)}) %collective-permute-start.1) | collective-permute-done | bytes 196640 | tf_op jit(solution)/shard_map/ppermute | solution.py:62
  10.4 2.0 %collective-permute-start.2 = (bf16[256,768]{1,0:T(8,128)(2,1)S(1)}, bf16[256,768]{1,0:T(8,128)(2,1)S(1)}, u32[]{:S(2)}, u32[]{:S(2)}) collective-permute-start(bf16[256,768]{1,0:T(8,128)(2,1)S(1)} %get-tuple-element.49.refs_0_), channel_id=1, source_target_pairs={{0,1},{1,0},{2,3},{3,2},{4,5},{5,4},{6,7},{7,6},{8,9},{9,8},{10,11... | collective-permute-start | bytes 1179656 | tf_op jit(solution)/shard_map/ppermute | solution.py:62
  12.4 2.5 %collective-permute-start.3 = (bf16[256,768]{1,0:T(8,128)(2,1)S(1)}, bf16[256,768]{1,0:T(8,128)(2,1)S(1)}, u32[]{:S(2)}, u32[]{:S(2)}) collective-permute-start(bf16[256,768]{1,0:T(8,128)(2,1)S(1)} %get-tuple-element.50.refs_2_), channel_id=1, source_target_pairs={{0,3},{1,2},{2,1},{3,0},{4,7},{5,6},{6,5},{7,4},{8,11},{9,10},{10,... | collective-permute-start | bytes 1179656 | tf_op jit(solution)/shard_map/ppermute | solution.py:62
  14.9 4.0 %collective-permute-done.4.refs_1_.token_ref = s32[1,16,256]{2,1,0:T(8,128)S(1)} collective-permute-done((s32[1,16,256]{2,1,0:T(8,128)S(1)}, s32[1,16,256]{2,1,0:T(8,128)S(1)}, u32[]{:S(2)}, u32[]{:S(2)}) %collective-permute-start.4) | collective-permute-done | bytes 16416 | tf_op jit(solution)/shard_map/ppermute | solution.py:62
  19.7 3.1 %collective-permute-done.5.refs_4_.refs_1_ = s32[2,16,256]{2,1,0:T(8,128)S(1)} collective-permute-done((s32[2,16,256]{2,1,0:T(8,128)S(1)}, s32[2,16,256]{2,1,0:T(8,128)S(1)}, u32[]{:S(2)}, u32[]{:S(2)}) %collective-permute-start.5) | collective-permute-done | bytes 32800 | tf_op jit(solution)/shard_map/ppermute | solution.py:62
  22.8 1.3 join.11
  24.1 1.9 collective-permute-start.6
  26.2 2.2 %pick_rows.2 = bf16[1024,768]{1,0:T(8,128)(2,1)} custom-call(s32[1,1024]{1,0:T(1,128)S(1)} %reshape.35.pick_ref, bf16[256,768]{1,0:T(8,128)(2,1)S(1)} %copy-done.6, bf16[256,768]{1,0:T(8,128)(2,1)S(1)} %copy-done.2, s32[1,16,256]{2,1,0:T(8,128)S(1)} %collective-permute-done.4.refs_1_.token_ref), custom_call_target="tpu_custom_call" | custom-call | flops 1 | bytes 1 | tf_op jit(solution)/shard_map/pick_rows/pallas_call | solution.py:164
  28.4 8.4 %all-to-all-start = ((bf16[128,8,768]{2,1,0:T(8,128)(2,1)}), bf16[128,8,768]{2,1,0:T(8,128)(2,1)}, u32[]{:S(2)}, u32[]{:S(2)}) async-start(bf16[128,8,768]{2,1,0:T(8,128)(2,1)} %bitcast.8), calls=%async_computation | async-start | bytes 3145728 | tf_op jit(solution)/shard_map/all_to_all | solution.py:153
  36.9 8.0 %cite_table.1.refs_4_.table_ref.refs_6_ = bf16[256,4096]{1,0:T(8,128)(2,1)S(1)} custom-call(s32[3]{0:T(128)S(1)} %pad_add_fusion.1.place_ref, s32[256,16]{1,0:T(8,128)S(1)} %copy.22.nbr_ref, bf16[512,768]{1,0:T(8,128)(2,1)} %get-tuple-element.51.token_ref.refs_0_), custom_call_target="tpu_custom_call" | custom-call | flops 1 | bytes 1 | tf_op jit(solution)/shard_map/cite_table/pallas_call | solution.py:106
  45.0 3.6 %join.12 = (bf16[1024,768]{1,0:T(8,128)(2,1)}, bf16[1024,768]{1,0:T(8,128)(2,1)}) custom-call(bf16[512,768]{1,0:T(8,128)(2,1)} %get-tuple-element.51.token_ref.refs_0_, bf16[512,768]{1,0:T(8,128)(2,1)} %collective-permute-done.6.refs_1_, bf16[512,768]{1,0:T(8,128)(2,1)} %get-tuple-element.52.refs_2_, bf16[512,768]{1,0:T(8,128)(2,1)} %collective-permute-done.7.refs_3_, ...), custom_call_target="tpu_custom_call" | custom-call | tf_op jit(solution)/shard_map/join/pallas_call | solution.py:47
  48.6 2.8 %collective-permute-start.8 = (bf16[1024,768]{1,0:T(8,128)(2,1)}, bf16[1024,768]{1,0:T(8,128)(2,1)}, u32[]{:S(2)}, u32[]{:S(2)}) collective-permute-start(bf16[1024,768]{1,0:T(8,128)(2,1)} %get-tuple-element.53.b0.refs_7_), channel_id=1, source_target_pairs={{0,3},{1,2},{2,1},{3,0},{4,7},{5,6},{6,5},{7,4},{8,11},{9,10},{10,... | collective-permute-start | bytes 4718600 | tf_op jit(solution)/shard_map/ppermute | solution.py:62
  53.1 7.7 %all-to-all-done = bf16[128,8,768]{2,1,0:T(8,128)(2,1)} async-done(((bf16[128,8,768]{2,1,0:T(8,128)(2,1)}), bf16[128,8,768]{2,1,0:T(8,128)(2,1)}, u32[]{:S(2)}, u32[]{:S(2)}) %all-to-all-start) | async-done | bytes 1572896 | tf_op jit(solution)/shard_map/all_to_all | solution.py:153
  60.9 8.3 %author_step.1 = (bf16[256,1024]{1,0:T(8,128)(2,1)}, bf16[256,768]{1,0:T(8,128)(2,1)}, bf16[256,768]{1,0:T(8,128)(2,1)}, bf16[256,1024]{1,0:T(8,128)(2,1)}, bf16...) custom-call(bf16[1024,768]{1,0:T(8,128)(2,1)} %bitcast.9.arrived_ref, ...), custom_call_target="tpu_custom_call" | custom-call | flops 1 | bytes 1 | tf_op jit(solution)/shard_map/author_step/pallas_call | solution.py:233
  69.9 2.4 %collective-permute-done.11.refs_3_ = bf16[256,768]{1,0:T(8,128)(2,1)S(1)} collective-permute-done((bf16[256,768]{1,0:T(8,128)(2,1)S(1)}, bf16[256,768]{1,0:T(8,128)(2,1)S(1)}, u32[]{:S(2)}, u32[]{:S(2)}) %collective-permute-start.11) | collective-permute-done | bytes 393248 | tf_op jit(solution)/shard_map/ppermute | solution.py:176
  72.5 1.0 copy-done.8
  73.5 1.0 copy-done.21
  74.5 1.8 weight_parts.2.token_a
  76.3 1.2 copy-done
  77.5 4.3 %all-to-all-start.1 = ((bf16[4,2,96,1024]{3,2,1,0:T(8,128)(2,1)}), bf16[4,2,96,1024]{3,2,1,0:T(8,128)(2,1)}, u32[]{:S(2)}, u32[]{:S(2)}) async-start(bf16[4,2,96,1024]{3,2,1,0:T(8,128)(2,1)} %copy-done), calls=%async_computation.1 | async-start | bytes 3145728 | tf_op jit(solution)/shard_map/all_to_all | solution.py:521
  82.6 3.2 %first_half.2.first_ref = f32[256,768]{1,0:T(8,128)S(1)} custom-call(bf16[256,4096]{1,0:T(8,128)(2,1)S(1)} %cite_table.1.refs_4_.table_ref.refs_6_, bf16[1024,768]{1,0:T(8,128)(2,1)} %get-tuple-element.53.b0.refs_7_, bf16[1024,768]{1,0:T(8,128)(2,1)} %get-tuple-element.54.b1), custom_call_target="tpu_custom_call" | custom-call | flops 1 | bytes 1 | tf_op jit(solution)/shard_map/first_half/pallas_call | solution.py:256
  85.8 1.9 collective-permute-done.13.token_b.refs_1_
  87.8 5.2 %paper_step.1 = (bf16[256,1024]{1,0:T(8,128)(2,1)}, bf16[256,1792]{1,0:T(8,128)(2,1)S(1)}, bf16[256,768]{1,0:T(8,128)(2,1)S(1)}) custom-call(bf16[256,4096]{1,0:T(8,128)(2,1)S(1)} %cite_table.1.refs_4_.table_ref.refs_6_, bf16[1024,768]{1,0:T(8,128)(2,1)} %collective-permute-done.8.b0, bf16[1024,768]{1,0:T(8,128)(2,1)} %collective-permute-done.9.b1, ...), custom_call_target="tpu_custom_call" | custom-call | flops 1 | bytes 1 | tf_op jit(solution)/shard_map/paper_step/pallas_call | solution.py:326
  93.8 1.5 collective-permute-start.16
  96.1 0.9 collective-permute-start.14
  97.0 1.7 edge_back.1
  98.8 3.2 %weight_parts.3 = (bf16[3,96,512]{2,1,0:T(8,128)(2,1)S(1)}, bf16[3,96,512]{2,1,0:T(8,128)(2,1)}, bf16[3,96,512]{2,1,0:T(8,128)(2,1)S(1)}, bf16[3,96,512]{2,1,0:T...) custom-call(s32[3]{0:T(128)S(1)} %pad_add_fusion.1.place_ref, ...), custom_call_target="tpu_custom_call" | custom-call | flops 1 | bytes 1 | tf_op jit(solution)/shard_map/weight_parts/pallas_call | solution.py:386
  104.5 2.0 %collective-permute-start.21 = (bf16[256,768]{1,0:T(8,128)(2,1)S(1)}, bf16[256,768]{1,0:T(8,128)(2,1)S(1)}, u32[]{:S(2)}, u32[]{:S(2)}) collective-permute-start(bf16[256,768]{1,0:T(8,128)(2,1)S(1)} %get-tuple-element.67.refs_2_), channel_id=1, source_target_pairs={{0,3},{1,2},{2,1},{3,0},{4,7},{5,6},{6,5},{7,4},{8,11},{9,10},{10,... | collective-permute-start | bytes 1179656 | tf_op jit(solution)/shard_map/ppermute | solution.py:62
  106.5 2.0 %collective-permute-start.22 = (bf16[3,96,512]{2,1,0:T(8,128)(2,1)}, bf16[3,96,512]{2,1,0:T(8,128)(2,1)S(1)}, u32[]{:S(2)}, u32[]{:S(2)}) collective-permute-start(bf16[3,96,512]{2,1,0:T(8,128)(2,1)} %get-tuple-element.68), channel_id=1, source_target_pairs={{0,32},{16,48},{32,64},{48,80},{64,96},{80,112},{96,0},{112,16},{1... | collective-permute-start | bytes 884744 | tf_op jit(solution)/shard_map/ppermute | solution.py:183
  108.5 2.7 %collective-permute-start.23 = (bf16[3,96,512]{2,1,0:T(8,128)(2,1)S(1)}, bf16[3,96,512]{2,1,0:T(8,128)(2,1)S(1)}, u32[]{:S(2)}, u32[]{:S(2)}) collective-permute-start(bf16[3,96,512]{2,1,0:T(8,128)(2,1)S(1)} %copy-done.36), channel_id=1, source_target_pairs={{0,64},{16,80},{32,96},{48,112},{64,0},{80,16},{96,32},{112,48},{1... | collective-permute-start | bytes 884744 | tf_op jit(solution)/shard_map/ppermute | solution.py:183
  111.2 1.4 collective-permute-start.24
  112.6 4.3 %collective-permute-done.22.refs_4_.refs_1_ = bf16[3,96,512]{2,1,0:T(8,128)(2,1)S(1)} collective-permute-done((bf16[3,96,512]{2,1,0:T(8,128)(2,1)}, bf16[3,96,512]{2,1,0:T(8,128)(2,1)S(1)}, u32[]{:S(2)}, u32[]{:S(2)}) %collective-permute-start.22) | collective-permute-done | bytes 294944 | tf_op jit(solution)/shard_map/ppermute | solution.py:183
  116.9 5.8 %collective-permute-done.23.refs_5_.refs_2_ = bf16[3,96,512]{2,1,0:T(8,128)(2,1)S(1)} collective-permute-done((bf16[3,96,512]{2,1,0:T(8,128)(2,1)S(1)}, bf16[3,96,512]{2,1,0:T(8,128)(2,1)S(1)}, u32[]{:S(2)}, u32[]{:S(2)}) %collective-permute-start.23) | collective-permute-done | bytes 294944 | tf_op jit(solution)/shard_map/ppermute | solution.py:183
  122.7 1.1 join.16
  123.8 2.1 %collective-permute-start.25 = (bf16[512,768]{1,0:T(8,128)(2,1)S(1)}, bf16[512,768]{1,0:T(8,128)(2,1)}, u32[]{:S(2)}, u32[]{:S(2)}) collective-permute-start(bf16[512,768]{1,0:T(8,128)(2,1)S(1)} %get-tuple-element.71.token_ref.refs_0_), channel_id=1, source_target_pairs={{0,12},{1,13},{2,14},{3,15},{4,8},{5,9},{6,10},{7,11},{8,4},{9,5},... | collective-permute-start | bytes 2359304 | tf_op jit(solution)/shard_map/ppermute | solution.py:62
  126.2 0.9 collective-permute-start.27
  127.2 2.4 %collective-permute-start.28 = (bf16[3,96,512]{2,1,0:T(8,128)(2,1)}, bf16[3,96,512]{2,1,0:T(8,128)(2,1)}, u32[]{:S(2)}, u32[]{:S(2)}) collective-permute-start(bf16[3,96,512]{2,1,0:T(8,128)(2,1)} %get-tuple-element.74), channel_id=1, source_target_pairs={{0,64},{16,80},{32,96},{48,112},{64,0},{80,16},{96,32},{112,48},{1... | collective-permute-start | bytes 884744 | tf_op jit(solution)/shard_map/ppermute | solution.py:183
  129.6 1.8 collective-permute-start.29
  131.3 2.2 %pick_rows.3 = bf16[1024,768]{1,0:T(8,128)(2,1)} custom-call(s32[1,1024]{1,0:T(1,128)S(1)} %reshape.35.pick_ref, bf16[256,768]{1,0:T(8,128)(2,1)S(1)} %copy-done.28, bf16[256,768]{1,0:T(8,128)(2,1)S(1)} %get-tuple-element.64.refs_8_.b_ref, bf16[256,768]{1,0:T(8,128)(2,1)S(1)} %get-tuple-element.66.refs_0_.token_ref), custom_call_target="tpu_custom_call" | custom-call | flops 1 | bytes 1 | tf_op jit(solution)/shard_map/pick_rows/pallas_call | solution.py:164
  133.5 6.6 %all-to-all-start.2 = ((bf16[128,8,768]{2,1,0:T(8,128)(2,1)}), bf16[128,8,768]{2,1,0:T(8,128)(2,1)}, u32[]{:S(2)}, u32[]{:S(2)}) async-start(bf16[128,8,768]{2,1,0:T(8,128)(2,1)} %bitcast.10), calls=%async_computation.2 | async-start | bytes 3145728 | tf_op jit(solution)/shard_map/all_to_all | solution.py:153
  141.9 4.0 %cited_by_table.1.refs_4_.table_ref = bf16[256,4096]{1,0:T(8,128)(2,1)S(1)} custom-call(s32[3]{0:T(128)S(1)} %pad_add_fusion.1.place_ref, s32[8,16,256]{2,1,0:T(8,128)S(1)} %copy-done.25, s32[8,16,256]{2,1,0:T(8,128)S(1)} %copy-done.23, bf16[512,768]{1,0:T(8,128)(2,1)S(1)} %get-tuple-element.71.token_ref.refs_0_), custom_call_target="tpu_custom_call" | custom-call | flops 1 | bytes 1 | tf_op jit(solution)/shard_map/cited_by_table/pallas_call | solution.py:132
  146.0 3.5 %join.17 = (bf16[1024,768]{1,0:T(8,128)(2,1)}, bf16[1024,768]{1,0:T(8,128)(2,1)}) custom-call(bf16[512,768]{1,0:T(8,128)(2,1)S(1)} %get-tuple-element.71.token_ref.refs_0_, bf16[512,768]{1,0:T(8,128)(2,1)} %collective-permute-done.25.refs_1_, bf16[512,768]{1,0:T(8,128)(2,1)} %get-tuple-element.72.refs_2_, bf16[512,768]{1,0:T(8,128)(2,1)} %collective-permute-done.26.refs_3_, ...), custom_call_target="tpu_custom_call" | custom-call | tf_op jit(solution)/shard_map/join/pallas_call | solution.py:47
  149.5 2.8 %collective-permute-start.30 = (bf16[1024,768]{1,0:T(8,128)(2,1)}, bf16[1024,768]{1,0:T(8,128)(2,1)}, u32[]{:S(2)}, u32[]{:S(2)}) collective-permute-start(bf16[1024,768]{1,0:T(8,128)(2,1)} %get-tuple-element.76.b0), channel_id=1, source_target_pairs={{0,3},{1,2},{2,1},{3,0},{4,7},{5,6},{6,5},{7,4},{8,11},{9,10},{10,... | collective-permute-start | bytes 4718600 | tf_op jit(solution)/shard_map/ppermute | solution.py:62
  152.3 3.3 %y_sum.1 = (bf16[256,512]{1,0:T(8,128)(2,1)S(1)}, bf16[256,512]{1,0:T(8,128)(2,1)}, bf16[256,512]{1,0:T(8,128)(2,1)}, bf16[256,512]{1,0:T(8,128)(2,1)}) custom-call(s32[3]{0:T(128)S(1)} %pad_add_fusion.1.place_ref, bf16[3,96,512]{2,1,0:T(8,128)(2,1)S(1)} %copy-done.14, bf16[3,96,512]{2,1,0:T(8,128)(2,1)S(1)} %collective-permute-done.22.refs_4_.refs_1_, ...), custom_call_target="tpu_custom_call" | custom-call | flops 1 | bytes 1 | tf_op jit(solution)/shard_map/y_sum/pallas_call | solution.py:418
  156.3 1.5 collective-permute-start.32
  157.8 2.7 %collective-permute-start.33 = (bf16[256,512]{1,0:T(8,128)(2,1)}, bf16[256,512]{1,0:T(8,128)(2,1)S(1)}, u32[]{:S(2)}, u32[]{:S(2)}) collective-permute-start(bf16[256,512]{1,0:T(8,128)(2,1)} %get-tuple-element.87), channel_id=1, source_target_pairs={{0,8},{1,9},{2,10},{3,11},{4,12},{5,13},{6,14},{7,15},{8,0},{9,1},... | collective-permute-start | bytes 786440 | tf_op jit(solution)/shard_map/ppermute | solution.py:462
  160.5 1.5 collective-permute-start.34
  162.0 2.9 %first_half.3.first_ref.token_a = f32[256,768]{1,0:T(8,128)S(1)} custom-call(bf16[256,4096]{1,0:T(8,128)(2,1)S(1)} %cited_by_table.1.refs_4_.table_ref, bf16[1024,768]{1,0:T(8,128)(2,1)} %get-tuple-element.76.b0, bf16[1024,768]{1,0:T(8,128)(2,1)} %get-tuple-element.77.b1), custom_call_target="tpu_custom_call" | custom-call | flops 1 | bytes 1 | tf_op jit(solution)/shard_map/first_half/pallas_call | solution.py:256
  164.8 1.2 copy-done.15
  166.1 1.1 copy-done.17
  167.2 1.1 copy-done.19
  168.3 3.2 %edge_add.1 = (bf16[256,768]{1,0:T(8,128)(2,1)}, f32[256,768]{1,0:T(8,128)S(1)}) custom-call(bf16[512,1024]{1,0:T(8,128)(2,1)S(1)} %copy-done.15, bf16[1024,768]{1,0:T(8,128)(2,1)} %bitcast.11.back_ref, f32[256,768]{1,0:T(8,128)S(1)} %copy-done.17, f32[256,768]{1,0:T(8,128)S(1)} %copy-done.19), custom_call_target="tpu_custom_call" | custom-call | flops 1 | bytes 1 | tf_op jit(solution)/shard_map/edge_add/pallas_call | solution.py:291
  171.5 2.0 %collective-permute-done.33.refs_2_ = bf16[256,512]{1,0:T(8,128)(2,1)S(1)} collective-permute-done((bf16[256,512]{1,0:T(8,128)(2,1)}, bf16[256,512]{1,0:T(8,128)(2,1)S(1)}, u32[]{:S(2)}, u32[]{:S(2)}) %collective-permute-start.33) | collective-permute-done | bytes 262176 | tf_op jit(solution)/shard_map/ppermute | solution.py:462
  173.6 1.0 copy-done.27
  174.6 1.2 x_sum.1
  175.7 2.1 %collective-permute-start.35 = (f32[64,512]{1,0:T(8,128)S(1)}, f32[64,512]{1,0:T(8,128)S(1)}, u32[]{:S(2)}, u32[]{:S(2)}) collective-permute-start(f32[64,512]{1,0:T(8,128)S(1)} %get-tuple-element.90), channel_id=1, source_target_pairs={{0,1},{1,2},{2,3},{3,0},{4,5},{5,6},{6,7},{7,4},{8,9},{9,10},{10,1... | collective-permute-start | bytes 393224 | tf_op jit(solution)/shard_map/ppermute | solution.py:462
  178.1 2.4 %collective-permute-start.37 = (f32[64,512]{1,0:T(8,128)S(1)}, f32[64,512]{1,0:T(8,128)S(1)}, u32[]{:S(2)}, u32[]{:S(2)}) collective-permute-start(f32[64,512]{1,0:T(8,128)S(1)} %get-tuple-element.92), channel_id=1, source_target_pairs={{0,3},{1,0},{2,1},{3,2},{4,7},{5,4},{6,5},{7,6},{8,11},{9,8},{10,9... | collective-permute-start | bytes 393224 | tf_op jit(solution)/shard_map/ppermute | solution.py:462
  180.6 4.6 %collective-permute-done.35.refs_1_ = f32[64,512]{1,0:T(8,128)S(1)} collective-permute-done((f32[64,512]{1,0:T(8,128)S(1)}, f32[64,512]{1,0:T(8,128)S(1)}, u32[]{:S(2)}, u32[]{:S(2)}) %collective-permute-start.35) | collective-permute-done | bytes 131104 | tf_op jit(solution)/shard_map/ppermute | solution.py:462
  185.1 1.6 collective-permute-done.36.refs_2_
  187.6 3.6 %last_half.1 = bf16[256,768]{1,0:T(8,128)(2,1)} custom-call(bf16[256,4096]{1,0:T(8,128)(2,1)S(1)} %cited_by_table.1.refs_4_.table_ref, bf16[1024,768]{1,0:T(8,128)(2,1)} %collective-permute-done.30.b0, bf16[1024,768]{1,0:T(8,128)(2,1)} %collective-permute-done.31.b1, f32[256,768]{1,0:T(8,128)S(1)} %first_half.3.first_ref.token_a, ...), custom_call_target="tpu_custom_call" | custom-call | flops 1 | bytes 1 | tf_op jit(solution)/shard_map/last_half/pallas_call | solution.py:273
  (135 shorter events, 12.5 us)
Async XLA Ops:
  0.6 25.5 %copy-start.2 = (bf16[256,768]{1,0:T(8,128)(2,1)S(1)}, bf16[256,768]{1,0:T(8,128)(2,1)}, u32[]{:S(2)}) copy-start(bf16[256,768]{1,0:T(8,128)(2,1)} %refs_2_.5) | copy-start | bytes 1179652
  0.6 14.3 %copy-start.34 = (s32[256,16]{0,1:T(8,128)S(1)}, s32[256,16]{0,1:T(8,128)}, u32[]{:S(2)}) copy-start(s32[256,16]{0,1:T(8,128)} %param.14) | copy-start | bytes 49156
  0.7 19.0 %copy-start.37 = (s32[1,128,4]{1,2,0:T(4,128)S(1)}, s32[1,128,4]{1,2,0:T(4,128)}, u32[]{:S(2)}) copy-start(s32[1,128,4]{1,2,0:T(4,128)} %param.16) | copy-start | bytes 6148
  0.7 25.3 %copy-start.38 = (s32[1,128,4]{1,2,0:T(4,128)S(1)}, s32[1,128,4]{1,2,0:T(4,128)}, u32[]{:S(2)}) copy-start(s32[1,128,4]{1,2,0:T(4,128)} %param.15) | copy-start | bytes 6148
  0.7 25.5 %copy-start.6 = (bf16[256,768]{1,0:T(8,128)(2,1)S(1)}, bf16[256,768]{1,0:T(8,128)(2,1)}, u32[]{:S(2)}) copy-start(bf16[256,768]{1,0:T(8,128)(2,1)} %refs_2_.4) | copy-start | bytes 1179652
  1.8 5.7 %collective-permute-start = (bf16[128,768]{1,0:T(8,128)(2,1)S(1)}, bf16[128,768]{1,0:T(8,128)(2,1)S(1)}, u32[]{:S(2)}, u32[]{:S(2)}) collective-permute-start(bf16[128,768]{1,0:T(8,128)(2,1)S(1)} %get-tuple-element.96.refs_0_), channel_id=1, source_target_pairs={{0,4},{1,5},{2,6},{3,7},{4,0},{5,1},{6,2},{7,3},{8,12},{9,13},{10,... | collective-permute-start | bytes 589832 | tf_op jit(solution)/shard_map/ppermute | solution.py:62
  3.5 6.9 %collective-permute-start.1 = (bf16[128,768]{1,0:T(8,128)(2,1)S(1)}, bf16[128,768]{1,0:T(8,128)(2,1)S(1)}, u32[]{:S(2)}, u32[]{:S(2)}) collective-permute-start(bf16[128,768]{1,0:T(8,128)(2,1)S(1)} %get-tuple-element.95.refs_2_), channel_id=1, source_target_pairs={{0,12},{1,13},{2,14},{3,15},{4,8},{5,9},{6,10},{7,11},{8,4},{9,5},... | collective-permute-start | bytes 589832 | tf_op jit(solution)/shard_map/ppermute | solution.py:62
  10.4 12.4 %collective-permute-start.2 = (bf16[256,768]{1,0:T(8,128)(2,1)S(1)}, bf16[256,768]{1,0:T(8,128)(2,1)S(1)}, u32[]{:S(2)}, u32[]{:S(2)}) collective-permute-start(bf16[256,768]{1,0:T(8,128)(2,1)S(1)} %get-tuple-element.49.refs_0_), channel_id=1, source_target_pairs={{0,1},{1,0},{2,3},{3,2},{4,5},{5,4},{6,7},{7,6},{8,9},{9,8},{10,11... | collective-permute-start | bytes 1179656 | tf_op jit(solution)/shard_map/ppermute | solution.py:62
  12.4 10.4 %collective-permute-start.3 = (bf16[256,768]{1,0:T(8,128)(2,1)S(1)}, bf16[256,768]{1,0:T(8,128)(2,1)S(1)}, u32[]{:S(2)}, u32[]{:S(2)}) collective-permute-start(bf16[256,768]{1,0:T(8,128)(2,1)S(1)} %get-tuple-element.50.refs_2_), channel_id=1, source_target_pairs={{0,3},{1,2},{2,1},{3,0},{4,7},{5,6},{6,5},{7,4},{8,11},{9,10},{10,... | collective-permute-start | bytes 1179656 | tf_op jit(solution)/shard_map/ppermute | solution.py:62
  14.9 4.0 %collective-permute-start.4 = (s32[1,16,256]{2,1,0:T(8,128)S(1)}, s32[1,16,256]{2,1,0:T(8,128)S(1)}, u32[]{:S(2)}, u32[]{:S(2)}) collective-permute-start(s32[1,16,256]{2,1,0:T(8,128)S(1)} %bitcast.14), channel_id=1, source_target_pairs={{0,4},{1,5},{2,6},{3,7},{4,0},{5,1},{6,2},{7,3},{8,12},{9,13},{10,... | collective-permute-start | bytes 49160 | tf_op jit(solution)/shard_map/ppermute | solution.py:62
  18.9 3.9 %collective-permute-start.5 = (s32[2,16,256]{2,1,0:T(8,128)S(1)}, s32[2,16,256]{2,1,0:T(8,128)S(1)}, u32[]{:S(2)}, u32[]{:S(2)}) collective-permute-start(s32[2,16,256]{2,1,0:T(8,128)S(1)} %join.10.refs_0_), channel_id=1, source_target_pairs={{0,1},{1,0},{2,3},{3,2},{4,5},{5,4},{6,7},{7,6},{8,9},{9,8},{10,11... | collective-permute-start | bytes 98312 | tf_op jit(solution)/shard_map/ppermute | solution.py:62
  24.1 20.9 %collective-permute-start.6 = (bf16[512,768]{1,0:T(8,128)(2,1)}, bf16[512,768]{1,0:T(8,128)(2,1)}, u32[]{:S(2)}, u32[]{:S(2)}) collective-permute-start(bf16[512,768]{1,0:T(8,128)(2,1)} %get-tuple-element.51.token_ref.refs_0_), channel_id=1, source_target_pairs={{0,12},{1,13},{2,14},{3,15},{4,8},{5,9},{6,10},{7,11},{8,4},{9,5},... | collective-permute-start | bytes 2359304 | tf_op jit(solution)/shard_map/ppermute | solution.py:62
  25.9 19.1 %collective-permute-start.7 = (bf16[512,768]{1,0:T(8,128)(2,1)}, bf16[512,768]{1,0:T(8,128)(2,1)}, u32[]{:S(2)}, u32[]{:S(2)}) collective-permute-start(bf16[512,768]{1,0:T(8,128)(2,1)} %get-tuple-element.52.refs_2_), channel_id=1, source_target_pairs={{0,4},{1,5},{2,6},{3,7},{4,0},{5,1},{6,2},{7,3},{8,12},{9,13},{10,... | collective-permute-start | bytes 2359304 | tf_op jit(solution)/shard_map/ppermute | solution.py:62
  28.4 32.5 %all-to-all-start = ((bf16[128,8,768]{2,1,0:T(8,128)(2,1)}), bf16[128,8,768]{2,1,0:T(8,128)(2,1)}, u32[]{:S(2)}, u32[]{:S(2)}) async-start(bf16[128,8,768]{2,1,0:T(8,128)(2,1)} %bitcast.8), calls=%async_computation | async-start | bytes 3145728 | tf_op jit(solution)/shard_map/all_to_all | solution.py:153
  48.6 39.0 %collective-permute-start.8 = (bf16[1024,768]{1,0:T(8,128)(2,1)}, bf16[1024,768]{1,0:T(8,128)(2,1)}, u32[]{:S(2)}, u32[]{:S(2)}) collective-permute-start(bf16[1024,768]{1,0:T(8,128)(2,1)} %get-tuple-element.53.b0.refs_7_), channel_id=1, source_target_pairs={{0,3},{1,2},{2,1},{3,0},{4,7},{5,6},{6,5},{7,4},{8,11},{9,10},{10,... | collective-permute-start | bytes 4718600 | tf_op jit(solution)/shard_map/ppermute | solution.py:62
  51.4 36.2 %collective-permute-start.9 = (bf16[1024,768]{1,0:T(8,128)(2,1)}, bf16[1024,768]{1,0:T(8,128)(2,1)}, u32[]{:S(2)}, u32[]{:S(2)}) collective-permute-start(bf16[1024,768]{1,0:T(8,128)(2,1)} %get-tuple-element.54.b1), channel_id=1, source_target_pairs={{0,1},{1,0},{2,3},{3,2},{4,5},{5,4},{6,7},{7,6},{8,9},{9,8},{10,11... | collective-permute-start | bytes 4718600 | tf_op jit(solution)/shard_map/ppermute | solution.py:62
  60.9 8.4 %copy-start.7 = (bf16[256,768]{1,0:T(8,128)(2,1)S(1)}, bf16[256,768]{1,0:T(8,128)(2,1)}, u32[]{:S(2)}) copy-start(bf16[256,768]{1,0:T(8,128)(2,1)} %refs_2_.4) | copy-start | bytes 1179652
  69.2 3.3 %collective-permute-start.10 = (bf16[256,1024]{1,0:T(8,128)(2,1)}, bf16[256,1024]{1,0:T(8,128)(2,1)S(1)}, u32[]{:S(2)}, u32[]{:S(2)}) collective-permute-start(bf16[256,1024]{1,0:T(8,128)(2,1)} %get-tuple-element.56.refs_0_), channel_id=1, source_target_pairs={{0,16},{16,0},{32,48},{48,32},{64,80},{80,64},{96,112},{112,96},{1... | collective-permute-start | bytes 1572872 | tf_op jit(solution)/shard_map/ppermute | solution.py:176
  69.3 3.0 %collective-permute-start.11 = (bf16[256,768]{1,0:T(8,128)(2,1)S(1)}, bf16[256,768]{1,0:T(8,128)(2,1)S(1)}, u32[]{:S(2)}, u32[]{:S(2)}) collective-permute-start(bf16[256,768]{1,0:T(8,128)(2,1)S(1)} %copy-done.7), channel_id=1, source_target_pairs={{0,16},{16,0},{32,48},{48,32},{64,80},{80,64},{96,112},{112,96},{1... | collective-permute-start | bytes 1179656 | tf_op jit(solution)/shard_map/ppermute | solution.py:176
  69.8 2.7 %collective-permute-start.12 = (bf16[256,768]{1,0:T(8,128)(2,1)}, bf16[256,768]{1,0:T(8,128)(2,1)S(1)}, u32[]{:S(2)}, u32[]{:S(2)}) collective-permute-start(bf16[256,768]{1,0:T(8,128)(2,1)} %get-tuple-element.57.refs_4_.token_c), channel_id=1, source_target_pairs={{0,16},{16,0},{32,48},{48,32},{64,80},{80,64},{96,112},{112,96},{1... | collective-permute-start | bytes 1179656 | tf_op jit(solution)/shard_map/ppermute | solution.py:176
  77.5 26.0 %all-to-all-start.1 = ((bf16[4,2,96,1024]{3,2,1,0:T(8,128)(2,1)}), bf16[4,2,96,1024]{3,2,1,0:T(8,128)(2,1)}, u32[]{:S(2)}, u32[]{:S(2)}) async-start(bf16[4,2,96,1024]{3,2,1,0:T(8,128)(2,1)} %copy-done), calls=%async_computation.1 | async-start | bytes 3145728 | tf_op jit(solution)/shard_map/all_to_all | solution.py:521
  81.9 5.8 %copy-start.1 = (bf16[4,2,96,1024]{3,2,1,0:T(8,128)(2,1)S(1)}, bf16[4,2,96,1024]{3,2,1,0:T(8,128)(2,1)}, u32[]{:S(2)}) copy-start(bf16[4,2,96,1024]{3,2,1,0:T(8,128)(2,1)} %copy-done) | copy-start | bytes 4718596
  81.9 5.8 %copy-start.9 = (bf16[256,768]{1,0:T(8,128)(2,1)S(1)}, bf16[256,768]{1,0:T(8,128)(2,1)}, u32[]{:S(2)}) copy-start(bf16[256,768]{1,0:T(8,128)(2,1)} %get-tuple-element.57.refs_4_.token_c) | copy-start | bytes 1179652
  81.9 5.8 %copy-start.10 = (bf16[768,1024]{1,0:T(8,128)(2,1)S(1)}, bf16[768,1024]{1,0:T(8,128)(2,1)}, u32[]{:S(2)}) copy-start(bf16[768,1024]{1,0:T(8,128)(2,1)} %w_hbm.1) | copy-start | bytes 4718596
  81.9 5.8 %copy-start.16 = (f32[256,1024]{1,0:T(8,128)S(1)}, f32[256,1024]{1,0:T(8,128)}, u32[]{:S(2)}) copy-start(f32[256,1024]{1,0:T(8,128)} %get-tuple-element.55.pre_ref) | copy-start | bytes 3145732
  81.9 5.8 %copy-start.20 = (bf16[256,1024]{1,0:T(8,128)(2,1)S(1)}, bf16[256,1024]{1,0:T(8,128)(2,1)}, u32[]{:S(2)}) copy-start(bf16[256,1024]{1,0:T(8,128)(2,1)} %grad_hbm.1) | copy-start | bytes 1572868
  81.9 5.7 %collective-permute-start.13 = (s32[4,16,256]{2,1,0:T(8,128)S(1)}, s32[4,16,256]{2,1,0:T(8,128)S(1)}, u32[]{:S(2)}, u32[]{:S(2)}) collective-permute-start(s32[4,16,256]{2,1,0:T(8,128)S(1)} %join.13.refs_0_), channel_id=1, source_target_pairs={{0,12},{1,13},{2,14},{3,15},{4,8},{5,9},{6,10},{7,11},{8,4},{9,5},... | collective-permute-start | bytes 196616 | tf_op jit(solution)/shard_map/ppermute | solution.py:62
  87.7 5.4 %copy-start.3 = (bf16[256,768]{1,0:T(8,128)(2,1)S(1)}, bf16[256,768]{1,0:T(8,128)(2,1)}, u32[]{:S(2)}) copy-start(bf16[256,768]{1,0:T(8,128)(2,1)} %refs_2_.5) | copy-start | bytes 1179652
  87.7 5.9 %copy-start.26 = (bf16[256,768]{1,0:T(8,128)(2,1)S(1)}, bf16[256,768]{1,0:T(8,128)(2,1)}, u32[]{:S(2)}) copy-start(bf16[256,768]{1,0:T(8,128)(2,1)} %get-tuple-element.62.refs_6_) | copy-start | bytes 1179652
  87.7 9.3 %copy-start.4 = (bf16[768,1024]{1,0:T(8,128)(2,1)S(1)}, bf16[768,1024]{1,0:T(8,128)(2,1)}, u32[]{:S(2)}) copy-start(bf16[768,1024]{1,0:T(8,128)(2,1)} %w_sp_hbm.1) | copy-start | bytes 4718596
  87.7 9.3 %copy-start.5 = (bf16[768,1024]{1,0:T(8,128)(2,1)S(1)}, bf16[768,1024]{1,0:T(8,128)(2,1)}, u32[]{:S(2)}) copy-start(bf16[768,1024]{1,0:T(8,128)(2,1)} %w_wr_hbm.1) | copy-start | bytes 4718596
  87.8 9.3 %copy-start.31 = (f32[512,128]{1,0:T(8,128)S(1)}, f32[512,128]{1,0:T(8,128)}, u32[]{:S(2)}) copy-start(f32[512,128]{1,0:T(8,128)} %get-tuple-element.63.cnt_ref) | copy-start | bytes 786436
  93.0 5.8 %collective-permute-start.17 = (bf16[256,1792]{1,0:T(8,128)(2,1)S(1)}, bf16[256,1792]{1,0:T(8,128)(2,1)S(1)}, u32[]{:S(2)}, u32[]{:S(2)}) collective-permute-start(bf16[256,1792]{1,0:T(8,128)(2,1)S(1)} %get-tuple-element.61.pack_ref.refs_0_.refs_4_), channel_id=1, source_target_pairs={{0,16},{16,0},{32,48},{48,32},{64,80},{80,64},{96,112},{112,96},{1... | collective-permute-start | bytes 2752520 | tf_op jit(solution)/shard_map/ppermute | solution.py:176
  93.1 3.0 %collective-permute-start.18 = (bf16[256,768]{1,0:T(8,128)(2,1)S(1)}, bf16[256,768]{1,0:T(8,128)(2,1)S(1)}, u32[]{:S(2)}, u32[]{:S(2)}) collective-permute-start(bf16[256,768]{1,0:T(8,128)(2,1)S(1)} %copy-done.3), channel_id=1, source_target_pairs={{0,16},{16,0},{32,48},{48,32},{64,80},{80,64},{96,112},{112,96},{1... | collective-permute-start | bytes 1179656 | tf_op jit(solution)/shard_map/ppermute | solution.py:176
  93.6 5.2 %collective-permute-start.19 = (bf16[256,768]{1,0:T(8,128)(2,1)S(1)}, bf16[256,768]{1,0:T(8,128)(2,1)S(1)}, u32[]{:S(2)}, u32[]{:S(2)}) collective-permute-start(bf16[256,768]{1,0:T(8,128)(2,1)S(1)} %copy-done.26), channel_id=1, source_target_pairs={{0,16},{16,0},{32,48},{48,32},{64,80},{80,64},{96,112},{112,96},{1... | collective-permute-start | bytes 1179656 | tf_op jit(solution)/shard_map/ppermute | solution.py:176
  93.7 9.8 %collective-permute-start.15 = (bf16[128,768]{1,0:T(8,128)(2,1)S(1)}, bf16[128,768]{1,0:T(8,128)(2,1)S(1)}, u32[]{:S(2)}, u32[]{:S(2)}) collective-permute-start(bf16[128,768]{1,0:T(8,128)(2,1)S(1)} %get-tuple-element.94.refs_0_), channel_id=1, source_target_pairs={{0,4},{1,5},{2,6},{3,7},{4,0},{5,1},{6,2},{7,3},{8,12},{9,13},{10,... | collective-permute-start | bytes 589832 | tf_op jit(solution)/shard_map/ppermute | solution.py:62
  93.8 9.7 %collective-permute-start.16 = (bf16[128,768]{1,0:T(8,128)(2,1)S(1)}, bf16[128,768]{1,0:T(8,128)(2,1)S(1)}, u32[]{:S(2)}, u32[]{:S(2)}) collective-permute-start(bf16[128,768]{1,0:T(8,128)(2,1)S(1)} %get-tuple-element.93.refs_2_), channel_id=1, source_target_pairs={{0,12},{1,13},{2,14},{3,15},{4,8},{5,9},{6,10},{7,11},{8,4},{9,5},... | collective-permute-start | bytes 589832 | tf_op jit(solution)/shard_map/ppermute | solution.py:62
  96.1 7.4 %collective-permute-start.14 = (s32[8,16,256]{2,1,0:T(8,128)S(1)}, s32[8,16,256]{2,1,0:T(8,128)S(1)}, u32[]{:S(2)}, u32[]{:S(2)}) collective-permute-start(s32[8,16,256]{2,1,0:T(8,128)S(1)} %join.14.a_ref), channel_id=1, source_target_pairs={{0,3},{1,2},{2,1},{3,0},{4,7},{5,6},{6,5},{7,4},{8,11},{9,10},{10,... | collective-permute-start | bytes 393224 | tf_op jit(solution)/shard_map/ppermute | solution.py:62
  103.5 20.3 %copy-start.13 = (bf16[3,96,512]{2,1,0:T(8,128)(2,1)}, bf16[3,96,512]{2,1,0:T(8,128)(2,1)S(1)}, u32[]{:S(2)}) copy-start(bf16[3,96,512]{2,1,0:T(8,128)(2,1)S(1)} %get-tuple-element.65.refs_4_.refs_0_) | copy-start | bytes 884740
  103.5 20.3 %copy-start.22 = (s32[8,16,256]{2,1,0:T(8,128)}, s32[8,16,256]{2,1,0:T(8,128)S(1)}, u32[]{:S(2)}) copy-start(s32[8,16,256]{2,1,0:T(8,128)S(1)} %collective-permute-done.14.refs_5_.b_ref) | copy-start | bytes 393220
  103.6 27.7 %copy-start.28 = (bf16[256,768]{1,0:T(8,128)(2,1)S(1)}, bf16[256,768]{1,0:T(8,128)(2,1)}, u32[]{:S(2)}) copy-start(bf16[256,768]{1,0:T(8,128)(2,1)} %get-tuple-element.79.a_ref) | copy-start | bytes 1179652
  103.6 19.1 %collective-permute-start.20 = (bf16[256,768]{1,0:T(8,128)(2,1)S(1)}, bf16[256,768]{1,0:T(8,128)(2,1)S(1)}, u32[]{:S(2)}, u32[]{:S(2)}) collective-permute-start(bf16[256,768]{1,0:T(8,128)(2,1)S(1)} %get-tuple-element.66.refs_0_.token_ref), channel_id=1, source_target_pairs={{0,1},{1,0},{2,3},{3,2},{4,5},{5,4},{6,7},{7,6},{8,9},{9,8},{10,11... | collective-permute-start | bytes 1179656 | tf_op jit(solution)/shard_map/ppermute | solution.py:62
  104.5 18.3 %collective-permute-start.21 = (bf16[256,768]{1,0:T(8,128)(2,1)S(1)}, bf16[256,768]{1,0:T(8,128)(2,1)S(1)}, u32[]{:S(2)}, u32[]{:S(2)}) collective-permute-start(bf16[256,768]{1,0:T(8,128)(2,1)S(1)} %get-tuple-element.67.refs_2_), channel_id=1, source_target_pairs={{0,3},{1,2},{2,1},{3,0},{4,7},{5,6},{6,5},{7,4},{8,11},{9,10},{10,... | collective-permute-start | bytes 1179656 | tf_op jit(solution)/shard_map/ppermute | solution.py:62
  106.5 10.4 %collective-permute-start.22 = (bf16[3,96,512]{2,1,0:T(8,128)(2,1)}, bf16[3,96,512]{2,1,0:T(8,128)(2,1)S(1)}, u32[]{:S(2)}, u32[]{:S(2)}) collective-permute-start(bf16[3,96,512]{2,1,0:T(8,128)(2,1)} %get-tuple-element.68), channel_id=1, source_target_pairs={{0,32},{16,48},{32,64},{48,80},{64,96},{80,112},{96,0},{112,16},{1... | collective-permute-start | bytes 884744 | tf_op jit(solution)/shard_map/ppermute | solution.py:183
  108.5 14.3 %collective-permute-start.23 = (bf16[3,96,512]{2,1,0:T(8,128)(2,1)S(1)}, bf16[3,96,512]{2,1,0:T(8,128)(2,1)S(1)}, u32[]{:S(2)}, u32[]{:S(2)}) collective-permute-start(bf16[3,96,512]{2,1,0:T(8,128)(2,1)S(1)} %copy-done.36), channel_id=1, source_target_pairs={{0,64},{16,80},{32,96},{48,112},{64,0},{80,16},{96,32},{112,48},{1... | collective-permute-start | bytes 884744 | tf_op jit(solution)/shard_map/ppermute | solution.py:183
  111.2 11.6 %collective-permute-start.24 = (bf16[3,96,512]{2,1,0:T(8,128)(2,1)S(1)}, bf16[3,96,512]{2,1,0:T(8,128)(2,1)S(1)}, u32[]{:S(2)}, u32[]{:S(2)}) collective-permute-start(bf16[3,96,512]{2,1,0:T(8,128)(2,1)S(1)} %get-tuple-element.70), channel_id=1, source_target_pairs={{0,96},{16,112},{32,0},{48,16},{64,32},{80,48},{96,64},{112,80},{1... | collective-permute-start | bytes 884744 | tf_op jit(solution)/shard_map/ppermute | solution.py:183
  123.8 22.2 %collective-permute-start.25 = (bf16[512,768]{1,0:T(8,128)(2,1)S(1)}, bf16[512,768]{1,0:T(8,128)(2,1)}, u32[]{:S(2)}, u32[]{:S(2)}) collective-permute-start(bf16[512,768]{1,0:T(8,128)(2,1)S(1)} %get-tuple-element.71.token_ref.refs_0_), channel_id=1, source_target_pairs={{0,12},{1,13},{2,14},{3,15},{4,8},{5,9},{6,10},{7,11},{8,4},{9,5},... | collective-permute-start | bytes 2359304 | tf_op jit(solution)/shard_map/ppermute | solution.py:62
  125.9 20.1 %collective-permute-start.26 = (bf16[512,768]{1,0:T(8,128)(2,1)}, bf16[512,768]{1,0:T(8,128)(2,1)}, u32[]{:S(2)}, u32[]{:S(2)}) collective-permute-start(bf16[512,768]{1,0:T(8,128)(2,1)} %get-tuple-element.72.refs_2_), channel_id=1, source_target_pairs={{0,4},{1,5},{2,6},{3,7},{4,0},{5,1},{6,2},{7,3},{8,12},{9,13},{10,... | collective-permute-start | bytes 2359304 | tf_op jit(solution)/shard_map/ppermute | solution.py:62
  126.2 19.7 %collective-permute-start.27 = (bf16[3,96,512]{2,1,0:T(8,128)(2,1)}, bf16[3,96,512]{2,1,0:T(8,128)(2,1)}, u32[]{:S(2)}, u32[]{:S(2)}) collective-permute-start(bf16[3,96,512]{2,1,0:T(8,128)(2,1)} %get-tuple-element.73), channel_id=1, source_target_pairs={{0,32},{16,48},{32,64},{48,80},{64,96},{80,112},{96,0},{112,16},{1... | collective-permute-start | bytes 884744 | tf_op jit(solution)/shard_map/ppermute | solution.py:183
  127.2 18.8 %collective-permute-start.28 = (bf16[3,96,512]{2,1,0:T(8,128)(2,1)}, bf16[3,96,512]{2,1,0:T(8,128)(2,1)}, u32[]{:S(2)}, u32[]{:S(2)}) collective-permute-start(bf16[3,96,512]{2,1,0:T(8,128)(2,1)} %get-tuple-element.74), channel_id=1, source_target_pairs={{0,64},{16,80},{32,96},{48,112},{64,0},{80,16},{96,32},{112,48},{1... | collective-permute-start | bytes 884744 | tf_op jit(solution)/shard_map/ppermute | solution.py:183
  129.6 16.4 %collective-permute-start.29 = (bf16[3,96,512]{2,1,0:T(8,128)(2,1)}, bf16[3,96,512]{2,1,0:T(8,128)(2,1)}, u32[]{:S(2)}, u32[]{:S(2)}) collective-permute-start(bf16[3,96,512]{2,1,0:T(8,128)(2,1)} %get-tuple-element.75), channel_id=1, source_target_pairs={{0,96},{16,112},{32,0},{48,16},{64,32},{80,48},{96,64},{112,80},{1... | collective-permute-start | bytes 884744 | tf_op jit(solution)/shard_map/ppermute | solution.py:183
  133.5 31.3 %all-to-all-start.2 = ((bf16[128,8,768]{2,1,0:T(8,128)(2,1)}), bf16[128,8,768]{2,1,0:T(8,128)(2,1)}, u32[]{:S(2)}, u32[]{:S(2)}) async-start(bf16[128,8,768]{2,1,0:T(8,128)(2,1)} %bitcast.10), calls=%async_computation.2 | async-start | bytes 3145728 | tf_op jit(solution)/shard_map/all_to_all | solution.py:153
  145.9 6.3 %copy-start.12 = (bf16[3,96,512]{2,1,0:T(8,128)(2,1)S(1)}, bf16[3,96,512]{2,1,0:T(8,128)(2,1)}, u32[]{:S(2)}) copy-start(bf16[3,96,512]{2,1,0:T(8,128)(2,1)} %copy-done.11) | copy-start | bytes 884740
  146.0 6.3 %copy-start.14 = (bf16[3,96,512]{2,1,0:T(8,128)(2,1)S(1)}, bf16[3,96,512]{2,1,0:T(8,128)(2,1)}, u32[]{:S(2)}) copy-start(bf16[3,96,512]{2,1,0:T(8,128)(2,1)} %copy-done.13) | copy-start | bytes 884740
  146.0 6.3 %copy-start.30 = (bf16[3,96,512]{2,1,0:T(8,128)(2,1)S(1)}, bf16[3,96,512]{2,1,0:T(8,128)(2,1)}, u32[]{:S(2)}) copy-start(bf16[3,96,512]{2,1,0:T(8,128)(2,1)} %copy-done.29) | copy-start | bytes 884740
  149.5 38.1 %collective-permute-start.30 = (bf16[1024,768]{1,0:T(8,128)(2,1)}, bf16[1024,768]{1,0:T(8,128)(2,1)}, u32[]{:S(2)}, u32[]{:S(2)}) collective-permute-start(bf16[1024,768]{1,0:T(8,128)(2,1)} %get-tuple-element.76.b0), channel_id=1, source_target_pairs={{0,3},{1,2},{2,1},{3,0},{4,7},{5,6},{6,5},{7,4},{8,11},{9,10},{10,... | collective-permute-start | bytes 4718600 | tf_op jit(solution)/shard_map/ppermute | solution.py:62
  152.2 35.3 %collective-permute-start.31 = (bf16[1024,768]{1,0:T(8,128)(2,1)}, bf16[1024,768]{1,0:T(8,128)(2,1)}, u32[]{:S(2)}, u32[]{:S(2)}) collective-permute-start(bf16[1024,768]{1,0:T(8,128)(2,1)} %get-tuple-element.77.b1), channel_id=1, source_target_pairs={{0,1},{1,0},{2,3},{3,2},{4,5},{5,4},{6,7},{7,6},{8,9},{9,8},{10,11... | collective-permute-start | bytes 4718600 | tf_op jit(solution)/shard_map/ppermute | solution.py:62
  156.3 15.2 %collective-permute-start.32 = (bf16[256,512]{1,0:T(8,128)(2,1)}, bf16[256,512]{1,0:T(8,128)(2,1)S(1)}, u32[]{:S(2)}, u32[]{:S(2)}) collective-permute-start(bf16[256,512]{1,0:T(8,128)(2,1)} %get-tuple-element.86), channel_id=1, source_target_pairs={{0,4},{1,5},{2,6},{3,7},{4,8},{5,9},{6,10},{7,11},{8,12},{9,13},{1... | collective-permute-start | bytes 786440 | tf_op jit(solution)/shard_map/ppermute | solution.py:462
  157.8 15.8 %collective-permute-start.33 = (bf16[256,512]{1,0:T(8,128)(2,1)}, bf16[256,512]{1,0:T(8,128)(2,1)S(1)}, u32[]{:S(2)}, u32[]{:S(2)}) collective-permute-start(bf16[256,512]{1,0:T(8,128)(2,1)} %get-tuple-element.87), channel_id=1, source_target_pairs={{0,8},{1,9},{2,10},{3,11},{4,12},{5,13},{6,14},{7,15},{8,0},{9,1},... | collective-permute-start | bytes 786440 | tf_op jit(solution)/shard_map/ppermute | solution.py:462
  160.5 13.1 %collective-permute-start.34 = (bf16[256,512]{1,0:T(8,128)(2,1)}, bf16[256,512]{1,0:T(8,128)(2,1)}, u32[]{:S(2)}, u32[]{:S(2)}) collective-permute-start(bf16[256,512]{1,0:T(8,128)(2,1)} %get-tuple-element.88), channel_id=1, source_target_pairs={{0,12},{1,13},{2,14},{3,15},{4,0},{5,1},{6,2},{7,3},{8,4},{9,5},{1... | collective-permute-start | bytes 786440 | tf_op jit(solution)/shard_map/ppermute | solution.py:462
  168.3 5.2 %copy-start.33 = (bf16[256,512]{1,0:T(8,128)(2,1)S(1)}, bf16[256,512]{1,0:T(8,128)(2,1)}, u32[]{:S(2)}) copy-start(bf16[256,512]{1,0:T(8,128)(2,1)} %copy-done.32) | copy-start | bytes 786436
  175.7 9.4 %collective-permute-start.35 = (f32[64,512]{1,0:T(8,128)S(1)}, f32[64,512]{1,0:T(8,128)S(1)}, u32[]{:S(2)}, u32[]{:S(2)}) collective-permute-start(f32[64,512]{1,0:T(8,128)S(1)} %get-tuple-element.90), channel_id=1, source_target_pairs={{0,1},{1,2},{2,3},{3,0},{4,5},{5,6},{6,7},{7,4},{8,9},{9,10},{10,1... | collective-permute-start | bytes 393224 | tf_op jit(solution)/shard_map/ppermute | solution.py:462
  177.8 8.9 %collective-permute-start.36 = (f32[64,512]{1,0:T(8,128)S(1)}, f32[64,512]{1,0:T(8,128)S(1)}, u32[]{:S(2)}, u32[]{:S(2)}) collective-permute-start(f32[64,512]{1,0:T(8,128)S(1)} %get-tuple-element.91), channel_id=1, source_target_pairs={{0,2},{1,3},{2,0},{3,1},{4,6},{5,7},{6,4},{7,5},{8,10},{9,11},{10,... | collective-permute-start | bytes 393224 | tf_op jit(solution)/shard_map/ppermute | solution.py:462
  178.1 8.6 %collective-permute-start.37 = (f32[64,512]{1,0:T(8,128)S(1)}, f32[64,512]{1,0:T(8,128)S(1)}, u32[]{:S(2)}, u32[]{:S(2)}) collective-permute-start(f32[64,512]{1,0:T(8,128)S(1)} %get-tuple-element.92), channel_id=1, source_target_pairs={{0,3},{1,0},{2,1},{3,2},{4,7},{5,4},{6,5},{7,6},{8,11},{9,8},{10,9... | collective-permute-start | bytes 393224 | tf_op jit(solution)/shard_map/ppermute | solution.py:462
  (16 other events, 24.4 us)

commit v7 on v6

--- a/solution.py
+++ b/solution.py
@@ -463,7 +463,7 @@
     return got
 
 
-def last_sum_kernel(*refs):
+def last_sum_kernel(token_ref, *refs):
     total = refs[0][...]
     for ref in refs[1:4]:
         total = total + ref[...]
@@ -472,16 +472,16 @@
         refs[-1][m] = total[:, 96 * m : 96 * m + 96]
 
 
-def last_sum(got):
+def last_sum(got, token):
     return pl.pallas_call(
         last_sum_kernel,
         out_shape=shape((5, 64, 96), F32),
-        in_specs=[IN_VMEM] * 4,
+        in_specs=[ANYWHERE] + [IN_VMEM] * 4,
         out_specs=IN_VMEM,
         compiler_params=params(8),
         cost_estimate=pl.CostEstimate(flops=1, bytes_accessed=1, transcendentals=0),
         name="last_sum",
-    )(*got)
+    )(token, *got)
 
 
 def per_device(
@@ -540,9 +540,9 @@
     left = over_y(left)
     rows = pick_rows(pick, dz_written, dz_write, parts[0])
     back = exchange(rows)
-    parts = join(pairs, left[1:])
+    back_table = cited_by_table(place, lists[0], lists[1], parts[0])
+    parts = join(pairs, (back_table, *left[1:]))
     right = over_y(right)
-    back_table = cited_by_table(place, lists[0], lists[1], parts[0])
     parts = join(travel(parts, 2), (back_table, *right[1:]))
     dx_author, dx_paper_own = edge_add(adder, back, dx_author_own, dx_paper_own)
     back_pairs = travel(parts, 3)
@@ -551,7 +551,7 @@
     got = over_col(y_sum(place, left, right, got_author), 0)
     got = over_col(x_sum(place, got, back_first, dx_author), 1)
     dx_paper = last_half(back_table, [pair[1] for pair in back_pairs], back_first, dx_paper_own)
-    dweights = last_sum(got).transpose(0, 2, 1)
+    dweights = last_sum(got, dx_paper).transpose(0, 2, 1)
     return (out_paper, out_author, dx_paper, dx_author, dweights)
 
 

time: 192 us -> 190 us (0.990)
  waiting for transfers between devices: 43.3 us -> 40.9 us
    ppermute x6, waiting for transfers between devices: 8.24 us -> 0.15 us  [over_col(): got.append(lax.ppermute(parts[d], ('row', 'col'), perm))]
    ppermute x20, waiting for transfers between devices: 13.8 us -> 18.3 us  [travel(): pairs.append((part, lax.ppermute(part, ('row', 'col'), perm)))]
    ppermute x6, starting transfers between devices: 10.5 us -> 13.1 us  [over_col(): got.append(lax.ppermute(parts[d], ('row', 'col'), perm))]
    all_to_all x2, waiting for transfers between devices: 7.73 us -> 10.2 us  [exchange(): lax.all_to_all(sent, ('row', 'col'), split_axis=0, concat_axis=0, tiled=T...]
    ppermute x20, starting transfers between devices: 24.9 us -> 22.7 us  [travel(): pairs.append((part, lax.ppermute(part, ('row', 'col'), perm)))]
    unnamed x81 -> x73, local copies, waits for them, and re-layouts: 12.1 us -> 13.4 us
  transfers between devices with their start and end apart: 41 -> 41, of which waited for: 14 -> 15; matrix products, arithmetic and copies ran while one was open for 1% -> 1% of each run, Pallas kernels for 30% -> 32%
where the time goes in v7:
time: 190 us; the launch traced here: 189 us
  starting transfers between devices  67.6 us (36%)
  Pallas kernels  63.2 us (33%)
  waiting for transfers between devices  40.9 us (22%)
  local copies, waits for them, and re-layouts  16.3 us (9%)
    ppermute x20, starting transfers between devices, travel(): pairs.append((part, lax.ppermute(part, ('row', 'col'), perm)))  22.7 us
    ppermute x20, waiting for transfers between devices, travel(): pairs.append((part, lax.ppermute(part, ('row', 'col'), perm)))  18.3 us
    all_to_all x2, starting transfers between devices, exchange(): lax.all_to_all(sent, ('row', 'col'), split_axis=0, concat_axis=0, tiled=T...  14.8 us
    unnamed x73, local copies, waits for them, and re-layouts  13.4 us
    ppermute x6, starting transfers between devices, over_col(): got.append(lax.ppermute(parts[d], ('row', 'col'), perm))  13.1 us
    ppermute x6, starting transfers between devices, over_y(): got.append(lax.ppermute(parts[d], 'row', perm))  11.4 us
    all_to_all x2, waiting for transfers between devices, exchange(): lax.all_to_all(sent, ('row', 'col'), split_axis=0, concat_axis=0, tiled=T...  10.2 us
    pallas_call x9, Pallas kernels, join(): pl.pallas_call(functools.partial(join_kernel, n), out_shape=outs, in_spec...  9.5 us
  transfers between devices with their start and end apart: 41, of which 15 were waited for; matrix products, arithmetic and copies ran while one was open for 1% of the time, Pallas kernels for 32%

profile of v7, /device:TPU:0, one launch (start us, length us, event | category | flops | bytes accessed | tf_op | source)
XLA Modules:
  0.0 189.3 jit_solution(4646322845054628570)
XLA Ops:
  0.7 1.1 fusion.1
  1.8 1.7 collective-permute-start
  3.5 2.1 %collective-permute-start.1 = (bf16[128,768]{1,0:T(8,128)(2,1)S(1)}, bf16[128,768]{1,0:T(8,128)(2,1)S(1)}, u32[]{:S(2)}, u32[]{:S(2)}) collective-permute-start(bf16[128,768]{1,0:T(8,128)(2,1)S(1)} %get-tuple-element.95.refs_2_), channel_id=1, source_target_pairs={{0,12},{1,13},{2,14},{3,15},{4,8},{5,9},{6,10},{7,11},{8,4},{9,5},... | collective-permute-start | bytes 589832 | tf_op jit(solution)/shard_map/ppermute | solution.py:62
  5.6 2.0 %collective-permute-done.refs_1_ = bf16[128,768]{1,0:T(8,128)(2,1)S(1)} collective-permute-done((bf16[128,768]{1,0:T(8,128)(2,1)S(1)}, bf16[128,768]{1,0:T(8,128)(2,1)S(1)}, u32[]{:S(2)}, u32[]{:S(2)}) %collective-permute-start) | collective-permute-done | bytes 196640 | tf_op jit(solution)/shard_map/ppermute | solution.py:62
  7.6 2.8 %collective-permute-done.1.refs_3_ = bf16[128,768]{1,0:T(8,128)(2,1)S(1)} collective-permute-done((bf16[128,768]{1,0:T(8,128)(2,1)S(1)}, bf16[128,768]{1,0:T(8,128)(2,1)S(1)}, u32[]{:S(2)}, u32[]{:S(2)}) %collective-permute-start.1) | collective-permute-done | bytes 196640 | tf_op jit(solution)/shard_map/ppermute | solution.py:62
  10.4 2.0 %collective-permute-start.2 = (bf16[256,768]{1,0:T(8,128)(2,1)S(1)}, bf16[256,768]{1,0:T(8,128)(2,1)S(1)}, u32[]{:S(2)}, u32[]{:S(2)}) collective-permute-start(bf16[256,768]{1,0:T(8,128)(2,1)S(1)} %get-tuple-element.49.refs_0_), channel_id=1, source_target_pairs={{0,1},{1,0},{2,3},{3,2},{4,5},{5,4},{6,7},{7,6},{8,9},{9,8},{10,11... | collective-permute-start | bytes 1179656 | tf_op jit(solution)/shard_map/ppermute | solution.py:62
  12.4 2.5 %collective-permute-start.3 = (bf16[256,768]{1,0:T(8,128)(2,1)S(1)}, bf16[256,768]{1,0:T(8,128)(2,1)S(1)}, u32[]{:S(2)}, u32[]{:S(2)}) collective-permute-start(bf16[256,768]{1,0:T(8,128)(2,1)S(1)} %get-tuple-element.50.refs_2_), channel_id=1, source_target_pairs={{0,3},{1,2},{2,1},{3,0},{4,7},{5,6},{6,5},{7,4},{8,11},{9,10},{10,... | collective-permute-start | bytes 1179656 | tf_op jit(solution)/shard_map/ppermute | solution.py:62
  14.9 4.0 %collective-permute-done.4.refs_1_.token_ref = s32[1,16,256]{2,1,0:T(8,128)S(1)} collective-permute-done((s32[1,16,256]{2,1,0:T(8,128)S(1)}, s32[1,16,256]{2,1,0:T(8,128)S(1)}, u32[]{:S(2)}, u32[]{:S(2)}) %collective-permute-start.4) | collective-permute-done | bytes 16416 | tf_op jit(solution)/shard_map/ppermute | solution.py:62
  19.7 3.1 %collective-permute-done.5.refs_4_.refs_1_ = s32[2,16,256]{2,1,0:T(8,128)S(1)} collective-permute-done((s32[2,16,256]{2,1,0:T(8,128)S(1)}, s32[2,16,256]{2,1,0:T(8,128)S(1)}, u32[]{:S(2)}, u32[]{:S(2)}) %collective-permute-start.5) | collective-permute-done | bytes 32800 | tf_op jit(solution)/shard_map/ppermute | solution.py:62
  23.8 1.9 collective-permute-start.6
  25.9 2.2 %pick_rows.2 = bf16[1024,768]{1,0:T(8,128)(2,1)} custom-call(s32[1,1024]{1,0:T(1,128)S(1)} %reshape.35.pick_ref, bf16[256,768]{1,0:T(8,128)(2,1)S(1)} %copy-done.7, bf16[256,768]{1,0:T(8,128)(2,1)S(1)} %copy-done.2, s32[1,16,256]{2,1,0:T(8,128)S(1)} %collective-permute-done.4.refs_1_.token_ref), custom_call_target="tpu_custom_call" | custom-call | flops 1 | bytes 1 | tf_op jit(solution)/shard_map/pick_rows/pallas_call | solution.py:164
  28.1 8.4 %all-to-all-start = ((bf16[128,8,768]{2,1,0:T(8,128)(2,1)}), bf16[128,8,768]{2,1,0:T(8,128)(2,1)}, u32[]{:S(2)}, u32[]{:S(2)}) async-start(bf16[128,8,768]{2,1,0:T(8,128)(2,1)} %bitcast.8), calls=%async_computation | async-start | bytes 3145728 | tf_op jit(solution)/shard_map/all_to_all | solution.py:153
  36.7 8.0 %cite_table.1.refs_4_.table_ref.refs_6_ = bf16[256,4096]{1,0:T(8,128)(2,1)S(1)} custom-call(s32[3]{0:T(128)S(1)} %pad_add_fusion.1.place_ref, s32[256,16]{1,0:T(8,128)S(1)} %copy.22.nbr_ref, bf16[512,768]{1,0:T(8,128)(2,1)S(1)} %get-tuple-element.51.token_ref.refs_0_), custom_call_target="tpu_custom_call" | custom-call | flops 1 | bytes 1 | tf_op jit(solution)/shard_map/cite_table/pallas_call | solution.py:106
  44.7 3.4 %join.12 = (bf16[1024,768]{1,0:T(8,128)(2,1)}, bf16[1024,768]{1,0:T(8,128)(2,1)}) custom-call(bf16[512,768]{1,0:T(8,128)(2,1)S(1)} %get-tuple-element.51.token_ref.refs_0_, bf16[512,768]{1,0:T(8,128)(2,1)} %collective-permute-done.6.refs_1_, bf16[512,768]{1,0:T(8,128)(2,1)} %get-tuple-element.52.refs_2_, bf16[512,768]{1,0:T(8,128)(2,1)} %collective-permute-done.7.refs_3_, ...), custom_call_target="tpu_custom_call" | custom-call | tf_op jit(solution)/shard_map/join/pallas_call | solution.py:47
  48.1 2.8 %collective-permute-start.8 = (bf16[1024,768]{1,0:T(8,128)(2,1)}, bf16[1024,768]{1,0:T(8,128)(2,1)}, u32[]{:S(2)}, u32[]{:S(2)}) collective-permute-start(bf16[1024,768]{1,0:T(8,128)(2,1)} %get-tuple-element.53.b0.refs_7_), channel_id=1, source_target_pairs={{0,3},{1,2},{2,1},{3,0},{4,7},{5,6},{6,5},{7,4},{8,11},{9,10},{10,... | collective-permute-start | bytes 4718600 | tf_op jit(solution)/shard_map/ppermute | solution.py:62
  52.6 8.0 %all-to-all-done = bf16[128,8,768]{2,1,0:T(8,128)(2,1)} async-done(((bf16[128,8,768]{2,1,0:T(8,128)(2,1)}), bf16[128,8,768]{2,1,0:T(8,128)(2,1)}, u32[]{:S(2)}, u32[]{:S(2)}) %all-to-all-start) | async-done | bytes 1572896 | tf_op jit(solution)/shard_map/all_to_all | solution.py:153
  60.6 8.3 %author_step.1 = (bf16[256,1024]{1,0:T(8,128)(2,1)}, bf16[256,768]{1,0:T(8,128)(2,1)}, bf16[256,768]{1,0:T(8,128)(2,1)}, bf16[256,1024]{1,0:T(8,128)(2,1)}, bf16...) custom-call(bf16[1024,768]{1,0:T(8,128)(2,1)} %bitcast.9.arrived_ref, ...), custom_call_target="tpu_custom_call" | custom-call | flops 1 | bytes 1 | tf_op jit(solution)/shard_map/author_step/pallas_call | solution.py:233
  69.6 2.4 %collective-permute-done.11.refs_3_ = bf16[256,768]{1,0:T(8,128)(2,1)S(1)} collective-permute-done((bf16[256,768]{1,0:T(8,128)(2,1)S(1)}, bf16[256,768]{1,0:T(8,128)(2,1)S(1)}, u32[]{:S(2)}, u32[]{:S(2)}) %collective-permute-start.11) | collective-permute-done | bytes 393248 | tf_op jit(solution)/shard_map/ppermute | solution.py:176
  72.2 1.0 copy-done.9
  73.2 1.0 copy-done.21
  74.2 1.8 weight_parts.2.token_a
  76.0 1.2 copy-done
  77.2 4.3 %all-to-all-start.1 = ((bf16[4,2,96,1024]{3,2,1,0:T(8,128)(2,1)}), bf16[4,2,96,1024]{3,2,1,0:T(8,128)(2,1)}, u32[]{:S(2)}, u32[]{:S(2)}) async-start(bf16[4,2,96,1024]{3,2,1,0:T(8,128)(2,1)} %copy-done), calls=%async_computation.1 | async-start | bytes 3145728 | tf_op jit(solution)/shard_map/all_to_all | solution.py:521
  82.2 3.2 %first_half.2.first_ref = f32[256,768]{1,0:T(8,128)S(1)} custom-call(bf16[256,4096]{1,0:T(8,128)(2,1)S(1)} %cite_table.1.refs_4_.table_ref.refs_6_, bf16[1024,768]{1,0:T(8,128)(2,1)} %get-tuple-element.53.b0.refs_7_, bf16[1024,768]{1,0:T(8,128)(2,1)} %get-tuple-element.54.b1), custom_call_target="tpu_custom_call" | custom-call | flops 1 | bytes 1 | tf_op jit(solution)/shard_map/first_half/pallas_call | solution.py:256
  85.4 1.9 %collective-permute-done.13.token_b.refs_1_ = s32[4,16,256]{2,1,0:T(8,128)S(1)} collective-permute-done((s32[4,16,256]{2,1,0:T(8,128)S(1)}, s32[4,16,256]{2,1,0:T(8,128)S(1)}, u32[]{:S(2)}, u32[]{:S(2)}) %collective-permute-start.13) | collective-permute-done | bytes 65568 | tf_op jit(solution)/shard_map/ppermute | solution.py:62
  87.4 5.2 %paper_step.1 = (bf16[256,1024]{1,0:T(8,128)(2,1)}, bf16[256,1792]{1,0:T(8,128)(2,1)S(1)}, bf16[256,768]{1,0:T(8,128)(2,1)S(1)}) custom-call(bf16[256,4096]{1,0:T(8,128)(2,1)S(1)} %cite_table.1.refs_4_.table_ref.refs_6_, bf16[1024,768]{1,0:T(8,128)(2,1)} %collective-permute-done.8.b0, bf16[1024,768]{1,0:T(8,128)(2,1)} %collective-permute-done.9.b1, ...), custom_call_target="tpu_custom_call" | custom-call | flops 1 | bytes 1 | tf_op jit(solution)/shard_map/paper_step/pallas_call | solution.py:326
  93.5 1.5 collective-permute-start.16
  96.7 1.7 edge_back.1
  99.4 3.3 %weight_parts.3 = (bf16[3,96,512]{2,1,0:T(8,128)(2,1)S(1)}, bf16[3,96,512]{2,1,0:T(8,128)(2,1)}, bf16[3,96,512]{2,1,0:T(8,128)(2,1)}, bf16[3,96,512]{2,1,0:T(8,1...) custom-call(s32[3]{0:T(128)S(1)} %pad_add_fusion.1.place_ref, ...), custom_call_target="tpu_custom_call" | custom-call | flops 1 | bytes 1 | tf_op jit(solution)/shard_map/weight_parts/pallas_call | solution.py:386
  104.1 2.3 %collective-permute-start.21 = (bf16[256,768]{1,0:T(8,128)(2,1)S(1)}, bf16[256,768]{1,0:T(8,128)(2,1)S(1)}, u32[]{:S(2)}, u32[]{:S(2)}) collective-permute-start(bf16[256,768]{1,0:T(8,128)(2,1)S(1)} %get-tuple-element.67.refs_2_), channel_id=1, source_target_pairs={{0,3},{1,2},{2,1},{3,0},{4,7},{5,6},{6,5},{7,4},{8,11},{9,10},{10,... | collective-permute-start | bytes 1179656 | tf_op jit(solution)/shard_map/ppermute | solution.py:62
  106.4 2.0 %collective-permute-start.22 = (bf16[3,96,512]{2,1,0:T(8,128)(2,1)}, bf16[3,96,512]{2,1,0:T(8,128)(2,1)S(1)}, u32[]{:S(2)}, u32[]{:S(2)}) collective-permute-start(bf16[3,96,512]{2,1,0:T(8,128)(2,1)} %get-tuple-element.68), channel_id=1, source_target_pairs={{0,32},{16,48},{32,64},{48,80},{64,96},{80,112},{96,0},{112,16},{1... | collective-permute-start | bytes 884744 | tf_op jit(solution)/shard_map/ppermute | solution.py:183
  108.4 2.7 %collective-permute-start.23 = (bf16[3,96,512]{2,1,0:T(8,128)(2,1)}, bf16[3,96,512]{2,1,0:T(8,128)(2,1)S(1)}, u32[]{:S(2)}, u32[]{:S(2)}) collective-permute-start(bf16[3,96,512]{2,1,0:T(8,128)(2,1)} %get-tuple-element.69), channel_id=1, source_target_pairs={{0,64},{16,80},{32,96},{48,112},{64,0},{80,16},{96,32},{112,48},{1... | collective-permute-start | bytes 884744 | tf_op jit(solution)/shard_map/ppermute | solution.py:183
  111.0 1.5 collective-permute-start.24
  113.4 4.0 %cited_by_table.1.refs_4_.table_ref = bf16[256,4096]{1,0:T(8,128)(2,1)S(1)} custom-call(s32[3]{0:T(128)S(1)} %pad_add_fusion.1.place_ref, s32[8,16,256]{2,1,0:T(8,128)S(1)} %copy-done.23, s32[8,16,256]{2,1,0:T(8,128)S(1)} %collective-permute-done.14.refs_5_.b_ref, bf16[256,768]{1,0:T(8,128)(2,1)S(1)} %get-tuple-element.66.token_ref.refs_0_), custom_call_target="tpu_custom_call" | custom-call | flops 1 | bytes 1 | tf_op jit(solution)/shard_map/cited_by_table/pallas_call | solution.py:132
  117.5 5.2 %collective-permute-done.23.refs_6_.refs_2_ = bf16[3,96,512]{2,1,0:T(8,128)(2,1)S(1)} collective-permute-done((bf16[3,96,512]{2,1,0:T(8,128)(2,1)}, bf16[3,96,512]{2,1,0:T(8,128)(2,1)S(1)}, u32[]{:S(2)}, u32[]{:S(2)}) %collective-permute-start.23) | collective-permute-done | bytes 294944 | tf_op jit(solution)/shard_map/ppermute | solution.py:183
  122.7 1.3 join.16
  124.0 2.0 %collective-permute-start.25 = (bf16[512,768]{1,0:T(8,128)(2,1)}, bf16[512,768]{1,0:T(8,128)(2,1)}, u32[]{:S(2)}, u32[]{:S(2)}) collective-permute-start(bf16[512,768]{1,0:T(8,128)(2,1)} %get-tuple-element.71.refs_0_), channel_id=1, source_target_pairs={{0,12},{1,13},{2,14},{3,15},{4,8},{5,9},{6,10},{7,11},{8,4},{9,5},... | collective-permute-start | bytes 2359304 | tf_op jit(solution)/shard_map/ppermute | solution.py:62
  126.3 1.1 collective-permute-start.27
  127.5 2.4 %collective-permute-start.28 = (bf16[3,96,512]{2,1,0:T(8,128)(2,1)}, bf16[3,96,512]{2,1,0:T(8,128)(2,1)}, u32[]{:S(2)}, u32[]{:S(2)}) collective-permute-start(bf16[3,96,512]{2,1,0:T(8,128)(2,1)} %get-tuple-element.74), channel_id=1, source_target_pairs={{0,64},{16,80},{32,96},{48,112},{64,0},{80,16},{96,32},{112,48},{1... | collective-permute-start | bytes 884744 | tf_op jit(solution)/shard_map/ppermute | solution.py:183
  129.8 1.8 collective-permute-start.29
  131.6 1.0 pick_rows.3
  132.7 1.1 copy-done.6
  133.8 6.4 %all-to-all-start.2 = ((bf16[128,8,768]{2,1,0:T(8,128)(2,1)}), bf16[128,8,768]{2,1,0:T(8,128)(2,1)}, u32[]{:S(2)}, u32[]{:S(2)}) async-start(bf16[128,8,768]{2,1,0:T(8,128)(2,1)} %bitcast.14), calls=%async_computation.2 | async-start | bytes 3145728 | tf_op jit(solution)/shard_map/all_to_all | solution.py:153
  140.3 2.1 %collective-permute-done.28.refs_6_ = bf16[3,96,512]{2,1,0:T(8,128)(2,1)} collective-permute-done((bf16[3,96,512]{2,1,0:T(8,128)(2,1)}, bf16[3,96,512]{2,1,0:T(8,128)(2,1)}, u32[]{:S(2)}, u32[]{:S(2)}) %collective-permute-start.28) | collective-permute-done | bytes 294944 | tf_op jit(solution)/shard_map/ppermute | solution.py:183
  142.4 1.5 collective-permute-done.29.refs_7_
  144.0 3.7 %join.17 = (bf16[1024,768]{1,0:T(8,128)(2,1)}, bf16[1024,768]{1,0:T(8,128)(2,1)}) custom-call(bf16[512,768]{1,0:T(8,128)(2,1)} %get-tuple-element.71.refs_0_, bf16[512,768]{1,0:T(8,128)(2,1)} %collective-permute-done.25.refs_1_, bf16[512,768]{1,0:T(8,128)(2,1)} %get-tuple-element.72.refs_2_, bf16[512,768]{1,0:T(8,128)(2,1)} %collective-permute-done.26.refs_3_, ...), custom_call_target="tpu_custom_call" | custom-call | tf_op jit(solution)/shard_map/join/pallas_call | solution.py:47
  148.2 3.3 %y_sum.1 = (bf16[256,512]{1,0:T(8,128)(2,1)S(1)}, bf16[256,512]{1,0:T(8,128)(2,1)}, bf16[256,512]{1,0:T(8,128)(2,1)}, bf16[256,512]{1,0:T(8,128)(2,1)}) custom-call(s32[3]{0:T(128)S(1)} %pad_add_fusion.1.place_ref, bf16[3,96,512]{2,1,0:T(8,128)(2,1)S(1)} %copy-done.14, bf16[3,96,512]{2,1,0:T(8,128)(2,1)S(1)} %collective-permute-done.22.refs_5_.refs_1_, ...), custom_call_target="tpu_custom_call" | custom-call | flops 1 | bytes 1 | tf_op jit(solution)/shard_map/y_sum/pallas_call | solution.py:418
  152.3 2.0 %collective-permute-start.32 = (bf16[256,512]{1,0:T(8,128)(2,1)}, bf16[256,512]{1,0:T(8,128)(2,1)S(1)}, u32[]{:S(2)}, u32[]{:S(2)}) collective-permute-start(bf16[256,512]{1,0:T(8,128)(2,1)} %get-tuple-element.86), channel_id=1, source_target_pairs={{0,4},{1,5},{2,6},{3,7},{4,8},{5,9},{6,10},{7,11},{8,12},{9,13},{1... | collective-permute-start | bytes 786440 | tf_op jit(solution)/shard_map/ppermute | solution.py:462
  154.2 2.6 %collective-permute-start.33 = (bf16[256,512]{1,0:T(8,128)(2,1)}, bf16[256,512]{1,0:T(8,128)(2,1)S(1)}, u32[]{:S(2)}, u32[]{:S(2)}) collective-permute-start(bf16[256,512]{1,0:T(8,128)(2,1)} %get-tuple-element.87), channel_id=1, source_target_pairs={{0,8},{1,9},{2,10},{3,11},{4,12},{5,13},{6,14},{7,15},{8,0},{9,1},... | collective-permute-start | bytes 786440 | tf_op jit(solution)/shard_map/ppermute | solution.py:462
  156.8 2.4 %collective-permute-start.34 = (bf16[256,512]{1,0:T(8,128)(2,1)}, bf16[256,512]{1,0:T(8,128)(2,1)}, u32[]{:S(2)}, u32[]{:S(2)}) collective-permute-start(bf16[256,512]{1,0:T(8,128)(2,1)} %get-tuple-element.88), channel_id=1, source_target_pairs={{0,12},{1,13},{2,14},{3,15},{4,0},{5,1},{6,2},{7,3},{8,4},{9,5},{1... | collective-permute-start | bytes 786440 | tf_op jit(solution)/shard_map/ppermute | solution.py:462
  159.2 2.9 %first_half.3.first_ref.token_a = f32[256,768]{1,0:T(8,128)S(1)} custom-call(bf16[256,4096]{1,0:T(8,128)(2,1)S(1)} %cited_by_table.1.refs_4_.table_ref, bf16[1024,768]{1,0:T(8,128)(2,1)} %get-tuple-element.76.b0, bf16[1024,768]{1,0:T(8,128)(2,1)} %get-tuple-element.77.b1), custom_call_target="tpu_custom_call" | custom-call | flops 1 | bytes 1 | tf_op jit(solution)/shard_map/first_half/pallas_call | solution.py:256
  162.1 2.2 %all-to-all-done.2 = bf16[128,8,768]{2,1,0:T(8,128)(2,1)} async-done(((bf16[128,8,768]{2,1,0:T(8,128)(2,1)}), bf16[128,8,768]{2,1,0:T(8,128)(2,1)}, u32[]{:S(2)}, u32[]{:S(2)}) %all-to-all-start.2) | async-done | bytes 1572896 | tf_op jit(solution)/shard_map/all_to_all | solution.py:153
  164.3 1.2 copy-done.15
  165.5 1.1 copy-done.17
  166.7 1.1 copy-done.19
  167.8 3.2 %edge_add.1 = (bf16[256,768]{1,0:T(8,128)(2,1)}, f32[256,768]{1,0:T(8,128)S(1)}) custom-call(bf16[512,1024]{1,0:T(8,128)(2,1)S(1)} %copy-done.15, bf16[1024,768]{1,0:T(8,128)(2,1)} %bitcast.11.back_ref, f32[256,768]{1,0:T(8,128)S(1)} %copy-done.17, f32[256,768]{1,0:T(8,128)S(1)} %copy-done.19), custom_call_target="tpu_custom_call" | custom-call | flops 1 | bytes 1 | tf_op jit(solution)/shard_map/edge_add/pallas_call | solution.py:291
  171.1 1.0 copy-done.25
  172.1 1.2 x_sum.1
  173.3 1.7 collective-permute-start.35
  175.0 3.2 %collective-permute-start.36 = (f32[64,512]{1,0:T(8,128)S(1)}, f32[64,512]{1,0:T(8,128)S(1)}, u32[]{:S(2)}, u32[]{:S(2)}) collective-permute-start(f32[64,512]{1,0:T(8,128)S(1)} %get-tuple-element.91), channel_id=1, source_target_pairs={{0,2},{1,3},{2,0},{3,1},{4,6},{5,7},{6,4},{7,5},{8,10},{9,11},{10,... | collective-permute-start | bytes 393224 | tf_op jit(solution)/shard_map/ppermute | solution.py:462
  178.2 1.2 collective-permute-start.37
  179.4 4.5 %collective-permute-done.30.b0 = bf16[1024,768]{1,0:T(8,128)(2,1)} collective-permute-done((bf16[1024,768]{1,0:T(8,128)(2,1)}, bf16[1024,768]{1,0:T(8,128)(2,1)}, u32[]{:S(2)}, u32[]{:S(2)}) %collective-permute-start.30) | collective-permute-done | bytes 1572896 | tf_op jit(solution)/shard_map/ppermute | solution.py:62
  183.9 3.6 %last_half.1.token_ref = bf16[256,768]{1,0:T(8,128)(2,1)} custom-call(bf16[256,4096]{1,0:T(8,128)(2,1)S(1)} %cited_by_table.1.refs_4_.table_ref, bf16[1024,768]{1,0:T(8,128)(2,1)} %collective-permute-done.30.b0, bf16[1024,768]{1,0:T(8,128)(2,1)} %collective-permute-done.31.b1, f32[256,768]{1,0:T(8,128)S(1)} %first_half.3.first_ref.token_a, ...), custom_call_target="tpu_custom_call" | custom-call | flops 1 | bytes 1 | tf_op jit(solution)/shard_map/last_half/pallas_call | solution.py:273
  187.5 1.0 copy-done.11
  (127 shorter events, 13.8 us)
Async XLA Ops:
  0.6 25.3 %copy-start.2 = (bf16[256,768]{1,0:T(8,128)(2,1)S(1)}, bf16[256,768]{1,0:T(8,128)(2,1)}, u32[]{:S(2)}) copy-start(bf16[256,768]{1,0:T(8,128)(2,1)} %refs_2_.5) | copy-start | bytes 1179652
  0.6 14.3 %copy-start.32 = (s32[256,16]{0,1:T(8,128)S(1)}, s32[256,16]{0,1:T(8,128)}, u32[]{:S(2)}) copy-start(s32[256,16]{0,1:T(8,128)} %param.14) | copy-start | bytes 49156
  0.7 19.0 %copy-start.33 = (s32[1,128,4]{1,2,0:T(4,128)S(1)}, s32[1,128,4]{1,2,0:T(4,128)}, u32[]{:S(2)}) copy-start(s32[1,128,4]{1,2,0:T(4,128)} %param.16) | copy-start | bytes 6148
  0.7 25.0 %copy-start.34 = (s32[1,128,4]{1,2,0:T(4,128)S(1)}, s32[1,128,4]{1,2,0:T(4,128)}, u32[]{:S(2)}) copy-start(s32[1,128,4]{1,2,0:T(4,128)} %param.15) | copy-start | bytes 6148
  0.7 25.2 %copy-start.7 = (bf16[256,768]{1,0:T(8,128)(2,1)S(1)}, bf16[256,768]{1,0:T(8,128)(2,1)}, u32[]{:S(2)}) copy-start(bf16[256,768]{1,0:T(8,128)(2,1)} %refs_2_.4) | copy-start | bytes 1179652
  1.8 5.7 %collective-permute-start = (bf16[128,768]{1,0:T(8,128)(2,1)S(1)}, bf16[128,768]{1,0:T(8,128)(2,1)S(1)}, u32[]{:S(2)}, u32[]{:S(2)}) collective-permute-start(bf16[128,768]{1,0:T(8,128)(2,1)S(1)} %get-tuple-element.96.refs_0_), channel_id=1, source_target_pairs={{0,4},{1,5},{2,6},{3,7},{4,0},{5,1},{6,2},{7,3},{8,12},{9,13},{10,... | collective-permute-start | bytes 589832 | tf_op jit(solution)/shard_map/ppermute | solution.py:62
  3.5 6.9 %collective-permute-start.1 = (bf16[128,768]{1,0:T(8,128)(2,1)S(1)}, bf16[128,768]{1,0:T(8,128)(2,1)S(1)}, u32[]{:S(2)}, u32[]{:S(2)}) collective-permute-start(bf16[128,768]{1,0:T(8,128)(2,1)S(1)} %get-tuple-element.95.refs_2_), channel_id=1, source_target_pairs={{0,12},{1,13},{2,14},{3,15},{4,8},{5,9},{6,10},{7,11},{8,4},{9,5},... | collective-permute-start | bytes 589832 | tf_op jit(solution)/shard_map/ppermute | solution.py:62
  10.4 12.4 %collective-permute-start.2 = (bf16[256,768]{1,0:T(8,128)(2,1)S(1)}, bf16[256,768]{1,0:T(8,128)(2,1)S(1)}, u32[]{:S(2)}, u32[]{:S(2)}) collective-permute-start(bf16[256,768]{1,0:T(8,128)(2,1)S(1)} %get-tuple-element.49.refs_0_), channel_id=1, source_target_pairs={{0,1},{1,0},{2,3},{3,2},{4,5},{5,4},{6,7},{7,6},{8,9},{9,8},{10,11... | collective-permute-start | bytes 1179656 | tf_op jit(solution)/shard_map/ppermute | solution.py:62
  12.4 10.4 %collective-permute-start.3 = (bf16[256,768]{1,0:T(8,128)(2,1)S(1)}, bf16[256,768]{1,0:T(8,128)(2,1)S(1)}, u32[]{:S(2)}, u32[]{:S(2)}) collective-permute-start(bf16[256,768]{1,0:T(8,128)(2,1)S(1)} %get-tuple-element.50.refs_2_), channel_id=1, source_target_pairs={{0,3},{1,2},{2,1},{3,0},{4,7},{5,6},{6,5},{7,4},{8,11},{9,10},{10,... | collective-permute-start | bytes 1179656 | tf_op jit(solution)/shard_map/ppermute | solution.py:62
  14.9 4.0 %collective-permute-start.4 = (s32[1,16,256]{2,1,0:T(8,128)S(1)}, s32[1,16,256]{2,1,0:T(8,128)S(1)}, u32[]{:S(2)}, u32[]{:S(2)}) collective-permute-start(s32[1,16,256]{2,1,0:T(8,128)S(1)} %bitcast.15), channel_id=1, source_target_pairs={{0,4},{1,5},{2,6},{3,7},{4,0},{5,1},{6,2},{7,3},{8,12},{9,13},{10,... | collective-permute-start | bytes 49160 | tf_op jit(solution)/shard_map/ppermute | solution.py:62
  18.9 3.9 %collective-permute-start.5 = (s32[2,16,256]{2,1,0:T(8,128)S(1)}, s32[2,16,256]{2,1,0:T(8,128)S(1)}, u32[]{:S(2)}, u32[]{:S(2)}) collective-permute-start(s32[2,16,256]{2,1,0:T(8,128)S(1)} %join.10.refs_0_), channel_id=1, source_target_pairs={{0,1},{1,0},{2,3},{3,2},{4,5},{5,4},{6,7},{7,6},{8,9},{9,8},{10,11... | collective-permute-start | bytes 98312 | tf_op jit(solution)/shard_map/ppermute | solution.py:62
  23.8 20.9 %collective-permute-start.6 = (bf16[512,768]{1,0:T(8,128)(2,1)S(1)}, bf16[512,768]{1,0:T(8,128)(2,1)}, u32[]{:S(2)}, u32[]{:S(2)}) collective-permute-start(bf16[512,768]{1,0:T(8,128)(2,1)S(1)} %get-tuple-element.51.token_ref.refs_0_), channel_id=1, source_target_pairs={{0,12},{1,13},{2,14},{3,15},{4,8},{5,9},{6,10},{7,11},{8,4},{9,5},... | collective-permute-start | bytes 2359304 | tf_op jit(solution)/shard_map/ppermute | solution.py:62
  25.7 19.0 %collective-permute-start.7 = (bf16[512,768]{1,0:T(8,128)(2,1)}, bf16[512,768]{1,0:T(8,128)(2,1)}, u32[]{:S(2)}, u32[]{:S(2)}) collective-permute-start(bf16[512,768]{1,0:T(8,128)(2,1)} %get-tuple-element.52.refs_2_), channel_id=1, source_target_pairs={{0,4},{1,5},{2,6},{3,7},{4,0},{5,1},{6,2},{7,3},{8,12},{9,13},{10,... | collective-permute-start | bytes 2359304 | tf_op jit(solution)/shard_map/ppermute | solution.py:62
  28.1 32.5 %all-to-all-start = ((bf16[128,8,768]{2,1,0:T(8,128)(2,1)}), bf16[128,8,768]{2,1,0:T(8,128)(2,1)}, u32[]{:S(2)}, u32[]{:S(2)}) async-start(bf16[128,8,768]{2,1,0:T(8,128)(2,1)} %bitcast.8), calls=%async_computation | async-start | bytes 3145728 | tf_op jit(solution)/shard_map/all_to_all | solution.py:153
  48.1 39.2 %collective-permute-start.8 = (bf16[1024,768]{1,0:T(8,128)(2,1)}, bf16[1024,768]{1,0:T(8,128)(2,1)}, u32[]{:S(2)}, u32[]{:S(2)}) collective-permute-start(bf16[1024,768]{1,0:T(8,128)(2,1)} %get-tuple-element.53.b0.refs_7_), channel_id=1, source_target_pairs={{0,3},{1,2},{2,1},{3,0},{4,7},{5,6},{6,5},{7,4},{8,11},{9,10},{10,... | collective-permute-start | bytes 4718600 | tf_op jit(solution)/shard_map/ppermute | solution.py:62
  50.9 36.4 %collective-permute-start.9 = (bf16[1024,768]{1,0:T(8,128)(2,1)}, bf16[1024,768]{1,0:T(8,128)(2,1)}, u32[]{:S(2)}, u32[]{:S(2)}) collective-permute-start(bf16[1024,768]{1,0:T(8,128)(2,1)} %get-tuple-element.54.b1), channel_id=1, source_target_pairs={{0,1},{1,0},{2,3},{3,2},{4,5},{5,4},{6,7},{7,6},{8,9},{9,8},{10,11... | collective-permute-start | bytes 4718600 | tf_op jit(solution)/shard_map/ppermute | solution.py:62
  60.6 8.4 %copy-start.8 = (bf16[256,768]{1,0:T(8,128)(2,1)S(1)}, bf16[256,768]{1,0:T(8,128)(2,1)}, u32[]{:S(2)}) copy-start(bf16[256,768]{1,0:T(8,128)(2,1)} %refs_2_.4) | copy-start | bytes 1179652
  68.9 3.3 %collective-permute-start.10 = (bf16[256,1024]{1,0:T(8,128)(2,1)}, bf16[256,1024]{1,0:T(8,128)(2,1)S(1)}, u32[]{:S(2)}, u32[]{:S(2)}) collective-permute-start(bf16[256,1024]{1,0:T(8,128)(2,1)} %get-tuple-element.56.refs_0_), channel_id=1, source_target_pairs={{0,16},{16,0},{32,48},{48,32},{64,80},{80,64},{96,112},{112,96},{1... | collective-permute-start | bytes 1572872 | tf_op jit(solution)/shard_map/ppermute | solution.py:176
  69.0 3.0 %collective-permute-start.11 = (bf16[256,768]{1,0:T(8,128)(2,1)S(1)}, bf16[256,768]{1,0:T(8,128)(2,1)S(1)}, u32[]{:S(2)}, u32[]{:S(2)}) collective-permute-start(bf16[256,768]{1,0:T(8,128)(2,1)S(1)} %copy-done.8), channel_id=1, source_target_pairs={{0,16},{16,0},{32,48},{48,32},{64,80},{80,64},{96,112},{112,96},{1... | collective-permute-start | bytes 1179656 | tf_op jit(solution)/shard_map/ppermute | solution.py:176
  69.5 2.7 %collective-permute-start.12 = (bf16[256,768]{1,0:T(8,128)(2,1)}, bf16[256,768]{1,0:T(8,128)(2,1)S(1)}, u32[]{:S(2)}, u32[]{:S(2)}) collective-permute-start(bf16[256,768]{1,0:T(8,128)(2,1)} %get-tuple-element.57.refs_4_.token_c), channel_id=1, source_target_pairs={{0,16},{16,0},{32,48},{48,32},{64,80},{80,64},{96,112},{112,96},{1... | collective-permute-start | bytes 1179656 | tf_op jit(solution)/shard_map/ppermute | solution.py:176
  77.2 26.2 %all-to-all-start.1 = ((bf16[4,2,96,1024]{3,2,1,0:T(8,128)(2,1)}), bf16[4,2,96,1024]{3,2,1,0:T(8,128)(2,1)}, u32[]{:S(2)}, u32[]{:S(2)}) async-start(bf16[4,2,96,1024]{3,2,1,0:T(8,128)(2,1)} %copy-done), calls=%async_computation.1 | async-start | bytes 3145728 | tf_op jit(solution)/shard_map/all_to_all | solution.py:521
  81.5 5.8 %copy-start.1 = (bf16[4,2,96,1024]{3,2,1,0:T(8,128)(2,1)S(1)}, bf16[4,2,96,1024]{3,2,1,0:T(8,128)(2,1)}, u32[]{:S(2)}) copy-start(bf16[4,2,96,1024]{3,2,1,0:T(8,128)(2,1)} %copy-done) | copy-start | bytes 4718596
  81.6 5.8 %copy-start.10 = (bf16[256,768]{1,0:T(8,128)(2,1)S(1)}, bf16[256,768]{1,0:T(8,128)(2,1)}, u32[]{:S(2)}) copy-start(bf16[256,768]{1,0:T(8,128)(2,1)} %get-tuple-element.57.refs_4_.token_c) | copy-start | bytes 1179652
  81.6 5.8 %copy-start.12 = (bf16[768,1024]{1,0:T(8,128)(2,1)S(1)}, bf16[768,1024]{1,0:T(8,128)(2,1)}, u32[]{:S(2)}) copy-start(bf16[768,1024]{1,0:T(8,128)(2,1)} %w_hbm.1) | copy-start | bytes 4718596
  81.6 5.8 %copy-start.16 = (f32[256,1024]{1,0:T(8,128)S(1)}, f32[256,1024]{1,0:T(8,128)}, u32[]{:S(2)}) copy-start(f32[256,1024]{1,0:T(8,128)} %get-tuple-element.55.pre_ref) | copy-start | bytes 3145732
  81.6 5.8 %copy-start.20 = (bf16[256,1024]{1,0:T(8,128)(2,1)S(1)}, bf16[256,1024]{1,0:T(8,128)(2,1)}, u32[]{:S(2)}) copy-start(bf16[256,1024]{1,0:T(8,128)(2,1)} %grad_hbm.1) | copy-start | bytes 1572868
  81.6 5.7 %collective-permute-start.13 = (s32[4,16,256]{2,1,0:T(8,128)S(1)}, s32[4,16,256]{2,1,0:T(8,128)S(1)}, u32[]{:S(2)}, u32[]{:S(2)}) collective-permute-start(s32[4,16,256]{2,1,0:T(8,128)S(1)} %join.13.refs_0_), channel_id=1, source_target_pairs={{0,12},{1,13},{2,14},{3,15},{4,8},{5,9},{6,10},{7,11},{8,4},{9,5},... | collective-permute-start | bytes 196616 | tf_op jit(solution)/shard_map/ppermute | solution.py:62
  87.4 5.4 %copy-start.3 = (bf16[256,768]{1,0:T(8,128)(2,1)S(1)}, bf16[256,768]{1,0:T(8,128)(2,1)}, u32[]{:S(2)}) copy-start(bf16[256,768]{1,0:T(8,128)(2,1)} %refs_2_.5) | copy-start | bytes 1179652
  87.4 5.9 %copy-start.24 = (bf16[256,768]{1,0:T(8,128)(2,1)S(1)}, bf16[256,768]{1,0:T(8,128)(2,1)}, u32[]{:S(2)}) copy-start(bf16[256,768]{1,0:T(8,128)(2,1)} %get-tuple-element.62.refs_6_) | copy-start | bytes 1179652
  87.4 9.3 %copy-start.4 = (bf16[768,1024]{1,0:T(8,128)(2,1)S(1)}, bf16[768,1024]{1,0:T(8,128)(2,1)}, u32[]{:S(2)}) copy-start(bf16[768,1024]{1,0:T(8,128)(2,1)} %w_sp_hbm.1) | copy-start | bytes 4718596
  87.4 9.3 %copy-start.5 = (bf16[768,1024]{1,0:T(8,128)(2,1)S(1)}, bf16[768,1024]{1,0:T(8,128)(2,1)}, u32[]{:S(2)}) copy-start(bf16[768,1024]{1,0:T(8,128)(2,1)} %w_wr_hbm.1) | copy-start | bytes 4718596
  87.4 9.3 %copy-start.29 = (f32[512,128]{1,0:T(8,128)S(1)}, f32[512,128]{1,0:T(8,128)}, u32[]{:S(2)}) copy-start(f32[512,128]{1,0:T(8,128)} %get-tuple-element.63.cnt_ref) | copy-start | bytes 786436
  92.7 6.7 %collective-permute-start.17 = (bf16[256,1792]{1,0:T(8,128)(2,1)S(1)}, bf16[256,1792]{1,0:T(8,128)(2,1)S(1)}, u32[]{:S(2)}, u32[]{:S(2)}) collective-permute-start(bf16[256,1792]{1,0:T(8,128)(2,1)S(1)} %get-tuple-element.61.pack_ref.refs_0_.refs_4_), channel_id=1, source_target_pairs={{0,16},{16,0},{32,48},{48,32},{64,80},{80,64},{96,112},{112,96},{1... | collective-permute-start | bytes 2752520 | tf_op jit(solution)/shard_map/ppermute | solution.py:176
  92.8 3.0 %collective-permute-start.18 = (bf16[256,768]{1,0:T(8,128)(2,1)S(1)}, bf16[256,768]{1,0:T(8,128)(2,1)S(1)}, u32[]{:S(2)}, u32[]{:S(2)}) collective-permute-start(bf16[256,768]{1,0:T(8,128)(2,1)S(1)} %copy-done.3), channel_id=1, source_target_pairs={{0,16},{16,0},{32,48},{48,32},{64,80},{80,64},{96,112},{112,96},{1... | collective-permute-start | bytes 1179656 | tf_op jit(solution)/shard_map/ppermute | solution.py:176
  93.3 6.1 %collective-permute-start.19 = (bf16[256,768]{1,0:T(8,128)(2,1)S(1)}, bf16[256,768]{1,0:T(8,128)(2,1)S(1)}, u32[]{:S(2)}, u32[]{:S(2)}) collective-permute-start(bf16[256,768]{1,0:T(8,128)(2,1)S(1)} %copy-done.24), channel_id=1, source_target_pairs={{0,16},{16,0},{32,48},{48,32},{64,80},{80,64},{96,112},{112,96},{1... | collective-permute-start | bytes 1179656 | tf_op jit(solution)/shard_map/ppermute | solution.py:176
  93.4 10.0 %collective-permute-start.15 = (bf16[128,768]{1,0:T(8,128)(2,1)S(1)}, bf16[128,768]{1,0:T(8,128)(2,1)S(1)}, u32[]{:S(2)}, u32[]{:S(2)}) collective-permute-start(bf16[128,768]{1,0:T(8,128)(2,1)S(1)} %get-tuple-element.94.refs_0_), channel_id=1, source_target_pairs={{0,4},{1,5},{2,6},{3,7},{4,0},{5,1},{6,2},{7,3},{8,12},{9,13},{10,... | collective-permute-start | bytes 589832 | tf_op jit(solution)/shard_map/ppermute | solution.py:62
  93.5 9.9 %collective-permute-start.16 = (bf16[128,768]{1,0:T(8,128)(2,1)S(1)}, bf16[128,768]{1,0:T(8,128)(2,1)S(1)}, u32[]{:S(2)}, u32[]{:S(2)}) collective-permute-start(bf16[128,768]{1,0:T(8,128)(2,1)S(1)} %get-tuple-element.93.refs_2_), channel_id=1, source_target_pairs={{0,12},{1,13},{2,14},{3,15},{4,8},{5,9},{6,10},{7,11},{8,4},{9,5},... | collective-permute-start | bytes 589832 | tf_op jit(solution)/shard_map/ppermute | solution.py:62
  95.0 3.4 %copy-start.22 = (s32[8,16,256]{2,1,0:T(8,128)}, s32[8,16,256]{2,1,0:T(8,128)S(1)}, u32[]{:S(2)}) copy-start(s32[8,16,256]{2,1,0:T(8,128)S(1)} %join.14.a_ref) | copy-start | bytes 393220
  95.8 7.6 %collective-permute-start.14 = (s32[8,16,256]{2,1,0:T(8,128)S(1)}, s32[8,16,256]{2,1,0:T(8,128)S(1)}, u32[]{:S(2)}, u32[]{:S(2)}) collective-permute-start(s32[8,16,256]{2,1,0:T(8,128)S(1)} %join.14.a_ref), channel_id=1, source_target_pairs={{0,3},{1,2},{2,1},{3,0},{4,7},{5,6},{6,5},{7,4},{8,11},{9,10},{10,... | collective-permute-start | bytes 393224 | tf_op jit(solution)/shard_map/ppermute | solution.py:62
  103.4 7.6 %copy-start.13 = (bf16[3,96,512]{2,1,0:T(8,128)(2,1)}, bf16[3,96,512]{2,1,0:T(8,128)(2,1)S(1)}, u32[]{:S(2)}) copy-start(bf16[3,96,512]{2,1,0:T(8,128)(2,1)S(1)} %get-tuple-element.65.refs_4_.refs_0_) | copy-start | bytes 884740
  103.5 19.2 %collective-permute-start.20 = (bf16[256,768]{1,0:T(8,128)(2,1)S(1)}, bf16[256,768]{1,0:T(8,128)(2,1)S(1)}, u32[]{:S(2)}, u32[]{:S(2)}) collective-permute-start(bf16[256,768]{1,0:T(8,128)(2,1)S(1)} %get-tuple-element.66.token_ref.refs_0_), channel_id=1, source_target_pairs={{0,1},{1,0},{2,3},{3,2},{4,5},{5,4},{6,7},{7,6},{8,9},{9,8},{10,11... | collective-permute-start | bytes 1179656 | tf_op jit(solution)/shard_map/ppermute | solution.py:62
  104.1 18.6 %collective-permute-start.21 = (bf16[256,768]{1,0:T(8,128)(2,1)S(1)}, bf16[256,768]{1,0:T(8,128)(2,1)S(1)}, u32[]{:S(2)}, u32[]{:S(2)}) collective-permute-start(bf16[256,768]{1,0:T(8,128)(2,1)S(1)} %get-tuple-element.67.refs_2_), channel_id=1, source_target_pairs={{0,3},{1,2},{2,1},{3,0},{4,7},{5,6},{6,5},{7,4},{8,11},{9,10},{10,... | collective-permute-start | bytes 1179656 | tf_op jit(solution)/shard_map/ppermute | solution.py:62
  106.4 11.0 %collective-permute-start.22 = (bf16[3,96,512]{2,1,0:T(8,128)(2,1)}, bf16[3,96,512]{2,1,0:T(8,128)(2,1)S(1)}, u32[]{:S(2)}, u32[]{:S(2)}) collective-permute-start(bf16[3,96,512]{2,1,0:T(8,128)(2,1)} %get-tuple-element.68), channel_id=1, source_target_pairs={{0,32},{16,48},{32,64},{48,80},{64,96},{80,112},{96,0},{112,16},{1... | collective-permute-start | bytes 884744 | tf_op jit(solution)/shard_map/ppermute | solution.py:183
  108.4 14.3 %collective-permute-start.23 = (bf16[3,96,512]{2,1,0:T(8,128)(2,1)}, bf16[3,96,512]{2,1,0:T(8,128)(2,1)S(1)}, u32[]{:S(2)}, u32[]{:S(2)}) collective-permute-start(bf16[3,96,512]{2,1,0:T(8,128)(2,1)} %get-tuple-element.69), channel_id=1, source_target_pairs={{0,64},{16,80},{32,96},{48,112},{64,0},{80,16},{96,32},{112,48},{1... | collective-permute-start | bytes 884744 | tf_op jit(solution)/shard_map/ppermute | solution.py:183
  111.0 11.6 %collective-permute-start.24 = (bf16[3,96,512]{2,1,0:T(8,128)(2,1)}, bf16[3,96,512]{2,1,0:T(8,128)(2,1)S(1)}, u32[]{:S(2)}, u32[]{:S(2)}) collective-permute-start(bf16[3,96,512]{2,1,0:T(8,128)(2,1)} %get-tuple-element.70), channel_id=1, source_target_pairs={{0,96},{16,112},{32,0},{48,16},{64,32},{80,48},{96,64},{112,80},{1... | collective-permute-start | bytes 884744 | tf_op jit(solution)/shard_map/ppermute | solution.py:183
  117.4 14.2 %copy-start.26 = (bf16[256,768]{1,0:T(8,128)(2,1)S(1)}, bf16[256,768]{1,0:T(8,128)(2,1)}, u32[]{:S(2)}) copy-start(bf16[256,768]{1,0:T(8,128)(2,1)} %get-tuple-element.79.a_ref) | copy-start | bytes 1179652
  124.0 20.0 %collective-permute-start.25 = (bf16[512,768]{1,0:T(8,128)(2,1)}, bf16[512,768]{1,0:T(8,128)(2,1)}, u32[]{:S(2)}, u32[]{:S(2)}) collective-permute-start(bf16[512,768]{1,0:T(8,128)(2,1)} %get-tuple-element.71.refs_0_), channel_id=1, source_target_pairs={{0,12},{1,13},{2,14},{3,15},{4,8},{5,9},{6,10},{7,11},{8,4},{9,5},... | collective-permute-start | bytes 2359304 | tf_op jit(solution)/shard_map/ppermute | solution.py:62
  126.0 17.9 %collective-permute-start.26 = (bf16[512,768]{1,0:T(8,128)(2,1)}, bf16[512,768]{1,0:T(8,128)(2,1)}, u32[]{:S(2)}, u32[]{:S(2)}) collective-permute-start(bf16[512,768]{1,0:T(8,128)(2,1)} %get-tuple-element.72.refs_2_), channel_id=1, source_target_pairs={{0,4},{1,5},{2,6},{3,7},{4,0},{5,1},{6,2},{7,3},{8,12},{9,13},{10,... | collective-permute-start | bytes 2359304 | tf_op jit(solution)/shard_map/ppermute | solution.py:62
  126.3 13.9 %collective-permute-start.27 = (bf16[3,96,512]{2,1,0:T(8,128)(2,1)}, bf16[3,96,512]{2,1,0:T(8,128)(2,1)}, u32[]{:S(2)}, u32[]{:S(2)}) collective-permute-start(bf16[3,96,512]{2,1,0:T(8,128)(2,1)} %get-tuple-element.73), channel_id=1, source_target_pairs={{0,32},{16,48},{32,64},{48,80},{64,96},{80,112},{96,0},{112,16},{1... | collective-permute-start | bytes 884744 | tf_op jit(solution)/shard_map/ppermute | solution.py:183
  127.5 15.0 %collective-permute-start.28 = (bf16[3,96,512]{2,1,0:T(8,128)(2,1)}, bf16[3,96,512]{2,1,0:T(8,128)(2,1)}, u32[]{:S(2)}, u32[]{:S(2)}) collective-permute-start(bf16[3,96,512]{2,1,0:T(8,128)(2,1)} %get-tuple-element.74), channel_id=1, source_target_pairs={{0,64},{16,80},{32,96},{48,112},{64,0},{80,16},{96,32},{112,48},{1... | collective-permute-start | bytes 884744 | tf_op jit(solution)/shard_map/ppermute | solution.py:183
  129.8 14.1 %collective-permute-start.29 = (bf16[3,96,512]{2,1,0:T(8,128)(2,1)}, bf16[3,96,512]{2,1,0:T(8,128)(2,1)}, u32[]{:S(2)}, u32[]{:S(2)}) collective-permute-start(bf16[3,96,512]{2,1,0:T(8,128)(2,1)} %get-tuple-element.75), channel_id=1, source_target_pairs={{0,96},{16,112},{32,0},{48,16},{64,32},{80,48},{96,64},{112,80},{1... | collective-permute-start | bytes 884744 | tf_op jit(solution)/shard_map/ppermute | solution.py:183
  133.8 30.5 %all-to-all-start.2 = ((bf16[128,8,768]{2,1,0:T(8,128)(2,1)}), bf16[128,8,768]{2,1,0:T(8,128)(2,1)}, u32[]{:S(2)}, u32[]{:S(2)}) async-start(bf16[128,8,768]{2,1,0:T(8,128)(2,1)} %bitcast.14), calls=%async_computation.2 | async-start | bytes 3145728 | tf_op jit(solution)/shard_map/all_to_all | solution.py:153
  140.2 8.0 %copy-start.14 = (bf16[3,96,512]{2,1,0:T(8,128)(2,1)S(1)}, bf16[3,96,512]{2,1,0:T(8,128)(2,1)}, u32[]{:S(2)}) copy-start(bf16[3,96,512]{2,1,0:T(8,128)(2,1)} %copy-done.13) | copy-start | bytes 884740
  140.2 8.0 %copy-start.28 = (bf16[3,96,512]{2,1,0:T(8,128)(2,1)S(1)}, bf16[3,96,512]{2,1,0:T(8,128)(2,1)}, u32[]{:S(2)}) copy-start(bf16[3,96,512]{2,1,0:T(8,128)(2,1)} %copy-done.27) | copy-start | bytes 884740
  147.6 36.3 %collective-permute-start.30 = (bf16[1024,768]{1,0:T(8,128)(2,1)}, bf16[1024,768]{1,0:T(8,128)(2,1)}, u32[]{:S(2)}, u32[]{:S(2)}) collective-permute-start(bf16[1024,768]{1,0:T(8,128)(2,1)} %get-tuple-element.76.b0), channel_id=1, source_target_pairs={{0,3},{1,2},{2,1},{3,0},{4,7},{5,6},{6,5},{7,4},{8,11},{9,10},{10,... | collective-permute-start | bytes 4718600 | tf_op jit(solution)/shard_map/ppermute | solution.py:62
  147.6 36.3 %collective-permute-start.31 = (bf16[1024,768]{1,0:T(8,128)(2,1)}, bf16[1024,768]{1,0:T(8,128)(2,1)}, u32[]{:S(2)}, u32[]{:S(2)}) collective-permute-start(bf16[1024,768]{1,0:T(8,128)(2,1)} %get-tuple-element.77.b1), channel_id=1, source_target_pairs={{0,1},{1,0},{2,3},{3,2},{4,5},{5,4},{6,7},{7,6},{8,9},{9,8},{10,11... | collective-permute-start | bytes 4718600 | tf_op jit(solution)/shard_map/ppermute | solution.py:62
  152.3 18.7 %collective-permute-start.32 = (bf16[256,512]{1,0:T(8,128)(2,1)}, bf16[256,512]{1,0:T(8,128)(2,1)S(1)}, u32[]{:S(2)}, u32[]{:S(2)}) collective-permute-start(bf16[256,512]{1,0:T(8,128)(2,1)} %get-tuple-element.86), channel_id=1, source_target_pairs={{0,4},{1,5},{2,6},{3,7},{4,8},{5,9},{6,10},{7,11},{8,12},{9,13},{1... | collective-permute-start | bytes 786440 | tf_op jit(solution)/shard_map/ppermute | solution.py:462
  154.2 16.9 %collective-permute-start.33 = (bf16[256,512]{1,0:T(8,128)(2,1)}, bf16[256,512]{1,0:T(8,128)(2,1)S(1)}, u32[]{:S(2)}, u32[]{:S(2)}) collective-permute-start(bf16[256,512]{1,0:T(8,128)(2,1)} %get-tuple-element.87), channel_id=1, source_target_pairs={{0,8},{1,9},{2,10},{3,11},{4,12},{5,13},{6,14},{7,15},{8,0},{9,1},... | collective-permute-start | bytes 786440 | tf_op jit(solution)/shard_map/ppermute | solution.py:462
  156.8 14.3 %collective-permute-start.34 = (bf16[256,512]{1,0:T(8,128)(2,1)}, bf16[256,512]{1,0:T(8,128)(2,1)}, u32[]{:S(2)}, u32[]{:S(2)}) collective-permute-start(bf16[256,512]{1,0:T(8,128)(2,1)} %get-tuple-element.88), channel_id=1, source_target_pairs={{0,12},{1,13},{2,14},{3,15},{4,0},{5,1},{6,2},{7,3},{8,4},{9,5},{1... | collective-permute-start | bytes 786440 | tf_op jit(solution)/shard_map/ppermute | solution.py:462
  164.3 1.2 copy-start.15
  167.8 3.3 %copy-start.31 = (bf16[256,512]{1,0:T(8,128)(2,1)S(1)}, bf16[256,512]{1,0:T(8,128)(2,1)}, u32[]{:S(2)}) copy-start(bf16[256,512]{1,0:T(8,128)(2,1)} %copy-done.30) | copy-start | bytes 786436
  173.3 14.2 %collective-permute-start.35 = (f32[64,512]{1,0:T(8,128)S(1)}, f32[64,512]{1,0:T(8,128)S(1)}, u32[]{:S(2)}, u32[]{:S(2)}) collective-permute-start(f32[64,512]{1,0:T(8,128)S(1)} %get-tuple-element.90), channel_id=1, source_target_pairs={{0,1},{1,2},{2,3},{3,0},{4,5},{5,6},{6,7},{7,4},{8,9},{9,10},{10,1... | collective-permute-start | bytes 393224 | tf_op jit(solution)/shard_map/ppermute | solution.py:462
  175.0 12.5 %collective-permute-start.36 = (f32[64,512]{1,0:T(8,128)S(1)}, f32[64,512]{1,0:T(8,128)S(1)}, u32[]{:S(2)}, u32[]{:S(2)}) collective-permute-start(f32[64,512]{1,0:T(8,128)S(1)} %get-tuple-element.91), channel_id=1, source_target_pairs={{0,2},{1,3},{2,0},{3,1},{4,6},{5,7},{6,4},{7,5},{8,10},{9,11},{10,... | collective-permute-start | bytes 393224 | tf_op jit(solution)/shard_map/ppermute | solution.py:462
  178.2 9.3 %collective-permute-start.37 = (f32[64,512]{1,0:T(8,128)S(1)}, f32[64,512]{1,0:T(8,128)S(1)}, u32[]{:S(2)}, u32[]{:S(2)}) collective-permute-start(f32[64,512]{1,0:T(8,128)S(1)} %get-tuple-element.92), channel_id=1, source_target_pairs={{0,3},{1,0},{2,1},{3,2},{4,7},{5,4},{6,5},{7,6},{8,11},{9,8},{10,9... | collective-permute-start | bytes 393224 | tf_op jit(solution)/shard_map/ppermute | solution.py:462
  (12 other events, 11.8 us)

commit v8 on v7

--- a/solution.py
+++ b/solution.py
@@ -526,7 +526,7 @@
 
     out_paper, pack, dz_cite = paper_step(
         table, [pair[1] for pair in pairs], cite_first, cite_nbr, pre_paper, grad_paper, w_cite,
-        parts_author, lists[0][1], authored,
+        parts_author, written_pair[1], authored,
     )
     back_pairs = travel([dz_cite[:128], dz_cite[128:]], 0)
     dz_write, dx_paper_own = edge_back(pack, cnt, w_write, w_self_paper)
@@ -534,8 +534,8 @@
     left, right = weight_parts(
         place, (pack, pack_other), [x_paper_pair, (pack, pack_other), written_pair], dz_write, 2,
     )
+    parts = join(back_pairs, (left[0], lists[0][1]))
     lists = travel(join(lists), 3)[0]
-    parts = join(back_pairs, (left[0], lists[1], got_author))
     pairs = travel(parts, 1)
     left = over_y(left)
     rows = pick_rows(pick, dz_written, dz_write, parts[0])

time: 190 us -> 190 us (level)
  starting transfers between devices: 67.6 us -> 76.3 us
  waiting for transfers between devices: 40.9 us -> 33 us
  local copies, waits for them, and re-layouts: 16.3 us -> 13.8 us
    ppermute x6, starting transfers between devices: 13.1 us -> 18.9 us  [over_col(): got.append(lax.ppermute(parts[d], ('row', 'col'), perm))]
    ppermute x6, waiting for transfers between devices: 8.91 us -> 5.37 us  [over_y(): got.append(lax.ppermute(parts[d], 'row', perm))]
    ppermute x6, waiting for transfers between devices: 3.38 us -> 0.02 us  [other_core(): return lax.ppermute(value, 'row', [(i, i ^ 1) for i in range(8)])]
    unnamed x73, local copies, waits for them, and re-layouts: 13.4 us -> 10.3 us
    ppermute x20, starting transfers between devices: 22.7 us -> 25.3 us  [travel(): pairs.append((part, lax.ppermute(part, ('row', 'col'), perm)))]
    all_to_all x2, waiting for transfers between devices: 10.2 us -> 7.94 us  [exchange(): lax.all_to_all(sent, ('row', 'col'), split_axis=0, concat_axis=0, tiled=T...]
  transfers between devices with their start and end apart: 41 -> 41, of which waited for: 15 -> 12; matrix products, arithmetic and copies ran while one was open for 1% -> 1% of each run, Pallas kernels for 32% -> 31%
where the time goes in v8:
time: 190 us; the launch traced here: 189 us
  starting transfers between devices  76.3 us (40%)
  Pallas kernels  64.9 us (34%)
  waiting for transfers between devices  33 us (17%)
  local copies, waits for them, and re-layouts  13.8 us (7%)
    ppermute x20, starting transfers between devices, travel(): pairs.append((part, lax.ppermute(part, ('row', 'col'), perm)))  25.3 us
    ppermute x6, starting transfers between devices, over_col(): got.append(lax.ppermute(parts[d], ('row', 'col'), perm))  18.9 us
    ppermute x20, waiting for transfers between devices, travel(): pairs.append((part, lax.ppermute(part, ('row', 'col'), perm)))  18.6 us
    all_to_all x2, starting transfers between devices, exchange(): lax.all_to_all(sent, ('row', 'col'), split_axis=0, concat_axis=0, tiled=T...  15.2 us
    ppermute x6, starting transfers between devices, over_y(): got.append(lax.ppermute(parts[d], 'row', perm))  11 us
    pallas_call x9, Pallas kernels, join(): pl.pallas_call(functools.partial(join_kernel, n), out_shape=outs, in_spec...  10.8 us
    unnamed x73, local copies, waits for them, and re-layouts  10.3 us
    pallas_call x1, Pallas kernels, author_step(): pl.pallas_call(author_kernel, out_shape=[shape((256, 1024), BF), shape((2...  8.24 us
  transfers between devices with their start and end apart: 41, of which 12 were waited for; matrix products, arithmetic and copies ran while one was open for 1% of the time, Pallas kernels for 31%

profile of v8, /device:TPU:0, one launch (start us, length us, event | category | flops | bytes accessed | tf_op | source)
XLA Modules:
  0.0 189.3 jit_solution(17060736808098712960)
XLA Ops:
  0.7 1.1 fusion.1
  1.8 1.7 collective-permute-start
  3.5 2.1 %collective-permute-start.1 = (bf16[128,768]{1,0:T(8,128)(2,1)S(1)}, bf16[128,768]{1,0:T(8,128)(2,1)S(1)}, u32[]{:S(2)}, u32[]{:S(2)}) collective-permute-start(bf16[128,768]{1,0:T(8,128)(2,1)S(1)} %get-tuple-element.95.refs_2_), channel_id=1, source_target_pairs={{0,12},{1,13},{2,14},{3,15},{4,8},{5,9},{6,10},{7,11},{8,4},{9,5},... | collective-permute-start | bytes 589832 | tf_op jit(solution)/shard_map/ppermute | solution.py:62
  5.6 2.0 %collective-permute-done.refs_1_ = bf16[128,768]{1,0:T(8,128)(2,1)S(1)} collective-permute-done((bf16[128,768]{1,0:T(8,128)(2,1)S(1)}, bf16[128,768]{1,0:T(8,128)(2,1)S(1)}, u32[]{:S(2)}, u32[]{:S(2)}) %collective-permute-start) | collective-permute-done | bytes 196640 | tf_op jit(solution)/shard_map/ppermute | solution.py:62
  7.6 2.8 %collective-permute-done.1.refs_3_ = bf16[128,768]{1,0:T(8,128)(2,1)S(1)} collective-permute-done((bf16[128,768]{1,0:T(8,128)(2,1)S(1)}, bf16[128,768]{1,0:T(8,128)(2,1)S(1)}, u32[]{:S(2)}, u32[]{:S(2)}) %collective-permute-start.1) | collective-permute-done | bytes 196640 | tf_op jit(solution)/shard_map/ppermute | solution.py:62
  10.4 2.0 %collective-permute-start.2 = (bf16[256,768]{1,0:T(8,128)(2,1)S(1)}, bf16[256,768]{1,0:T(8,128)(2,1)S(1)}, u32[]{:S(2)}, u32[]{:S(2)}) collective-permute-start(bf16[256,768]{1,0:T(8,128)(2,1)S(1)} %get-tuple-element.49.refs_0_), channel_id=1, source_target_pairs={{0,1},{1,0},{2,3},{3,2},{4,5},{5,4},{6,7},{7,6},{8,9},{9,8},{10,11... | collective-permute-start | bytes 1179656 | tf_op jit(solution)/shard_map/ppermute | solution.py:62
  12.4 2.5 %collective-permute-start.3 = (bf16[256,768]{1,0:T(8,128)(2,1)S(1)}, bf16[256,768]{1,0:T(8,128)(2,1)S(1)}, u32[]{:S(2)}, u32[]{:S(2)}) collective-permute-start(bf16[256,768]{1,0:T(8,128)(2,1)S(1)} %get-tuple-element.50.refs_2_), channel_id=1, source_target_pairs={{0,3},{1,2},{2,1},{3,0},{4,7},{5,6},{6,5},{7,4},{8,11},{9,10},{10,... | collective-permute-start | bytes 1179656 | tf_op jit(solution)/shard_map/ppermute | solution.py:62
  14.9 4.0 %collective-permute-done.4.refs_1_.token_ref = s32[1,16,256]{2,1,0:T(8,128)S(1)} collective-permute-done((s32[1,16,256]{2,1,0:T(8,128)S(1)}, s32[1,16,256]{2,1,0:T(8,128)S(1)}, u32[]{:S(2)}, u32[]{:S(2)}) %collective-permute-start.4) | collective-permute-done | bytes 16416 | tf_op jit(solution)/shard_map/ppermute | solution.py:62
  19.7 3.1 %collective-permute-done.5.refs_4_.refs_1_ = s32[2,16,256]{2,1,0:T(8,128)S(1)} collective-permute-done((s32[2,16,256]{2,1,0:T(8,128)S(1)}, s32[2,16,256]{2,1,0:T(8,128)S(1)}, u32[]{:S(2)}, u32[]{:S(2)}) %collective-permute-start.5) | collective-permute-done | bytes 32800 | tf_op jit(solution)/shard_map/ppermute | solution.py:62
  22.8 1.0 join.11
  23.8 1.9 collective-permute-start.6
  25.9 2.2 %pick_rows.2 = bf16[1024,768]{1,0:T(8,128)(2,1)} custom-call(s32[1,1024]{1,0:T(1,128)S(1)} %reshape.35.pick_ref, bf16[256,768]{1,0:T(8,128)(2,1)S(1)} %copy-done.6, bf16[256,768]{1,0:T(8,128)(2,1)S(1)} %copy-done.1, s32[1,16,256]{2,1,0:T(8,128)S(1)} %collective-permute-done.4.refs_1_.token_ref), custom_call_target="tpu_custom_call" | custom-call | flops 1 | bytes 1 | tf_op jit(solution)/shard_map/pick_rows/pallas_call | solution.py:164
  28.1 8.4 %all-to-all-start = ((bf16[128,8,768]{2,1,0:T(8,128)(2,1)}), bf16[128,8,768]{2,1,0:T(8,128)(2,1)}, u32[]{:S(2)}, u32[]{:S(2)}) async-start(bf16[128,8,768]{2,1,0:T(8,128)(2,1)} %bitcast.8), calls=%async_computation | async-start | bytes 3145728 | tf_op jit(solution)/shard_map/all_to_all | solution.py:153
  36.7 8.0 %cite_table.1.refs_4_.table_ref.refs_6_ = bf16[256,4096]{1,0:T(8,128)(2,1)S(1)} custom-call(s32[3]{0:T(128)S(1)} %pad_add_fusion.1.place_ref, s32[256,16]{1,0:T(8,128)S(1)} %copy.22.nbr_ref, bf16[512,768]{1,0:T(8,128)(2,1)S(1)} %get-tuple-element.51.token_ref.refs_0_), custom_call_target="tpu_custom_call" | custom-call | flops 1 | bytes 1 | tf_op jit(solution)/shard_map/cite_table/pallas_call | solution.py:106
  44.7 3.4 %join.12 = (bf16[1024,768]{1,0:T(8,128)(2,1)}, bf16[1024,768]{1,0:T(8,128)(2,1)}) custom-call(bf16[512,768]{1,0:T(8,128)(2,1)S(1)} %get-tuple-element.51.token_ref.refs_0_, bf16[512,768]{1,0:T(8,128)(2,1)} %collective-permute-done.6.refs_1_, bf16[512,768]{1,0:T(8,128)(2,1)} %get-tuple-element.52.refs_2_, bf16[512,768]{1,0:T(8,128)(2,1)} %collective-permute-done.7.refs_3_, ...), custom_call_target="tpu_custom_call" | custom-call | tf_op jit(solution)/shard_map/join/pallas_call | solution.py:47
  48.2 2.8 %collective-permute-start.8 = (bf16[1024,768]{1,0:T(8,128)(2,1)}, bf16[1024,768]{1,0:T(8,128)(2,1)}, u32[]{:S(2)}, u32[]{:S(2)}) collective-permute-start(bf16[1024,768]{1,0:T(8,128)(2,1)} %get-tuple-element.53.b0.refs_7_), channel_id=1, source_target_pairs={{0,3},{1,2},{2,1},{3,0},{4,7},{5,6},{6,5},{7,4},{8,11},{9,10},{10,... | collective-permute-start | bytes 4718600 | tf_op jit(solution)/shard_map/ppermute | solution.py:62
  52.6 7.9 %all-to-all-done = bf16[128,8,768]{2,1,0:T(8,128)(2,1)} async-done(((bf16[128,8,768]{2,1,0:T(8,128)(2,1)}), bf16[128,8,768]{2,1,0:T(8,128)(2,1)}, u32[]{:S(2)}, u32[]{:S(2)}) %all-to-all-start) | async-done | bytes 1572896 | tf_op jit(solution)/shard_map/all_to_all | solution.py:153
  60.6 8.2 %author_step.1 = (bf16[256,1024]{1,0:T(8,128)(2,1)}, bf16[256,768]{1,0:T(8,128)(2,1)}, bf16[256,768]{1,0:T(8,128)(2,1)}, bf16[256,1024]{1,0:T(8,128)(2,1)}, bf16...) custom-call(bf16[1024,768]{1,0:T(8,128)(2,1)} %bitcast.9.arrived_ref, ...), custom_call_target="tpu_custom_call" | custom-call | flops 1 | bytes 1 | tf_op jit(solution)/shard_map/author_step/pallas_call | solution.py:233
  69.8 2.9 %first_half.2.first_ref = f32[256,768]{1,0:T(8,128)S(1)} custom-call(bf16[256,4096]{1,0:T(8,128)(2,1)S(1)} %cite_table.1.refs_4_.table_ref.refs_6_, bf16[1024,768]{1,0:T(8,128)(2,1)} %get-tuple-element.53.b0.refs_7_, bf16[1024,768]{1,0:T(8,128)(2,1)} %get-tuple-element.54.b1), custom_call_target="tpu_custom_call" | custom-call | flops 1 | bytes 1 | tf_op jit(solution)/shard_map/first_half/pallas_call | solution.py:256
  72.8 1.8 weight_parts.2.token_a
  75.2 5.1 %paper_step.1 = (bf16[256,1024]{1,0:T(8,128)(2,1)}, bf16[256,1792]{1,0:T(8,128)(2,1)S(1)}, bf16[256,768]{1,0:T(8,128)(2,1)S(1)}) custom-call(bf16[256,4096]{1,0:T(8,128)(2,1)S(1)} %cite_table.1.refs_4_.table_ref.refs_6_, bf16[1024,768]{1,0:T(8,128)(2,1)} %collective-permute-done.8.b0, bf16[1024,768]{1,0:T(8,128)(2,1)} %collective-permute-done.9.b1, ...), custom_call_target="tpu_custom_call" | custom-call | flops 1 | bytes 1 | tf_op jit(solution)/shard_map/paper_step/pallas_call | solution.py:326
  82.3 2.2 %collective-permute-start.17 = (bf16[128,768]{1,0:T(8,128)(2,1)S(1)}, bf16[128,768]{1,0:T(8,128)(2,1)}, u32[]{:S(2)}, u32[]{:S(2)}) collective-permute-start(bf16[128,768]{1,0:T(8,128)(2,1)S(1)} %get-tuple-element.93.refs_2_), channel_id=1, source_target_pairs={{0,12},{1,13},{2,14},{3,15},{4,8},{5,9},{6,10},{7,11},{8,4},{9,5},... | collective-permute-start | bytes 589832 | tf_op jit(solution)/shard_map/ppermute | solution.py:62
  84.5 4.3 %all-to-all-start.2 = ((bf16[4,2,96,1024]{3,2,1,0:T(8,128)(2,1)}), bf16[4,2,96,1024]{3,2,1,0:T(8,128)(2,1)}, u32[]{:S(2)}, u32[]{:S(2)}) async-start(bf16[4,2,96,1024]{3,2,1,0:T(8,128)(2,1)} %copy-done), calls=%async_computation.2 | async-start | bytes 3145728 | tf_op jit(solution)/shard_map/all_to_all | solution.py:521
  88.9 1.1 collective-permute-start.14
  90.0 4.4 %collective-permute-done.14.refs_1_.refs_5_ = s32[4,16,256]{2,1,0:T(8,128)S(1)} collective-permute-done((s32[4,16,256]{2,1,0:T(8,128)S(1)}, s32[4,16,256]{2,1,0:T(8,128)S(1)}, u32[]{:S(2)}, u32[]{:S(2)}) %collective-permute-start.14) | collective-permute-done | bytes 65568 | tf_op jit(solution)/shard_map/ppermute | solution.py:62
  95.0 1.4 copy-done.4
  97.3 1.7 edge_back.1
  100.0 4.2 %weight_parts.3 = (bf16[3,96,512]{2,1,0:T(8,128)(2,1)S(1)}, bf16[3,96,512]{2,1,0:T(8,128)(2,1)S(1)}, bf16[3,96,512]{2,1,0:T(8,128)(2,1)S(1)}, bf16[3,96,512]{2,1...) custom-call(s32[3]{0:T(128)S(1)} %pad_add_fusion.1.place_ref, ...), custom_call_target="tpu_custom_call" | custom-call | flops 1 | bytes 1 | tf_op jit(solution)/shard_map/weight_parts/pallas_call | solution.py:386
  104.2 1.4 join.15
  106.5 2.0 %collective-permute-start.21 = (bf16[256,768]{1,0:T(8,128)(2,1)S(1)}, bf16[256,768]{1,0:T(8,128)(2,1)S(1)}, u32[]{:S(2)}, u32[]{:S(2)}) collective-permute-start(bf16[256,768]{1,0:T(8,128)(2,1)S(1)} %get-tuple-element.67.refs_2_), channel_id=1, source_target_pairs={{0,3},{1,2},{2,1},{3,0},{4,7},{5,6},{6,5},{7,4},{8,11},{9,10},{10,... | collective-permute-start | bytes 1179656 | tf_op jit(solution)/shard_map/ppermute | solution.py:62
  108.5 2.0 %collective-permute-start.22 = (bf16[3,96,512]{2,1,0:T(8,128)(2,1)S(1)}, bf16[3,96,512]{2,1,0:T(8,128)(2,1)S(1)}, u32[]{:S(2)}, u32[]{:S(2)}) collective-permute-start(bf16[3,96,512]{2,1,0:T(8,128)(2,1)S(1)} %get-tuple-element.68), channel_id=1, source_target_pairs={{0,32},{16,48},{32,64},{48,80},{64,96},{80,112},{96,0},{112,16},{1... | collective-permute-start | bytes 884744 | tf_op jit(solution)/shard_map/ppermute | solution.py:183
  110.5 2.7 %collective-permute-start.23 = (bf16[3,96,512]{2,1,0:T(8,128)(2,1)S(1)}, bf16[3,96,512]{2,1,0:T(8,128)(2,1)S(1)}, u32[]{:S(2)}, u32[]{:S(2)}) collective-permute-start(bf16[3,96,512]{2,1,0:T(8,128)(2,1)S(1)} %get-tuple-element.69), channel_id=1, source_target_pairs={{0,64},{16,80},{32,96},{48,112},{64,0},{80,16},{96,32},{112,48},{1... | collective-permute-start | bytes 884744 | tf_op jit(solution)/shard_map/ppermute | solution.py:183
  113.2 1.5 collective-permute-start.24
  114.6 4.0 %cited_by_table.1.refs_4_.table_ref = bf16[256,4096]{1,0:T(8,128)(2,1)S(1)} custom-call(s32[3]{0:T(128)S(1)} %pad_add_fusion.1.place_ref, s32[8,16,256]{2,1,0:T(8,128)S(1)} %join.14.a_ref, s32[8,16,256]{2,1,0:T(8,128)S(1)} %collective-permute-done.15.b_ref, bf16[256,768]{1,0:T(8,128)(2,1)S(1)} %get-tuple-element.66.token_ref.refs_0_), custom_call_target="tpu_custom_call" | custom-call | flops 1 | bytes 1 | tf_op jit(solution)/shard_map/cited_by_table/pallas_call | solution.py:132
  118.7 0.9 collective-permute-done.22.refs_5_.refs_1_
  119.6 3.7 %collective-permute-done.23.refs_6_.refs_2_ = bf16[3,96,512]{2,1,0:T(8,128)(2,1)S(1)} collective-permute-done((bf16[3,96,512]{2,1,0:T(8,128)(2,1)S(1)}, bf16[3,96,512]{2,1,0:T(8,128)(2,1)S(1)}, u32[]{:S(2)}, u32[]{:S(2)}) %collective-permute-start.23) | collective-permute-done | bytes 294944 | tf_op jit(solution)/shard_map/ppermute | solution.py:183
  123.3 1.3 join.16
  124.7 1.4 collective-permute-start.25
  126.7 1.1 collective-permute-start.27
  127.8 2.4 %collective-permute-start.28 = (bf16[3,96,512]{2,1,0:T(8,128)(2,1)}, bf16[3,96,512]{2,1,0:T(8,128)(2,1)}, u32[]{:S(2)}, u32[]{:S(2)}) collective-permute-start(bf16[3,96,512]{2,1,0:T(8,128)(2,1)} %get-tuple-element.74), channel_id=1, source_target_pairs={{0,64},{16,80},{32,96},{48,112},{64,0},{80,16},{96,32},{112,48},{1... | collective-permute-start | bytes 884744 | tf_op jit(solution)/shard_map/ppermute | solution.py:183
  130.2 1.4 collective-permute-start.29
  131.6 1.0 pick_rows.3
  132.6 1.1 copy-done.5
  133.7 6.9 %all-to-all-start.1 = ((bf16[128,8,768]{2,1,0:T(8,128)(2,1)}), bf16[128,8,768]{2,1,0:T(8,128)(2,1)}, u32[]{:S(2)}, u32[]{:S(2)}) async-start(bf16[128,8,768]{2,1,0:T(8,128)(2,1)} %bitcast.14), calls=%async_computation.1 | async-start | bytes 3145728 | tf_op jit(solution)/shard_map/all_to_all | solution.py:153
  141.4 3.7 %join.17 = (bf16[1024,768]{1,0:T(8,128)(2,1)}, bf16[1024,768]{1,0:T(8,128)(2,1)}) custom-call(bf16[512,768]{1,0:T(8,128)(2,1)} %get-tuple-element.71.refs_0_, bf16[512,768]{1,0:T(8,128)(2,1)} %collective-permute-done.25.refs_1_, bf16[512,768]{1,0:T(8,128)(2,1)} %get-tuple-element.72.refs_2_, bf16[512,768]{1,0:T(8,128)(2,1)} %collective-permute-done.26.refs_3_, ...), custom_call_target="tpu_custom_call" | custom-call | tf_op jit(solution)/shard_map/join/pallas_call | solution.py:47
  145.0 2.1 %collective-permute-start.30 = (bf16[1024,768]{1,0:T(8,128)(2,1)}, bf16[1024,768]{1,0:T(8,128)(2,1)}, u32[]{:S(2)}, u32[]{:S(2)}) collective-permute-start(bf16[1024,768]{1,0:T(8,128)(2,1)} %get-tuple-element.76.b0), channel_id=1, source_target_pairs={{0,3},{1,2},{2,1},{3,0},{4,7},{5,6},{6,5},{7,4},{8,11},{9,10},{10,... | collective-permute-start | bytes 4718600 | tf_op jit(solution)/shard_map/ppermute | solution.py:62
  147.3 3.2 %y_sum.1 = (bf16[256,512]{1,0:T(8,128)(2,1)S(1)}, bf16[256,512]{1,0:T(8,128)(2,1)}, bf16[256,512]{1,0:T(8,128)(2,1)}, bf16[256,512]{1,0:T(8,128)(2,1)}) custom-call(s32[3]{0:T(128)S(1)} %pad_add_fusion.1.place_ref, bf16[3,96,512]{2,1,0:T(8,128)(2,1)S(1)} %copy-done.14, bf16[3,96,512]{2,1,0:T(8,128)(2,1)S(1)} %collective-permute-done.22.refs_5_.refs_1_, ...), custom_call_target="tpu_custom_call" | custom-call | flops 1 | bytes 1 | tf_op jit(solution)/shard_map/y_sum/pallas_call | solution.py:418
  150.5 7.2 %collective-permute-start.32 = (bf16[256,512]{1,0:T(8,128)(2,1)}, bf16[256,512]{1,0:T(8,128)(2,1)S(1)}, u32[]{:S(2)}, u32[]{:S(2)}) collective-permute-start(bf16[256,512]{1,0:T(8,128)(2,1)} %get-tuple-element.86), channel_id=1, source_target_pairs={{0,4},{1,5},{2,6},{3,7},{4,8},{5,9},{6,10},{7,11},{8,12},{9,13},{1... | collective-permute-start | bytes 786440 | tf_op jit(solution)/shard_map/ppermute | solution.py:462
  157.7 1.7 collective-permute-start.33
  159.4 2.6 %collective-permute-start.34 = (bf16[256,512]{1,0:T(8,128)(2,1)}, bf16[256,512]{1,0:T(8,128)(2,1)}, u32[]{:S(2)}, u32[]{:S(2)}) collective-permute-start(bf16[256,512]{1,0:T(8,128)(2,1)} %get-tuple-element.88), channel_id=1, source_target_pairs={{0,12},{1,13},{2,14},{3,15},{4,0},{5,1},{6,2},{7,3},{8,4},{9,5},{1... | collective-permute-start | bytes 786440 | tf_op jit(solution)/shard_map/ppermute | solution.py:462
  162.0 2.9 %first_half.3.first_ref.token_a = f32[256,768]{1,0:T(8,128)S(1)} custom-call(bf16[256,4096]{1,0:T(8,128)(2,1)S(1)} %cited_by_table.1.refs_4_.table_ref, bf16[1024,768]{1,0:T(8,128)(2,1)} %get-tuple-element.76.b0, bf16[1024,768]{1,0:T(8,128)(2,1)} %get-tuple-element.77.b1), custom_call_target="tpu_custom_call" | custom-call | flops 1 | bytes 1 | tf_op jit(solution)/shard_map/first_half/pallas_call | solution.py:256
  164.9 1.2 copy-done.16
  166.1 1.1 copy-done.17
  167.2 1.1 copy-done.19
  168.4 3.1 %edge_add.1 = (bf16[256,768]{1,0:T(8,128)(2,1)}, f32[256,768]{1,0:T(8,128)S(1)}) custom-call(bf16[512,1024]{1,0:T(8,128)(2,1)S(1)} %copy-done.16, bf16[1024,768]{1,0:T(8,128)(2,1)} %bitcast.11.back_ref, f32[256,768]{1,0:T(8,128)S(1)} %copy-done.17, f32[256,768]{1,0:T(8,128)S(1)} %copy-done.19), custom_call_target="tpu_custom_call" | custom-call | flops 1 | bytes 1 | tf_op jit(solution)/shard_map/edge_add/pallas_call | solution.py:291
  171.5 1.0 collective-permute-done.33.refs_2_
  172.5 1.0 copy-done.23
  173.5 1.3 x_sum.1
  174.8 2.1 %collective-permute-start.35 = (f32[64,512]{1,0:T(8,128)S(1)}, f32[64,512]{1,0:T(8,128)S(1)}, u32[]{:S(2)}, u32[]{:S(2)}) collective-permute-start(f32[64,512]{1,0:T(8,128)S(1)} %get-tuple-element.90), channel_id=1, source_target_pairs={{0,1},{1,2},{2,3},{3,0},{4,5},{5,6},{6,7},{7,4},{8,9},{9,10},{10,1... | collective-permute-start | bytes 393224 | tf_op jit(solution)/shard_map/ppermute | solution.py:462
  176.9 2.8 %collective-permute-start.36 = (f32[64,512]{1,0:T(8,128)S(1)}, f32[64,512]{1,0:T(8,128)S(1)}, u32[]{:S(2)}, u32[]{:S(2)}) collective-permute-start(f32[64,512]{1,0:T(8,128)S(1)} %get-tuple-element.91), channel_id=1, source_target_pairs={{0,2},{1,3},{2,0},{3,1},{4,6},{5,7},{6,4},{7,5},{8,10},{9,11},{10,... | collective-permute-start | bytes 393224 | tf_op jit(solution)/shard_map/ppermute | solution.py:462
  179.6 2.5 %collective-permute-start.37 = (f32[64,512]{1,0:T(8,128)S(1)}, f32[64,512]{1,0:T(8,128)S(1)}, u32[]{:S(2)}, u32[]{:S(2)}) collective-permute-start(f32[64,512]{1,0:T(8,128)S(1)} %get-tuple-element.92), channel_id=1, source_target_pairs={{0,3},{1,0},{2,1},{3,2},{4,7},{5,4},{6,5},{7,6},{8,11},{9,8},{10,9... | collective-permute-start | bytes 393224 | tf_op jit(solution)/shard_map/ppermute | solution.py:462
  182.2 1.7 collective-permute-done.30.b0
  183.9 3.6 %last_half.1.token_ref = bf16[256,768]{1,0:T(8,128)(2,1)} custom-call(bf16[256,4096]{1,0:T(8,128)(2,1)S(1)} %cited_by_table.1.refs_4_.table_ref, bf16[1024,768]{1,0:T(8,128)(2,1)} %collective-permute-done.30.b0, bf16[1024,768]{1,0:T(8,128)(2,1)} %collective-permute-done.31.b1, f32[256,768]{1,0:T(8,128)S(1)} %first_half.3.first_ref.token_a, ...), custom_call_target="tpu_custom_call" | custom-call | flops 1 | bytes 1 | tf_op jit(solution)/shard_map/last_half/pallas_call | solution.py:273
  187.5 1.0 copy-done.11
  (127 shorter events, 12.1 us)
Async XLA Ops:
  0.6 25.3 %copy-start.1 = (bf16[256,768]{1,0:T(8,128)(2,1)S(1)}, bf16[256,768]{1,0:T(8,128)(2,1)}, u32[]{:S(2)}) copy-start(bf16[256,768]{1,0:T(8,128)(2,1)} %refs_2_.5) | copy-start | bytes 1179652
  0.6 14.3 %copy-start.32 = (s32[256,16]{0,1:T(8,128)S(1)}, s32[256,16]{0,1:T(8,128)}, u32[]{:S(2)}) copy-start(s32[256,16]{0,1:T(8,128)} %param.14) | copy-start | bytes 49156
  0.7 25.0 %copy-start.33 = (s32[1,128,4]{1,2,0:T(4,128)S(1)}, s32[1,128,4]{1,2,0:T(4,128)}, u32[]{:S(2)}) copy-start(s32[1,128,4]{1,2,0:T(4,128)} %param.16) | copy-start | bytes 6148
  0.7 25.0 %copy-start.34 = (s32[1,128,4]{1,2,0:T(4,128)S(1)}, s32[1,128,4]{1,2,0:T(4,128)}, u32[]{:S(2)}) copy-start(s32[1,128,4]{1,2,0:T(4,128)} %param.15) | copy-start | bytes 6148
  0.7 25.2 %copy-start.6 = (bf16[256,768]{1,0:T(8,128)(2,1)S(1)}, bf16[256,768]{1,0:T(8,128)(2,1)}, u32[]{:S(2)}) copy-start(bf16[256,768]{1,0:T(8,128)(2,1)} %refs_2_.4) | copy-start | bytes 1179652
  1.8 5.7 %collective-permute-start = (bf16[128,768]{1,0:T(8,128)(2,1)S(1)}, bf16[128,768]{1,0:T(8,128)(2,1)S(1)}, u32[]{:S(2)}, u32[]{:S(2)}) collective-permute-start(bf16[128,768]{1,0:T(8,128)(2,1)S(1)} %get-tuple-element.96.refs_0_), channel_id=1, source_target_pairs={{0,4},{1,5},{2,6},{3,7},{4,0},{5,1},{6,2},{7,3},{8,12},{9,13},{10,... | collective-permute-start | bytes 589832 | tf_op jit(solution)/shard_map/ppermute | solution.py:62
  3.5 6.9 %collective-permute-start.1 = (bf16[128,768]{1,0:T(8,128)(2,1)S(1)}, bf16[128,768]{1,0:T(8,128)(2,1)S(1)}, u32[]{:S(2)}, u32[]{:S(2)}) collective-permute-start(bf16[128,768]{1,0:T(8,128)(2,1)S(1)} %get-tuple-element.95.refs_2_), channel_id=1, source_target_pairs={{0,12},{1,13},{2,14},{3,15},{4,8},{5,9},{6,10},{7,11},{8,4},{9,5},... | collective-permute-start | bytes 589832 | tf_op jit(solution)/shard_map/ppermute | solution.py:62
  10.4 12.4 %collective-permute-start.2 = (bf16[256,768]{1,0:T(8,128)(2,1)S(1)}, bf16[256,768]{1,0:T(8,128)(2,1)S(1)}, u32[]{:S(2)}, u32[]{:S(2)}) collective-permute-start(bf16[256,768]{1,0:T(8,128)(2,1)S(1)} %get-tuple-element.49.refs_0_), channel_id=1, source_target_pairs={{0,1},{1,0},{2,3},{3,2},{4,5},{5,4},{6,7},{7,6},{8,9},{9,8},{10,11... | collective-permute-start | bytes 1179656 | tf_op jit(solution)/shard_map/ppermute | solution.py:62
  12.4 10.4 %collective-permute-start.3 = (bf16[256,768]{1,0:T(8,128)(2,1)S(1)}, bf16[256,768]{1,0:T(8,128)(2,1)S(1)}, u32[]{:S(2)}, u32[]{:S(2)}) collective-permute-start(bf16[256,768]{1,0:T(8,128)(2,1)S(1)} %get-tuple-element.50.refs_2_), channel_id=1, source_target_pairs={{0,3},{1,2},{2,1},{3,0},{4,7},{5,6},{6,5},{7,4},{8,11},{9,10},{10,... | collective-permute-start | bytes 1179656 | tf_op jit(solution)/shard_map/ppermute | solution.py:62
  14.9 4.0 %collective-permute-start.4 = (s32[1,16,256]{2,1,0:T(8,128)S(1)}, s32[1,16,256]{2,1,0:T(8,128)S(1)}, u32[]{:S(2)}, u32[]{:S(2)}) collective-permute-start(s32[1,16,256]{2,1,0:T(8,128)S(1)} %bitcast.15), channel_id=1, source_target_pairs={{0,4},{1,5},{2,6},{3,7},{4,0},{5,1},{6,2},{7,3},{8,12},{9,13},{10,... | collective-permute-start | bytes 49160 | tf_op jit(solution)/shard_map/ppermute | solution.py:62
  18.9 4.9 %copy-start.30 = (s32[2,16,256]{2,1,0:T(8,128)}, s32[2,16,256]{2,1,0:T(8,128)S(1)}, u32[]{:S(2)}) copy-start(s32[2,16,256]{2,1,0:T(8,128)S(1)} %join.10.refs_0_) | copy-start | bytes 98308
  18.9 3.9 %collective-permute-start.5 = (s32[2,16,256]{2,1,0:T(8,128)S(1)}, s32[2,16,256]{2,1,0:T(8,128)S(1)}, u32[]{:S(2)}, u32[]{:S(2)}) collective-permute-start(s32[2,16,256]{2,1,0:T(8,128)S(1)} %join.10.refs_0_), channel_id=1, source_target_pairs={{0,1},{1,0},{2,3},{3,2},{4,5},{5,4},{6,7},{7,6},{8,9},{9,8},{10,11... | collective-permute-start | bytes 98312 | tf_op jit(solution)/shard_map/ppermute | solution.py:62
  22.8 5.3 %copy-start.28 = (s32[2,16,256]{2,1,0:T(8,128)}, s32[2,16,256]{2,1,0:T(8,128)S(1)}, u32[]{:S(2)}) copy-start(s32[2,16,256]{2,1,0:T(8,128)S(1)} %collective-permute-done.5.refs_4_.refs_1_) | copy-start | bytes 98308
  23.8 20.9 %collective-permute-start.6 = (bf16[512,768]{1,0:T(8,128)(2,1)S(1)}, bf16[512,768]{1,0:T(8,128)(2,1)}, u32[]{:S(2)}, u32[]{:S(2)}) collective-permute-start(bf16[512,768]{1,0:T(8,128)(2,1)S(1)} %get-tuple-element.51.token_ref.refs_0_), channel_id=1, source_target_pairs={{0,12},{1,13},{2,14},{3,15},{4,8},{5,9},{6,10},{7,11},{8,4},{9,5},... | collective-permute-start | bytes 2359304 | tf_op jit(solution)/shard_map/ppermute | solution.py:62
  25.7 19.1 %collective-permute-start.7 = (bf16[512,768]{1,0:T(8,128)(2,1)}, bf16[512,768]{1,0:T(8,128)(2,1)}, u32[]{:S(2)}, u32[]{:S(2)}) collective-permute-start(bf16[512,768]{1,0:T(8,128)(2,1)} %get-tuple-element.52.refs_2_), channel_id=1, source_target_pairs={{0,4},{1,5},{2,6},{3,7},{4,0},{5,1},{6,2},{7,3},{8,12},{9,13},{10,... | collective-permute-start | bytes 2359304 | tf_op jit(solution)/shard_map/ppermute | solution.py:62
  28.1 32.5 %all-to-all-start = ((bf16[128,8,768]{2,1,0:T(8,128)(2,1)}), bf16[128,8,768]{2,1,0:T(8,128)(2,1)}, u32[]{:S(2)}, u32[]{:S(2)}) async-start(bf16[128,8,768]{2,1,0:T(8,128)(2,1)} %bitcast.8), calls=%async_computation | async-start | bytes 3145728 | tf_op jit(solution)/shard_map/all_to_all | solution.py:153
  48.2 27.0 %collective-permute-start.8 = (bf16[1024,768]{1,0:T(8,128)(2,1)}, bf16[1024,768]{1,0:T(8,128)(2,1)}, u32[]{:S(2)}, u32[]{:S(2)}) collective-permute-start(bf16[1024,768]{1,0:T(8,128)(2,1)} %get-tuple-element.53.b0.refs_7_), channel_id=1, source_target_pairs={{0,3},{1,2},{2,1},{3,0},{4,7},{5,6},{6,5},{7,4},{8,11},{9,10},{10,... | collective-permute-start | bytes 4718600 | tf_op jit(solution)/shard_map/ppermute | solution.py:62
  50.9 24.2 %collective-permute-start.9 = (bf16[1024,768]{1,0:T(8,128)(2,1)}, bf16[1024,768]{1,0:T(8,128)(2,1)}, u32[]{:S(2)}, u32[]{:S(2)}) collective-permute-start(bf16[1024,768]{1,0:T(8,128)(2,1)} %get-tuple-element.54.b1), channel_id=1, source_target_pairs={{0,1},{1,0},{2,3},{3,2},{4,5},{5,4},{6,7},{7,6},{8,9},{9,8},{10,11... | collective-permute-start | bytes 4718600 | tf_op jit(solution)/shard_map/ppermute | solution.py:62
  50.9 18.5 %collective-permute-start.11 = (bf16[256,768]{1,0:T(8,128)(2,1)S(1)}, bf16[256,768]{1,0:T(8,128)(2,1)S(1)}, u32[]{:S(2)}, u32[]{:S(2)}) collective-permute-start(bf16[256,768]{1,0:T(8,128)(2,1)S(1)} %copy-done.6), channel_id=1, source_target_pairs={{0,16},{16,0},{32,48},{48,32},{64,80},{80,64},{96,112},{112,96},{1... | collective-permute-start | bytes 1179656 | tf_op jit(solution)/shard_map/ppermute | solution.py:176
  68.8 3.9 %collective-permute-start.10 = (bf16[256,1024]{1,0:T(8,128)(2,1)}, bf16[256,1024]{1,0:T(8,128)(2,1)S(1)}, u32[]{:S(2)}, u32[]{:S(2)}) collective-permute-start(bf16[256,1024]{1,0:T(8,128)(2,1)} %get-tuple-element.56.refs_0_), channel_id=1, source_target_pairs={{0,16},{16,0},{32,48},{48,32},{64,80},{80,64},{96,112},{112,96},{1... | collective-permute-start | bytes 1572872 | tf_op jit(solution)/shard_map/ppermute | solution.py:176
  68.9 3.8 %collective-permute-start.12 = (bf16[256,768]{1,0:T(8,128)(2,1)}, bf16[256,768]{1,0:T(8,128)(2,1)S(1)}, u32[]{:S(2)}, u32[]{:S(2)}) collective-permute-start(bf16[256,768]{1,0:T(8,128)(2,1)} %get-tuple-element.57.refs_4_.token_c), channel_id=1, source_target_pairs={{0,16},{16,0},{32,48},{48,32},{64,80},{80,64},{96,112},{112,96},{1... | collective-permute-start | bytes 1179656 | tf_op jit(solution)/shard_map/ppermute | solution.py:176
  69.4 3.3 %copy-start.7 = (bf16[256,768]{1,0:T(8,128)(2,1)S(1)}, bf16[256,768]{1,0:T(8,128)(2,1)}, u32[]{:S(2)}) copy-start(bf16[256,768]{1,0:T(8,128)(2,1)} %refs_2_.4) | copy-start | bytes 1179652
  69.4 3.3 %copy-start.10 = (bf16[256,768]{1,0:T(8,128)(2,1)S(1)}, bf16[256,768]{1,0:T(8,128)(2,1)}, u32[]{:S(2)}) copy-start(bf16[256,768]{1,0:T(8,128)(2,1)} %get-tuple-element.57.refs_4_.token_c) | copy-start | bytes 1179652
  69.4 3.3 %copy-start.21 = (bf16[256,1024]{1,0:T(8,128)(2,1)S(1)}, bf16[256,1024]{1,0:T(8,128)(2,1)}, u32[]{:S(2)}) copy-start(bf16[256,1024]{1,0:T(8,128)(2,1)} %get-tuple-element.56.refs_0_) | copy-start | bytes 1572868
  69.4 5.1 %collective-permute-start.13 = (bf16[256,768]{1,0:T(8,128)(2,1)}, bf16[256,768]{1,0:T(8,128)(2,1)S(1)}, u32[]{:S(2)}, u32[]{:S(2)}) collective-permute-start(bf16[256,768]{1,0:T(8,128)(2,1)} %get-tuple-element.58.refs_6_), channel_id=1, source_target_pairs={{0,16},{16,0},{32,48},{48,32},{64,80},{80,64},{96,112},{112,96},{1... | collective-permute-start | bytes 1179656 | tf_op jit(solution)/shard_map/ppermute | solution.py:176
  74.6 5.8 %copy-start = (bf16[4,2,96,1024]{3,2,1,0:T(8,128)(2,1)}, bf16[4,2,96,1024]{3,2,1,0:T(8,128)(2,1)S(1)}, u32[]{:S(2)}) copy-start(bf16[4,2,96,1024]{3,2,1,0:T(8,128)(2,1)S(1)} %weight_parts.2.token_a) | copy-start | bytes 4718596
  74.6 5.8 %copy-start.8 = (bf16[256,768]{1,0:T(8,128)(2,1)}, bf16[256,768]{1,0:T(8,128)(2,1)S(1)}, u32[]{:S(2)}) copy-start(bf16[256,768]{1,0:T(8,128)(2,1)S(1)} %collective-permute-done.13.token_b.refs_7_) | copy-start | bytes 1179652
  75.2 5.7 %copy-start.2 = (bf16[256,768]{1,0:T(8,128)(2,1)S(1)}, bf16[256,768]{1,0:T(8,128)(2,1)}, u32[]{:S(2)}) copy-start(bf16[256,768]{1,0:T(8,128)(2,1)} %refs_2_.5) | copy-start | bytes 1179652
  80.4 19.6 %collective-permute-start.18 = (bf16[256,1792]{1,0:T(8,128)(2,1)S(1)}, bf16[256,1792]{1,0:T(8,128)(2,1)}, u32[]{:S(2)}, u32[]{:S(2)}) collective-permute-start(bf16[256,1792]{1,0:T(8,128)(2,1)S(1)} %get-tuple-element.62.pack_ref.refs_0_.refs_4_), channel_id=1, source_target_pairs={{0,16},{16,0},{32,48},{48,32},{64,80},{80,64},{96,112},{112,96},{1... | collective-permute-start | bytes 2752520 | tf_op jit(solution)/shard_map/ppermute | solution.py:176
  80.9 19.1 %collective-permute-start.19 = (bf16[256,768]{1,0:T(8,128)(2,1)S(1)}, bf16[256,768]{1,0:T(8,128)(2,1)}, u32[]{:S(2)}, u32[]{:S(2)}) collective-permute-start(bf16[256,768]{1,0:T(8,128)(2,1)S(1)} %copy-done.2), channel_id=1, source_target_pairs={{0,16},{16,0},{32,48},{48,32},{64,80},{80,64},{96,112},{112,96},{1... | collective-permute-start | bytes 1179656 | tf_op jit(solution)/shard_map/ppermute | solution.py:176
  81.7 22.5 %collective-permute-start.16 = (bf16[128,768]{1,0:T(8,128)(2,1)}, bf16[128,768]{1,0:T(8,128)(2,1)}, u32[]{:S(2)}, u32[]{:S(2)}) collective-permute-start(bf16[128,768]{1,0:T(8,128)(2,1)} %get-tuple-element.94.refs_0_), channel_id=1, source_target_pairs={{0,4},{1,5},{2,6},{3,7},{4,0},{5,1},{6,2},{7,3},{8,12},{9,13},{10,... | collective-permute-start | bytes 589832 | tf_op jit(solution)/shard_map/ppermute | solution.py:62
  82.3 6.5 %copy-start.29 = (s32[2,16,256]{2,1,0:T(8,128)S(1)}, s32[2,16,256]{2,1,0:T(8,128)}, u32[]{:S(2)}) copy-start(s32[2,16,256]{2,1,0:T(8,128)} %copy-done.28) | copy-start | bytes 98308
  82.3 6.5 %copy-start.31 = (s32[2,16,256]{2,1,0:T(8,128)S(1)}, s32[2,16,256]{2,1,0:T(8,128)}, u32[]{:S(2)}) copy-start(s32[2,16,256]{2,1,0:T(8,128)} %copy-done.30) | copy-start | bytes 98308
  82.3 12.7 %copy-start.3 = (bf16[768,1024]{1,0:T(8,128)(2,1)S(1)}, bf16[768,1024]{1,0:T(8,128)(2,1)}, u32[]{:S(2)}) copy-start(bf16[768,1024]{1,0:T(8,128)(2,1)} %w_sp_hbm.1) | copy-start | bytes 4718596
  82.3 21.9 %collective-permute-start.17 = (bf16[128,768]{1,0:T(8,128)(2,1)S(1)}, bf16[128,768]{1,0:T(8,128)(2,1)}, u32[]{:S(2)}, u32[]{:S(2)}) collective-permute-start(bf16[128,768]{1,0:T(8,128)(2,1)S(1)} %get-tuple-element.93.refs_2_), channel_id=1, source_target_pairs={{0,12},{1,13},{2,14},{3,15},{4,8},{5,9},{6,10},{7,11},{8,4},{9,5},... | collective-permute-start | bytes 589832 | tf_op jit(solution)/shard_map/ppermute | solution.py:62
  84.5 49.3 %all-to-all-start.2 = ((bf16[4,2,96,1024]{3,2,1,0:T(8,128)(2,1)}), bf16[4,2,96,1024]{3,2,1,0:T(8,128)(2,1)}, u32[]{:S(2)}, u32[]{:S(2)}) async-start(bf16[4,2,96,1024]{3,2,1,0:T(8,128)(2,1)} %copy-done), calls=%async_computation.2 | async-start | bytes 3145728 | tf_op jit(solution)/shard_map/all_to_all | solution.py:521
  88.9 5.6 %collective-permute-start.14 = (s32[4,16,256]{2,1,0:T(8,128)S(1)}, s32[4,16,256]{2,1,0:T(8,128)S(1)}, u32[]{:S(2)}, u32[]{:S(2)}) collective-permute-start(s32[4,16,256]{2,1,0:T(8,128)S(1)} %join.13.refs_0_), channel_id=1, source_target_pairs={{0,12},{1,13},{2,14},{3,15},{4,8},{5,9},{6,10},{7,11},{8,4},{9,5},... | collective-permute-start | bytes 196616 | tf_op jit(solution)/shard_map/ppermute | solution.py:62
  94.4 18.7 %collective-permute-start.15 = (s32[8,16,256]{2,1,0:T(8,128)S(1)}, s32[8,16,256]{2,1,0:T(8,128)S(1)}, u32[]{:S(2)}, u32[]{:S(2)}) collective-permute-start(s32[8,16,256]{2,1,0:T(8,128)S(1)} %join.14.a_ref), channel_id=1, source_target_pairs={{0,3},{1,2},{2,1},{3,0},{4,7},{5,6},{6,5},{7,4},{8,11},{9,10},{10,... | collective-permute-start | bytes 393224 | tf_op jit(solution)/shard_map/ppermute | solution.py:62
  97.3 2.7 %copy-start.9 = (bf16[256,768]{1,0:T(8,128)(2,1)S(1)}, bf16[256,768]{1,0:T(8,128)(2,1)}, u32[]{:S(2)}) copy-start(bf16[256,768]{1,0:T(8,128)(2,1)} %copy-done.8) | copy-start | bytes 1179652
  97.3 2.7 %copy-start.22 = (bf16[256,768]{1,0:T(8,128)(2,1)S(1)}, bf16[256,768]{1,0:T(8,128)(2,1)}, u32[]{:S(2)}) copy-start(bf16[256,768]{1,0:T(8,128)(2,1)} %get-tuple-element.58.refs_6_) | copy-start | bytes 1179652
  104.2 14.5 %copy-start.13 = (bf16[3,96,512]{2,1,0:T(8,128)(2,1)}, bf16[3,96,512]{2,1,0:T(8,128)(2,1)S(1)}, u32[]{:S(2)}) copy-start(bf16[3,96,512]{2,1,0:T(8,128)(2,1)S(1)} %get-tuple-element.65.refs_4_.refs_0_) | copy-start | bytes 884740
  104.2 14.5 %copy-start.25 = (bf16[3,96,512]{2,1,0:T(8,128)(2,1)}, bf16[3,96,512]{2,1,0:T(8,128)(2,1)S(1)}, u32[]{:S(2)}) copy-start(bf16[3,96,512]{2,1,0:T(8,128)(2,1)S(1)} %get-tuple-element.84.refs_4_) | copy-start | bytes 884740
  105.6 17.7 %collective-permute-start.20 = (bf16[256,768]{1,0:T(8,128)(2,1)S(1)}, bf16[256,768]{1,0:T(8,128)(2,1)S(1)}, u32[]{:S(2)}, u32[]{:S(2)}) collective-permute-start(bf16[256,768]{1,0:T(8,128)(2,1)S(1)} %get-tuple-element.66.token_ref.refs_0_), channel_id=1, source_target_pairs={{0,1},{1,0},{2,3},{3,2},{4,5},{5,4},{6,7},{7,6},{8,9},{9,8},{10,11... | collective-permute-start | bytes 1179656 | tf_op jit(solution)/shard_map/ppermute | solution.py:62
  106.5 16.8 %collective-permute-start.21 = (bf16[256,768]{1,0:T(8,128)(2,1)S(1)}, bf16[256,768]{1,0:T(8,128)(2,1)S(1)}, u32[]{:S(2)}, u32[]{:S(2)}) collective-permute-start(bf16[256,768]{1,0:T(8,128)(2,1)S(1)} %get-tuple-element.67.refs_2_), channel_id=1, source_target_pairs={{0,3},{1,2},{2,1},{3,0},{4,7},{5,6},{6,5},{7,4},{8,11},{9,10},{10,... | collective-permute-start | bytes 1179656 | tf_op jit(solution)/shard_map/ppermute | solution.py:62
  108.5 11.1 %collective-permute-start.22 = (bf16[3,96,512]{2,1,0:T(8,128)(2,1)S(1)}, bf16[3,96,512]{2,1,0:T(8,128)(2,1)S(1)}, u32[]{:S(2)}, u32[]{:S(2)}) collective-permute-start(bf16[3,96,512]{2,1,0:T(8,128)(2,1)S(1)} %get-tuple-element.68), channel_id=1, source_target_pairs={{0,32},{16,48},{32,64},{48,80},{64,96},{80,112},{96,0},{112,16},{1... | collective-permute-start | bytes 884744 | tf_op jit(solution)/shard_map/ppermute | solution.py:183
  110.5 12.8 %collective-permute-start.23 = (bf16[3,96,512]{2,1,0:T(8,128)(2,1)S(1)}, bf16[3,96,512]{2,1,0:T(8,128)(2,1)S(1)}, u32[]{:S(2)}, u32[]{:S(2)}) collective-permute-start(bf16[3,96,512]{2,1,0:T(8,128)(2,1)S(1)} %get-tuple-element.69), channel_id=1, source_target_pairs={{0,64},{16,80},{32,96},{48,112},{64,0},{80,16},{96,32},{112,48},{1... | collective-permute-start | bytes 884744 | tf_op jit(solution)/shard_map/ppermute | solution.py:183
  113.2 10.2 %collective-permute-start.24 = (bf16[3,96,512]{2,1,0:T(8,128)(2,1)S(1)}, bf16[3,96,512]{2,1,0:T(8,128)(2,1)S(1)}, u32[]{:S(2)}, u32[]{:S(2)}) collective-permute-start(bf16[3,96,512]{2,1,0:T(8,128)(2,1)S(1)} %get-tuple-element.70), channel_id=1, source_target_pairs={{0,96},{16,112},{32,0},{48,16},{64,32},{80,48},{96,64},{112,80},{1... | collective-permute-start | bytes 884744 | tf_op jit(solution)/shard_map/ppermute | solution.py:183
  118.7 12.9 %copy-start.24 = (bf16[256,768]{1,0:T(8,128)(2,1)S(1)}, bf16[256,768]{1,0:T(8,128)(2,1)}, u32[]{:S(2)}) copy-start(bf16[256,768]{1,0:T(8,128)(2,1)} %get-tuple-element.79.a_ref) | copy-start | bytes 1179652
  124.7 16.7 %collective-permute-start.25 = (bf16[512,768]{1,0:T(8,128)(2,1)}, bf16[512,768]{1,0:T(8,128)(2,1)}, u32[]{:S(2)}, u32[]{:S(2)}) collective-permute-start(bf16[512,768]{1,0:T(8,128)(2,1)} %get-tuple-element.71.refs_0_), channel_id=1, source_target_pairs={{0,12},{1,13},{2,14},{3,15},{4,8},{5,9},{6,10},{7,11},{8,4},{9,5},... | collective-permute-start | bytes 2359304 | tf_op jit(solution)/shard_map/ppermute | solution.py:62
  126.1 15.3 %collective-permute-start.26 = (bf16[512,768]{1,0:T(8,128)(2,1)}, bf16[512,768]{1,0:T(8,128)(2,1)}, u32[]{:S(2)}, u32[]{:S(2)}) collective-permute-start(bf16[512,768]{1,0:T(8,128)(2,1)} %get-tuple-element.72.refs_2_), channel_id=1, source_target_pairs={{0,4},{1,5},{2,6},{3,7},{4,0},{5,1},{6,2},{7,3},{8,12},{9,13},{10,... | collective-permute-start | bytes 2359304 | tf_op jit(solution)/shard_map/ppermute | solution.py:62
  126.7 14.0 %collective-permute-start.27 = (bf16[3,96,512]{2,1,0:T(8,128)(2,1)}, bf16[3,96,512]{2,1,0:T(8,128)(2,1)S(1)}, u32[]{:S(2)}, u32[]{:S(2)}) collective-permute-start(bf16[3,96,512]{2,1,0:T(8,128)(2,1)} %get-tuple-element.73), channel_id=1, source_target_pairs={{0,32},{16,48},{32,64},{48,80},{64,96},{80,112},{96,0},{112,16},{1... | collective-permute-start | bytes 884744 | tf_op jit(solution)/shard_map/ppermute | solution.py:183
  127.8 13.6 %collective-permute-start.28 = (bf16[3,96,512]{2,1,0:T(8,128)(2,1)}, bf16[3,96,512]{2,1,0:T(8,128)(2,1)}, u32[]{:S(2)}, u32[]{:S(2)}) collective-permute-start(bf16[3,96,512]{2,1,0:T(8,128)(2,1)} %get-tuple-element.74), channel_id=1, source_target_pairs={{0,64},{16,80},{32,96},{48,112},{64,0},{80,16},{96,32},{112,48},{1... | collective-permute-start | bytes 884744 | tf_op jit(solution)/shard_map/ppermute | solution.py:183
  130.2 11.2 %collective-permute-start.29 = (bf16[3,96,512]{2,1,0:T(8,128)(2,1)}, bf16[3,96,512]{2,1,0:T(8,128)(2,1)}, u32[]{:S(2)}, u32[]{:S(2)}) collective-permute-start(bf16[3,96,512]{2,1,0:T(8,128)(2,1)} %get-tuple-element.75), channel_id=1, source_target_pairs={{0,96},{16,112},{32,0},{48,16},{64,32},{80,48},{96,64},{112,80},{1... | collective-permute-start | bytes 884744 | tf_op jit(solution)/shard_map/ppermute | solution.py:183
  133.7 31.1 %all-to-all-start.1 = ((bf16[128,8,768]{2,1,0:T(8,128)(2,1)}), bf16[128,8,768]{2,1,0:T(8,128)(2,1)}, u32[]{:S(2)}, u32[]{:S(2)}) async-start(bf16[128,8,768]{2,1,0:T(8,128)(2,1)} %bitcast.14), calls=%async_computation.1 | async-start | bytes 3145728 | tf_op jit(solution)/shard_map/all_to_all | solution.py:153
  140.6 6.7 %copy-start.14 = (bf16[3,96,512]{2,1,0:T(8,128)(2,1)S(1)}, bf16[3,96,512]{2,1,0:T(8,128)(2,1)}, u32[]{:S(2)}) copy-start(bf16[3,96,512]{2,1,0:T(8,128)(2,1)} %copy-done.13) | copy-start | bytes 884740
  140.6 6.7 %copy-start.26 = (bf16[3,96,512]{2,1,0:T(8,128)(2,1)S(1)}, bf16[3,96,512]{2,1,0:T(8,128)(2,1)}, u32[]{:S(2)}) copy-start(bf16[3,96,512]{2,1,0:T(8,128)(2,1)} %copy-done.25) | copy-start | bytes 884740
  145.0 38.8 %collective-permute-start.30 = (bf16[1024,768]{1,0:T(8,128)(2,1)}, bf16[1024,768]{1,0:T(8,128)(2,1)}, u32[]{:S(2)}, u32[]{:S(2)}) collective-permute-start(bf16[1024,768]{1,0:T(8,128)(2,1)} %get-tuple-element.76.b0), channel_id=1, source_target_pairs={{0,3},{1,2},{2,1},{3,0},{4,7},{5,6},{6,5},{7,4},{8,11},{9,10},{10,... | collective-permute-start | bytes 4718600 | tf_op jit(solution)/shard_map/ppermute | solution.py:62
  147.2 36.7 %collective-permute-start.31 = (bf16[1024,768]{1,0:T(8,128)(2,1)}, bf16[1024,768]{1,0:T(8,128)(2,1)}, u32[]{:S(2)}, u32[]{:S(2)}) collective-permute-start(bf16[1024,768]{1,0:T(8,128)(2,1)} %get-tuple-element.77.b1), channel_id=1, source_target_pairs={{0,1},{1,0},{2,3},{3,2},{4,5},{5,4},{6,7},{7,6},{8,9},{9,8},{10,11... | collective-permute-start | bytes 4718600 | tf_op jit(solution)/shard_map/ppermute | solution.py:62
  150.5 21.0 %collective-permute-start.32 = (bf16[256,512]{1,0:T(8,128)(2,1)}, bf16[256,512]{1,0:T(8,128)(2,1)S(1)}, u32[]{:S(2)}, u32[]{:S(2)}) collective-permute-start(bf16[256,512]{1,0:T(8,128)(2,1)} %get-tuple-element.86), channel_id=1, source_target_pairs={{0,4},{1,5},{2,6},{3,7},{4,8},{5,9},{6,10},{7,11},{8,12},{9,13},{1... | collective-permute-start | bytes 786440 | tf_op jit(solution)/shard_map/ppermute | solution.py:462
  157.7 14.8 %collective-permute-start.33 = (bf16[256,512]{1,0:T(8,128)(2,1)}, bf16[256,512]{1,0:T(8,128)(2,1)}, u32[]{:S(2)}, u32[]{:S(2)}) collective-permute-start(bf16[256,512]{1,0:T(8,128)(2,1)} %get-tuple-element.87), channel_id=1, source_target_pairs={{0,8},{1,9},{2,10},{3,11},{4,12},{5,13},{6,14},{7,15},{8,0},{9,1},... | collective-permute-start | bytes 786440 | tf_op jit(solution)/shard_map/ppermute | solution.py:462
  159.4 13.2 %collective-permute-start.34 = (bf16[256,512]{1,0:T(8,128)(2,1)}, bf16[256,512]{1,0:T(8,128)(2,1)}, u32[]{:S(2)}, u32[]{:S(2)}) collective-permute-start(bf16[256,512]{1,0:T(8,128)(2,1)} %get-tuple-element.88), channel_id=1, source_target_pairs={{0,12},{1,13},{2,14},{3,15},{4,0},{5,1},{6,2},{7,3},{8,4},{9,5},{1... | collective-permute-start | bytes 786440 | tf_op jit(solution)/shard_map/ppermute | solution.py:462
  174.8 12.7 %collective-permute-start.35 = (f32[64,512]{1,0:T(8,128)S(1)}, f32[64,512]{1,0:T(8,128)S(1)}, u32[]{:S(2)}, u32[]{:S(2)}) collective-permute-start(f32[64,512]{1,0:T(8,128)S(1)} %get-tuple-element.90), channel_id=1, source_target_pairs={{0,1},{1,2},{2,3},{3,0},{4,5},{5,6},{6,7},{7,4},{8,9},{9,10},{10,1... | collective-permute-start | bytes 393224 | tf_op jit(solution)/shard_map/ppermute | solution.py:462
  176.9 10.6 %collective-permute-start.36 = (f32[64,512]{1,0:T(8,128)S(1)}, f32[64,512]{1,0:T(8,128)S(1)}, u32[]{:S(2)}, u32[]{:S(2)}) collective-permute-start(f32[64,512]{1,0:T(8,128)S(1)} %get-tuple-element.91), channel_id=1, source_target_pairs={{0,2},{1,3},{2,0},{3,1},{4,6},{5,7},{6,4},{7,5},{8,10},{9,11},{10,... | collective-permute-start | bytes 393224 | tf_op jit(solution)/shard_map/ppermute | solution.py:462
  179.6 7.9 %collective-permute-start.37 = (f32[64,512]{1,0:T(8,128)S(1)}, f32[64,512]{1,0:T(8,128)S(1)}, u32[]{:S(2)}, u32[]{:S(2)}) collective-permute-start(f32[64,512]{1,0:T(8,128)S(1)} %get-tuple-element.92), channel_id=1, source_target_pairs={{0,3},{1,0},{2,1},{3,2},{4,7},{5,4},{6,5},{7,6},{8,11},{9,8},{10,9... | collective-permute-start | bytes 393224 | tf_op jit(solution)/shard_map/ppermute | solution.py:462
  (12 other events, 17.3 us)
